TPU v7x, 32 devices: a whole 2x2x4 slice. The times are simulated.
32 devices in a mesh: batch: 4 (over y, x), fsdp: 8 (over z, core).
Axes of the slice: x: 2, y: 2, z: 4, core: 2. Of those that a mesh axis runs over, the one named last changes fastest.
Arguments:
- x_small: bfloat16 [64, 10, 10, 256], P(('batch', 'fsdp')), may hold values from -6 to 6
- x_mid: bfloat16 [64, 14, 14, 256], P(('batch', 'fsdp')), may hold values from -6 to 6
- x_large: bfloat16 [64, 18, 18, 256], P(('batch', 'fsdp')), may hold values from -6 to 6
- cot_small: bfloat16 [64, 5, 5, 512], P(('batch', 'fsdp')), may hold values from -6 to 6
- cot_mid: bfloat16 [64, 7, 7, 512], P(('batch', 'fsdp')), may hold values from -6 to 6
- cot_large: bfloat16 [64, 9, 9, 512], P(('batch', 'fsdp')), may hold values from -6 to 6
- counts: int32 [32, 3], P(('batch', 'fsdp')), may hold values from 1 to 2, as said below
- w_first: bfloat16 [3, 3, 256, 512], P(None, None, None, 'fsdp'), may hold values from -0.125 to 0.125
- gain_first: bfloat16 [512], P('fsdp'), may hold values from 0.5 to 1.5
- shift_first: bfloat16 [512], P('fsdp'), may hold values from -3 to 3
- w_second: bfloat16 [3, 3, 512, 512], P(None, None, None, 'fsdp'), may hold values from -0.09375 to 0.09375
- gain_second: bfloat16 [512], P('fsdp'), may hold values from 0.5 to 1.5
- shift_second: bfloat16 [512], P('fsdp'), may hold values from -3 to 3
- w_short: bfloat16 [256, 512], P(None, 'fsdp'), may hold values from -0.375 to 0.375
- gain_short: bfloat16 [512], P('fsdp'), may hold values from 0.5 to 1.5
- shift_short: bfloat16 [512], P('fsdp'), may hold values from -3 to 3
Outputs:
- out_small: bfloat16 [64, 5, 5, 512], P(('batch', 'fsdp'))
- out_mid: bfloat16 [64, 7, 7, 512], P(('batch', 'fsdp'))
- out_large: bfloat16 [64, 9, 9, 512], P(('batch', 'fsdp'))
- dx_small: bfloat16 [64, 10, 10, 256], P(('batch', 'fsdp'))
- dx_mid: bfloat16 [64, 14, 14, 256], P(('batch', 'fsdp'))
- dx_large: bfloat16 [64, 18, 18, 256], P(('batch', 'fsdp'))
- grad_w_first: float32 [3, 3, 256, 512], P(None, None, None, 'fsdp')
- grad_gain_first: float32 [512], P('fsdp')
- grad_shift_first: float32 [512], P('fsdp')
- grad_w_second: float32 [3, 3, 512, 512], P(None, None, None, 'fsdp')
- grad_gain_second: float32 [512], P('fsdp')
- grad_shift_second: float32 [512], P('fsdp')
- grad_w_short: float32 [256, 512], P(None, 'fsdp')
- grad_gain_short: float32 [512], P('fsdp')
- grad_shift_short: float32 [512], P('fsdp')
Inputs may be any that keep to these rules, and one draw needn't show every extreme that they name: counts[d, g] live slots of device d in group g come first among its 2 slots; some device has 2 in some group and another 1.
All inputs are finite; a program needn't handle non-finite values.
Results may differ from a plain program's by a relative error of at most 0.0095.
Values may be sent and summed in bfloat16 or wider, within the bound.
No kernel may reach another device: no remote copies, remote signals or barrier semaphores. Data moves between devices by JAX's collectives and lax.ppermute only.
A program may use at most 128 MiB of HBM per device.

v0:
```python
import jax
import jax.numpy as jnp
from jax import lax
from jax.sharding import PartitionSpec as P

EPSILON = 1e-05


def conv_forward(field, kernel, stride, margin):
    return lax.conv_general_dilated(
        field,
        kernel,
        (stride, stride),
        ((margin, margin), (margin, margin)),
        dimension_numbers=("NHWC", "HWIO", "NHWC"),
        preferred_element_type=jnp.float32,
    )


def conv_input_grad(grad, kernel, stride, margin, extent):
    reach = kernel.shape[0]
    outer = grad.shape[1]
    low_pad = reach - 1 - margin
    high_pad = extent + reach - 2 - low_pad - stride * (outer - 1)
    flipped = jnp.transpose(kernel[::-1, ::-1], (0, 1, 3, 2))
    return lax.conv_general_dilated(
        grad,
        flipped,
        (1, 1),
        ((low_pad, high_pad), (low_pad, high_pad)),
        lhs_dilation=(stride, stride),
        dimension_numbers=("NHWC", "HWIO", "NHWC"),
        preferred_element_type=jnp.float32,
    )


def conv_weight_grad(field, grad, stride, margin, reach):
    outer = grad.shape[1]
    extent = field.shape[1]
    high_pad = stride * (outer - 1) + reach - extent - margin
    return lax.conv_general_dilated(
        field,
        grad,
        (1, 1),
        ((margin, high_pad), (margin, high_pad)),
        rhs_dilation=(stride, stride),
        dimension_numbers=("CHWN", "IHWO", "HWNC"),
        preferred_element_type=jnp.float32,
    )


def silu_slope(value):
    gate_value = jax.nn.sigmoid(value)
    return gate_value * (1.0 + value * (1.0 - gate_value))


def moments(parts, masks):
    first = sum(
        (jnp.sum(mask_one * value, axis=(0, 1, 2)) for value, mask_one in zip(parts, masks))
    )
    second = sum(
        (jnp.sum(mask_one * value * value, axis=(0, 1, 2)) for value, mask_one in zip(parts, masks))
    )
    return (first, second)


def normalize(parts, first, second, total, gain, shift):
    center = first / total
    spread = second / total - center * center
    factor = lax.rsqrt(spread + EPSILON)
    normed = [(value - center) * factor for value in parts]
    return (normed, factor, [value * gain + shift for value in normed])


def norm_back(grad, normed, factor, gain, mask_one, sum_grad, sum_prod, total):
    return (gain * factor * (grad - mask_one * (sum_grad + normed * sum_prod) / total)).astype(
        jnp.bfloat16
    )


def masked_total(parts, masks):
    return sum((jnp.sum(mask_one * value, axis=(0, 1, 2)) for value, mask_one in zip(parts, masks)))


def local(
    x_small,
    x_mid,
    x_large,
    cot_small,
    cot_mid,
    cot_large,
    counts,
    w_first,
    gain_first,
    shift_first,
    w_second,
    gain_second,
    shift_second,
    w_short,
    gain_short,
    shift_short,
):
    fields = (x_small, x_mid, x_large)
    slots = x_small.shape[0]
    cin = x_small.shape[3]
    owned = gain_first.shape[0]
    whole = (
        lax.all_gather(w_first, "fsdp", axis=3, tiled=True),
        lax.all_gather(w_second, "fsdp", axis=3, tiled=True),
        lax.all_gather(w_short, "fsdp", axis=1, tiled=True),
        lax.all_gather(gain_first, "fsdp", axis=0, tiled=True),
        lax.all_gather(shift_first, "fsdp", axis=0, tiled=True),
        lax.all_gather(gain_second, "fsdp", axis=0, tiled=True),
        lax.all_gather(shift_second, "fsdp", axis=0, tiled=True),
        lax.all_gather(gain_short, "fsdp", axis=0, tiled=True),
        lax.all_gather(shift_short, "fsdp", axis=0, tiled=True),
    )
    kern_first = whole[0]
    kern_second = whole[1]
    cout = kern_first.shape[3]
    kern_short = whole[2].reshape(1, 1, cin, cout)
    gain_one = whole[3].astype(jnp.float32)
    shift_one = whole[4].astype(jnp.float32)
    gain_two = whole[5].astype(jnp.float32)
    shift_two = whole[6].astype(jnp.float32)
    gain_side = whole[7].astype(jnp.float32)
    shift_side = whole[8].astype(jnp.float32)
    extents = [field.shape[1] for field in fields]
    outers = [(extent + 1) // 2 for extent in extents]
    live = (jnp.arange(slots, dtype=jnp.int32)[None, :] < counts[0][:, None]).astype(jnp.float32)
    masks = [live[group][:, None, None, None] for group in range(3)]
    areas = jnp.array([float(outer * outer) for outer in outers], jnp.float32)
    total_local = jnp.sum(live * areas[:, None])
    conv_first = [conv_forward(field, kern_first, 2, 1) for field in fields]
    conv_short = [conv_forward(field, kern_short, 2, 0) for field in fields]
    first_a, first_b = moments(conv_first, masks)
    side_a, side_b = moments(conv_short, masks)
    first_a, first_b, side_a, side_b, total = lax.psum(
        (first_a, first_b, side_a, side_b, total_local), ("batch", "fsdp")
    )
    normed_one, factor_one, pre_one = normalize(
        conv_first, first_a, first_b, total, gain_one, shift_one
    )
    hidden = [jax.nn.silu(value).astype(jnp.bfloat16) for value in pre_one]
    conv_second = [conv_forward(value, kern_second, 1, 1) for value in hidden]
    second_a, second_b = moments(conv_second, masks)
    second_a, second_b = lax.psum((second_a, second_b), ("batch", "fsdp"))
    normed_two, factor_two, pre_two = normalize(
        conv_second, second_a, second_b, total, gain_two, shift_two
    )
    normed_side, factor_side, pre_side = normalize(
        conv_short, side_a, side_b, total, gain_side, shift_side
    )
    summed = [left + right for left, right in zip(pre_two, pre_side)]
    outputs = [
        (jax.nn.silu(value) * mask_one).astype(jnp.bfloat16)
        for value, mask_one in zip(summed, masks)
    ]
    cots = (cot_small, cot_mid, cot_large)
    grad_sum = [
        cot.astype(jnp.float32) * mask_one * silu_slope(value)
        for cot, mask_one, value in zip(cots, masks, summed)
    ]
    sum_grad, prod_two, prod_side = lax.psum(
        (
            masked_total(grad_sum, [1.0, 1.0, 1.0]),
            masked_total([g * n for g, n in zip(grad_sum, normed_two)], [1.0, 1.0, 1.0]),
            masked_total([g * n for g, n in zip(grad_sum, normed_side)], [1.0, 1.0, 1.0]),
        ),
        ("batch", "fsdp"),
    )
    grad_two = [
        norm_back(g, n, factor_two, gain_two, m, sum_grad, prod_two, total)
        for g, n, m in zip(grad_sum, normed_two, masks)
    ]
    grad_side = [
        norm_back(g, n, factor_side, gain_side, m, sum_grad, prod_side, total)
        for g, n, m in zip(grad_sum, normed_side, masks)
    ]
    again = (
        lax.all_gather(w_first, "fsdp", axis=3, tiled=True),
        lax.all_gather(w_second, "fsdp", axis=3, tiled=True),
        lax.all_gather(w_short, "fsdp", axis=1, tiled=True),
    )
    back_first = again[0]
    back_second = again[1]
    back_short = again[2].reshape(1, 1, cin, cout)
    dw_second = sum((conv_weight_grad(h, g, 1, 1, 3) for h, g in zip(hidden, grad_two)))
    dw_short = sum((conv_weight_grad(f, g, 2, 0, 1) for f, g in zip(fields, grad_side))).reshape(
        cin, cout
    )
    hidden_grad = [
        conv_input_grad(g, back_second, 1, 1, outer) for g, outer in zip(grad_two, outers)
    ]
    grad_pre = [h * silu_slope(p) for h, p in zip(hidden_grad, pre_one)]
    sum_one, prod_one = lax.psum(
        (
            masked_total(grad_pre, masks),
            masked_total([g * n for g, n in zip(grad_pre, normed_one)], masks),
        ),
        ("batch", "fsdp"),
    )
    grad_one = [
        norm_back(g, n, factor_one, gain_one, m, sum_one, prod_one, total)
        for g, n, m in zip(grad_pre, normed_one, masks)
    ]
    dw_first = sum((conv_weight_grad(f, g, 2, 1, 3) for f, g in zip(fields, grad_one)))
    input_grads = []
    for part_one, part_side, extent in zip(grad_one, grad_side, extents):
        from_first = conv_input_grad(part_one, back_first, 2, 1, extent)
        from_short = conv_input_grad(part_side, back_short, 2, 0, extent)
        input_grads.append((from_first + from_short).astype(jnp.bfloat16))
    part_first, part_second, part_short = (
        lax.psum_scatter(dw_first, "fsdp", scatter_dimension=3, tiled=True),
        lax.psum_scatter(dw_second, "fsdp", scatter_dimension=3, tiled=True),
        lax.psum_scatter(dw_short, "fsdp", scatter_dimension=1, tiled=True),
    )
    part_first, part_second, part_short = (
        lax.psum(part_first.astype(jnp.bfloat16), "batch").astype(jnp.float32),
        lax.psum(part_second.astype(jnp.bfloat16), "batch").astype(jnp.float32),
        lax.psum(part_short.astype(jnp.bfloat16), "batch").astype(jnp.float32),
    )
    offset = lax.axis_index("fsdp") * owned

    def mine(vector):
        return lax.dynamic_slice_in_dim(vector, offset, owned)

    return (
        outputs[0],
        outputs[1],
        outputs[2],
        input_grads[0],
        input_grads[1],
        input_grads[2],
        part_first,
        mine(prod_one),
        mine(sum_one),
        part_second,
        mine(prod_two),
        mine(sum_grad),
        part_short,
        mine(prod_side),
        mine(sum_grad),
    )


def solution(mesh):
    in_specs = (
        P(("batch", "fsdp"), None, None, None),
        P(("batch", "fsdp"), None, None, None),
        P(("batch", "fsdp"), None, None, None),
        P(("batch", "fsdp"), None, None, None),
        P(("batch", "fsdp"), None, None, None),
        P(("batch", "fsdp"), None, None, None),
        P(("batch", "fsdp"), None),
        P(None, None, None, "fsdp"),
        P("fsdp"),
        P("fsdp"),
        P(None, None, None, "fsdp"),
        P("fsdp"),
        P("fsdp"),
        P(None, "fsdp"),
        P("fsdp"),
        P("fsdp"),
    )
    out_specs = (
        P(("batch", "fsdp"), None, None, None),
        P(("batch", "fsdp"), None, None, None),
        P(("batch", "fsdp"), None, None, None),
        P(("batch", "fsdp"), None, None, None),
        P(("batch", "fsdp"), None, None, None),
        P(("batch", "fsdp"), None, None, None),
        P(None, None, None, "fsdp"),
        P("fsdp"),
        P("fsdp"),
        P(None, None, None, "fsdp"),
        P("fsdp"),
        P("fsdp"),
        P(None, "fsdp"),
        P("fsdp"),
        P("fsdp"),
    )
    return jax.shard_map(local, mesh=mesh, in_specs=in_specs, out_specs=out_specs, check_vma=False)
```

profile of v0, /device:TPU:0, one launch (start us, length us, event | category | flops | bytes accessed | tf_op | source)
XLA Modules:
  0.0 560.0 jit_solution(10746402087017152189)
XLA Ops:
  15.8 19.1 %all-reduce.10 = (bf16[512]{0:T(512)(128)(2,1)S(1)}, bf16[512]{0:T(512)(128)(2,1)S(1)}, bf16[512]{0:T(512)(128)(2,1)S(1)}, bf16[512]{0:T(512)(128)(2,1)S(1)}, bf...) all-reduce(bf16[512]{0:T(512)(128)(2,1)S(1)} %dynamic-update-slice., ...), channel_id=1, replica_groups=mesh['batch'=4,'fsdp'=8] {'fsdp'}, use_global_device_ids=true, to_apply=%add.5 | all-reduce | flops 3072 | bytes 12288
  39.7 14.2 %all_gather.36 = bf16[256,512]{0,1:T(8,128)(2,1)S(1)} all-gather(bf16[256,64]{0,1:T(8,128)(2,1)S(1)} %copy-done.67), channel_id=1, replica_groups=mesh['batch'=4,'fsdp'=8] {'fsdp'}, dimensions={1}, use_global_device_ids=true | all-gather | bytes 294912 | tf_op jit(solution)/shard_map/all_gather | solution.py:110
  54.6 1.9 multiply_reduce_fusion.1
  56.5 2.8 multiply_reduce_fusion.6
  59.3 2.6 fusion.66
  63.0 41.2 %all-reduce.9 = (f32[512]{0:T(512)S(1)}, f32[]{:T(128)}, f32[512]{0:T(512)S(1)}) all-reduce(f32[512]{0:T(512)S(1)} %add_add_fusion.12, f32[]{:T(128)} %select_reduce_fusion.6, f32[512]{0:T(512)S(1)} %add_add_fusion.13), channel_id=1, replica_groups=mesh['batch'=4,'fsdp'=8] {'batch','fsdp'}, use_global_device_ids=true, to_apply=%region_9.0 | all-reduce | flops 1025 | bytes 8200 | tf_op jit(solution)/shard_map/psum | solution.py:138
  111.3 4.2 fusion.102
  115.9 1.6 fusion.13
  117.5 2.5 select_reduce_fusion.1
  120.0 1.6 fusion.63
  121.7 40.8 %all-reduce.8 = (f32[512]{0:T(512)S(1)}, f32[512]{0:T(512)S(1)}, f32[512]{0:T(512)S(1)}, f32[512]{0:T(512)S(1)}) all-reduce(f32[512]{0:T(512)S(1)} %add_add_fusion.10, f32[512]{0:T(512)S(1)} %add_add_fusion.11, f32[512]{0:T(512)S(1)} %get-tuple-element.172, ...), channel_id=1, replica_groups=mesh['batch'=4,'fsdp'=8] {'batch','fsdp'}, use_global_device_ids=true, to_apply=%region_17.0 | all-reduce | flops 2048 | bytes 16384 | tf_op jit(solution)/shard_map/psum | solution.py:147
  165.8 1.6 add_multiply_fusion
  168.7 2.3 reshape.126
  172.3 2.3 reshape.144
  175.9 2.3 reshape.130
  178.2 1.7 multiply_reduce_fusion.10
  179.9 3.2 fusion.84
  183.1 3.0 fusion.45
  187.3 40.5 %all-reduce.7 = (f32[512]{0:T(512)}, f32[512]{0:T(512)}) all-reduce(f32[512]{0:T(512)} %add_add_fusion.7, f32[512]{0:T(512)} %add_add_fusion.6), channel_id=1, replica_groups=mesh['batch'=4,'fsdp'=8] {'batch','fsdp'}, use_global_device_ids=true, to_apply=%region_29.30 | all-reduce | flops 1024 | bytes 8192 | tf_op jit(solution)/shard_map/psum | solution.py:164
  227.7 2.4 fusion.72
  232.9 2.3 reshape.136
  236.3 1.6 fusion.43
  239.3 5.6 multiply_reduce_fusion.9
  244.9 2.8 multiply_reduce_fusion.3
  247.7 3.8 multiply_reduce_fusion
  252.7 40.8 %all-reduce.6 = (f32[512]{0:T(512)}, f32[512]{0:T(512)}, f32[512]{0:T(512)}) all-reduce(f32[512]{0:T(512)} %add_add_fusion.3, f32[512]{0:T(512)} %add_add_fusion.4, f32[512]{0:T(512)} %add_add_fusion.5), channel_id=1, replica_groups=mesh['batch'=4,'fsdp'=8] {'batch','fsdp'}, use_global_device_ids=true, to_apply=%region_45.46 | all-reduce | flops 1536 | bytes 12288 | tf_op jit(solution)/shard_map/psum | solution.py:164
  293.5 2.1 fusion.70
  295.6 2.7 multiply_divide_fusion
  299.2 2.7 fusion.103
  303.6 3.9 add_add_fusion
  310.8 2.6 fusion.28
  313.5 2.4 fusion.101
  315.9 6.5 %bitcast_add_fusion = f32[3,3,512,512]{2,3,1,0:T(8,128)} fusion(f32[3,3,512,512]{2,3,1,0:T(8,128)S(1)} %fusion.101, f32[3,3,512,512,1]{2,3,1,4,0:T(8,128)S(1)} %fusion.28, bf16[9,16,2,512,1]{3,2,1,0,4:T(2,128)(2,1)S(1)} %reshape.110, bf16[9,16,2,512,1]{3,1,2,0,4:T(8,128)(2,1)S(1)} %get-tuple-element.175, bf16[9,16,2,512,1]{3,1,2,0,4:T(8,128)(2,1)S(1)} %fusion.146, ...), kind=kOutput, calls=%fused_computation | convolution fusion | flops 1263894528 | bytes 29491200 | tf_op jit(solution)/shard_map/conv_general_dilated | solution.py:41
  324.4 1.5 multiply_convert_fusion.5
  326.6 1.8 multiply_convert_fusion.3
  330.9 3.1 fusion.109
  334.1 2.9 fusion.110
  337.0 26.5 %reduce-scatter.6.cloned.1.call-done = f32[3,3,256,64]{2,3,1,0:T(8,128)} async-done(((f32[3,3,256,512]{2,3,1,0:T(8,128)}), f32[3,3,256,64]{2,3,1,0:T(8,128)}) %reduce-scatter.6.cloned.1.call-update) | async-done | bytes 589840 | tf_op jit(solution)/shard_map/reduce_scatter | solution.py:214
  363.5 1.8 convert_element_type.130
  365.3 98.2 %reduce-scatter.8.cloned.1.call-done = f32[3,3,512,64]{2,3,1,0:T(8,128)} async-done(((f32[3,3,512,512]{2,3,1,0:T(8,128)}), f32[3,3,512,64]{2,3,1,0:T(8,128)}) %reduce-scatter.8.cloned.1.call-update) | async-done | bytes 1179664 | tf_op jit(solution)/shard_map/reduce_scatter | solution.py:215
  463.6 2.2 convert_element_type.132
  470.3 2.3 fusion.1
  472.6 2.2 fusion.4
  474.8 20.2 %reduce-scatter.10.cloned.1.call-done = f32[64,256]{1,0:T(8,128)} async-done(((f32[512,256]{1,0:T(8,128)}), f32[64,256]{1,0:T(8,128)}) %reduce-scatter.10.cloned.1.call-update) | async-done | bytes 65552
  495.9 16.9 %psum.119 = bf16[256,64]{1,0:T(8,128)(2,1)S(1)} all-reduce(bf16[256,64]{1,0:T(8,128)(2,1)S(1)} %copy.146), channel_id=1, replica_groups=mesh['batch'=4,'fsdp'=8] {'batch'}, use_global_device_ids=true, to_apply=%region_51.52 | all-reduce | flops 16384 | bytes 65536 | tf_op jit(solution)/shard_map/psum | solution.py:221
  513.6 34.6 %all-reduce.14.cloned.1.call-done = (bf16[3,3,256,64]{2,3,1,0:T(8,128)(2,1)}, bf16[3,3,512,64]{2,3,1,0:T(8,128)(2,1)}) async-done(((bf16[3,3,256,64]{2,3,1,0:T(8,128)(2,1)}, bf16[3,3,512,64]{2,3,1,0:T(8,128)(2,1)}), (bf16[3,3,256,64]{2,3,1,0:T(8,128)(2,1)}, bf16[3,3,512,64]{2,3,1,0:T(8,128)(2,1)})) %all-reduce.14.cloned.1.call-update) | async-done | bytes 884752 | tf_op jit(solution)/shard_map/psum | solution.py:219
  548.1 1.8 convert_element_type.131
  550.0 2.2 convert_element_type.133
  (306 shorter events, 53.6 us)
Async XLA Ops:
  7.2 49.3 %copy-start = (bf16[2,10,10,256]{3,0,2,1:T(2,128)(2,1)S(1)}, bf16[2,10,10,256]{3,0,2,1:T(2,128)(2,1)}, u32[]{:S(2)}) copy-start(bf16[2,10,10,256]{3,0,2,1:T(2,128)(2,1)} %param.17) | copy-start | bytes 307204
  7.2 31.1 %copy-start.1 = (bf16[2,18,18,256]{3,0,2,1:T(2,128)(2,1)S(1)}, bf16[2,18,18,256]{3,0,2,1:T(2,128)(2,1)}, u32[]{:S(2)}) copy-start(bf16[2,18,18,256]{3,0,2,1:T(2,128)(2,1)} %param.19) | copy-start | bytes 995332
  7.2 31.9 %copy-start.84 = (s32[1,3]{1,0:T(1,128)S(1)}, s32[1,3]{1,0:T(1,128)}, u32[]{:S(2)}) copy-start(s32[1,3]{1,0:T(1,128)} %param.23) | copy-start | bytes 40
  7.2 49.3 %all-gather.3.cloned.1.call-start = ((), (), s32[]{:S(2)}) async-start(), calls=%async_computation.3 | async-start | bytes 2654208 | tf_op jit(solution)/shard_map/all_gather | solution.py:108
  8.0 31.7 %copy-start.67 = (bf16[256,64]{0,1:T(8,128)(2,1)S(1)}, bf16[256,64]{0,1:T(8,128)(2,1)}, u32[]{:S(2)}) copy-start(bf16[256,64]{0,1:T(8,128)(2,1)} %param.30) | copy-start | bytes 98308
  8.0 103.3 %all-gather.5.cloned.1.call-start = ((), (), s32[]{:S(2)}) async-start(), calls=%async_computation.4 | async-start | bytes 5308416 | tf_op jit(solution)/shard_map/all_gather | solution.py:109
  8.7 45.2 %copy-start.88 = (f32[3]{0:T(128)S(1)}, f32[3]{0:T(128)}, u32[]{:S(2)}) copy-start(f32[3]{0:T(128)} %constant.30.clone) | copy-start | bytes 40
  8.7 354.8 %reduce-scatter.6.cloned.1.call-start = ((), (), s32[]{:S(2)}) async-start(), calls=%async_computation.5 | async-start | bytes 5308416 | tf_op jit(solution)/shard_map/reduce_scatter | solution.py:214
  34.9 143.3 %copy-start.61 = (f32[512]{0:T(512)}, f32[512]{0:T(512)S(1)}, u32[]{:S(2)}) copy-start(f32[512]{0:T(512)S(1)} %convert_element_type.111) | copy-start | bytes 6148
  34.9 76.3 %copy-start.44 = (f32[512]{0:T(512)}, f32[512]{0:T(512)S(1)}, u32[]{:S(2)}) copy-start(f32[512]{0:T(512)S(1)} %convert_element_type.104) | copy-start | bytes 6148
  34.9 76.3 %copy-start.46 = (f32[512]{0:T(512)}, f32[512]{0:T(512)S(1)}, u32[]{:S(2)}) copy-start(f32[512]{0:T(512)S(1)} %convert_element_type.103) | copy-start | bytes 6148
  35.0 143.2 %copy-start.62 = (f32[512]{0:T(512)}, f32[512]{0:T(512)S(1)}, u32[]{:S(2)}) copy-start(f32[512]{0:T(512)S(1)} %convert_element_type.109) | copy-start | bytes 6148
  35.0 143.2 %copy-start.63 = (f32[512]{0:T(512)}, f32[512]{0:T(512)S(1)}, u32[]{:S(2)}) copy-start(f32[512]{0:T(512)S(1)} %convert_element_type.110) | copy-start | bytes 6148
  35.0 143.2 %copy-start.64 = (f32[512]{0:T(512)}, f32[512]{0:T(512)S(1)}, u32[]{:S(2)}) copy-start(f32[512]{0:T(512)S(1)} %convert_element_type.108) | copy-start | bytes 6148
  38.3 21.0 %copy-start.82 = (pred[16]{0:T(512)(128)(4,1)S(1)}, pred[16]{0:T(512)(128)(4,1)}, u32[]{:S(2)}) copy-start(pred[16]{0:T(512)(128)(4,1)} %constant.93) | copy-start | bytes 52
  39.2 22.8 %copy-start.78 = (f32[2]{0:T(128)}, f32[2]{0:T(128)S(1)}, u32[]{:S(2)}) copy-start(f32[2]{0:T(128)S(1)} %get-tuple-element.154) | copy-start | bytes 28
  39.2 80.8 %copy-start.75 = (f32[2]{0:T(128)}, f32[2]{0:T(128)S(1)}, u32[]{:S(2)}) copy-start(f32[2]{0:T(128)S(1)} %get-tuple-element.153) | copy-start | bytes 28
  39.2 139.0 %copy-start.73 = (f32[2]{0:T(128)}, f32[2]{0:T(128)S(1)}, u32[]{:S(2)}) copy-start(f32[2]{0:T(128)S(1)} %get-tuple-element.155) | copy-start | bytes 28
  59.3 51.9 %copy-start.5 = (f32[2,5,5,512]{3,0,2,1:T(2,128)}, f32[2,5,5,512]{3,0,2,1:T(2,128)S(1)}, u32[]{:S(2)}) copy-start(f32[2,5,5,512]{3,0,2,1:T(2,128)S(1)} %get-tuple-element.161) | copy-start | bytes 307204
  105.4 5.8 %copy-start.40 = (f32[512]{0:T(512)}, f32[512]{0:T(512)S(1)}, u32[]{:S(2)}) copy-start(f32[512]{0:T(512)S(1)} %get-tuple-element.118) | copy-start | bytes 6148
  105.4 5.8 %copy-start.42 = (f32[512]{0:T(512)}, f32[512]{0:T(512)S(1)}, u32[]{:S(2)}) copy-start(f32[512]{0:T(512)S(1)} %get-tuple-element.152) | copy-start | bytes 6148
  109.3 6.6 %copy-start.2 = (bf16[9,2,8,2,512]{4,2,1,3,0:T(8,128)(2,1)}, bf16[9,2,8,2,512]{4,2,1,3,0:T(8,128)(2,1)S(1)}, u32[]{:S(2)}) copy-start(bf16[9,2,8,2,512]{4,2,1,3,0:T(8,128)(2,1)S(1)} %fusion.149) | copy-start | bytes 884740
  109.4 6.5 %copy-start.18 = (bf16[9,2,8,1,512]{4,2,1,3,0:T(8,128)(2,1)}, bf16[9,2,8,1,512]{4,2,1,3,0:T(8,128)(2,1)S(1)}, u32[]{:S(2)}) copy-start(bf16[9,2,8,1,512]{4,2,1,3,0:T(8,128)(2,1)S(1)} %pad.9) | copy-start | bytes 442372
  109.4 6.4 %copy-start.20 = (bf16[9,2,8,1,512]{4,2,1,3,0:T(8,128)(2,1)}, bf16[9,2,8,1,512]{4,2,1,3,0:T(8,128)(2,1)S(1)}, u32[]{:S(2)}) copy-start(bf16[9,2,8,1,512]{4,2,1,3,0:T(8,128)(2,1)S(1)} %pad.10) | copy-start | bytes 442372
  109.5 5.9 %copy-start.36 = (bf16[256,512]{0,1:T(8,128)(2,1)S(1)}, bf16[256,512]{0,1:T(8,128)(2,1)}, u32[]{:S(2)}) copy-start(bf16[256,512]{0,1:T(8,128)(2,1)} %copy-done.35) | copy-start | bytes 786436
  115.9 62.3 %copy-start.25 = (f32[2,5,5,512]{3,0,2,1:T(2,128)}, f32[2,5,5,512]{3,0,2,1:T(2,128)S(1)}, u32[]{:S(2)}) copy-start(f32[2,5,5,512]{3,0,2,1:T(2,128)S(1)} %get-tuple-element.164) | copy-start | bytes 307204
  121.6 54.3 %copy-start.11 = (f32[7,16,1,512]{3,1,2,0:T(8,128)}, f32[7,16,1,512]{3,1,2,0:T(8,128)S(1)}, u32[]{:S(2)}) copy-start(f32[7,16,1,512]{3,1,2,0:T(8,128)S(1)} %get-tuple-element.165) | copy-start | bytes 688132
  163.7 14.5 %copy-start.56 = (f32[512]{0:T(512)}, f32[512]{0:T(512)S(1)}, u32[]{:S(2)}) copy-start(f32[512]{0:T(512)S(1)} %get-tuple-element.124) | copy-start | bytes 6148
  163.7 14.5 %copy-start.58 = (f32[512]{0:T(512)}, f32[512]{0:T(512)S(1)}, u32[]{:S(2)}) copy-start(f32[512]{0:T(512)S(1)} %get-tuple-element.151) | copy-start | bytes 6148
  165.0 13.2 %copy-start.51 = (f32[512]{0:T(512)}, f32[512]{0:T(512)S(1)}, u32[]{:S(2)}) copy-start(f32[512]{0:T(512)S(1)} %get-tuple-element.120) | copy-start | bytes 6148
  165.0 13.2 %copy-start.53 = (f32[512]{0:T(512)}, f32[512]{0:T(512)S(1)}, u32[]{:S(2)}) copy-start(f32[512]{0:T(512)S(1)} %get-tuple-element.150) | copy-start | bytes 6148
  165.8 12.4 %copy-start.29 = (f32[2,5,5,512]{3,0,2,1:T(2,128)S(1)}, f32[2,5,5,512]{3,0,2,1:T(2,128)}, u32[]{:S(2)}) copy-start(f32[2,5,5,512]{3,0,2,1:T(2,128)} %copy-done.28) | copy-start | bytes 307204
  165.8 12.4 %copy-start.60 = (bf16[2,5,5,512]{3,0,2,1:T(2,128)(2,1)S(1)}, bf16[2,5,5,512]{3,0,2,1:T(2,128)(2,1)}, u32[]{:S(2)}) copy-start(bf16[2,5,5,512]{3,0,2,1:T(2,128)(2,1)} %param.20) | copy-start | bytes 153604
  236.3 8.5 %copy-start.33 = (bf16[2,7,7,512]{3,0,2,1:T(2,128)(2,1)}, bf16[2,7,7,512]{3,0,2,1:T(2,128)(2,1)S(1)}, u32[]{:S(2)}) copy-start(bf16[2,7,7,512]{3,0,2,1:T(2,128)(2,1)S(1)} %fusion.82) | copy-start | bytes 301060
  236.3 8.5 %slice-start.2 = ((s8[4718592]{0:T(1024)(128)(4,1)}), s8[4194304]{0:T(1024)(128)(4,1)S(1)}, s32[]{:S(2)}) async-start(s8[4718592]{0:T(1024)(128)(4,1)} %bitcast.311), calls=%async_computation.11 | async-start | bytes 8388608
  237.9 9.8 %copy-start.16 = (bf16[2,9,9,512]{3,0,2,1:T(2,128)(2,1)}, bf16[2,9,9,512]{3,0,2,1:T(2,128)(2,1)S(1)}, u32[]{:S(2)}) copy-start(bf16[2,9,9,512]{3,0,2,1:T(2,128)(2,1)S(1)} %fusion.43) | copy-start | bytes 497668
  239.3 5.6 %copy-start.39 = (f32[7,2,8,512]{3,2,1,0:T(8,128)S(1)}, f32[7,2,8,512]{3,2,1,0:T(8,128)}, u32[]{:S(2)}) copy-start(f32[7,2,8,512]{3,2,1,0:T(8,128)} %get-tuple-element.141) | copy-start | bytes 688132
  239.3 5.6 %copy-start.76 = (f32[2]{0:T(128)S(1)}, f32[2]{0:T(128)}, u32[]{:S(2)}) copy-start(f32[2]{0:T(128)} %copy-done.75) | copy-start | bytes 28
  239.3 5.7 %slice-start.3 = ((s8[4718592]{0:T(1024)(128)(4,1)}), s8[524288]{0:T(1024)(128)(4,1)S(1)}, s32[]{:S(2)}) async-start(s8[4718592]{0:T(1024)(128)(4,1)} %bitcast.311), calls=%async_computation.12 | async-start | bytes 1048576
  307.6 156.0 %reduce-scatter.8.cloned.1.call-start = ((), (), s32[]{:S(2)}) async-start(), calls=%async_computation.6 | async-start | bytes 10616832 | tf_op jit(solution)/shard_map/reduce_scatter | solution.py:215
  322.5 172.5 %reduce-scatter.10.cloned.1.call-start = ((), (), s32[]{:S(2)}) async-start(), calls=%async_computation.7 | async-start | bytes 589824
  330.3 217.8 %all-reduce.14.cloned.1.call-start = ((), (), s32[]{:S(2)}) async-start(), calls=%async_computation.8 | async-start | bytes 1769472 | tf_op jit(solution)/shard_map/psum | solution.py:219
  334.0 131.7 %copy-start.37 = (bf16[256,512]{0,1:T(8,128)(2,1)S(1)}, bf16[256,512]{0,1:T(8,128)(2,1)}, u32[]{:S(2)}) copy-start(bf16[256,512]{0,1:T(8,128)(2,1)} %copy-done.35) | copy-start | bytes 786436
  334.0 133.2 %copy-start.69 = (f32[512]{0:T(512)S(1)}, f32[512]{0:T(512)}, u32[]{:S(2)}) copy-start(f32[512]{0:T(512)} %get-tuple-element.98) | copy-start | bytes 6148
  334.0 133.8 %copy-start.70 = (f32[512]{0:T(512)S(1)}, f32[512]{0:T(512)}, u32[]{:S(2)}) copy-start(f32[512]{0:T(512)} %get-tuple-element.99) | copy-start | bytes 6148
  365.3 107.3 %copy-start.50 = (f32[2,5,5,512]{3,0,2,1:T(2,128)S(1)}, f32[2,5,5,512]{3,0,2,1:T(2,128)}, u32[]{:S(2)}) copy-start(f32[2,5,5,512]{3,0,2,1:T(2,128)} %get-tuple-element.168) | copy-start | bytes 307204
  465.8 6.8 %copy-start.87 = (bf16[3,3,256,512]{2,3,1,0:T(8,128)(2,1)S(1)}, bf16[3,3,256,512]{2,3,1,0:T(8,128)(2,1)}, u32[]{:S(2)}) copy-start(bf16[3,3,256,512]{2,3,1,0:T(8,128)(2,1)} %all-gather.3.cloned.1.call-done) | copy-start | bytes 7077892
  466.1 86.1 %copy-start.89 = (f32[64]{0:T(128)}, f32[64]{0:T(128)S(1)}, u32[]{:S(2)}) copy-start(f32[64]{0:T(128)S(1)} %dynamic_slice.19) | copy-start | bytes 772
  (52 other events, 141.8 us)
Sparse Core Ops, SparseCore 0:
  9.7 35.5 all-gather.2
  46.9 51.5 all-gather.4
  307.7 55.7 reduce-scatter.5
  365.7 97.8 reduce-scatter.7
  465.7 29.2 reduce-scatter.9
  498.9 49.1 all-reduce.13
where the time goes:
time: 567 us; the launch traced here: 560 us
  blocking collectives  213 us (38%)
  waiting for transfers between devices  181 us (32%)
  matrix products  62.7 us (11%)
  other arithmetic  44.4 us (8%)
  local copies, waits for them, and re-layouts  41.1 us (7%)
  between operations  16.8 us (3%)
    reduce_scatter x1, waiting for transfers between devices, local(): lax.psum_scatter(dw_second, 'fsdp', scatter_dimension=3, tiled=True)  98.2 us
    psum x2, blocking collectives, local(): lax.psum((masked_total(grad_sum, [1.0, 1.0, 1.0]), masked_total([g * n fo...  81.3 us
    psum x1, blocking collectives, local(): lax.psum((first_a, first_b, side_a, side_b, total_local), ('batch', 'fsdp'))  41.2 us
    psum x1, blocking collectives, local(): second_a, second_b = lax.psum((second_a, second_b), ('batch', 'fsdp'))  40.8 us
    psum x1, waiting for transfers between devices, local(): lax.psum(part_first.astype(jnp.bfloat16), 'batch').astype(jnp.float32)  34.6 us
    reduce_scatter x1, waiting for transfers between devices, local(): lax.psum_scatter(dw_first, 'fsdp', scatter_dimension=3, tiled=True)  26.5 us
    conv_general_dilated x9, matrix products, conv_input_grad(): lax.conv_general_dilated(grad, flipped, (1, 1), ((low_pad, high_pad), (lo...  23.9 us
    unnamed x7, waiting for transfers between devices  21.7 us
  transfers between devices with their start and end apart: 6, of which 4 were waited for; matrix products, arithmetic and copies ran while one was open for 12% of the time, Pallas kernels for 0%

commit v1 on v0

v1 whole, which is shorter than its diff:
```python
import functools

import jax
import jax.numpy as jnp
import numpy as np
from jax import lax
from jax.experimental import pallas as pl
from jax.experimental.pallas import tpu as pltpu
from jax.sharding import PartitionSpec as P

EPSILON = 1e-05
F32 = jnp.float32
BF16 = jnp.bfloat16
ROWS = 16
VMEM_LIMIT = 56 * 2**20


def up(value, step):
    return -(-value // step) * step


class Plan:
    def __init__(self, sides, slots):
        self.sides, self.slots = sides, slots
        self.starts, self.sizes, row = [], [], 0
        for index, side in enumerate(sides):
            width = side + 1
            after = sides[index + 1] + 1 if index + 1 < len(sides) else 0
            size = up(slots * (width * width + max(0, width + 1 - after)), ROWS)
            self.starts.append(row)
            self.sizes.append(size)
            row += size
        self.rows = row
        self.margin = up(slots * (max(sides) + 2), ROWS)
        self.span = self.rows + 2 * self.margin

    def segments(self):
        return list(zip(self.starts, self.sizes, [side + 1 for side in self.sides]))


def cells(plan, group, value):
    slots, side = value.shape[0], value.shape[1]
    value = jnp.pad(jnp.transpose(value, (1, 2, 0, 3)), ((1, 0), (1, 0), (0, 0), (0, 0)))
    value = value.reshape((side + 1) * (side + 1) * slots, value.shape[3])
    return jnp.pad(value, ((0, plan.sizes[group] - value.shape[0]), (0, 0)))


def images(plan, group, rows):
    side, slots = plan.sides[group], plan.slots
    start, count = plan.starts[group], (side + 1) * (side + 1) * slots
    value = rows[start : start + count].reshape(side + 1, side + 1, slots, rows.shape[1])
    return jnp.transpose(value[1:, 1:], (2, 0, 1, 3))


def nn(left, right):
    return lax.dot_general(left, right, (((1,), (0,)), ((), ())), preferred_element_type=F32)


def nt(left, right):
    return lax.dot_general(left, right, (((1,), (1,)), ((), ())), preferred_element_type=F32)


def column(value):
    return jnp.sum(value, axis=0, keepdims=True)


def wide(mask_ref, channels):
    return jnp.concatenate([mask_ref[...]] * (channels // mask_ref.shape[1]), axis=1)


def silu_slope(value):
    gate = jax.nn.sigmoid(value)
    return gate * (1.0 + value * (1.0 - gate))


def norm(value, sums, row, total):
    center = sums[row : row + 1] / total
    spread = sums[row + 1 : row + 2] / total - center * center
    factor = lax.rsqrt(spread + EPSILON)
    return (value - center) * factor, factor


def put_rows(ref, rows):
    for index, row in enumerate(rows):
        ref[index : index + 1, :] = row
    ref[len(rows) :, :] = jnp.zeros((ref.shape[0] - len(rows), ref.shape[1]), F32)


def offsets(plan, width):
    return [plan.slots * (dy * width + dx) for dy in (-1, 0, 1) for dx in (-1, 0, 1)]


def unfold(plan, padded_ref, out_ref, sign):
    channels = padded_ref.shape[1]
    for start, size, width in plan.segments():
        for tap, offset in enumerate(offsets(plan, width)):
            first = plan.margin + start + sign * offset
            out_ref[start : start + size, tap * channels : (tap + 1) * channels] = padded_ref[
                first : first + size, :
            ].astype(BF16)


def fill(plan, padded_ref, value):
    edge = jnp.zeros((plan.margin, padded_ref.shape[1]), F32)
    padded_ref[: plan.margin, :] = edge
    padded_ref[plan.margin : plan.margin + plan.rows, :] = value
    padded_ref[plan.margin + plan.rows :, :] = edge


def patches_kernel(plan, planes_ref, out_ref, held_ref):
    channels = planes_ref.shape[2]
    held_ref[...] = planes_ref[...].astype(F32)
    for start, size, width in plan.segments():
        for ky in range(3):
            for kx in range(3):
                tap = ky * 3 + kx
                shift = plan.slots * (width * (ky == 0) + (kx == 0))
                first = plan.margin + start - shift
                out_ref[start : start + size, tap * channels : (tap + 1) * channels] = held_ref[
                    2 * (ky != 1) + (kx != 1), first : first + size, :
                ].astype(BF16)


def first_kernel(patches_ref, weights_ref, mask_ref, first_ref, side_ref, sums_ref):
    cin = weights_ref.shape[2]
    cout = weights_ref.shape[1]
    total = nt(patches_ref[:, :cin], weights_ref[0])
    for tap in range(1, 9):
        total += nt(patches_ref[:, tap * cin : (tap + 1) * cin], weights_ref[tap])
    side = nt(patches_ref[:, 4 * cin : 5 * cin], weights_ref[9])
    first_ref[...] = total
    side_ref[...] = side
    mask = wide(mask_ref, cout)
    put_rows(
        sums_ref,
        [
            column(mask * total),
            column(mask * total * total),
            column(mask * side),
            column(mask * side * side),
            column(mask),
        ],
    )


def second_kernel(plan, sums_ref, first_ref, mask_ref, vec_ref, weights_ref, second_ref, patches_ref, out_ref, held_ref):
    cout = first_ref.shape[1]
    mask = wide(mask_ref, cout)
    sums = sums_ref[...]
    normed, _ = norm(first_ref[...], sums, 0, sums[4:5])
    pre = normed * vec_ref[0:1] + vec_ref[1:2]
    fill(plan, held_ref, jax.nn.silu(pre) * mask)
    unfold(plan, held_ref, patches_ref, 1)
    total = nt(patches_ref[:, :cout], weights_ref[0])
    for tap in range(1, 9):
        total += nt(patches_ref[:, tap * cout : (tap + 1) * cout], weights_ref[tap])
    second_ref[...] = total
    put_rows(out_ref, [column(mask * total), column(mask * total * total)])


def output_kernel(sums_ref, sums_two_ref, second_ref, side_ref, cot_ref, mask_ref, vec_ref, out_ref, dz_ref, sums_out_ref):
    cout = second_ref.shape[1]
    mask = wide(mask_ref, cout)
    sums = sums_ref[...]
    total = sums[4:5]
    normed_two, _ = norm(second_ref[...], sums_two_ref[...], 0, total)
    normed_side, _ = norm(side_ref[...], sums, 2, total)
    value = (normed_two * vec_ref[2:3] + vec_ref[3:4]) + (normed_side * vec_ref[4:5] + vec_ref[5:6])
    gate = jax.nn.sigmoid(value)
    out_ref[...] = (value * gate * mask).astype(BF16)
    grad = cot_ref[...].astype(F32) * mask * (gate * (1.0 + value * (1.0 - gate)))
    dz_ref[...] = grad
    put_rows(sums_out_ref, [column(grad), column(grad * normed_two), column(grad * normed_side)])


def back_second_kernel(
    plan, sums_ref, sums_two_ref, sums_z_ref, first_ref, second_ref, side_ref, dz_ref, mask_ref, vec_ref, weights_ref,
    grad_two_ref, grad_side_ref, dy_ref, out_ref, held_ref, patches_ref,
):
    cout = first_ref.shape[1]
    mask = wide(mask_ref, cout)
    sums, sums_z = sums_ref[...], sums_z_ref[...]
    total = sums[4:5]
    grad = dz_ref[...]
    normed, factor = norm(second_ref[...], sums_two_ref[...], 0, total)
    two = vec_ref[2:3] * factor * (grad - mask * (sums_z[0:1] + normed * sums_z[1:2]) / total)
    normed, factor = norm(side_ref[...], sums, 2, total)
    side = vec_ref[4:5] * factor * (grad - mask * (sums_z[0:1] + normed * sums_z[2:3]) / total)
    grad_side_ref[...] = side.astype(BF16)
    grad_two_ref[...] = two.astype(BF16)
    fill(plan, held_ref, two)
    unfold(plan, held_ref, patches_ref, -1)
    back = nn(patches_ref[:, :cout], weights_ref[0])
    for tap in range(1, 9):
        back += nn(patches_ref[:, tap * cout : (tap + 1) * cout], weights_ref[tap])
    normed, _ = norm(first_ref[...], sums, 0, total)
    pre = normed * vec_ref[0:1] + vec_ref[1:2]
    grad = back * silu_slope(pre) * mask
    dy_ref[...] = grad
    put_rows(out_ref, [column(grad), column(grad * normed)])


def back_first_kernel(sums_ref, sums_y_ref, first_ref, dy_ref, mask_ref, vec_ref, grad_ref):
    cout = first_ref.shape[1]
    mask = wide(mask_ref, cout)
    sums, sums_y = sums_ref[...], sums_y_ref[...]
    total = sums[4:5]
    normed, factor = norm(first_ref[...], sums, 0, total)
    grad = vec_ref[0:1] * factor * (dy_ref[...] - mask * (sums_y[0:1] + normed * sums_y[1:2]) / total)
    grad_ref[...] = grad.astype(BF16)


class Order:
    def __init__(self, batch, fsdp, owned):
        self.zs, self.quarter, self.owned = fsdp // 2, owned // batch, owned
        half = self.zs // 2
        self.parts = []
        for core in range(2):
            self.parts.append([(core, b, z) for b in (0, 2, 1, 3) for z in range(half)])
            self.parts.append([(core, b, z) for b in (0, 1, 2, 3) for z in range(half, self.zs)])

    def starts(self, place_ref):
        core, b, z = place_ref[0], place_ref[1], place_ref[2]
        for part in self.parts:
            for rel_core, rel_b, rel_z in part:
                row = ((z ^ rel_z) * 2 + (core ^ rel_core)) * self.owned + (b ^ rel_b) * self.quarter
                yield pl.multiple_of(row, self.quarter)


def correlate(order, place_ref, grads, patch_refs, out_refs, turned_ref, lhs_ref):
    quarter = order.quarter
    for index, grad in enumerate(grads):
        turned_ref[...] = grad.T
        for block, start in enumerate(order.starts(place_ref)):
            lhs_ref[block * quarter : (block + 1) * quarter, :] = turned_ref[pl.ds(start, quarter), :]
        left = lhs_ref[...]
        for tap, (ref, first, size) in patch_refs[index]:
            value = nn(left, ref[:, first : first + size]).astype(BF16)
            begin = 0
            for out_ref in out_refs:
                count = out_ref.shape[0]
                out_ref[:, tap] = value[begin : begin + count * quarter].reshape(count, quarter, size)
                begin += count * quarter


def weight_second_kernel(order, place_ref, grad_ref, patches_ref, *refs):
    outs, (turned_ref, lhs_ref) = refs[:-2], refs[-2:]
    cout = grad_ref.shape[1]
    taps = [(tap, (patches_ref, tap * cout, cout)) for tap in range(9)]
    correlate(order, place_ref, [grad_ref[...]], [taps], outs, turned_ref, lhs_ref)


def weight_first_kernel(order, place_ref, grad_ref, side_ref, patches_ref, *refs):
    outs, (turned_ref, lhs_ref) = refs[:-2], refs[-2:]
    cin = patches_ref.shape[1] // 9
    taps = [(tap, (patches_ref, tap * cin, cin)) for tap in range(9)]
    center = [(9, (patches_ref, 4 * cin, cin))]
    correlate(order, place_ref, [grad_ref[...], side_ref[...]], [taps, center], outs, turned_ref, lhs_ref)


def plain_weight_kernel(taps, grad_ref, patches_ref, out_ref):
    turned = grad_ref[...].T
    channels = out_ref.shape[2]
    for index, tap in enumerate(taps):
        out_ref[index] = nn(turned, patches_ref[:, tap * channels : (tap + 1) * channels]).astype(BF16)


def input_kernel(plan, grad_ref, side_ref, weights_ref, out_ref, held_ref, moved_ref):
    rows = plan.rows
    fill(plan, held_ref, grad_ref[...].astype(F32))
    for index, (down, right) in enumerate(((0, 0), (0, 1), (1, 0), (1, 1))):
        for start, size, width in plan.segments():
            first = plan.margin + start + plan.slots * (down * width + right)
            moved_ref[index, start : start + size, :] = held_ref[first : first + size, :].astype(BF16)
    for py in range(2):
        for px in range(2):
            total = None
            for ky in (0, 2) if py else (1,):
                for kx in (0, 2) if px else (1,):
                    index = 2 * (ky == 0) + (kx == 0)
                    term = nn(moved_ref[index], weights_ref[ky * 3 + kx])
                    total = term if total is None else total + term
            if py + px == 0:
                total += nn(side_ref[...], weights_ref[9])
            out_ref[2 * py + px] = total.astype(BF16)


def finish_kernel(order, place_ref, *refs):
    parts, outs = refs[:4], refs[4:]
    b, quarter = place_ref[1], order.quarter
    taps = outs[0].shape[0]
    for rel, ref in enumerate(parts):
        rows = pl.ds(pl.multiple_of((b ^ rel) * quarter, quarter), quarter)
        outs[0][:, rows, :] = ref[:taps].astype(F32)
        if len(outs) > 1:
            outs[1][rows, :] = ref[taps].astype(F32)


def call(body, out_shapes, *args, scratch=(), scalars=0, flops=0):
    vmem = pl.BlockSpec(memory_space=pltpu.VMEM)
    specs = [pl.BlockSpec(memory_space=pltpu.SMEM)] * scalars + [vmem] * (len(args) - scalars)
    many = isinstance(out_shapes, (list, tuple))
    moved = sum(arg.size * arg.dtype.itemsize for arg in args)
    return pl.pallas_call(
        body,
        in_specs=specs,
        out_specs=[vmem] * len(out_shapes) if many else vmem,
        out_shape=list(out_shapes) if many else out_shapes,
        scratch_shapes=list(scratch),
        compiler_params=pltpu.CompilerParams(vmem_limit_bytes=VMEM_LIMIT),
        cost_estimate=pl.CostEstimate(flops=flops, bytes_accessed=moved, transcendentals=0),
    )(*args)


def shape(dims, dtype=F32):
    return jax.ShapeDtypeStruct(tuple(dims), dtype)


def exchange(value, axis, count, bit):
    return lax.ppermute(value, axis, [(index, index ^ bit) for index in range(count)])


def bits(count):
    return [1 << index for index in range(count.bit_length() - 1)]


def sum_over(value, axes):
    for axis, count in axes:
        if count & (count - 1):
            value = lax.psum(value, axis)
            continue
        for bit in bits(count):
            value = value + exchange(value, axis, count, bit)
    return value


def reduce_in_plane(parts, core, batch):
    keep_p, keep_q, send_p, send_q = parts
    half_p = keep_p + exchange(send_p, "fsdp", core, 1)
    half_q = keep_q + exchange(send_q, "fsdp", core, 1)
    n_p, n_q = half_p.shape[0] // 4, half_q.shape[0] // 4
    got_p = exchange(half_p[2 * n_p :], "batch", batch, 1)
    got_q = exchange(half_q[2 * n_q :], "batch", batch, 2)
    half_p = half_p[: 2 * n_p] + got_p
    half_q = half_q[: 2 * n_q] + got_q
    got_p = exchange(half_p[n_p:], "batch", batch, 2)
    got_q = exchange(half_q[n_q:], "batch", batch, 1)
    return half_p[:n_p] + got_p, half_q[:n_q] + got_q


def reduce_weights(order, place, parts, batch, fsdp, outs):
    low, high = reduce_in_plane(parts, fsdp, batch)
    pieces = [low[index] for index in range(low.shape[0])] + [high[index] for index in range(high.shape[0])]
    total = pieces[0].astype(F32)
    for rel in range(1, len(pieces)):
        total = total + exchange(pieces[rel], "fsdp", fsdp, 2 * rel).astype(F32)
    mine = total.astype(BF16)
    spread = [mine] + [exchange(mine, "batch", batch, rel) for rel in (1, 2, 3)]
    return call(functools.partial(finish_kernel, order), outs, place, *spread, scalars=1)


def local(
    x_small,
    x_mid,
    x_large,
    cot_small,
    cot_mid,
    cot_large,
    counts,
    w_first,
    gain_first,
    shift_first,
    w_second,
    gain_second,
    shift_second,
    w_short,
    gain_short,
    shift_short,
    *,
    batch,
    fsdp,
):
    fields = (x_small, x_mid, x_large)
    cots = (cot_small, cot_mid, cot_large)
    slots, cin, owned = x_small.shape[0], x_small.shape[3], gain_first.shape[0]
    cout = owned * fsdp
    plan = Plan([cot.shape[1] for cot in cots], slots)
    rows, span = plan.rows, plan.span
    everywhere = (("fsdp", fsdp), ("batch", batch))
    me = lax.axis_index("fsdp")
    fast = batch == 4 and fsdp >= 4 and fsdp & (fsdp - 1) == 0 and owned % (ROWS * batch) == 0
    order = Order(batch, fsdp, owned) if fast else None
    place = jnp.stack([me % 2, lax.axis_index("batch"), me // 2]).astype(jnp.int32)

    own_first = jnp.transpose(w_first, (0, 1, 3, 2)).reshape(9, owned, cin)
    own_second = jnp.transpose(w_second, (0, 1, 3, 2)).reshape(9, owned, cout)
    own_side = jnp.transpose(w_short).reshape(1, owned, cin)
    kern_first = lax.all_gather(jnp.concatenate([own_first, own_side]), "fsdp", axis=1, tiled=True)
    kern_second = lax.all_gather(own_second, "fsdp", axis=1, tiled=True)
    vectors = jnp.stack([gain_first, shift_first, gain_second, shift_second, gain_short, shift_short]).astype(F32)
    vec = lax.dynamic_update_slice(jnp.zeros((8, cout), F32), vectors, (0, me * owned))
    vec = sum_over(vec, (("fsdp", fsdp),))

    planes = []
    for group, field in enumerate(fields):
        side = plan.sides[group]
        split = field.reshape(slots, side, 2, side, 2, cin)
        planes.append(
            jnp.stack([cells(plan, group, split[:, :, py, :, px]) for py in range(2) for px in range(2)])
        )
    planes = jnp.pad(jnp.concatenate(planes, axis=1), ((0, 0), (plan.margin, 0), (0, 0)))
    cot_rows = jnp.concatenate([cells(plan, group, cot) for group, cot in enumerate(cots)])
    mask = []
    for group, side in enumerate(plan.sides):
        valid = np.zeros((side + 1, side + 1, slots), bool)
        valid[1:, 1:] = True
        valid = np.pad(valid.reshape(-1), (0, plan.sizes[group] - valid.size))
        slot = np.arange(plan.sizes[group]) % slots
        mask.append(jnp.asarray(valid) & (jnp.asarray(slot, jnp.int32) < counts[0, group]))
    mask = jnp.broadcast_to(jnp.concatenate(mask).astype(F32)[:, None], (rows, 128))

    patches = call(
        functools.partial(patches_kernel, plan),
        shape((rows, 9 * cin), BF16),
        planes,
        scratch=[pltpu.VMEM((4, plan.margin + rows, cin), F32)],
    )
    flops = 2 * rows * cout * cin * 9
    first, side, sums = call(
        first_kernel,
        [shape((rows, cout)), shape((rows, cout)), shape((8, cout))],
        patches,
        kern_first,
        mask,
        flops=flops,
    )
    sums = sum_over(sums, everywhere)
    second, patches_two, sums_two = call(
        functools.partial(second_kernel, plan),
        [shape((rows, cout)), shape((rows, 9 * cout), BF16), shape((8, cout))],
        sums,
        first,
        mask,
        vec,
        kern_second,
        scratch=[pltpu.VMEM((span, cout), F32)],
        flops=2 * flops,
    )
    sums_two = sum_over(sums_two, everywhere)
    out, dz, sums_z = call(
        output_kernel,
        [shape((rows, cout), BF16), shape((rows, cout)), shape((8, cout))],
        sums,
        sums_two,
        second,
        side,
        cot_rows,
        mask,
        vec,
        flops=50 * rows * cout,
    )
    sums_z = sum_over(sums_z, everywhere)
    grad_two, grad_side, dy, sums_y = call(
        functools.partial(back_second_kernel, plan),
        [shape((rows, cout), BF16), shape((rows, cout), BF16), shape((rows, cout)), shape((8, cout))],
        sums,
        sums_two,
        sums_z,
        first,
        second,
        side,
        dz,
        mask,
        vec,
        kern_second,
        scratch=[pltpu.VMEM((span, cout), F32), pltpu.VMEM((rows, 9 * cout), BF16)],
        flops=2 * flops,
    )
    sums_y = sum_over(sums_y, everywhere)
    if fast:
        turned = [pltpu.VMEM((cout, rows), BF16), pltpu.VMEM((cout, rows), BF16)]
        parts_two = call(
            functools.partial(weight_second_kernel, order),
            [shape((len(part), 9, order.quarter, cout), BF16) for part in order.parts],
            place,
            grad_two,
            patches_two,
            scratch=turned,
            scalars=1,
            flops=2 * flops,
        )
        dw_second = reduce_weights(order, place, parts_two, batch, fsdp, [shape((9, owned, cout))])[0]
    grad_one = call(
        back_first_kernel, shape((rows, cout), BF16), sums, sums_y, first, dy, mask, vec, flops=20 * rows * cout
    )
    if fast:
        parts_one = call(
            functools.partial(weight_first_kernel, order),
            [shape((len(part), 10, order.quarter, cin), BF16) for part in order.parts],
            place,
            grad_one,
            grad_side,
            patches,
            scratch=turned,
            scalars=1,
            flops=flops,
        )
        dw_first, dw_side = reduce_weights(
            order, place, parts_one, batch, fsdp, [shape((9, owned, cin)), shape((owned, cin))]
        )
    else:
        taps = tuple(range(9))
        whole = [
            call(functools.partial(plain_weight_kernel, taps), shape((9, cout, cout), BF16), grad_two, patches_two),
            call(functools.partial(plain_weight_kernel, taps), shape((9, cout, cin), BF16), grad_one, patches),
            call(functools.partial(plain_weight_kernel, (4,)), shape((1, cout, cin), BF16), grad_side, patches),
        ]
        dw_second, dw_first, dw_side = [
            lax.psum(lax.psum_scatter(value, "fsdp", scatter_dimension=1, tiled=True), "batch").astype(F32)
            for value in whole
        ]
        dw_side = dw_side[0]
    dx = call(
        functools.partial(input_kernel, plan),
        shape((4, rows, cin), BF16),
        grad_one,
        grad_side,
        kern_first,
        scratch=[pltpu.VMEM((span, cout), F32), pltpu.VMEM((4, rows, cout), BF16)],
        flops=flops,
    )
    outputs = [images(plan, group, out) for group in range(3)]
    input_grads = []
    for group, side_length in enumerate(plan.sides):
        quarter = [images(plan, group, dx[index]) for index in range(4)]
        whole_rows = [jnp.stack(quarter[2 * py : 2 * py + 2], axis=3) for py in range(2)]
        value = jnp.stack(whole_rows, axis=2)
        input_grads.append(value.reshape(slots, 2 * side_length, 2 * side_length, cin))

    def mine(sums, row):
        return lax.dynamic_slice(sums, (row, me * owned), (1, owned))[0]

    def as_weight(value):
        return jnp.transpose(value.reshape(3, 3, owned, value.shape[2]), (0, 1, 3, 2))

    return (
        outputs[0],
        outputs[1],
        outputs[2],
        input_grads[0],
        input_grads[1],
        input_grads[2],
        as_weight(dw_first),
        mine(sums_y, 1),
        mine(sums_y, 0),
        as_weight(dw_second),
        mine(sums_z, 1),
        mine(sums_z, 0),
        jnp.transpose(dw_side),
        mine(sums_z, 2),
        mine(sums_z, 0),
    )


def solution(mesh):
    split = ("batch", "fsdp")
    image = P(split, None, None, None)
    kernel = P(None, None, None, "fsdp")
    vector = P("fsdp")
    in_specs = (image,) * 6 + (
        P(split, None),
        kernel,
        vector,
        vector,
        kernel,
        vector,
        vector,
        P(None, "fsdp"),
        vector,
        vector,
    )
    out_specs = (image,) * 6 + (
        kernel,
        vector,
        vector,
        kernel,
        vector,
        vector,
        P(None, "fsdp"),
        vector,
        vector,
    )
    body = functools.partial(local, batch=mesh.shape["batch"], fsdp=mesh.shape["fsdp"])
    return jax.shard_map(body, mesh=mesh, in_specs=in_specs, out_specs=out_specs, check_vma=False)
```

time: 567 us -> 281 us (0.50); the launches traced: 560 us -> 280 us
  blocking collectives: 213 us -> 0 us
  matrix products: 62.7 us -> 0 us
  waiting for transfers between devices: 181 us -> 131 us
  Pallas kernels: 0 us -> 48.6 us
  starting transfers between devices: 0.49 us -> 40 us
  other arithmetic: 44.4 us -> 18.4 us
  local copies, waits for them, and re-layouts: 41.1 us -> 27.2 us
    psum x5 -> x0, blocking collectives: 180 us -> none  [the longest x2 81.3 us: local(): lax.psum((masked_total(grad_sum, [1.0, 1.0, 1.0]), masked_total([g * n fo...]
    reduce_scatter x2 -> x0, waiting for transfers between devices: 125 us -> none  [the longest x1 98.2 us: local(): lax.psum_scatter(dw_second, 'fsdp', scatter_dimension=3, tiled=True)]
    ppermute x0 -> x47, waiting for transfers between devices: none -> 75.6 us  [exchange(): lax.ppermute(value, axis, [(index, index ^ bit) for index in range(count)])]
    conv_general_dilated x27 -> x0, matrix products: 62.7 us -> none  [the longest x9 23.9 us: conv_input_grad(): lax.conv_general_dilated(grad, flipped, (1, 1), ((low_pad, high_pad), (lo...]
    all_gather x2, waiting for transfers between devices: 0.01 us -> 54.4 us  [the longest x1 27.7 us: local(): lax.all_gather(jnp.concatenate([own_first, own_side]), 'fsdp', axis=1, ti...]
    pallas_call x0 -> x11, Pallas kernels: none -> 48.6 us  [call(): pl.pallas_call(body, in_specs=specs, out_specs=[vmem] * len(out_shapes) i...]
    ppermute x0 -> x47, starting transfers between devices: none -> 40 us  [exchange(): lax.ppermute(value, axis, [(index, index ^ bit) for index in range(count)])]
    psum x1 -> x0, waiting for transfers between devices: 34.6 us -> none  [local(): lax.psum(part_first.astype(jnp.bfloat16), 'batch').astype(jnp.float32)]
  transfers between devices with their start and end apart: 6 -> 49, of which waited for: 4 -> 29; matrix products, arithmetic and copies ran while one was open for 12% -> 14% of each run, Pallas kernels for 0% -> 10%
where the time goes in v1:
time: 281 us; the launch traced here: 280 us
  waiting for transfers between devices  131 us (47%)
  Pallas kernels  48.6 us (17%)
  starting transfers between devices  40 us (14%)
  local copies, waits for them, and re-layouts  27.2 us (10%)
  other arithmetic  18.4 us (7%)
  between operations  15.1 us (5%)
    ppermute x47, waiting for transfers between devices, exchange(): lax.ppermute(value, axis, [(index, index ^ bit) for index in range(count)])  75.6 us
    pallas_call x11, Pallas kernels, call(): pl.pallas_call(body, in_specs=specs, out_specs=[vmem] * len(out_shapes) i...  48.6 us
    ppermute x47, starting transfers between devices, exchange(): lax.ppermute(value, axis, [(index, index ^ bit) for index in range(count)])  40 us
    all_gather x1, waiting for transfers between devices, local(): lax.all_gather(jnp.concatenate([own_first, own_side]), 'fsdp', axis=1, ti...  27.7 us
    all_gather x1, waiting for transfers between devices, local(): kern_second = lax.all_gather(own_second, 'fsdp', axis=1, tiled=True)  26.7 us
    add x22, other arithmetic, sum_over(): value = value + exchange(value, axis, count, bit)  5.99 us
    slice x6, local copies, waits for them, and re-layouts, images(): rows[start:start + count].reshape(side + 1, side + 1, slots, rows.shape[1])  5.82 us
  transfers between devices with their start and end apart: 49, of which 29 were waited for; matrix products, arithmetic and copies ran while one was open for 14% of the time, Pallas kernels for 10%

profile of v1, /device:TPU:0, one launch (start us, length us, event | category | flops | bytes accessed | tf_op | source)
XLA Modules:
  0.0 280.0 jit_solution(17880993218700977920)
XLA Ops:
  7.2 1.8 pad_maximum_fusion.1
  13.6 2.8 %shard_map.325.patches_ref = bf16[432,2304]{1,0:T(8,128)(2,1)} custom-call(bf16[4,464,256]{2,1,0:T(8,128)(2,1)} %fusion.16.planes_ref), custom_call_target="tpu_custom_call" | custom-call | bytes 950272 | tf_op jit(solution)/shard_map/pallas_call | solution.py:304
  19.2 27.7 %all-gather.3.cloned.1.call-done.weights_ref = bf16[10,512,256]{2,1,0:T(8,128)(2,1)} async-done(((bf16[10,64,256]{2,1,0:T(8,128)(2,1)}), bf16[10,512,256]{2,1,0:T(8,128)(2,1)}) %all-gather.3.cloned.1.call-update) | async-done | bytes 2621456 | tf_op jit(solution)/shard_map/all_gather | solution.py:398
  47.7 4.8 %shard_map.326 = (f32[432,512]{1,0:T(8,128)}, f32[432,512]{1,0:T(8,128)}, f32[8,512]{1,0:T(8,128)}) custom-call(bf16[432,2304]{1,0:T(8,128)(2,1)} %shard_map.325.patches_ref, bf16[10,512,256]{2,1,0:T(8,128)(2,1)} %all-gather.3.cloned.1.call-done.weights_ref, f32[432,128]{1,0:T(8,128)} %broadcast_in_dim.4.mask_ref), custom_call_target="tpu_custom_call" | custom-call | flops 1019215872 | bytes 4833280 | tf_op jit(solution)/shard_map/pallas_call | solution.py:304
  55.9 2.6 collective-permute-done.1
  61.1 4.1 %collective-permute-done.2 = f32[8,512]{1,0:T(8,128)S(1)} collective-permute-done((f32[8,512]{1,0:T(8,128)S(1)}, f32[8,512]{1,0:T(8,128)S(1)}, u32[]{:S(2)}, u32[]{:S(2)}) %collective-permute-start.2) | collective-permute-done | bytes 16416 | tf_op jit(solution)/shard_map/ppermute | solution.py:320
  65.1 1.5 collective-permute-start.3
  66.7 2.2 collective-permute-done.3
  68.9 1.5 collective-permute-start.4
  70.4 2.2 collective-permute-done.7
  73.8 26.7 %all-gather.5.cloned.1.call-done.weights_ref = bf16[9,512,512]{2,1,0:T(8,128)(2,1)} async-done(((bf16[9,64,512]{2,1,0:T(8,128)(2,1)}), bf16[9,512,512]{2,1,0:T(8,128)(2,1)}) %all-gather.5.cloned.1.call-update) | async-done | bytes 4718608 | tf_op jit(solution)/shard_map/all_gather | solution.py:399
  100.4 7.1 %shard_map.327 = (f32[432,512]{1,0:T(8,128)}, bf16[432,4608]{1,0:T(8,128)(2,1)}, f32[8,512]{1,0:T(8,128)}) custom-call(f32[8,512]{1,0:T(8,128)} %add.194.sums_ref, f32[432,512]{1,0:T(8,128)} %get-tuple-element.39.first_ref, f32[432,128]{1,0:T(8,128)} %broadcast_in_dim.4.mask_ref, f32[8,512]{1,0:T(8,128)} %add.198.vec_ref, ...), custom_call_target="tpu_custom_call" | custom-call | flops 2038431744 | bytes 5857280 | tf_op jit(solution)/shard_map/pallas_call | solution.py:304
  109.7 3.7 %collective-permute-done.9 = f32[8,512]{1,0:T(8,128)S(1)} collective-permute-done((f32[8,512]{1,0:T(8,128)S(1)}, f32[8,512]{1,0:T(8,128)S(1)}, u32[]{:S(2)}, u32[]{:S(2)}) %collective-permute-start.9) | collective-permute-done | bytes 16416 | tf_op jit(solution)/shard_map/ppermute | solution.py:320
  114.3 3.8 %collective-permute-done.10 = f32[8,512]{1,0:T(8,128)S(1)} collective-permute-done((f32[8,512]{1,0:T(8,128)S(1)}, f32[8,512]{1,0:T(8,128)S(1)}, u32[]{:S(2)}, u32[]{:S(2)}) %collective-permute-start.10) | collective-permute-done | bytes 16416 | tf_op jit(solution)/shard_map/ppermute | solution.py:320
  118.1 1.5 collective-permute-start.11
  120.1 1.7 collective-permute-done.11
  121.8 1.5 collective-permute-start.12
  124.1 1.4 collective-permute-done.12
  126.2 3.5 %shard_map.328 = (bf16[432,512]{1,0:T(8,128)(2,1)}, f32[432,512]{1,0:T(8,128)}, f32[8,512]{1,0:T(8,128)}) custom-call(f32[8,512]{1,0:T(8,128)} %add.194.sums_ref, f32[8,512]{1,0:T(8,128)} %add.203.sums_two_ref, f32[432,512]{1,0:T(8,128)} %get-tuple-element.41.second_ref, f32[432,512]{1,0:T(8,128)} %get-tuple-element.42.side_ref, ...), custom_call_target="tpu_custom_call" | custom-call | flops 11059200 | bytes 2482176 | tf_op jit(solution)/shard_map/pallas_call | solution.py:304
  129.7 1.4 collective-permute-done.13
  131.8 3.7 %collective-permute-done.14 = f32[8,512]{1,0:T(8,128)S(1)} collective-permute-done((f32[8,512]{1,0:T(8,128)S(1)}, f32[8,512]{1,0:T(8,128)S(1)}, u32[]{:S(2)}, u32[]{:S(2)}) %collective-permute-start.14) | collective-permute-done | bytes 16416 | tf_op jit(solution)/shard_map/ppermute | solution.py:320
  136.3 3.8 %collective-permute-done.15 = f32[8,512]{1,0:T(8,128)S(1)} collective-permute-done((f32[8,512]{1,0:T(8,128)S(1)}, f32[8,512]{1,0:T(8,128)S(1)}, u32[]{:S(2)}, u32[]{:S(2)}) %collective-permute-start.15) | collective-permute-done | bytes 16416 | tf_op jit(solution)/shard_map/ppermute | solution.py:320
  140.2 1.5 collective-permute-start.16
  141.7 2.2 collective-permute-done.16
  143.9 1.5 collective-permute-start.17
  148.2 7.3 %shard_map.329 = (bf16[432,512]{1,0:T(8,128)(2,1)}, bf16[432,512]{1,0:T(8,128)(2,1)}, f32[432,512]{1,0:T(8,128)}, f32[8,512]{1,0:T(8,128)}) custom-call(f32[8,512]{1,0:T(8,128)} %add.194.sums_ref, f32[8,512]{1,0:T(8,128)} %add.203.sums_two_ref, f32[8,512]{1,0:T(8,128)} %add.208.sums_z_ref, f32[432,512]{1,0:T(8,128)} %get-tuple-element.39.first_ref, ...), custom_call_target="tpu_custom_call" | custom-call | flops 2038431744 | bytes 8544256 | tf_op jit(solution)/shard_map/pallas_call | solution.py:304
  159.7 2.1 collective-permute-done.19
  163.3 3.2 %collective-permute-done.20 = f32[8,512]{1,0:T(8,128)S(1)} collective-permute-done((f32[8,512]{1,0:T(8,128)S(1)}, f32[8,512]{1,0:T(8,128)S(1)}, u32[]{:S(2)}, u32[]{:S(2)}) %collective-permute-start.20) | collective-permute-done | bytes 16416 | tf_op jit(solution)/shard_map/ppermute | solution.py:320
  166.4 1.5 collective-permute-start.21
  167.9 7.2 %shard_map.334 = (bf16[8,9,16,512]{3,2,1,0:T(8,128)(2,1)}, bf16[8,9,16,512]{3,2,1,0:T(8,128)(2,1)}, bf16[8,9,16,512]{3,2,1,0:T(8,128)(2,1)}, bf16[8,9,16,512]{3,2,1,0:T(8,128)(2,1)}) custom-call(s32[3]{0:T(128)} %pad_add_fusion.place_ref, bf16[432,512]{1,0:T(8,128)(2,1)} %get-tuple-element.54.grad_ref, bf16[432,4608]{1,0:T(8,128)(2,1)} %get-tuple-element.55.patches_ref), custom_call_target="tpu_custom_call" | custom-call | flops 2038431744 | bytes 4423692 | tf_op jit(solution)/shard_map/pallas_call | solution.py:304
  175.1 1.5 collective-permute-start.22
  176.7 1.4 dynamic-slice_bitcast_fusion
  179.5 2.5 shard_map.330.grad_ref
  182.1 4.3 %shard_map.331 = bf16[4,432,256]{2,1,0:T(8,128)(2,1)} custom-call(bf16[432,512]{1,0:T(8,128)(2,1)} %shard_map.330.grad_ref, bf16[432,512]{1,0:T(8,128)(2,1)} %get-tuple-element.48.side_ref, bf16[10,512,256]{2,1,0:T(8,128)(2,1)} %all-gather.3.cloned.1.call-done.weights_ref), custom_call_target="tpu_custom_call" | custom-call | flops 1019215872 | bytes 3506176 | tf_op jit(solution)/shard_map/pallas_call | solution.py:304
  189.4 4.9 %shard_map.332 = (bf16[8,10,16,256]{3,2,1,0:T(8,128)(2,1)}, bf16[8,10,16,256]{3,2,1,0:T(8,128)(2,1)}, bf16[8,10,16,256]{3,2,1,0:T(8,128)(2,1)}, bf16[8,10,16,256]{3,2,1,0:T(8,128)(2,1)}) custom-call(s32[3]{0:T(128)} %pad_add_fusion.place_ref, bf16[432,512]{1,0:T(8,128)(2,1)} %shard_map.330.grad_ref, bf16[432,512]{1,0:T(8,128)(2,1)} %get-tuple-element.48.side_ref, ...), custom_call_target="tpu_custom_call" | custom-call | flops 1019215872 | bytes 2875404 | tf_op jit(solution)/shard_map/pallas_call | solution.py:304
  205.3 1.5 collective-permute-start.28
  207.8 7.2 %collective-permute-done.28 = bf16[4,10,16,256]{3,2,1,0:T(8,128)(2,1)S(1)} collective-permute-done((bf16[4,10,16,256]{3,2,1,0:T(8,128)(2,1)S(1)}, bf16[4,10,16,256]{3,2,1,0:T(8,128)(2,1)S(1)}, u32[]{:S(2)}, u32[]{:S(2)}) %collective-permute-start.28) | collective-permute-done | bytes 327712 | tf_op jit(solution)/shard_map/ppermute | solution.py:320
  217.9 1.5 collective-permute-start.40
  222.3 1.6 collective-permute-done.25
  223.9 10.5 %collective-permute-done.40 = bf16[4,9,16,512]{3,2,1,0:T(8,128)(2,1)S(1)} collective-permute-done((bf16[4,9,16,512]{3,2,1,0:T(8,128)(2,1)S(1)}, bf16[4,9,16,512]{3,2,1,0:T(8,128)(2,1)S(1)}, u32[]{:S(2)}, u32[]{:S(2)}) %collective-permute-start.40) | collective-permute-done | bytes 589856 | tf_op jit(solution)/shard_map/ppermute | solution.py:320
  235.4 1.5 collective-permute-start.37
  236.9 4.6 %collective-permute-done.41 = bf16[2,9,16,512]{3,2,1,0:T(8,128)(2,1)S(1)} collective-permute-done((bf16[2,9,16,512]{3,2,1,0:T(8,128)(2,1)S(1)}, bf16[2,9,16,512]{3,2,1,0:T(8,128)(2,1)S(1)}, u32[]{:S(2)}, u32[]{:S(2)}) %collective-permute-start.41) | collective-permute-done | bytes 294944 | tf_op jit(solution)/shard_map/ppermute | solution.py:320
  244.0 2.1 collective-permute-start.38
  247.1 2.5 collective-permute-done.43
  249.6 4.5 %collective-permute-done.42 = bf16[9,16,512]{2,1,0:T(8,128)(2,1)S(1)} collective-permute-done((bf16[9,16,512]{2,1,0:T(8,128)(2,1)S(1)}, bf16[9,16,512]{2,1,0:T(8,128)(2,1)S(1)}, u32[]{:S(2)}, u32[]{:S(2)}) %collective-permute-start.42) | collective-permute-done | bytes 147488 | tf_op jit(solution)/shard_map/ppermute | solution.py:320
  261.2 1.7 collective-permute-start.34
  267.1 1.9 shard_map.333
  270.4 2.2 shard_map.335
  (283 shorter events, 69.4 us)
Async XLA Ops:
  7.2 39.6 %all-gather.3.cloned.1.call-start = ((), (), s32[]{:S(2)}) async-start(), calls=%async_computation | async-start | bytes 2949120 | tf_op jit(solution)/shard_map/all_gather | solution.py:398
  9.1 91.4 %all-gather.5.cloned.1.call-start = ((), (), s32[]{:S(2)}) async-start(), calls=%async_computation.1 | async-start | bytes 5308416 | tf_op jit(solution)/shard_map/all_gather | solution.py:399
  52.5 1.4 collective-permute-start
  54.6 3.9 %collective-permute-start.1 = (f32[8,512]{1,0:T(8,128)S(1)}, f32[8,512]{1,0:T(8,128)S(1)}, u32[]{:S(2)}, u32[]{:S(2)}) collective-permute-start(f32[8,512]{1,0:T(8,128)S(1)} %add.190), channel_id=1, source_target_pairs={{0,2},{1,3},{2,0},{3,1},{4,6},{5,7},{6,4},{7,5},{8,10},{9,11},{10,... | collective-permute-start | bytes 49160 | tf_op jit(solution)/shard_map/ppermute | solution.py:320
  55.7 4.1 %collective-permute-start.5 = (f32[8,512]{1,0:T(8,128)S(1)}, f32[8,512]{1,0:T(8,128)S(1)}, u32[]{:S(2)}, u32[]{:S(2)}) collective-permute-start(f32[8,512]{1,0:T(8,128)S(1)} %dynamic_update_slice.5), channel_id=1, source_target_pairs={{0,1},{1,0},{2,3},{3,2},{4,5},{5,4},{6,7},{7,6},{8,9},{9,8},{10,11... | collective-permute-start | bytes 49160 | tf_op jit(solution)/shard_map/ppermute | solution.py:320
  58.5 6.6 %collective-permute-start.2 = (f32[8,512]{1,0:T(8,128)S(1)}, f32[8,512]{1,0:T(8,128)S(1)}, u32[]{:S(2)}, u32[]{:S(2)}) collective-permute-start(f32[8,512]{1,0:T(8,128)S(1)} %add.191), channel_id=1, source_target_pairs={{0,4},{1,5},{2,6},{3,7},{4,0},{5,1},{6,2},{7,3},{8,12},{9,13},{10,... | collective-permute-start | bytes 49160 | tf_op jit(solution)/shard_map/ppermute | solution.py:320
  60.4 6.2 %collective-permute-start.6 = (f32[8,512]{1,0:T(8,128)S(1)}, f32[8,512]{1,0:T(8,128)S(1)}, u32[]{:S(2)}, u32[]{:S(2)}) collective-permute-start(f32[8,512]{1,0:T(8,128)S(1)} %add.196), channel_id=1, source_target_pairs={{0,2},{1,3},{2,0},{3,1},{4,6},{5,7},{6,4},{7,5},{8,10},{9,11},{10,... | collective-permute-start | bytes 49160 | tf_op jit(solution)/shard_map/ppermute | solution.py:320
  65.1 3.7 %collective-permute-start.3 = (f32[8,512]{1,0:T(8,128)S(1)}, f32[8,512]{1,0:T(8,128)S(1)}, u32[]{:S(2)}, u32[]{:S(2)}) collective-permute-start(f32[8,512]{1,0:T(8,128)S(1)} %add.192), channel_id=1, source_target_pairs={{0,8},{8,0},{16,24},{24,16},{1,9},{9,1},{17,25},{25,17},{2,10},{10... | collective-permute-start | bytes 49160 | tf_op jit(solution)/shard_map/ppermute | solution.py:320
  66.6 5.9 %collective-permute-start.7 = (f32[8,512]{1,0:T(8,128)S(1)}, f32[8,512]{1,0:T(8,128)S(1)}, u32[]{:S(2)}, u32[]{:S(2)}) collective-permute-start(f32[8,512]{1,0:T(8,128)S(1)} %add.197), channel_id=1, source_target_pairs={{0,4},{1,5},{2,6},{3,7},{4,0},{5,1},{6,2},{7,3},{8,12},{9,13},{10,... | collective-permute-start | bytes 49160 | tf_op jit(solution)/shard_map/ppermute | solution.py:320
  68.9 4.3 %collective-permute-start.4 = (f32[8,512]{1,0:T(8,128)S(1)}, f32[8,512]{1,0:T(8,128)S(1)}, u32[]{:S(2)}, u32[]{:S(2)}) collective-permute-start(f32[8,512]{1,0:T(8,128)S(1)} %add.193), channel_id=1, source_target_pairs={{0,16},{8,24},{16,0},{24,8},{1,17},{9,25},{17,1},{25,9},{2,18},{10... | collective-permute-start | bytes 49160 | tf_op jit(solution)/shard_map/ppermute | solution.py:320
  107.6 1.4 collective-permute-start.8
  109.7 3.7 %collective-permute-start.9 = (f32[8,512]{1,0:T(8,128)S(1)}, f32[8,512]{1,0:T(8,128)S(1)}, u32[]{:S(2)}, u32[]{:S(2)}) collective-permute-start(f32[8,512]{1,0:T(8,128)S(1)} %add.199), channel_id=1, source_target_pairs={{0,2},{1,3},{2,0},{3,1},{4,6},{5,7},{6,4},{7,5},{8,10},{9,11},{10,... | collective-permute-start | bytes 49160 | tf_op jit(solution)/shard_map/ppermute | solution.py:320
  113.4 4.6 %collective-permute-start.10 = (f32[8,512]{1,0:T(8,128)S(1)}, f32[8,512]{1,0:T(8,128)S(1)}, u32[]{:S(2)}, u32[]{:S(2)}) collective-permute-start(f32[8,512]{1,0:T(8,128)S(1)} %add.200), channel_id=1, source_target_pairs={{0,4},{1,5},{2,6},{3,7},{4,0},{5,1},{6,2},{7,3},{8,12},{9,13},{10,... | collective-permute-start | bytes 49160 | tf_op jit(solution)/shard_map/ppermute | solution.py:320
  118.1 3.7 %collective-permute-start.11 = (f32[8,512]{1,0:T(8,128)S(1)}, f32[8,512]{1,0:T(8,128)S(1)}, u32[]{:S(2)}, u32[]{:S(2)}) collective-permute-start(f32[8,512]{1,0:T(8,128)S(1)} %add.201), channel_id=1, source_target_pairs={{0,8},{8,0},{16,24},{24,16},{1,9},{9,1},{17,25},{25,17},{2,10},{10... | collective-permute-start | bytes 49160 | tf_op jit(solution)/shard_map/ppermute | solution.py:320
  121.8 3.7 %collective-permute-start.12 = (f32[8,512]{1,0:T(8,128)S(1)}, f32[8,512]{1,0:T(8,128)S(1)}, u32[]{:S(2)}, u32[]{:S(2)}) collective-permute-start(f32[8,512]{1,0:T(8,128)S(1)} %add.202), channel_id=1, source_target_pairs={{0,16},{8,24},{16,0},{24,8},{1,17},{9,25},{17,1},{25,9},{2,18},{10... | collective-permute-start | bytes 49160 | tf_op jit(solution)/shard_map/ppermute | solution.py:320
  131.8 3.7 %collective-permute-start.14 = (f32[8,512]{1,0:T(8,128)S(1)}, f32[8,512]{1,0:T(8,128)S(1)}, u32[]{:S(2)}, u32[]{:S(2)}) collective-permute-start(f32[8,512]{1,0:T(8,128)S(1)} %add.204), channel_id=1, source_target_pairs={{0,2},{1,3},{2,0},{3,1},{4,6},{5,7},{6,4},{7,5},{8,10},{9,11},{10,... | collective-permute-start | bytes 49160 | tf_op jit(solution)/shard_map/ppermute | solution.py:320
  135.5 4.6 %collective-permute-start.15 = (f32[8,512]{1,0:T(8,128)S(1)}, f32[8,512]{1,0:T(8,128)S(1)}, u32[]{:S(2)}, u32[]{:S(2)}) collective-permute-start(f32[8,512]{1,0:T(8,128)S(1)} %add.205), channel_id=1, source_target_pairs={{0,4},{1,5},{2,6},{3,7},{4,0},{5,1},{6,2},{7,3},{8,12},{9,13},{10,... | collective-permute-start | bytes 49160 | tf_op jit(solution)/shard_map/ppermute | solution.py:320
  140.2 3.7 %collective-permute-start.16 = (f32[8,512]{1,0:T(8,128)S(1)}, f32[8,512]{1,0:T(8,128)S(1)}, u32[]{:S(2)}, u32[]{:S(2)}) collective-permute-start(f32[8,512]{1,0:T(8,128)S(1)} %add.206), channel_id=1, source_target_pairs={{0,8},{8,0},{16,24},{24,16},{1,9},{9,1},{17,25},{25,17},{2,10},{10... | collective-permute-start | bytes 49160 | tf_op jit(solution)/shard_map/ppermute | solution.py:320
  143.9 3.7 %collective-permute-start.17 = (f32[8,512]{1,0:T(8,128)S(1)}, f32[8,512]{1,0:T(8,128)S(1)}, u32[]{:S(2)}, u32[]{:S(2)}) collective-permute-start(f32[8,512]{1,0:T(8,128)S(1)} %add.207), channel_id=1, source_target_pairs={{0,16},{8,24},{16,0},{24,8},{1,17},{9,25},{17,1},{25,9},{2,18},{10... | collective-permute-start | bytes 49160 | tf_op jit(solution)/shard_map/ppermute | solution.py:320
  155.6 1.8 collective-permute-start.18
  158.1 3.7 %collective-permute-start.19 = (f32[8,512]{1,0:T(8,128)S(1)}, f32[8,512]{1,0:T(8,128)S(1)}, u32[]{:S(2)}, u32[]{:S(2)}) collective-permute-start(f32[8,512]{1,0:T(8,128)S(1)} %add.209), channel_id=1, source_target_pairs={{0,2},{1,3},{2,0},{3,1},{4,6},{5,7},{6,4},{7,5},{8,10},{9,11},{10,... | collective-permute-start | bytes 49160 | tf_op jit(solution)/shard_map/ppermute | solution.py:320
  161.8 4.6 %collective-permute-start.20 = (f32[8,512]{1,0:T(8,128)S(1)}, f32[8,512]{1,0:T(8,128)S(1)}, u32[]{:S(2)}, u32[]{:S(2)}) collective-permute-start(f32[8,512]{1,0:T(8,128)S(1)} %add.210), channel_id=1, source_target_pairs={{0,4},{1,5},{2,6},{3,7},{4,0},{5,1},{6,2},{7,3},{8,12},{9,13},{10,... | collective-permute-start | bytes 49160 | tf_op jit(solution)/shard_map/ppermute | solution.py:320
  166.4 8.7 %collective-permute-start.21 = (f32[8,512]{1,0:T(8,128)S(1)}, f32[8,512]{1,0:T(8,128)S(1)}, u32[]{:S(2)}, u32[]{:S(2)}) collective-permute-start(f32[8,512]{1,0:T(8,128)S(1)} %add.211), channel_id=1, source_target_pairs={{0,8},{8,0},{16,24},{24,16},{1,9},{9,1},{17,25},{25,17},{2,10},{10... | collective-permute-start | bytes 49160 | tf_op jit(solution)/shard_map/ppermute | solution.py:320
  175.1 3.8 %collective-permute-start.22 = (f32[8,512]{1,0:T(8,128)S(1)}, f32[8,512]{1,0:T(8,128)S(1)}, u32[]{:S(2)}, u32[]{:S(2)}) collective-permute-start(f32[8,512]{1,0:T(8,128)S(1)} %add.212), channel_id=1, source_target_pairs={{0,16},{8,24},{16,0},{24,8},{1,17},{9,25},{17,1},{25,9},{2,18},{10... | collective-permute-start | bytes 49160 | tf_op jit(solution)/shard_map/ppermute | solution.py:320
  178.0 39.3 %collective-permute-start.39 = (bf16[8,9,16,512]{3,2,1,0:T(8,128)(2,1)}, bf16[8,9,16,512]{3,2,1,0:T(8,128)(2,1)S(1)}, u32[]{:S(2)}, u32[]{:S(2)}) collective-permute-start(bf16[8,9,16,512]{3,2,1,0:T(8,128)(2,1)} %get-tuple-element.59), channel_id=1, source_target_pairs={{0,1},{1,0},{2,3},{3,2},{4,5},{5,4},{6,7},{7,6},{8,9},{9,8},{10,11... | collective-permute-start | bytes 3538952 | tf_op jit(solution)/shard_map/ppermute | solution.py:320
  178.0 41.3 %collective-permute-start.35 = (bf16[8,9,16,512]{3,2,1,0:T(8,128)(2,1)}, bf16[8,9,16,512]{3,2,1,0:T(8,128)(2,1)S(1)}, u32[]{:S(2)}, u32[]{:S(2)}) collective-permute-start(bf16[8,9,16,512]{3,2,1,0:T(8,128)(2,1)} %get-tuple-element.57), channel_id=1, source_target_pairs={{0,1},{1,0},{2,3},{3,2},{4,5},{5,4},{6,7},{7,6},{8,9},{9,8},{10,11... | collective-permute-start | bytes 3538952 | tf_op jit(solution)/shard_map/ppermute | solution.py:320
  200.2 4.9 %collective-permute-start.27 = (bf16[8,10,16,256]{3,2,1,0:T(8,128)(2,1)}, bf16[8,10,16,256]{3,2,1,0:T(8,128)(2,1)S(1)}, u32[]{:S(2)}, u32[]{:S(2)}) collective-permute-start(bf16[8,10,16,256]{3,2,1,0:T(8,128)(2,1)} %get-tuple-element.52), channel_id=1, source_target_pairs={{0,1},{1,0},{2,3},{3,2},{4,5},{5,4},{6,7},{7,6},{8,9},{9,8},{10,11... | collective-permute-start | bytes 1966088 | tf_op jit(solution)/shard_map/ppermute | solution.py:320
  200.3 6.6 %collective-permute-start.23 = (bf16[8,10,16,256]{3,2,1,0:T(8,128)(2,1)}, bf16[8,10,16,256]{3,2,1,0:T(8,128)(2,1)S(1)}, u32[]{:S(2)}, u32[]{:S(2)}) collective-permute-start(bf16[8,10,16,256]{3,2,1,0:T(8,128)(2,1)} %get-tuple-element.50), channel_id=1, source_target_pairs={{0,1},{1,0},{2,3},{3,2},{4,5},{5,4},{6,7},{7,6},{8,9},{9,8},{10,11... | collective-permute-start | bytes 1966088 | tf_op jit(solution)/shard_map/ppermute | solution.py:320
  205.3 9.8 %collective-permute-start.28 = (bf16[4,10,16,256]{3,2,1,0:T(8,128)(2,1)S(1)}, bf16[4,10,16,256]{3,2,1,0:T(8,128)(2,1)S(1)}, u32[]{:S(2)}, u32[]{:S(2)}) collective-permute-start(bf16[4,10,16,256]{3,2,1,0:T(8,128)(2,1)S(1)} %slice.358), channel_id=1, source_target_pairs={{0,16},{8,24},{16,0},{24,8},{1,17},{9,25},{17,1},{25,9},{2,18},{10... | collective-permute-start | bytes 983048 | tf_op jit(solution)/shard_map/ppermute | solution.py:320
  207.1 9.5 %collective-permute-start.24 = (bf16[4,10,16,256]{3,2,1,0:T(8,128)(2,1)S(1)}, bf16[4,10,16,256]{3,2,1,0:T(8,128)(2,1)S(1)}, u32[]{:S(2)}, u32[]{:S(2)}) collective-permute-start(bf16[4,10,16,256]{3,2,1,0:T(8,128)(2,1)S(1)} %slice.352), channel_id=1, source_target_pairs={{0,8},{8,0},{16,24},{24,16},{1,9},{9,1},{17,25},{25,17},{2,10},{10... | collective-permute-start | bytes 983048 | tf_op jit(solution)/shard_map/ppermute | solution.py:320
  215.1 5.6 %collective-permute-start.29 = (bf16[2,10,16,256]{3,2,1,0:T(8,128)(2,1)S(1)}, bf16[2,10,16,256]{3,2,1,0:T(8,128)(2,1)S(1)}, u32[]{:S(2)}, u32[]{:S(2)}) collective-permute-start(bf16[2,10,16,256]{3,2,1,0:T(8,128)(2,1)S(1)} %slice.360), channel_id=1, source_target_pairs={{0,8},{8,0},{16,24},{24,16},{1,9},{9,1},{17,25},{25,17},{2,10},{10... | collective-permute-start | bytes 491528 | tf_op jit(solution)/shard_map/ppermute | solution.py:320
  216.6 7.2 %collective-permute-start.25 = (bf16[2,10,16,256]{3,2,1,0:T(8,128)(2,1)S(1)}, bf16[2,10,16,256]{3,2,1,0:T(8,128)(2,1)S(1)}, u32[]{:S(2)}, u32[]{:S(2)}) collective-permute-start(bf16[2,10,16,256]{3,2,1,0:T(8,128)(2,1)S(1)} %slice.354), channel_id=1, source_target_pairs={{0,16},{8,24},{16,0},{24,8},{1,17},{9,25},{17,1},{25,9},{2,18},{10... | collective-permute-start | bytes 491528 | tf_op jit(solution)/shard_map/ppermute | solution.py:320
  217.9 16.5 %collective-permute-start.40 = (bf16[4,9,16,512]{3,2,1,0:T(8,128)(2,1)S(1)}, bf16[4,9,16,512]{3,2,1,0:T(8,128)(2,1)S(1)}, u32[]{:S(2)}, u32[]{:S(2)}) collective-permute-start(bf16[4,9,16,512]{3,2,1,0:T(8,128)(2,1)S(1)} %slice.370), channel_id=1, source_target_pairs={{0,16},{8,24},{16,0},{24,8},{1,17},{9,25},{17,1},{25,9},{2,18},{10... | collective-permute-start | bytes 1769480 | tf_op jit(solution)/shard_map/ppermute | solution.py:320
  219.9 15.4 %collective-permute-start.36 = (bf16[4,9,16,512]{3,2,1,0:T(8,128)(2,1)S(1)}, bf16[4,9,16,512]{3,2,1,0:T(8,128)(2,1)S(1)}, u32[]{:S(2)}, u32[]{:S(2)}) collective-permute-start(bf16[4,9,16,512]{3,2,1,0:T(8,128)(2,1)S(1)} %slice.364), channel_id=1, source_target_pairs={{0,8},{8,0},{16,24},{24,16},{1,9},{9,1},{17,25},{25,17},{2,10},{10... | collective-permute-start | bytes 1769480 | tf_op jit(solution)/shard_map/ppermute | solution.py:320
  220.7 23.3 %collective-permute-start.31 = (bf16[10,16,256]{2,1,0:T(8,128)(2,1)S(1)}, bf16[10,16,256]{2,1,0:T(8,128)(2,1)S(1)}, u32[]{:S(2)}, u32[]{:S(2)}) collective-permute-start(bf16[10,16,256]{2,1,0:T(8,128)(2,1)S(1)} %get-tuple-element.84), channel_id=1, source_target_pairs={{0,6},{1,7},{2,4},{3,5},{4,2},{5,3},{6,0},{7,1},{8,14},{9,15},{10,... | collective-permute-start | bytes 245768 | tf_op jit(solution)/shard_map/ppermute | solution.py:320
  222.0 24.1 %collective-permute-start.30 = (bf16[10,16,256]{2,1,0:T(8,128)(2,1)S(1)}, bf16[10,16,256]{2,1,0:T(8,128)(2,1)S(1)}, u32[]{:S(2)}, u32[]{:S(2)}) collective-permute-start(bf16[10,16,256]{2,1,0:T(8,128)(2,1)S(1)} %get-tuple-element.83), channel_id=1, source_target_pairs={{0,4},{1,5},{2,6},{3,7},{4,0},{5,1},{6,2},{7,3},{8,12},{9,13},{10,... | collective-permute-start | bytes 245768 | tf_op jit(solution)/shard_map/ppermute | solution.py:320
  234.5 7.0 %collective-permute-start.41 = (bf16[2,9,16,512]{3,2,1,0:T(8,128)(2,1)S(1)}, bf16[2,9,16,512]{3,2,1,0:T(8,128)(2,1)S(1)}, u32[]{:S(2)}, u32[]{:S(2)}) collective-permute-start(bf16[2,9,16,512]{3,2,1,0:T(8,128)(2,1)S(1)} %slice.372), channel_id=1, source_target_pairs={{0,8},{8,0},{16,24},{24,16},{1,9},{9,1},{17,25},{25,17},{2,10},{10... | collective-permute-start | bytes 884744 | tf_op jit(solution)/shard_map/ppermute | solution.py:320
  235.2 10.9 %collective-permute-start.26 = (bf16[10,16,256]{2,1,0:T(8,128)(2,1)S(1)}, bf16[10,16,256]{2,1,0:T(8,128)(2,1)S(1)}, u32[]{:S(2)}, u32[]{:S(2)}) collective-permute-start(bf16[10,16,256]{2,1,0:T(8,128)(2,1)S(1)} %slice_bitcast_fusion.16), channel_id=1, source_target_pairs={{0,2},{1,3},{2,0},{3,1},{4,6},{5,7},{6,4},{7,5},{8,10},{9,11},{10,... | collective-permute-start | bytes 245768 | tf_op jit(solution)/shard_map/ppermute | solution.py:320
  235.4 7.4 %collective-permute-start.37 = (bf16[2,9,16,512]{3,2,1,0:T(8,128)(2,1)S(1)}, bf16[2,9,16,512]{3,2,1,0:T(8,128)(2,1)S(1)}, u32[]{:S(2)}, u32[]{:S(2)}) collective-permute-start(bf16[2,9,16,512]{3,2,1,0:T(8,128)(2,1)S(1)} %slice.366), channel_id=1, source_target_pairs={{0,16},{8,24},{16,0},{24,8},{1,17},{9,25},{17,1},{25,9},{2,18},{10... | collective-permute-start | bytes 884744 | tf_op jit(solution)/shard_map/ppermute | solution.py:320
  241.5 8.1 %collective-permute-start.43 = (bf16[9,16,512]{2,1,0:T(8,128)(2,1)S(1)}, bf16[9,16,512]{2,1,0:T(8,128)(2,1)S(1)}, u32[]{:S(2)}, u32[]{:S(2)}) collective-permute-start(bf16[9,16,512]{2,1,0:T(8,128)(2,1)S(1)} %get-tuple-element.78), channel_id=1, source_target_pairs={{0,6},{1,7},{2,4},{3,5},{4,2},{5,3},{6,0},{7,1},{8,14},{9,15},{10,... | collective-permute-start | bytes 442376 | tf_op jit(solution)/shard_map/ppermute | solution.py:320
  242.8 11.3 %collective-permute-start.42 = (bf16[9,16,512]{2,1,0:T(8,128)(2,1)S(1)}, bf16[9,16,512]{2,1,0:T(8,128)(2,1)S(1)}, u32[]{:S(2)}, u32[]{:S(2)}) collective-permute-start(bf16[9,16,512]{2,1,0:T(8,128)(2,1)S(1)} %get-tuple-element.77), channel_id=1, source_target_pairs={{0,4},{1,5},{2,6},{3,7},{4,0},{5,1},{6,2},{7,3},{8,12},{9,13},{10,... | collective-permute-start | bytes 442376 | tf_op jit(solution)/shard_map/ppermute | solution.py:320
  244.0 10.1 %collective-permute-start.38 = (bf16[9,16,512]{2,1,0:T(8,128)(2,1)S(1)}, bf16[9,16,512]{2,1,0:T(8,128)(2,1)S(1)}, u32[]{:S(2)}, u32[]{:S(2)}) collective-permute-start(bf16[9,16,512]{2,1,0:T(8,128)(2,1)S(1)} %slice_bitcast_fusion.3), channel_id=1, source_target_pairs={{0,2},{1,3},{2,0},{3,1},{4,6},{5,7},{6,4},{7,5},{8,10},{9,11},{10,... | collective-permute-start | bytes 442376 | tf_op jit(solution)/shard_map/ppermute | solution.py:320
  246.2 15.0 %collective-permute-start.32 = (bf16[10,16,256]{2,1,0:T(8,128)(2,1)S(1)}, bf16[10,16,256]{2,1,0:T(8,128)(2,1)S(1)}, u32[]{:S(2)}, u32[]{:S(2)}) collective-permute-start(bf16[10,16,256]{2,1,0:T(8,128)(2,1)S(1)} %fusion.32.refs_0_), channel_id=1, source_target_pairs={{0,8},{8,0},{16,24},{24,16},{1,9},{9,1},{17,25},{25,17},{2,10},{10... | collective-permute-start | bytes 245768 | tf_op jit(solution)/shard_map/ppermute | solution.py:320
  254.2 14.8 %collective-permute-start.44 = (bf16[9,16,512]{2,1,0:T(8,128)(2,1)S(1)}, bf16[9,16,512]{2,1,0:T(8,128)(2,1)S(1)}, u32[]{:S(2)}, u32[]{:S(2)}) collective-permute-start(bf16[9,16,512]{2,1,0:T(8,128)(2,1)S(1)} %fusion.29.refs_0_), channel_id=1, source_target_pairs={{0,8},{8,0},{16,24},{24,16},{1,9},{9,1},{17,25},{25,17},{2,10},{10... | collective-permute-start | bytes 442376 | tf_op jit(solution)/shard_map/ppermute | solution.py:320
  255.3 13.8 %collective-permute-start.45 = (bf16[9,16,512]{2,1,0:T(8,128)(2,1)S(1)}, bf16[9,16,512]{2,1,0:T(8,128)(2,1)S(1)}, u32[]{:S(2)}, u32[]{:S(2)}) collective-permute-start(bf16[9,16,512]{2,1,0:T(8,128)(2,1)S(1)} %fusion.29.refs_0_), channel_id=1, source_target_pairs={{0,16},{8,24},{16,0},{24,8},{1,17},{9,25},{17,1},{25,9},{2,18},{10... | collective-permute-start | bytes 442376 | tf_op jit(solution)/shard_map/ppermute | solution.py:320
  256.5 12.6 %collective-permute-start.46 = (bf16[9,16,512]{2,1,0:T(8,128)(2,1)S(1)}, bf16[9,16,512]{2,1,0:T(8,128)(2,1)S(1)}, u32[]{:S(2)}, u32[]{:S(2)}) collective-permute-start(bf16[9,16,512]{2,1,0:T(8,128)(2,1)S(1)} %fusion.29.refs_0_), channel_id=1, source_target_pairs={{0,24},{8,16},{16,8},{24,0},{1,25},{9,17},{17,9},{25,1},{2,26},{10... | collective-permute-start | bytes 442376 | tf_op jit(solution)/shard_map/ppermute | solution.py:320
  260.4 5.0 %collective-permute-start.33 = (bf16[10,16,256]{2,1,0:T(8,128)(2,1)S(1)}, bf16[10,16,256]{2,1,0:T(8,128)(2,1)S(1)}, u32[]{:S(2)}, u32[]{:S(2)}) collective-permute-start(bf16[10,16,256]{2,1,0:T(8,128)(2,1)S(1)} %fusion.32.refs_0_), channel_id=1, source_target_pairs={{0,16},{8,24},{16,0},{24,8},{1,17},{9,25},{17,1},{25,9},{2,18},{10... | collective-permute-start | bytes 245768 | tf_op jit(solution)/shard_map/ppermute | solution.py:320
  261.2 5.3 %collective-permute-start.34 = (bf16[10,16,256]{2,1,0:T(8,128)(2,1)S(1)}, bf16[10,16,256]{2,1,0:T(8,128)(2,1)S(1)}, u32[]{:S(2)}, u32[]{:S(2)}) collective-permute-start(bf16[10,16,256]{2,1,0:T(8,128)(2,1)S(1)} %fusion.32.refs_0_), channel_id=1, source_target_pairs={{0,24},{8,16},{16,8},{24,0},{1,25},{9,17},{17,9},{25,1},{2,26},{10... | collective-permute-start | bytes 245768 | tf_op jit(solution)/shard_map/ppermute | solution.py:320
  (35 other events, 222.7 us)
Sparse Core Ops, SparseCore 0:
  10.2 36.5 all-gather.2
  48.4 51.9 all-gather.4

commit v2 on v1

--- a/solution.py
+++ b/solution.py
@@ -12,7 +12,7 @@
 F32 = jnp.float32
 BF16 = jnp.bfloat16
 ROWS = 16
-VMEM_LIMIT = 56 * 2**20
+VMEM_LIMIT = 20 * 2**20
 
 
 def up(value, step):
@@ -38,18 +38,11 @@
         return list(zip(self.starts, self.sizes, [side + 1 for side in self.sides]))
 
 
-def cells(plan, group, value):
-    slots, side = value.shape[0], value.shape[1]
-    value = jnp.pad(jnp.transpose(value, (1, 2, 0, 3)), ((1, 0), (1, 0), (0, 0), (0, 0)))
-    value = value.reshape((side + 1) * (side + 1) * slots, value.shape[3])
-    return jnp.pad(value, ((0, plan.sizes[group] - value.shape[0]), (0, 0)))
-
-
-def images(plan, group, rows):
-    side, slots = plan.sides[group], plan.slots
-    start, count = plan.starts[group], (side + 1) * (side + 1) * slots
-    value = rows[start : start + count].reshape(side + 1, side + 1, slots, rows.shape[1])
-    return jnp.transpose(value[1:, 1:], (2, 0, 1, 3))
+    def cells(self):
+        for group, (start, side) in enumerate(zip(self.starts, self.sides)):
+            for down in range(side):
+                for right in range(side):
+                    yield group, down, right, start + self.slots * ((down + 1) * (side + 1) + right + 1)
 
 
 def nn(left, right):
@@ -107,21 +100,39 @@
     padded_ref[plan.margin + plan.rows :, :] = edge
 
 
-def patches_kernel(plan, planes_ref, out_ref, held_ref):
-    channels = planes_ref.shape[2]
-    held_ref[...] = planes_ref[...].astype(F32)
+def prepare_kernel(plan, counts_ref, *refs):
+    fields, cots, (patches_ref, cot_ref, mask_ref, held_ref) = refs[:3], refs[3:6], refs[6:]
+    slots, channels = plan.slots, fields[0].shape[3]
+    held_ref[...] = jnp.zeros(held_ref.shape, F32)
+    cot_ref[...] = jnp.zeros(cot_ref.shape, F32)
+    mask_ref[...] = jnp.zeros(mask_ref.shape, F32)
+    slot = lax.broadcasted_iota(jnp.int32, (slots, mask_ref.shape[1]), 0)
+    live = [(slot < counts_ref[0, group]).astype(F32) for group in range(3)]
+    for group, down, right, row in plan.cells():
+        mask_ref[row : row + slots, :] = live[group]
+        cot_ref[row : row + slots, :] = cots[group][down, right].astype(F32)
+        for py in range(2):
+            for px in range(2):
+                first = plan.margin + row
+                held_ref[2 * py + px, first : first + slots, :] = fields[group][2 * down + py, 2 * right + px].astype(F32)
     for start, size, width in plan.segments():
         for ky in range(3):
             for kx in range(3):
                 tap = ky * 3 + kx
                 shift = plan.slots * (width * (ky == 0) + (kx == 0))
                 first = plan.margin + start - shift
-                out_ref[start : start + size, tap * channels : (tap + 1) * channels] = held_ref[
+                patches_ref[start : start + size, tap * channels : (tap + 1) * channels] = held_ref[
                     2 * (ky != 1) + (kx != 1), first : first + size, :
                 ].astype(BF16)
 
 
-def first_kernel(patches_ref, weights_ref, mask_ref, first_ref, side_ref, sums_ref):
+def output_rows_kernel(plan, rows_ref, *outs):
+    for group, down, right, row in plan.cells():
+        outs[group][down, right] = rows_ref[row : row + plan.slots, :].astype(BF16)
+
+
+def first_kernel(patches_ref, mask_ref, vec_ref, weights_ref, ready, first_ref, side_ref, sums_ref):
+    ready()
     cin = weights_ref.shape[2]
     cout = weights_ref.shape[1]
     total = nt(patches_ref[:, :cin], weights_ref[0])
@@ -139,74 +150,87 @@
             column(mask * side),
             column(mask * side * side),
             column(mask),
+            vec_ref[0:1],
+            vec_ref[1:2],
         ],
     )
 
 
-def second_kernel(plan, sums_ref, first_ref, mask_ref, vec_ref, weights_ref, second_ref, patches_ref, out_ref, held_ref):
+def second_kernel(
+    plan, sums_ref, got_ref, first_ref, mask_ref, vec_ref, weights_ref, ready, second_ref, patches_ref, out_ref, held_ref
+):
     cout = first_ref.shape[1]
     mask = wide(mask_ref, cout)
-    sums = sums_ref[...]
+    sums = sums_ref[...] + got_ref[...]
     normed, _ = norm(first_ref[...], sums, 0, sums[4:5])
-    pre = normed * vec_ref[0:1] + vec_ref[1:2]
+    pre = normed * sums[5:6] + sums[6:7]
     fill(plan, held_ref, jax.nn.silu(pre) * mask)
     unfold(plan, held_ref, patches_ref, 1)
+    ready()
     total = nt(patches_ref[:, :cout], weights_ref[0])
     for tap in range(1, 9):
         total += nt(patches_ref[:, tap * cout : (tap + 1) * cout], weights_ref[tap])
     second_ref[...] = total
-    put_rows(out_ref, [column(mask * total), column(mask * total * total)])
-
-
-def output_kernel(sums_ref, sums_two_ref, second_ref, side_ref, cot_ref, mask_ref, vec_ref, out_ref, dz_ref, sums_out_ref):
+    put_rows(
+        out_ref, [column(mask * total), column(mask * total * total)] + [vec_ref[row : row + 1] for row in range(2, 6)]
+    )
+
+
+def output_kernel(
+    sums_ref, got_ref, sums_two_ref, got_two_ref, second_ref, side_ref, cot_ref, mask_ref, out_ref, dz_ref, sums_out_ref
+):
     cout = second_ref.shape[1]
     mask = wide(mask_ref, cout)
-    sums = sums_ref[...]
+    sums, sums_two = sums_ref[...] + got_ref[...], sums_two_ref[...] + got_two_ref[...]
     total = sums[4:5]
-    normed_two, _ = norm(second_ref[...], sums_two_ref[...], 0, total)
+    normed_two, _ = norm(second_ref[...], sums_two, 0, total)
     normed_side, _ = norm(side_ref[...], sums, 2, total)
-    value = (normed_two * vec_ref[2:3] + vec_ref[3:4]) + (normed_side * vec_ref[4:5] + vec_ref[5:6])
+    value = (normed_two * sums_two[2:3] + sums_two[3:4]) + (normed_side * sums_two[4:5] + sums_two[5:6])
     gate = jax.nn.sigmoid(value)
-    out_ref[...] = (value * gate * mask).astype(BF16)
-    grad = cot_ref[...].astype(F32) * mask * (gate * (1.0 + value * (1.0 - gate)))
+    out_ref[...] = value * gate * mask
+    grad = cot_ref[...] * mask * (gate * (1.0 + value * (1.0 - gate)))
     dz_ref[...] = grad
-    put_rows(sums_out_ref, [column(grad), column(grad * normed_two), column(grad * normed_side)])
+    total = column(grad)
+    put_rows(sums_out_ref, [total, column(grad * normed_two), column(grad * normed_side), total])
 
 
 def back_second_kernel(
-    plan, sums_ref, sums_two_ref, sums_z_ref, first_ref, second_ref, side_ref, dz_ref, mask_ref, vec_ref, weights_ref,
+    plan, sums_ref, got_ref, sums_two_ref, got_two_ref, sums_z_ref, got_z_ref,
+    first_ref, second_ref, side_ref, dz_ref, mask_ref, weights_ref, ready,
     grad_two_ref, grad_side_ref, dy_ref, out_ref, held_ref, patches_ref,
 ):
     cout = first_ref.shape[1]
     mask = wide(mask_ref, cout)
-    sums, sums_z = sums_ref[...], sums_z_ref[...]
+    sums, sums_two = sums_ref[...] + got_ref[...], sums_two_ref[...] + got_two_ref[...]
+    sums_z = sums_z_ref[...] + got_z_ref[...]
     total = sums[4:5]
     grad = dz_ref[...]
-    normed, factor = norm(second_ref[...], sums_two_ref[...], 0, total)
-    two = vec_ref[2:3] * factor * (grad - mask * (sums_z[0:1] + normed * sums_z[1:2]) / total)
+    normed, factor = norm(second_ref[...], sums_two, 0, total)
+    two = sums_two[2:3] * factor * (grad - mask * (sums_z[0:1] + normed * sums_z[1:2]) / total)
     normed, factor = norm(side_ref[...], sums, 2, total)
-    side = vec_ref[4:5] * factor * (grad - mask * (sums_z[0:1] + normed * sums_z[2:3]) / total)
+    side = sums_two[4:5] * factor * (grad - mask * (sums_z[0:1] + normed * sums_z[2:3]) / total)
     grad_side_ref[...] = side.astype(BF16)
     grad_two_ref[...] = two.astype(BF16)
     fill(plan, held_ref, two)
     unfold(plan, held_ref, patches_ref, -1)
+    ready()
     back = nn(patches_ref[:, :cout], weights_ref[0])
     for tap in range(1, 9):
         back += nn(patches_ref[:, tap * cout : (tap + 1) * cout], weights_ref[tap])
     normed, _ = norm(first_ref[...], sums, 0, total)
-    pre = normed * vec_ref[0:1] + vec_ref[1:2]
+    pre = normed * sums[5:6] + sums[6:7]
     grad = back * silu_slope(pre) * mask
     dy_ref[...] = grad
     put_rows(out_ref, [column(grad), column(grad * normed)])
 
 
-def back_first_kernel(sums_ref, sums_y_ref, first_ref, dy_ref, mask_ref, vec_ref, grad_ref):
+def back_first(sums_ref, got_ref, sums_y_ref, got_y_ref, first_ref, dy_ref, mask_ref, grad_ref):
     cout = first_ref.shape[1]
     mask = wide(mask_ref, cout)
-    sums, sums_y = sums_ref[...], sums_y_ref[...]
+    sums, sums_y = sums_ref[...] + got_ref[...], sums_y_ref[...] + got_y_ref[...]
     total = sums[4:5]
     normed, factor = norm(first_ref[...], sums, 0, total)
-    grad = vec_ref[0:1] * factor * (dy_ref[...] - mask * (sums_y[0:1] + normed * sums_y[1:2]) / total)
+    grad = sums[5:6] * factor * (dy_ref[...] - mask * (sums_y[0:1] + normed * sums_y[1:2]) / total)
     grad_ref[...] = grad.astype(BF16)
 
 
@@ -250,8 +274,11 @@
     correlate(order, place_ref, [grad_ref[...]], [taps], outs, turned_ref, lhs_ref)
 
 
-def weight_first_kernel(order, place_ref, grad_ref, side_ref, patches_ref, *refs):
-    outs, (turned_ref, lhs_ref) = refs[:-2], refs[-2:]
+def weight_first_kernel(
+    order, place_ref, sums_ref, got_ref, sums_y_ref, got_y_ref, first_ref, dy_ref, mask_ref, side_ref, patches_ref, *refs
+):
+    grad_ref, outs, (turned_ref, lhs_ref) = refs[0], refs[1:-2], refs[-2:]
+    back_first(sums_ref, got_ref, sums_y_ref, got_y_ref, first_ref, dy_ref, mask_ref, grad_ref)
     cin = patches_ref.shape[1] // 9
     taps = [(tap, (patches_ref, tap * cin, cin)) for tap in range(9)]
     center = [(9, (patches_ref, 4 * cin, cin))]
@@ -265,7 +292,9 @@
         out_ref[index] = nn(turned, patches_ref[:, tap * channels : (tap + 1) * channels]).astype(BF16)
 
 
-def input_kernel(plan, grad_ref, side_ref, weights_ref, out_ref, held_ref, moved_ref):
+def input_kernel(plan, grad_ref, side_ref, weights_ref, ready, *refs):
+    outs, (held_ref, moved_ref, total_ref) = refs[:3], refs[3:]
+    ready()
     rows = plan.rows
     fill(plan, held_ref, grad_ref[...].astype(F32))
     for index, (down, right) in enumerate(((0, 0), (0, 1), (1, 0), (1, 1))):
@@ -282,7 +311,9 @@
                     total = term if total is None else total + term
             if py + px == 0:
                 total += nn(side_ref[...], weights_ref[9])
-            out_ref[2 * py + px] = total.astype(BF16)
+            total_ref[...] = total
+            for group, down, right, row in plan.cells():
+                outs[group][2 * down + py, 2 * right + px] = total_ref[row : row + plan.slots, :].astype(BF16)
 
 
 def finish_kernel(order, place_ref, *refs):
@@ -296,9 +327,63 @@
             outs[1][rows, :] = ref[taps].astype(F32)
 
 
-def call(body, out_shapes, *args, scratch=(), scalars=0, flops=0):
+class Gathered:
+    def __init__(self, arrays, place=None, order=None):
+        self.arrays, self.place, self.order = arrays, place, order
+
+    def dims(self):
+        if self.order is None:
+            return self.arrays[0].shape
+        zs, taps, quarter, channels = self.arrays[0].shape
+        return taps, 2 * zs * self.order.owned, channels
+
+    def wrap(self, body, scalars, count):
+        if self.order is None:
+            return lambda *refs: body(*refs[: count + 1], lambda: None, *refs[count + 1 :])
+        order, many = self.order, len(self.arrays)
+
+        def whole(place_ref, *refs):
+            inputs, bundles, rest = refs[:count], refs[count : count + many], refs[count + many :]
+            outs, (weights_ref, semaphores) = rest[:-2], rest[-2:]
+            core, b, z = place_ref[0], place_ref[1], place_ref[2]
+            copies = []
+            for index, bundle in enumerate(bundles):
+                for rel_z in range(order.zs):
+                    row = ((z ^ rel_z) * 2 + (core ^ (index // 4))) * order.owned + (b ^ (index % 4)) * order.quarter
+                    rows = pl.ds(pl.multiple_of(row, order.quarter), order.quarter)
+                    copies.append(
+                        pltpu.make_async_copy(
+                            bundle.at[rel_z], weights_ref.at[:, rows, :], semaphores.at[index * order.zs + rel_z]
+                        )
+                    )
+            for copy in copies:
+                copy.start()
+
+            def ready():
+                for copy in copies:
+                    copy.wait()
+
+            body(*inputs, weights_ref, ready, *outs)
+
+        return whole
+
+
+def call(body, out_shapes, *args, scratch=(), scalars=0, flops=0, weights=None):
     vmem = pl.BlockSpec(memory_space=pltpu.VMEM)
     specs = [pl.BlockSpec(memory_space=pltpu.SMEM)] * scalars + [vmem] * (len(args) - scalars)
+    if weights is not None:
+        body = weights.wrap(body, scalars, len(args))
+        scratch = list(scratch)
+        if weights.order is None:
+            args = args + tuple(weights.arrays)
+            specs = specs + [vmem]
+        else:
+            args = (weights.place,) + args + tuple(weights.arrays)
+            specs = [pl.BlockSpec(memory_space=pltpu.SMEM)] + specs + [pl.BlockSpec(memory_space=pl.ANY)] * len(weights.arrays)
+            scratch += [
+                pltpu.VMEM(weights.dims(), BF16),
+                pltpu.SemaphoreType.DMA((len(weights.arrays) * weights.order.zs,)),
+            ]
     many = isinstance(out_shapes, (list, tuple))
     moved = sum(arg.size * arg.dtype.itemsize for arg in args)
     return pl.pallas_call(
@@ -324,20 +409,54 @@
     return [1 << index for index in range(count.bit_length() - 1)]
 
 
-def sum_over(value, axes):
+def after(value, *others):
+    return lax.optimization_barrier((value, *others))[0]
+
+
+def sum_over(value, axes, hooks=()):
+    steps = []
     for axis, count in axes:
         if count & (count - 1):
             value = lax.psum(value, axis)
-            continue
-        for bit in bits(count):
-            value = value + exchange(value, axis, count, bit)
-    return value
-
-
-def reduce_in_plane(parts, core, batch):
+        else:
+            steps += [(axis, count, bit) for bit in bits(count)]
+    got = jnp.zeros_like(value)
+    for index, (axis, count, bit) in enumerate(steps):
+        if index:
+            value = value + got
+        if index < len(hooks) and hooks[index] is not None:
+            value = after(value, *hooks[index]())
+        got = exchange(value, axis, count, bit)
+    return value, got
+
+
+def piece_kernel(order, place_ref, first_ref, side_ref, second_ref, first_out_ref, second_out_ref):
+    rows = pl.ds(pl.multiple_of(place_ref[1] * order.quarter, order.quarter), order.quarter)
+    first_out_ref[:9] = first_ref[:, rows, :]
+    first_out_ref[9] = side_ref[rows, :]
+    second_out_ref[...] = second_ref[:, rows, :]
+
+
+def spread_line(order, piece, fsdp):
+    return [piece] + [exchange(piece, "fsdp", fsdp, 2 * rel) for rel in range(1, order.zs)]
+
+
+def spread_plane(pieces, batch):
+    bundle = jnp.stack(pieces)
+    return [bundle] + [exchange(bundle, "batch", batch, rel) for rel in (1, 2, 3)]
+
+
+def spread_cores(bundles, fsdp):
+    return bundles + [exchange(value, "fsdp", fsdp, 1) for value in bundles]
+
+
+def reduce_cores(parts, fsdp):
     keep_p, keep_q, send_p, send_q = parts
-    half_p = keep_p + exchange(send_p, "fsdp", core, 1)
-    half_q = keep_q + exchange(send_q, "fsdp", core, 1)
+    return keep_p + exchange(send_p, "fsdp", fsdp, 1), keep_q + exchange(send_q, "fsdp", fsdp, 1)
+
+
+def finish_weights(order, place, halves, batch, fsdp, outs):
+    half_p, half_q = halves
     n_p, n_q = half_p.shape[0] // 4, half_q.shape[0] // 4
     got_p = exchange(half_p[2 * n_p :], "batch", batch, 1)
     got_q = exchange(half_q[2 * n_q :], "batch", batch, 2)
@@ -345,12 +464,8 @@
     half_q = half_q[: 2 * n_q] + got_q
     got_p = exchange(half_p[n_p:], "batch", batch, 2)
     got_q = exchange(half_q[n_q:], "batch", batch, 1)
-    return half_p[:n_p] + got_p, half_q[:n_q] + got_q
-
-
-def reduce_weights(order, place, parts, batch, fsdp, outs):
-    low, high = reduce_in_plane(parts, fsdp, batch)
-    pieces = [low[index] for index in range(low.shape[0])] + [high[index] for index in range(high.shape[0])]
+    low, high = half_p[:n_p] + got_p, half_q[:n_q] + got_q
+    pieces = [low[index] for index in range(n_p)] + [high[index] for index in range(n_q)]
     total = pieces[0].astype(F32)
     for rel in range(1, len(pieces)):
         total = total + exchange(pieces[rel], "fsdp", fsdp, 2 * rel).astype(F32)
@@ -394,89 +509,90 @@
 
     own_first = jnp.transpose(w_first, (0, 1, 3, 2)).reshape(9, owned, cin)
     own_second = jnp.transpose(w_second, (0, 1, 3, 2)).reshape(9, owned, cout)
-    own_side = jnp.transpose(w_short).reshape(1, owned, cin)
-    kern_first = lax.all_gather(jnp.concatenate([own_first, own_side]), "fsdp", axis=1, tiled=True)
-    kern_second = lax.all_gather(own_second, "fsdp", axis=1, tiled=True)
+    own_side = jnp.transpose(w_short)
+    if fast:
+        piece_first, piece_second = call(
+            functools.partial(piece_kernel, order),
+            [shape((10, order.quarter, cin), BF16), shape((9, order.quarter, cout), BF16)],
+            place,
+            own_first,
+            own_side,
+            own_second,
+            scalars=1,
+        )
+        along_first = spread_line(order, piece_first, fsdp)
+        plane_first = spread_plane(along_first, batch)
+        along_second = spread_line(order, after(piece_second, *along_first), fsdp)
+        plane_second = spread_plane(along_second, batch)
+        kern_first = Gathered(spread_cores(plane_first, fsdp), place, order)
+    else:
+        kern_first = Gathered([lax.all_gather(jnp.concatenate([own_first, own_side[None]]), "fsdp", axis=1, tiled=True)])
+        kern_second = Gathered([lax.all_gather(own_second, "fsdp", axis=1, tiled=True)])
     vectors = jnp.stack([gain_first, shift_first, gain_second, shift_second, gain_short, shift_short]).astype(F32)
+    vectors = jnp.where(lax.axis_index("batch") == 0, vectors, 0.0)
     vec = lax.dynamic_update_slice(jnp.zeros((8, cout), F32), vectors, (0, me * owned))
-    vec = sum_over(vec, (("fsdp", fsdp),))
-
-    planes = []
-    for group, field in enumerate(fields):
-        side = plan.sides[group]
-        split = field.reshape(slots, side, 2, side, 2, cin)
-        planes.append(
-            jnp.stack([cells(plan, group, split[:, :, py, :, px]) for py in range(2) for px in range(2)])
-        )
-    planes = jnp.pad(jnp.concatenate(planes, axis=1), ((0, 0), (plan.margin, 0), (0, 0)))
-    cot_rows = jnp.concatenate([cells(plan, group, cot) for group, cot in enumerate(cots)])
-    mask = []
-    for group, side in enumerate(plan.sides):
-        valid = np.zeros((side + 1, side + 1, slots), bool)
-        valid[1:, 1:] = True
-        valid = np.pad(valid.reshape(-1), (0, plan.sizes[group] - valid.size))
-        slot = np.arange(plan.sizes[group]) % slots
-        mask.append(jnp.asarray(valid) & (jnp.asarray(slot, jnp.int32) < counts[0, group]))
-    mask = jnp.broadcast_to(jnp.concatenate(mask).astype(F32)[:, None], (rows, 128))
-
-    patches = call(
-        functools.partial(patches_kernel, plan),
-        shape((rows, 9 * cin), BF16),
-        planes,
+
+    patches, cot_rows, mask = call(
+        functools.partial(prepare_kernel, plan),
+        [shape((rows, 9 * cin), BF16), shape((rows, cout)), shape((rows, 128))],
+        counts,
+        *[jnp.transpose(value, (1, 2, 0, 3)) for value in fields + cots],
         scratch=[pltpu.VMEM((4, plan.margin + rows, cin), F32)],
+        scalars=1,
     )
     flops = 2 * rows * cout * cin * 9
     first, side, sums = call(
         first_kernel,
         [shape((rows, cout)), shape((rows, cout)), shape((8, cout))],
         patches,
-        kern_first,
         mask,
+        vec,
         flops=flops,
+        weights=kern_first,
     )
     sums = sum_over(sums, everywhere)
+    if fast:
+        kern_second = Gathered(spread_cores([after(value, *sums) for value in plane_second], fsdp), place, order)
     second, patches_two, sums_two = call(
         functools.partial(second_kernel, plan),
         [shape((rows, cout)), shape((rows, 9 * cout), BF16), shape((8, cout))],
-        sums,
+        *sums,
         first,
         mask,
         vec,
-        kern_second,
         scratch=[pltpu.VMEM((span, cout), F32)],
         flops=2 * flops,
+        weights=kern_second,
     )
     sums_two = sum_over(sums_two, everywhere)
-    out, dz, sums_z = call(
+    out_rows, dz, sums_z = call(
         output_kernel,
-        [shape((rows, cout), BF16), shape((rows, cout)), shape((8, cout))],
-        sums,
-        sums_two,
+        [shape((rows, cout)), shape((rows, cout)), shape((8, cout))],
+        *sums,
+        *sums_two,
         second,
         side,
         cot_rows,
         mask,
-        vec,
         flops=50 * rows * cout,
     )
     sums_z = sum_over(sums_z, everywhere)
     grad_two, grad_side, dy, sums_y = call(
         functools.partial(back_second_kernel, plan),
         [shape((rows, cout), BF16), shape((rows, cout), BF16), shape((rows, cout)), shape((8, cout))],
-        sums,
-        sums_two,
-        sums_z,
+        *sums,
+        *sums_two,
+        *sums_z,
         first,
         second,
         side,
         dz,
         mask,
-        vec,
-        kern_second,
         scratch=[pltpu.VMEM((span, cout), F32), pltpu.VMEM((rows, 9 * cout), BF16)],
         flops=2 * flops,
-    )
-    sums_y = sum_over(sums_y, everywhere)
+        weights=kern_second,
+    )
+    hooks = ()
     if fast:
         turned = [pltpu.VMEM((cout, rows), BF16), pltpu.VMEM((cout, rows), BF16)]
         parts_two = call(
@@ -489,26 +605,33 @@
             scalars=1,
             flops=2 * flops,
         )
-        dw_second = reduce_weights(order, place, parts_two, batch, fsdp, [shape((9, owned, cout))])[0]
-    grad_one = call(
-        back_first_kernel, shape((rows, cout), BF16), sums, sums_y, first, dy, mask, vec, flops=20 * rows * cout
-    )
+        halves_two = reduce_cores(parts_two, fsdp)
+        hooks = (None, None, lambda: parts_two, None, lambda: halves_two)
+    sums_y = sum_over(sums_y, everywhere, hooks)
     if fast:
-        parts_one = call(
+        grad_one, *parts_one = call(
             functools.partial(weight_first_kernel, order),
-            [shape((len(part), 10, order.quarter, cin), BF16) for part in order.parts],
+            [shape((rows, cout), BF16)] + [shape((len(part), 10, order.quarter, cin), BF16) for part in order.parts],
             place,
-            grad_one,
+            *sums,
+            *sums_y,
+            first,
+            dy,
+            mask,
             grad_side,
             patches,
             scratch=turned,
             scalars=1,
             flops=flops,
         )
-        dw_first, dw_side = reduce_weights(
-            order, place, parts_one, batch, fsdp, [shape((9, owned, cin)), shape((owned, cin))]
+        halves_one = reduce_cores(parts_one, fsdp)
+        dw_first, dw_side = finish_weights(
+            order, place, halves_one, batch, fsdp, [shape((9, owned, cin)), shape((owned, cin))]
         )
+        dw_second = finish_weights(order, place, halves_two, batch, fsdp, [shape((9, owned, cout))])[0]
+        grad_late, out_rows = after(grad_one, *halves_one), after(out_rows, *halves_one)
     else:
+        grad_one = call(back_first, shape((rows, cout), BF16), *sums, *sums_y, first, dy, mask)
         taps = tuple(range(9))
         whole = [
             call(functools.partial(plain_weight_kernel, taps), shape((9, cout, cout), BF16), grad_two, patches_two),
@@ -520,36 +643,31 @@
             for value in whole
         ]
         dw_side = dw_side[0]
-    dx = call(
+        grad_late = grad_one
+    input_grads = call(
         functools.partial(input_kernel, plan),
-        shape((4, rows, cin), BF16),
-        grad_one,
+        [shape((2 * length, 2 * length, slots, cin), BF16) for length in plan.sides],
+        grad_late,
         grad_side,
-        kern_first,
-        scratch=[pltpu.VMEM((span, cout), F32), pltpu.VMEM((4, rows, cout), BF16)],
+        scratch=[pltpu.VMEM((span, cout), F32), pltpu.VMEM((4, rows, cout), BF16), pltpu.VMEM((rows, cin), F32)],
         flops=flops,
-    )
-    outputs = [images(plan, group, out) for group in range(3)]
-    input_grads = []
-    for group, side_length in enumerate(plan.sides):
-        quarter = [images(plan, group, dx[index]) for index in range(4)]
-        whole_rows = [jnp.stack(quarter[2 * py : 2 * py + 2], axis=3) for py in range(2)]
-        value = jnp.stack(whole_rows, axis=2)
-        input_grads.append(value.reshape(slots, 2 * side_length, 2 * side_length, cin))
+        weights=kern_first,
+    )
+    outputs = call(
+        functools.partial(output_rows_kernel, plan),
+        [shape((length, length, slots, cout), BF16) for length in plan.sides],
+        out_rows,
+    )
 
     def mine(sums, row):
-        return lax.dynamic_slice(sums, (row, me * owned), (1, owned))[0]
+        value = sums[0][row : row + 1] + sums[1][row : row + 1]
+        return lax.dynamic_slice(value, (0, me * owned), (1, owned))[0]
 
     def as_weight(value):
         return jnp.transpose(value.reshape(3, 3, owned, value.shape[2]), (0, 1, 3, 2))
 
     return (
-        outputs[0],
-        outputs[1],
-        outputs[2],
-        input_grads[0],
-        input_grads[1],
-        input_grads[2],
+        *[jnp.transpose(value, (2, 0, 1, 3)) for value in (*outputs, *input_grads)],
         as_weight(dw_first),
         mine(sums_y, 1),
         mine(sums_y, 0),
@@ -558,7 +676,7 @@
         mine(sums_z, 0),
         jnp.transpose(dw_side),
         mine(sums_z, 2),
-        mine(sums_z, 0),
+        mine(sums_z, 3),
     )
 
 

time: 281 us -> 201 us (0.72)
  waiting for transfers between devices: 131 us -> 73.4 us
  starting transfers between devices: 40 us -> 76.2 us
  Pallas kernels: 48.6 us -> 32.1 us
  local copies, waits for them, and re-layouts: 27.2 us -> 12.7 us
  between operations: 15.1 us -> 1.16 us
  other arithmetic: 18.4 us -> 5.14 us
    all_gather x2 -> x0, waiting for transfers between devices: 54.4 us -> none  [the longest x1 27.7 us: local(): lax.all_gather(jnp.concatenate([own_first, own_side]), 'fsdp', axis=1, ti...]
    ppermute x47 -> x64, starting transfers between devices: 40 us -> 76.2 us  [exchange(): lax.ppermute(value, axis, [(index, index ^ bit) for index in range(count)])]
    pallas_call x11 -> x12, Pallas kernels: 48.6 us -> 32.1 us  [call(): pl.pallas_call(body, in_specs=specs, out_specs=[vmem] * len(out_shapes) i...]
    slice x15 -> x12, local copies, waits for them, and re-layouts: 6.6 us -> 0.22 us  [the longest x2 0.06 us: finish_weights(): got_q = exchange(half_q[2 * n_q:], 'batch', batch, 2)]
    another operation x23 -> x0, local copies, waits for them, and re-layouts: 6.25 us -> none  [the longest x12 3.58 us: local(): jnp.stack(quarter[2 * py:2 * py + 2], axis=3)]
    unnamed x69 -> x32, local copies, waits for them, and re-layouts: 2.61 us -> 8.54 us
    add x34 -> x28, other arithmetic: 7.64 us -> 1.76 us  [the longest x2 0.69 us: reduce_cores(): keep_p + exchange(send_p, 'fsdp', fsdp, 1)]
    another operation x9 -> x2, other arithmetic: 4.35 us -> 0.12 us  [spread_plane(): bundle = jnp.stack(pieces)]
  transfers between devices with their start and end apart: 49 -> 64, of which waited for: 29 -> 34; matrix products, arithmetic and copies ran while one was open for 14% -> 5% of each run, Pallas kernels for 10% -> 7%
where the time goes in v2:
time: 201 us
  starting transfers between devices  76.2 us (38%)
  waiting for transfers between devices  73.4 us (37%)
  Pallas kernels  32.1 us (16%)
  local copies, waits for them, and re-layouts  12.7 us (6%)
  other arithmetic  5.14 us (3%)
    ppermute x64, starting transfers between devices, exchange(): lax.ppermute(value, axis, [(index, index ^ bit) for index in range(count)])  76.2 us
    ppermute x64, waiting for transfers between devices, exchange(): lax.ppermute(value, axis, [(index, index ^ bit) for index in range(count)])  73.4 us
    pallas_call x12, Pallas kernels, call(): pl.pallas_call(body, in_specs=specs, out_specs=[vmem] * len(out_shapes) i...  32.1 us
    unnamed x32, local copies, waits for them, and re-layouts  8.54 us
  transfers between devices with their start and end apart: 64, of which 34 were waited for; matrix products, arithmetic and copies ran while one was open for 5% of the time, Pallas kernels for 7%

profile of v2, /device:TPU:0, one launch (start us, length us, event | category | flops | bytes accessed | tf_op | source)
XLA Modules:
  0.0 200.7 jit_solution(8811654082257382736)
XLA Ops:
  4.1 5.1 %collective-permute-start.2 = (bf16[10,16,256]{2,1,0:T(8,128)(2,1)S(1)}, bf16[10,16,256]{2,1,0:T(8,128)(2,1)S(1)}, u32[]{:S(2)}, u32[]{:S(2)}) collective-permute-start(bf16[10,16,256]{2,1,0:T(8,128)(2,1)S(1)} %get-tuple-element.61), channel_id=1, source_target_pairs={{0,6},{1,7},{2,4},{3,5},{4,2},{5,3},{6,0},{7,1},{8,14},{9,15},{10,... | collective-permute-start | bytes 245768 | tf_op jit(solution)/shard_map/ppermute | solution.py:405
  9.9 2.4 %collective-permute-done.2 = bf16[10,16,256]{2,1,0:T(8,128)(2,1)S(1)} collective-permute-done((bf16[10,16,256]{2,1,0:T(8,128)(2,1)S(1)}, bf16[10,16,256]{2,1,0:T(8,128)(2,1)S(1)}, u32[]{:S(2)}, u32[]{:S(2)}) %collective-permute-start.2) | collective-permute-done | bytes 81952 | tf_op jit(solution)/shard_map/ppermute | solution.py:405
  12.3 3.8 %collective-permute-done.1 = bf16[10,16,256]{2,1,0:T(8,128)(2,1)S(1)} collective-permute-done((bf16[10,16,256]{2,1,0:T(8,128)(2,1)S(1)}, bf16[10,16,256]{2,1,0:T(8,128)(2,1)S(1)}, u32[]{:S(2)}, u32[]{:S(2)}) %collective-permute-start.1) | collective-permute-done | bytes 81952 | tf_op jit(solution)/shard_map/ppermute | solution.py:405
  17.7 2.7 %collective-permute-start.17 = (bf16[9,16,512]{2,1,0:T(8,128)(2,1)S(1)}, bf16[9,16,512]{2,1,0:T(8,128)(2,1)S(1)}, u32[]{:S(2)}, u32[]{:S(2)}) collective-permute-start(bf16[9,16,512]{2,1,0:T(8,128)(2,1)S(1)} %get-tuple-element.65), channel_id=1, source_target_pairs={{0,6},{1,7},{2,4},{3,5},{4,2},{5,3},{6,0},{7,1},{8,14},{9,15},{10,... | collective-permute-start | bytes 442376 | tf_op jit(solution)/shard_map/ppermute | solution.py:405
  22.4 4.0 %collective-permute-done.17 = bf16[9,16,512]{2,1,0:T(8,128)(2,1)S(1)} collective-permute-done((bf16[9,16,512]{2,1,0:T(8,128)(2,1)S(1)}, bf16[9,16,512]{2,1,0:T(8,128)(2,1)S(1)}, u32[]{:S(2)}, u32[]{:S(2)}) %collective-permute-start.17) | collective-permute-done | bytes 147488 | tf_op jit(solution)/shard_map/ppermute | solution.py:405
  26.4 4.9 %collective-permute-start.15 = (bf16[9,16,512]{2,1,0:T(8,128)(2,1)S(1)}, bf16[9,16,512]{2,1,0:T(8,128)(2,1)S(1)}, u32[]{:S(2)}, u32[]{:S(2)}) collective-permute-start(bf16[9,16,512]{2,1,0:T(8,128)(2,1)S(1)} %get-tuple-element.65), channel_id=1, source_target_pairs={{0,2},{1,3},{2,0},{3,1},{4,6},{5,7},{6,4},{7,5},{8,10},{9,11},{10,... | collective-permute-start | bytes 442376 | tf_op jit(solution)/shard_map/ppermute | solution.py:405
  32.9 1.6 collective-permute-done.15
  43.2 2.0 dynamic_update_slice.3.refs_2_.refs_4_
  51.2 3.7 %shard_map.273 = (f32[432,512]{1,0:T(8,128)S(1)}, f32[432,512]{1,0:T(8,128)S(1)}, f32[8,512]{1,0:T(8,128)S(1)}) custom-call(s32[3]{0:T(128)S(1)} %pad_add_fusion.place_ref, bf16[432,2304]{1,0:T(8,128)(2,1)S(1)} %get-tuple-element.59.refs_0_.patches_ref, f32[432,128]{1,0:T(8,128)S(1)} %get-tuple-element.60.refs_1_.refs_3_.mask_ref.refs_10_, ...), custom_call_target="tpu_custom_call" | custom-call | flops 1019215872 | bytes 4849676 | tf_op jit(solution)/shard_map/pallas_call | solution.py:389
  56.1 2.0 %collective-permute-start.11 = (f32[8,512]{1,0:T(8,128)S(1)}, f32[8,512]{1,0:T(8,128)S(1)}, u32[]{:S(2)}, u32[]{:S(2)}) collective-permute-start(f32[8,512]{1,0:T(8,128)S(1)} %add.136), channel_id=1, source_target_pairs={{0,2},{1,3},{2,0},{3,1},{4,6},{5,7},{6,4},{7,5},{8,10},{9,11},{10,... | collective-permute-start | bytes 49160 | tf_op jit(solution)/shard_map/ppermute | solution.py:405
  58.2 1.7 collective-permute-done.11
  59.9 2.2 %collective-permute-start.12 = (f32[8,512]{1,0:T(8,128)S(1)}, f32[8,512]{1,0:T(8,128)S(1)}, u32[]{:S(2)}, u32[]{:S(2)}) collective-permute-start(f32[8,512]{1,0:T(8,128)S(1)} %add.137), channel_id=1, source_target_pairs={{0,4},{1,5},{2,6},{3,7},{4,0},{5,1},{6,2},{7,3},{8,12},{9,13},{10,... | collective-permute-start | bytes 49160 | tf_op jit(solution)/shard_map/ppermute | solution.py:405
  62.1 2.4 %collective-permute-done.12 = f32[8,512]{1,0:T(8,128)S(1)} collective-permute-done((f32[8,512]{1,0:T(8,128)S(1)}, f32[8,512]{1,0:T(8,128)S(1)}, u32[]{:S(2)}, u32[]{:S(2)}) %collective-permute-start.12) | collective-permute-done | bytes 16416 | tf_op jit(solution)/shard_map/ppermute | solution.py:405
  65.4 2.9 %collective-permute-done.13 = f32[8,512]{1,0:T(8,128)S(1)} collective-permute-done((f32[8,512]{1,0:T(8,128)S(1)}, f32[8,512]{1,0:T(8,128)S(1)}, u32[]{:S(2)}, u32[]{:S(2)}) %collective-permute-start.13) | collective-permute-done | bytes 16416 | tf_op jit(solution)/shard_map/ppermute | solution.py:405
  69.8 2.2 %collective-permute-done.14.refs_1_.got_ref = f32[8,512]{1,0:T(8,128)S(1)} collective-permute-done((f32[8,512]{1,0:T(8,128)S(1)}, f32[8,512]{1,0:T(8,128)S(1)}, u32[]{:S(2)}, u32[]{:S(2)}) %collective-permute-start.14) | collective-permute-done | bytes 16416 | tf_op jit(solution)/shard_map/ppermute | solution.py:405
  76.6 5.0 %shard_map.274 = (f32[432,512]{1,0:T(8,128)S(1)}, bf16[432,4608]{1,0:T(8,128)(2,1)S(1)}, f32[8,512]{1,0:T(8,128)S(1)}) custom-call(s32[3]{0:T(128)S(1)} %pad_add_fusion.place_ref, f32[8,512]{1,0:T(8,128)S(1)} %add.139.refs_0_.sums_ref, f32[8,512]{1,0:T(8,128)S(1)} %collective-permute-done.14.refs_1_.got_ref, ...), custom_call_target="tpu_custom_call" | custom-call | flops 2038431744 | bytes 5873676 | tf_op jit(solution)/shard_map/pallas_call | solution.py:389
  82.9 2.0 %collective-permute-start.26 = (f32[8,512]{1,0:T(8,128)S(1)}, f32[8,512]{1,0:T(8,128)S(1)}, u32[]{:S(2)}, u32[]{:S(2)}) collective-permute-start(f32[8,512]{1,0:T(8,128)S(1)} %add.140), channel_id=1, source_target_pairs={{0,2},{1,3},{2,0},{3,1},{4,6},{5,7},{6,4},{7,5},{8,10},{9,11},{10,... | collective-permute-start | bytes 49160 | tf_op jit(solution)/shard_map/ppermute | solution.py:405
  84.9 1.7 collective-permute-done.26
  86.6 2.2 %collective-permute-start.27 = (f32[8,512]{1,0:T(8,128)S(1)}, f32[8,512]{1,0:T(8,128)S(1)}, u32[]{:S(2)}, u32[]{:S(2)}) collective-permute-start(f32[8,512]{1,0:T(8,128)S(1)} %add.141), channel_id=1, source_target_pairs={{0,4},{1,5},{2,6},{3,7},{4,0},{5,1},{6,2},{7,3},{8,12},{9,13},{10,... | collective-permute-start | bytes 49160 | tf_op jit(solution)/shard_map/ppermute | solution.py:405
  88.9 2.4 %collective-permute-done.27 = f32[8,512]{1,0:T(8,128)S(1)} collective-permute-done((f32[8,512]{1,0:T(8,128)S(1)}, f32[8,512]{1,0:T(8,128)S(1)}, u32[]{:S(2)}, u32[]{:S(2)}) %collective-permute-start.27) | collective-permute-done | bytes 16416 | tf_op jit(solution)/shard_map/ppermute | solution.py:405
  92.1 2.9 %collective-permute-done.28 = f32[8,512]{1,0:T(8,128)S(1)} collective-permute-done((f32[8,512]{1,0:T(8,128)S(1)}, f32[8,512]{1,0:T(8,128)S(1)}, u32[]{:S(2)}, u32[]{:S(2)}) %collective-permute-start.28) | collective-permute-done | bytes 16416 | tf_op jit(solution)/shard_map/ppermute | solution.py:405
  96.5 2.2 %collective-permute-done.29.got_two_ref.refs_3_ = f32[8,512]{1,0:T(8,128)S(1)} collective-permute-done((f32[8,512]{1,0:T(8,128)S(1)}, f32[8,512]{1,0:T(8,128)S(1)}, u32[]{:S(2)}, u32[]{:S(2)}) %collective-permute-start.29) | collective-permute-done | bytes 16416 | tf_op jit(solution)/shard_map/ppermute | solution.py:405
  100.9 2.0 %collective-permute-start.31 = (f32[8,512]{1,0:T(8,128)S(1)}, f32[8,512]{1,0:T(8,128)S(1)}, u32[]{:S(2)}, u32[]{:S(2)}) collective-permute-start(f32[8,512]{1,0:T(8,128)S(1)} %add.144), channel_id=1, source_target_pairs={{0,2},{1,3},{2,0},{3,1},{4,6},{5,7},{6,4},{7,5},{8,10},{9,11},{10,... | collective-permute-start | bytes 49160 | tf_op jit(solution)/shard_map/ppermute | solution.py:405
  102.9 1.7 collective-permute-done.31
  104.6 2.2 %collective-permute-start.32 = (f32[8,512]{1,0:T(8,128)S(1)}, f32[8,512]{1,0:T(8,128)S(1)}, u32[]{:S(2)}, u32[]{:S(2)}) collective-permute-start(f32[8,512]{1,0:T(8,128)S(1)} %add.145), channel_id=1, source_target_pairs={{0,4},{1,5},{2,6},{3,7},{4,0},{5,1},{6,2},{7,3},{8,12},{9,13},{10,... | collective-permute-start | bytes 49160 | tf_op jit(solution)/shard_map/ppermute | solution.py:405
  106.8 2.4 %collective-permute-done.32 = f32[8,512]{1,0:T(8,128)S(1)} collective-permute-done((f32[8,512]{1,0:T(8,128)S(1)}, f32[8,512]{1,0:T(8,128)S(1)}, u32[]{:S(2)}, u32[]{:S(2)}) %collective-permute-start.32) | collective-permute-done | bytes 16416 | tf_op jit(solution)/shard_map/ppermute | solution.py:405
  110.1 2.9 %collective-permute-done.33 = f32[8,512]{1,0:T(8,128)S(1)} collective-permute-done((f32[8,512]{1,0:T(8,128)S(1)}, f32[8,512]{1,0:T(8,128)S(1)}, u32[]{:S(2)}, u32[]{:S(2)}) %collective-permute-start.33) | collective-permute-done | bytes 16416 | tf_op jit(solution)/shard_map/ppermute | solution.py:405
  114.5 2.2 %collective-permute-done.34.refs_5_ = f32[8,512]{1,0:T(8,128)S(1)} collective-permute-done((f32[8,512]{1,0:T(8,128)S(1)}, f32[8,512]{1,0:T(8,128)S(1)}, u32[]{:S(2)}, u32[]{:S(2)}) %collective-permute-start.34) | collective-permute-done | bytes 16416 | tf_op jit(solution)/shard_map/ppermute | solution.py:405
  116.7 6.1 %shard_map.276 = (bf16[432,512]{1,0:T(8,128)(2,1)S(1)}, bf16[432,512]{1,0:T(8,128)(2,1)S(1)}, f32[432,512]{1,0:T(8,128)S(1)}, f32[8,512]{1,0:T(8,128)S(1)}) custom-call(s32[3]{0:T(128)S(1)} %pad_add_fusion.place_ref, f32[8,512]{1,0:T(8,128)S(1)} %add.139.refs_0_.sums_ref, f32[8,512]{1,0:T(8,128)S(1)} %collective-permute-done.14.refs_1_.got_ref, ...), custom_call_target="tpu_custom_call" | custom-call | flops 2038431744 | bytes 8577036 | tf_op jit(solution)/shard_map/pallas_call | solution.py:389
  122.9 3.3 %shard_map.277 = (bf16[8,9,16,512]{3,2,1,0:T(8,128)(2,1)S(1)}, bf16[8,9,16,512]{3,2,1,0:T(8,128)(2,1)S(1)}, bf16[8,9,16,512]{3,2,1,0:T(8,128)(2,1)S(1)}, bf16[8,9,16,512]{3,2,1,0:T(8,128)(2,1)S(1)}) custom-call(s32[3]{0:T(128)S(1)} %pad_add_fusion.place_ref, bf16[432,512]{1,0:T(8,128)(2,1)S(1)} %get-tuple-element.78.grad_ref, ...), custom_call_target="tpu_custom_call" | custom-call | flops 2038431744 | bytes 4423692 | tf_op jit(solution)/shard_map/pallas_call | solution.py:389
  126.9 4.0 %collective-permute-done.35 = f32[8,512]{1,0:T(8,128)S(1)} collective-permute-done((f32[8,512]{1,0:T(8,128)S(1)}, f32[8,512]{1,0:T(8,128)S(1)}, u32[]{:S(2)}, u32[]{:S(2)}) %collective-permute-start.35) | collective-permute-done | bytes 16416 | tf_op jit(solution)/shard_map/ppermute | solution.py:405
  130.9 2.0 %collective-permute-start.36 = (f32[8,512]{1,0:T(8,128)S(1)}, f32[8,512]{1,0:T(8,128)S(1)}, u32[]{:S(2)}, u32[]{:S(2)}) collective-permute-start(f32[8,512]{1,0:T(8,128)S(1)} %add.148), channel_id=1, source_target_pairs={{0,2},{1,3},{2,0},{3,1},{4,6},{5,7},{6,4},{7,5},{8,10},{9,11},{10,... | collective-permute-start | bytes 49160 | tf_op jit(solution)/shard_map/ppermute | solution.py:405
  132.9 1.7 collective-permute-done.36
  134.6 2.2 %collective-permute-start.37 = (f32[8,512]{1,0:T(8,128)S(1)}, f32[8,512]{1,0:T(8,128)S(1)}, u32[]{:S(2)}, u32[]{:S(2)}) collective-permute-start(f32[8,512]{1,0:T(8,128)S(1)} %add.149), channel_id=1, source_target_pairs={{0,4},{1,5},{2,6},{3,7},{4,0},{5,1},{6,2},{7,3},{8,12},{9,13},{10,... | collective-permute-start | bytes 49160 | tf_op jit(solution)/shard_map/ppermute | solution.py:405
  137.4 1.8 collective-permute-done.37
  140.7 1.6 collective-permute-start.57
  143.5 1.6 collective-permute-start.41
  146.1 8.1 %collective-permute-done.41.got_y_ref = f32[8,512]{1,0:T(8,128)S(1)} collective-permute-done((f32[8,512]{1,0:T(8,128)S(1)}, f32[8,512]{1,0:T(8,128)S(1)}, u32[]{:S(2)}, u32[]{:S(2)}) %collective-permute-start.41) | collective-permute-done | bytes 16416 | tf_op jit(solution)/shard_map/ppermute | solution.py:405
  154.2 2.4 %shard_map.278 = (bf16[432,512]{1,0:T(8,128)(2,1)S(1)}, bf16[8,10,16,256]{3,2,1,0:T(8,128)(2,1)S(1)}, bf16[8,10,16,256]{3,2,1,0:T(8,128)(2,1)S(1)}, bf16[8,10,16...) custom-call(s32[3]{0:T(128)S(1)} %pad_add_fusion.place_ref, f32[8,512]{1,0:T(8,128)S(1)} %add.139.refs_0_.sums_ref, ...), custom_call_target="tpu_custom_call" | custom-call | flops 1019215872 | bytes 4489228 | tf_op jit(solution)/shard_map/pallas_call | solution.py:389
  159.2 1.6 collective-permute-start.55
  163.7 3.5 %collective-permute-done.58 = bf16[2,9,16,512]{3,2,1,0:T(8,128)(2,1)S(1)} collective-permute-done((bf16[2,9,16,512]{3,2,1,0:T(8,128)(2,1)S(1)}, bf16[2,9,16,512]{3,2,1,0:T(8,128)(2,1)S(1)}, u32[]{:S(2)}, u32[]{:S(2)}) %collective-permute-start.58) | collective-permute-done | bytes 294944 | tf_op jit(solution)/shard_map/ppermute | solution.py:405
  167.3 1.9 collective-permute-start.60
  171.9 3.1 %collective-permute-done.47 = bf16[4,10,16,256]{3,2,1,0:T(8,128)(2,1)S(1)} collective-permute-done((bf16[4,10,16,256]{3,2,1,0:T(8,128)(2,1)S(1)}, bf16[4,10,16,256]{3,2,1,0:T(8,128)(2,1)S(1)}, u32[]{:S(2)}, u32[]{:S(2)}) %collective-permute-start.47) | collective-permute-done | bytes 327712 | tf_op jit(solution)/shard_map/ppermute | solution.py:405
  176.1 1.6 collective-permute-start.45
  177.7 2.8 %collective-permute-done.48 = bf16[2,10,16,256]{3,2,1,0:T(8,128)(2,1)S(1)} collective-permute-done((bf16[2,10,16,256]{3,2,1,0:T(8,128)(2,1)S(1)}, bf16[2,10,16,256]{3,2,1,0:T(8,128)(2,1)S(1)}, u32[]{:S(2)}, u32[]{:S(2)}) %collective-permute-start.48) | collective-permute-done | bytes 163872 | tf_op jit(solution)/shard_map/ppermute | solution.py:405
  180.5 1.7 collective-permute-start.50
  193.0 4.6 %shard_map.280 = (bf16[10,10,2,256]{3,2,1,0:T(2,128)(2,1)}, bf16[14,14,2,256]{3,2,1,0:T(2,128)(2,1)}, bf16[18,18,2,256]{3,2,1,0:T(2,128)(2,1)}) custom-call(s32[3]{0:T(128)S(1)} %pad_add_fusion.place_ref, bf16[432,512]{1,0:T(8,128)(2,1)S(1)} %get-tuple-element.97.refs_0_, bf16[432,512]{1,0:T(8,128)(2,1)S(1)} %get-tuple-element.87.side_ref.refs_1_, ...), custom_call_target="tpu_custom_call" | custom-call | flops 1019215872 | bytes 3506188 | tf_op jit(solution)/shard_map/pallas_call | solution.py:389
  197.7 1.6 shard_map.282
  (180 shorter events, 66.6 us)
Async XLA Ops:
  4.1 8.1 %collective-permute-start.2 = (bf16[10,16,256]{2,1,0:T(8,128)(2,1)S(1)}, bf16[10,16,256]{2,1,0:T(8,128)(2,1)S(1)}, u32[]{:S(2)}, u32[]{:S(2)}) collective-permute-start(bf16[10,16,256]{2,1,0:T(8,128)(2,1)S(1)} %get-tuple-element.61), channel_id=1, source_target_pairs={{0,6},{1,7},{2,4},{3,5},{4,2},{5,3},{6,0},{7,1},{8,14},{9,15},{10,... | collective-permute-start | bytes 245768 | tf_op jit(solution)/shard_map/ppermute | solution.py:405
  9.3 6.9 %collective-permute-start.1 = (bf16[10,16,256]{2,1,0:T(8,128)(2,1)S(1)}, bf16[10,16,256]{2,1,0:T(8,128)(2,1)S(1)}, u32[]{:S(2)}, u32[]{:S(2)}) collective-permute-start(bf16[10,16,256]{2,1,0:T(8,128)(2,1)S(1)} %get-tuple-element.61), channel_id=1, source_target_pairs={{0,4},{1,5},{2,6},{3,7},{4,0},{5,1},{6,2},{7,3},{8,12},{9,13},{10,... | collective-permute-start | bytes 245768 | tf_op jit(solution)/shard_map/ppermute | solution.py:405
  9.3 6.9 %collective-permute-start = (bf16[10,16,256]{2,1,0:T(8,128)(2,1)S(1)}, bf16[10,16,256]{2,1,0:T(8,128)(2,1)S(1)}, u32[]{:S(2)}, u32[]{:S(2)}) collective-permute-start(bf16[10,16,256]{2,1,0:T(8,128)(2,1)S(1)} %get-tuple-element.61), channel_id=1, source_target_pairs={{0,2},{1,3},{2,0},{3,1},{4,6},{5,7},{6,4},{7,5},{8,10},{9,11},{10,... | collective-permute-start | bytes 245768 | tf_op jit(solution)/shard_map/ppermute | solution.py:405
  16.2 16.2 %collective-permute-start.3 = (bf16[4,10,16,256]{3,2,1,0:T(8,128)(2,1)S(1)}, bf16[4,10,16,256]{3,2,1,0:T(8,128)(2,1)S(1)}, u32[]{:S(2)}, u32[]{:S(2)}) collective-permute-start(bf16[4,10,16,256]{3,2,1,0:T(8,128)(2,1)S(1)} %pad_maximum_fusion.1.refs_3_.refs_2_), channel_id=1, source_target_pairs={{0,8},{8,0},{16,24},{24,16},{1,9},{9,1},{17,25},{25,17},{2,10},{10... | collective-permute-start | bytes 983048 | tf_op jit(solution)/shard_map/ppermute | solution.py:405
  17.7 8.6 %collective-permute-start.17 = (bf16[9,16,512]{2,1,0:T(8,128)(2,1)S(1)}, bf16[9,16,512]{2,1,0:T(8,128)(2,1)S(1)}, u32[]{:S(2)}, u32[]{:S(2)}) collective-permute-start(bf16[9,16,512]{2,1,0:T(8,128)(2,1)S(1)} %get-tuple-element.65), channel_id=1, source_target_pairs={{0,6},{1,7},{2,4},{3,5},{4,2},{5,3},{6,0},{7,1},{8,14},{9,15},{10,... | collective-permute-start | bytes 442376 | tf_op jit(solution)/shard_map/ppermute | solution.py:405
  20.4 11.9 %collective-permute-start.16 = (bf16[9,16,512]{2,1,0:T(8,128)(2,1)S(1)}, bf16[9,16,512]{2,1,0:T(8,128)(2,1)S(1)}, u32[]{:S(2)}, u32[]{:S(2)}) collective-permute-start(bf16[9,16,512]{2,1,0:T(8,128)(2,1)S(1)} %get-tuple-element.65), channel_id=1, source_target_pairs={{0,4},{1,5},{2,6},{3,7},{4,0},{5,1},{6,2},{7,3},{8,12},{9,13},{10,... | collective-permute-start | bytes 442376 | tf_op jit(solution)/shard_map/ppermute | solution.py:405
  20.4 14.8 %collective-permute-start.4 = (bf16[4,10,16,256]{3,2,1,0:T(8,128)(2,1)S(1)}, bf16[4,10,16,256]{3,2,1,0:T(8,128)(2,1)}, u32[]{:S(2)}, u32[]{:S(2)}) collective-permute-start(bf16[4,10,16,256]{3,2,1,0:T(8,128)(2,1)S(1)} %pad_maximum_fusion.1.refs_3_.refs_2_), channel_id=1, source_target_pairs={{0,16},{8,24},{16,0},{24,8},{1,17},{9,25},{17,1},{25,9},{2,18},{10... | collective-permute-start | bytes 983048 | tf_op jit(solution)/shard_map/ppermute | solution.py:405
  21.9 14.8 %collective-permute-start.5 = (bf16[4,10,16,256]{3,2,1,0:T(8,128)(2,1)S(1)}, bf16[4,10,16,256]{3,2,1,0:T(8,128)(2,1)}, u32[]{:S(2)}, u32[]{:S(2)}) collective-permute-start(bf16[4,10,16,256]{3,2,1,0:T(8,128)(2,1)S(1)} %pad_maximum_fusion.1.refs_3_.refs_2_), channel_id=1, source_target_pairs={{0,24},{8,16},{16,8},{24,0},{1,25},{9,17},{17,9},{25,1},{2,26},{10... | collective-permute-start | bytes 983048 | tf_op jit(solution)/shard_map/ppermute | solution.py:405
  26.4 8.1 %collective-permute-start.15 = (bf16[9,16,512]{2,1,0:T(8,128)(2,1)S(1)}, bf16[9,16,512]{2,1,0:T(8,128)(2,1)S(1)}, u32[]{:S(2)}, u32[]{:S(2)}) collective-permute-start(bf16[9,16,512]{2,1,0:T(8,128)(2,1)S(1)} %get-tuple-element.65), channel_id=1, source_target_pairs={{0,2},{1,3},{2,0},{3,1},{4,6},{5,7},{6,4},{7,5},{8,10},{9,11},{10,... | collective-permute-start | bytes 442376 | tf_op jit(solution)/shard_map/ppermute | solution.py:405
  32.3 5.7 %collective-permute-start.6 = (bf16[4,10,16,256]{3,2,1,0:T(8,128)(2,1)S(1)}, bf16[4,10,16,256]{3,2,1,0:T(8,128)(2,1)S(1)}, u32[]{:S(2)}, u32[]{:S(2)}) collective-permute-start(bf16[4,10,16,256]{3,2,1,0:T(8,128)(2,1)S(1)} %pad_maximum_fusion.1.refs_3_.refs_2_), channel_id=1, source_target_pairs={{0,1},{1,0},{2,3},{3,2},{4,5},{5,4},{6,7},{7,6},{8,9},{9,8},{10,11... | collective-permute-start | bytes 983048 | tf_op jit(solution)/shard_map/ppermute | solution.py:405
  32.4 6.4 %collective-permute-start.7 = (bf16[4,10,16,256]{3,2,1,0:T(8,128)(2,1)S(1)}, bf16[4,10,16,256]{3,2,1,0:T(8,128)(2,1)S(1)}, u32[]{:S(2)}, u32[]{:S(2)}) collective-permute-start(bf16[4,10,16,256]{3,2,1,0:T(8,128)(2,1)S(1)} %collective-permute-done.3.refs_4_.refs_3_), channel_id=1, source_target_pairs={{0,1},{1,0},{2,3},{3,2},{4,5},{5,4},{6,7},{7,6},{8,9},{9,8},{10,11... | collective-permute-start | bytes 983048 | tf_op jit(solution)/shard_map/ppermute | solution.py:405
  34.5 37.5 %collective-permute-start.18 = (bf16[4,9,16,512]{3,2,1,0:T(8,128)(2,1)S(1)}, bf16[4,9,16,512]{3,2,1,0:T(8,128)(2,1)S(1)}, u32[]{:S(2)}, u32[]{:S(2)}) collective-permute-start(bf16[4,9,16,512]{3,2,1,0:T(8,128)(2,1)S(1)} %pad_maximum_fusion.refs_5_.refs_11_), channel_id=1, source_target_pairs={{0,8},{8,0},{16,24},{24,16},{1,9},{9,1},{17,25},{25,17},{2,10},{10... | collective-permute-start | bytes 1769480 | tf_op jit(solution)/shard_map/ppermute | solution.py:405
  35.2 36.8 %collective-permute-start.19 = (bf16[4,9,16,512]{3,2,1,0:T(8,128)(2,1)S(1)}, bf16[4,9,16,512]{3,2,1,0:T(8,128)(2,1)S(1)}, u32[]{:S(2)}, u32[]{:S(2)}) collective-permute-start(bf16[4,9,16,512]{3,2,1,0:T(8,128)(2,1)S(1)} %pad_maximum_fusion.refs_5_.refs_11_), channel_id=1, source_target_pairs={{0,16},{8,24},{16,0},{24,8},{1,17},{9,25},{17,1},{25,9},{2,18},{10... | collective-permute-start | bytes 1769480 | tf_op jit(solution)/shard_map/ppermute | solution.py:405
  36.8 35.3 %collective-permute-start.20 = (bf16[4,9,16,512]{3,2,1,0:T(8,128)(2,1)S(1)}, bf16[4,9,16,512]{3,2,1,0:T(8,128)(2,1)S(1)}, u32[]{:S(2)}, u32[]{:S(2)}) collective-permute-start(bf16[4,9,16,512]{3,2,1,0:T(8,128)(2,1)S(1)} %pad_maximum_fusion.refs_5_.refs_11_), channel_id=1, source_target_pairs={{0,24},{8,16},{16,8},{24,0},{1,25},{9,17},{17,9},{25,1},{2,26},{10... | collective-permute-start | bytes 1769480 | tf_op jit(solution)/shard_map/ppermute | solution.py:405
  38.8 11.6 %collective-permute-start.8 = (bf16[4,10,16,256]{3,2,1,0:T(8,128)(2,1)}, bf16[4,10,16,256]{3,2,1,0:T(8,128)(2,1)}, u32[]{:S(2)}, u32[]{:S(2)}) collective-permute-start(bf16[4,10,16,256]{3,2,1,0:T(8,128)(2,1)} %collective-permute-done.4.refs_5_.refs_4_), channel_id=1, source_target_pairs={{0,1},{1,0},{2,3},{3,2},{4,5},{5,4},{6,7},{7,6},{8,9},{9,8},{10,11... | collective-permute-start | bytes 983048 | tf_op jit(solution)/shard_map/ppermute | solution.py:405
  39.5 10.9 %collective-permute-start.9 = (bf16[4,10,16,256]{3,2,1,0:T(8,128)(2,1)}, bf16[4,10,16,256]{3,2,1,0:T(8,128)(2,1)}, u32[]{:S(2)}, u32[]{:S(2)}) collective-permute-start(bf16[4,10,16,256]{3,2,1,0:T(8,128)(2,1)} %collective-permute-done.5.refs_6_.refs_5_), channel_id=1, source_target_pairs={{0,1},{1,0},{2,3},{3,2},{4,5},{5,4},{6,7},{7,6},{8,9},{9,8},{10,11... | collective-permute-start | bytes 983048 | tf_op jit(solution)/shard_map/ppermute | solution.py:405
  56.1 3.7 %collective-permute-start.11 = (f32[8,512]{1,0:T(8,128)S(1)}, f32[8,512]{1,0:T(8,128)S(1)}, u32[]{:S(2)}, u32[]{:S(2)}) collective-permute-start(f32[8,512]{1,0:T(8,128)S(1)} %add.136), channel_id=1, source_target_pairs={{0,2},{1,3},{2,0},{3,1},{4,6},{5,7},{6,4},{7,5},{8,10},{9,11},{10,... | collective-permute-start | bytes 49160 | tf_op jit(solution)/shard_map/ppermute | solution.py:405
  59.9 4.6 %collective-permute-start.12 = (f32[8,512]{1,0:T(8,128)S(1)}, f32[8,512]{1,0:T(8,128)S(1)}, u32[]{:S(2)}, u32[]{:S(2)}) collective-permute-start(f32[8,512]{1,0:T(8,128)S(1)} %add.137), channel_id=1, source_target_pairs={{0,4},{1,5},{2,6},{3,7},{4,0},{5,1},{6,2},{7,3},{8,12},{9,13},{10,... | collective-permute-start | bytes 49160 | tf_op jit(solution)/shard_map/ppermute | solution.py:405
  72.7 3.9 %collective-permute-start.24 = (bf16[4,9,16,512]{3,2,1,0:T(8,128)(2,1)S(1)}, bf16[4,9,16,512]{3,2,1,0:T(8,128)(2,1)S(1)}, u32[]{:S(2)}, u32[]{:S(2)}) collective-permute-start(bf16[4,9,16,512]{3,2,1,0:T(8,128)(2,1)S(1)} %collective-permute-done.20.refs_8_.refs_14_), channel_id=1, source_target_pairs={{0,1},{1,0},{2,3},{3,2},{4,5},{5,4},{6,7},{7,6},{8,9},{9,8},{10,11... | collective-permute-start | bytes 1769480 | tf_op jit(solution)/shard_map/ppermute | solution.py:405
  86.6 4.6 %collective-permute-start.27 = (f32[8,512]{1,0:T(8,128)S(1)}, f32[8,512]{1,0:T(8,128)S(1)}, u32[]{:S(2)}, u32[]{:S(2)}) collective-permute-start(f32[8,512]{1,0:T(8,128)S(1)} %add.141), channel_id=1, source_target_pairs={{0,4},{1,5},{2,6},{3,7},{4,0},{5,1},{6,2},{7,3},{8,12},{9,13},{10,... | collective-permute-start | bytes 49160 | tf_op jit(solution)/shard_map/ppermute | solution.py:405
  104.6 4.6 %collective-permute-start.32 = (f32[8,512]{1,0:T(8,128)S(1)}, f32[8,512]{1,0:T(8,128)S(1)}, u32[]{:S(2)}, u32[]{:S(2)}) collective-permute-start(f32[8,512]{1,0:T(8,128)S(1)} %add.145), channel_id=1, source_target_pairs={{0,4},{1,5},{2,6},{3,7},{4,0},{5,1},{6,2},{7,3},{8,12},{9,13},{10,... | collective-permute-start | bytes 49160 | tf_op jit(solution)/shard_map/ppermute | solution.py:405
  126.2 13.9 %collective-permute-start.40 = (bf16[8,9,16,512]{3,2,1,0:T(8,128)(2,1)S(1)}, bf16[8,9,16,512]{3,2,1,0:T(8,128)(2,1)S(1)}, u32[]{:S(2)}, u32[]{:S(2)}) collective-permute-start(bf16[8,9,16,512]{3,2,1,0:T(8,128)(2,1)S(1)} %get-tuple-element.83), channel_id=1, source_target_pairs={{0,1},{1,0},{2,3},{3,2},{4,5},{5,4},{6,7},{7,6},{8,9},{9,8},{10,11... | collective-permute-start | bytes 3538952 | tf_op jit(solution)/shard_map/ppermute | solution.py:405
  126.3 16.7 %collective-permute-start.39 = (bf16[8,9,16,512]{3,2,1,0:T(8,128)(2,1)S(1)}, bf16[8,9,16,512]{3,2,1,0:T(8,128)(2,1)S(1)}, u32[]{:S(2)}, u32[]{:S(2)}) collective-permute-start(bf16[8,9,16,512]{3,2,1,0:T(8,128)(2,1)S(1)} %get-tuple-element.82), channel_id=1, source_target_pairs={{0,1},{1,0},{2,3},{3,2},{4,5},{5,4},{6,7},{7,6},{8,9},{9,8},{10,11... | collective-permute-start | bytes 3538952 | tf_op jit(solution)/shard_map/ppermute | solution.py:405
  126.8 4.0 %collective-permute-start.35 = (f32[8,512]{1,0:T(8,128)S(1)}, f32[8,512]{1,0:T(8,128)S(1)}, u32[]{:S(2)}, u32[]{:S(2)}) collective-permute-start(f32[8,512]{1,0:T(8,128)S(1)} %get-tuple-element.77), channel_id=1, source_target_pairs={{0,1},{1,0},{2,3},{3,2},{4,5},{5,4},{6,7},{7,6},{8,9},{9,8},{10,11... | collective-permute-start | bytes 49160 | tf_op jit(solution)/shard_map/ppermute | solution.py:405
  134.6 4.6 %collective-permute-start.37 = (f32[8,512]{1,0:T(8,128)S(1)}, f32[8,512]{1,0:T(8,128)S(1)}, u32[]{:S(2)}, u32[]{:S(2)}) collective-permute-start(f32[8,512]{1,0:T(8,128)S(1)} %add.149), channel_id=1, source_target_pairs={{0,4},{1,5},{2,6},{3,7},{4,0},{5,1},{6,2},{7,3},{8,12},{9,13},{10,... | collective-permute-start | bytes 49160 | tf_op jit(solution)/shard_map/ppermute | solution.py:405
  140.7 16.5 %collective-permute-start.57 = (bf16[4,9,16,512]{3,2,1,0:T(8,128)(2,1)S(1)}, bf16[4,9,16,512]{3,2,1,0:T(8,128)(2,1)S(1)}, u32[]{:S(2)}, u32[]{:S(2)}) collective-permute-start(bf16[4,9,16,512]{3,2,1,0:T(8,128)(2,1)S(1)} %slice.165), channel_id=1, source_target_pairs={{0,16},{8,24},{16,0},{24,8},{1,17},{9,25},{17,1},{25,9},{2,18},{10... | collective-permute-start | bytes 1769480 | tf_op jit(solution)/shard_map/ppermute | solution.py:405
  143.5 10.7 %collective-permute-start.41 = (f32[8,512]{1,0:T(8,128)S(1)}, f32[8,512]{1,0:T(8,128)S(1)}, u32[]{:S(2)}, u32[]{:S(2)}) collective-permute-start(f32[8,512]{1,0:T(8,128)S(1)} %add.151.sums_y_ref), channel_id=1, source_target_pairs={{0,16},{8,24},{16,0},{24,8},{1,17},{9,25},{17,1},{25,9},{2,18},{10... | collective-permute-start | bytes 49160 | tf_op jit(solution)/shard_map/ppermute | solution.py:405
  145.1 14.0 %collective-permute-start.54 = (bf16[4,9,16,512]{3,2,1,0:T(8,128)(2,1)S(1)}, bf16[4,9,16,512]{3,2,1,0:T(8,128)(2,1)S(1)}, u32[]{:S(2)}, u32[]{:S(2)}) collective-permute-start(bf16[4,9,16,512]{3,2,1,0:T(8,128)(2,1)S(1)} %slice.159), channel_id=1, source_target_pairs={{0,8},{8,0},{16,24},{24,16},{1,9},{9,1},{17,25},{25,17},{2,10},{10... | collective-permute-start | bytes 1769480 | tf_op jit(solution)/shard_map/ppermute | solution.py:405
  156.6 4.4 %collective-permute-start.42 = (bf16[8,10,16,256]{3,2,1,0:T(8,128)(2,1)S(1)}, bf16[8,10,16,256]{3,2,1,0:T(8,128)(2,1)S(1)}, u32[]{:S(2)}, u32[]{:S(2)}) collective-permute-start(bf16[8,10,16,256]{3,2,1,0:T(8,128)(2,1)S(1)} %get-tuple-element.89), channel_id=1, source_target_pairs={{0,1},{1,0},{2,3},{3,2},{4,5},{5,4},{6,7},{7,6},{8,9},{9,8},{10,11... | collective-permute-start | bytes 1966088 | tf_op jit(solution)/shard_map/ppermute | solution.py:405
  156.7 4.1 %collective-permute-start.43 = (bf16[8,10,16,256]{3,2,1,0:T(8,128)(2,1)S(1)}, bf16[8,10,16,256]{3,2,1,0:T(8,128)(2,1)S(1)}, u32[]{:S(2)}, u32[]{:S(2)}) collective-permute-start(bf16[8,10,16,256]{3,2,1,0:T(8,128)(2,1)S(1)} %get-tuple-element.91), channel_id=1, source_target_pairs={{0,1},{1,0},{2,3},{3,2},{4,5},{5,4},{6,7},{7,6},{8,9},{9,8},{10,11... | collective-permute-start | bytes 1966088 | tf_op jit(solution)/shard_map/ppermute | solution.py:405
  157.3 9.9 %collective-permute-start.58 = (bf16[2,9,16,512]{3,2,1,0:T(8,128)(2,1)S(1)}, bf16[2,9,16,512]{3,2,1,0:T(8,128)(2,1)S(1)}, u32[]{:S(2)}, u32[]{:S(2)}) collective-permute-start(bf16[2,9,16,512]{3,2,1,0:T(8,128)(2,1)S(1)} %slice.167), channel_id=1, source_target_pairs={{0,8},{8,0},{16,24},{24,16},{1,9},{9,1},{17,25},{25,17},{2,10},{10... | collective-permute-start | bytes 884744 | tf_op jit(solution)/shard_map/ppermute | solution.py:405
  159.2 11.4 %collective-permute-start.55 = (bf16[2,9,16,512]{3,2,1,0:T(8,128)(2,1)S(1)}, bf16[2,9,16,512]{3,2,1,0:T(8,128)(2,1)S(1)}, u32[]{:S(2)}, u32[]{:S(2)}) collective-permute-start(bf16[2,9,16,512]{3,2,1,0:T(8,128)(2,1)S(1)} %slice.161), channel_id=1, source_target_pairs={{0,16},{8,24},{16,0},{24,8},{1,17},{9,25},{17,1},{25,9},{2,18},{10... | collective-permute-start | bytes 884744 | tf_op jit(solution)/shard_map/ppermute | solution.py:405
  162.1 12.9 %collective-permute-start.47 = (bf16[4,10,16,256]{3,2,1,0:T(8,128)(2,1)S(1)}, bf16[4,10,16,256]{3,2,1,0:T(8,128)(2,1)S(1)}, u32[]{:S(2)}, u32[]{:S(2)}) collective-permute-start(bf16[4,10,16,256]{3,2,1,0:T(8,128)(2,1)S(1)} %slice.151), channel_id=1, source_target_pairs={{0,16},{8,24},{16,0},{24,8},{1,17},{9,25},{17,1},{25,9},{2,18},{10... | collective-permute-start | bytes 983048 | tf_op jit(solution)/shard_map/ppermute | solution.py:405
  162.6 13.4 %collective-permute-start.44 = (bf16[4,10,16,256]{3,2,1,0:T(8,128)(2,1)S(1)}, bf16[4,10,16,256]{3,2,1,0:T(8,128)(2,1)S(1)}, u32[]{:S(2)}, u32[]{:S(2)}) collective-permute-start(bf16[4,10,16,256]{3,2,1,0:T(8,128)(2,1)S(1)} %slice.145), channel_id=1, source_target_pairs={{0,8},{8,0},{16,24},{24,16},{1,9},{9,1},{17,25},{25,17},{2,10},{10... | collective-permute-start | bytes 983048 | tf_op jit(solution)/shard_map/ppermute | solution.py:405
  167.3 16.5 %collective-permute-start.60 = (bf16[9,16,512]{2,1,0:T(8,128)(2,1)S(1)}, bf16[9,16,512]{2,1,0:T(8,128)(2,1)S(1)}, u32[]{:S(2)}, u32[]{:S(2)}) collective-permute-start(bf16[9,16,512]{2,1,0:T(8,128)(2,1)S(1)} %get-tuple-element.104), channel_id=1, source_target_pairs={{0,6},{1,7},{2,4},{3,5},{4,2},{5,3},{6,0},{7,1},{8,14},{9,15},{10,... | collective-permute-start | bytes 442376 | tf_op jit(solution)/shard_map/ppermute | solution.py:405
  169.2 15.8 %collective-permute-start.59 = (bf16[9,16,512]{2,1,0:T(8,128)(2,1)S(1)}, bf16[9,16,512]{2,1,0:T(8,128)(2,1)S(1)}, u32[]{:S(2)}, u32[]{:S(2)}) collective-permute-start(bf16[9,16,512]{2,1,0:T(8,128)(2,1)S(1)} %get-tuple-element.103), channel_id=1, source_target_pairs={{0,4},{1,5},{2,6},{3,7},{4,0},{5,1},{6,2},{7,3},{8,12},{9,13},{10,... | collective-permute-start | bytes 442376 | tf_op jit(solution)/shard_map/ppermute | solution.py:405
  170.6 14.4 %collective-permute-start.56 = (bf16[9,16,512]{2,1,0:T(8,128)(2,1)S(1)}, bf16[9,16,512]{2,1,0:T(8,128)(2,1)S(1)}, u32[]{:S(2)}, u32[]{:S(2)}) collective-permute-start(bf16[9,16,512]{2,1,0:T(8,128)(2,1)S(1)} %slice_bitcast_fusion.2), channel_id=1, source_target_pairs={{0,2},{1,3},{2,0},{3,1},{4,6},{5,7},{6,4},{7,5},{8,10},{9,11},{10,... | collective-permute-start | bytes 442376 | tf_op jit(solution)/shard_map/ppermute | solution.py:405
  175.1 5.4 %collective-permute-start.48 = (bf16[2,10,16,256]{3,2,1,0:T(8,128)(2,1)S(1)}, bf16[2,10,16,256]{3,2,1,0:T(8,128)(2,1)S(1)}, u32[]{:S(2)}, u32[]{:S(2)}) collective-permute-start(bf16[2,10,16,256]{3,2,1,0:T(8,128)(2,1)S(1)} %slice.153), channel_id=1, source_target_pairs={{0,8},{8,0},{16,24},{24,16},{1,9},{9,1},{17,25},{25,17},{2,10},{10... | collective-permute-start | bytes 491528 | tf_op jit(solution)/shard_map/ppermute | solution.py:405
  176.1 6.2 %collective-permute-start.45 = (bf16[2,10,16,256]{3,2,1,0:T(8,128)(2,1)S(1)}, bf16[2,10,16,256]{3,2,1,0:T(8,128)(2,1)S(1)}, u32[]{:S(2)}, u32[]{:S(2)}) collective-permute-start(bf16[2,10,16,256]{3,2,1,0:T(8,128)(2,1)S(1)} %slice.147), channel_id=1, source_target_pairs={{0,16},{8,24},{16,0},{24,8},{1,17},{9,25},{17,1},{25,9},{2,18},{10... | collective-permute-start | bytes 491528 | tf_op jit(solution)/shard_map/ppermute | solution.py:405
  180.5 7.1 %collective-permute-start.50 = (bf16[10,16,256]{2,1,0:T(8,128)(2,1)S(1)}, bf16[10,16,256]{2,1,0:T(8,128)(2,1)S(1)}, u32[]{:S(2)}, u32[]{:S(2)}) collective-permute-start(bf16[10,16,256]{2,1,0:T(8,128)(2,1)S(1)} %get-tuple-element.106), channel_id=1, source_target_pairs={{0,6},{1,7},{2,4},{3,5},{4,2},{5,3},{6,0},{7,1},{8,14},{9,15},{10,... | collective-permute-start | bytes 245768 | tf_op jit(solution)/shard_map/ppermute | solution.py:405
  182.2 7.2 %collective-permute-start.49 = (bf16[10,16,256]{2,1,0:T(8,128)(2,1)S(1)}, bf16[10,16,256]{2,1,0:T(8,128)(2,1)S(1)}, u32[]{:S(2)}, u32[]{:S(2)}) collective-permute-start(bf16[10,16,256]{2,1,0:T(8,128)(2,1)S(1)} %get-tuple-element.105), channel_id=1, source_target_pairs={{0,4},{1,5},{2,6},{3,7},{4,0},{5,1},{6,2},{7,3},{8,12},{9,13},{10,... | collective-permute-start | bytes 245768 | tf_op jit(solution)/shard_map/ppermute | solution.py:405
  183.8 5.6 %collective-permute-start.46 = (bf16[10,16,256]{2,1,0:T(8,128)(2,1)S(1)}, bf16[10,16,256]{2,1,0:T(8,128)(2,1)S(1)}, u32[]{:S(2)}, u32[]{:S(2)}) collective-permute-start(bf16[10,16,256]{2,1,0:T(8,128)(2,1)S(1)} %slice_bitcast_fusion.6), channel_id=1, source_target_pairs={{0,2},{1,3},{2,0},{3,1},{4,6},{5,7},{6,4},{7,5},{8,10},{9,11},{10,... | collective-permute-start | bytes 245768 | tf_op jit(solution)/shard_map/ppermute | solution.py:405
  185.2 6.8 %collective-permute-start.61 = (bf16[9,16,512]{2,1,0:T(8,128)(2,1)S(1)}, bf16[9,16,512]{2,1,0:T(8,128)(2,1)S(1)}, u32[]{:S(2)}, u32[]{:S(2)}) collective-permute-start(bf16[9,16,512]{2,1,0:T(8,128)(2,1)S(1)} %fusion.2.refs_0_), channel_id=1, source_target_pairs={{0,8},{8,0},{16,24},{24,16},{1,9},{9,1},{17,25},{25,17},{2,10},{10... | collective-permute-start | bytes 442376 | tf_op jit(solution)/shard_map/ppermute | solution.py:405
  186.1 11.5 %collective-permute-start.62 = (bf16[9,16,512]{2,1,0:T(8,128)(2,1)S(1)}, bf16[9,16,512]{2,1,0:T(8,128)(2,1)S(1)}, u32[]{:S(2)}, u32[]{:S(2)}) collective-permute-start(bf16[9,16,512]{2,1,0:T(8,128)(2,1)S(1)} %fusion.2.refs_0_), channel_id=1, source_target_pairs={{0,16},{8,24},{16,0},{24,8},{1,17},{9,25},{17,1},{25,9},{2,18},{10... | collective-permute-start | bytes 442376 | tf_op jit(solution)/shard_map/ppermute | solution.py:405
  187.6 10.0 %collective-permute-start.63 = (bf16[9,16,512]{2,1,0:T(8,128)(2,1)S(1)}, bf16[9,16,512]{2,1,0:T(8,128)(2,1)S(1)}, u32[]{:S(2)}, u32[]{:S(2)}) collective-permute-start(bf16[9,16,512]{2,1,0:T(8,128)(2,1)S(1)} %fusion.2.refs_0_), channel_id=1, source_target_pairs={{0,24},{8,16},{16,8},{24,0},{1,25},{9,17},{17,9},{25,1},{2,26},{10... | collective-permute-start | bytes 442376 | tf_op jit(solution)/shard_map/ppermute | solution.py:405
  189.5 9.8 %collective-permute-start.51 = (bf16[10,16,256]{2,1,0:T(8,128)(2,1)S(1)}, bf16[10,16,256]{2,1,0:T(8,128)(2,1)S(1)}, u32[]{:S(2)}, u32[]{:S(2)}) collective-permute-start(bf16[10,16,256]{2,1,0:T(8,128)(2,1)S(1)} %fusion.5.refs_0_), channel_id=1, source_target_pairs={{0,8},{8,0},{16,24},{24,16},{1,9},{9,1},{17,25},{25,17},{2,10},{10... | collective-permute-start | bytes 245768 | tf_op jit(solution)/shard_map/ppermute | solution.py:405
  190.4 8.9 %collective-permute-start.52 = (bf16[10,16,256]{2,1,0:T(8,128)(2,1)S(1)}, bf16[10,16,256]{2,1,0:T(8,128)(2,1)S(1)}, u32[]{:S(2)}, u32[]{:S(2)}) collective-permute-start(bf16[10,16,256]{2,1,0:T(8,128)(2,1)S(1)} %fusion.5.refs_0_), channel_id=1, source_target_pairs={{0,16},{8,24},{16,0},{24,8},{1,17},{9,25},{17,1},{25,9},{2,18},{10... | collective-permute-start | bytes 245768 | tf_op jit(solution)/shard_map/ppermute | solution.py:405
  192.0 7.4 %collective-permute-start.53 = (bf16[10,16,256]{2,1,0:T(8,128)(2,1)S(1)}, bf16[10,16,256]{2,1,0:T(8,128)(2,1)S(1)}, u32[]{:S(2)}, u32[]{:S(2)}) collective-permute-start(bf16[10,16,256]{2,1,0:T(8,128)(2,1)S(1)} %fusion.5.refs_0_), channel_id=1, source_target_pairs={{0,24},{8,16},{16,8},{24,0},{1,25},{9,17},{17,9},{25,1},{2,26},{10... | collective-permute-start | bytes 245768 | tf_op jit(solution)/shard_map/ppermute | solution.py:405
  (32 other events, 217.1 us)

commit v3 on v2

--- a/solution.py
+++ b/solution.py
@@ -100,12 +100,19 @@
     padded_ref[plan.margin + plan.rows :, :] = edge
 
 
-def prepare_kernel(plan, counts_ref, *refs):
-    fields, cots, (patches_ref, cot_ref, mask_ref, held_ref) = refs[:3], refs[3:6], refs[6:]
+def prepare_kernel(plan, owned, place_ref, counts_ref, *refs):
+    fields, cots, vectors = refs[:3], refs[3:6], refs[6:12]
+    patches_ref, cot_ref, mask_ref, vec_ref, held_ref = refs[12:]
     slots, channels = plan.slots, fields[0].shape[3]
     held_ref[...] = jnp.zeros(held_ref.shape, F32)
     cot_ref[...] = jnp.zeros(cot_ref.shape, F32)
     mask_ref[...] = jnp.zeros(mask_ref.shape, F32)
+    cout = vec_ref.shape[1]
+    first = (place_ref[2] * 2 + place_ref[0]) * owned
+    spot = lax.broadcasted_iota(jnp.int32, (owned, cout), 1) - lax.broadcasted_iota(jnp.int32, (owned, cout), 0)
+    own = ((spot == first) & (place_ref[1] == 0)).astype(BF16)
+    held = [ref[...].astype(F32) for ref in vectors] + [jnp.zeros((vec_ref.shape[0] - 6, owned), F32)]
+    vec_ref[...] = nn(jnp.concatenate(held, axis=0).astype(BF16), own)
     slot = lax.broadcasted_iota(jnp.int32, (slots, mask_ref.shape[1]), 0)
     live = [(slot < counts_ref[0, group]).astype(F32) for group in range(3)]
     for group, down, right, row in plan.cells():
@@ -124,11 +131,6 @@
                 patches_ref[start : start + size, tap * channels : (tap + 1) * channels] = held_ref[
                     2 * (ky != 1) + (kx != 1), first : first + size, :
                 ].astype(BF16)
-
-
-def output_rows_kernel(plan, rows_ref, *outs):
-    for group, down, right, row in plan.cells():
-        outs[group][down, right] = rows_ref[row : row + plan.slots, :].astype(BF16)
 
 
 def first_kernel(patches_ref, mask_ref, vec_ref, weights_ref, ready, first_ref, side_ref, sums_ref):
@@ -177,8 +179,9 @@
 
 
 def output_kernel(
-    sums_ref, got_ref, sums_two_ref, got_two_ref, second_ref, side_ref, cot_ref, mask_ref, out_ref, dz_ref, sums_out_ref
+    plan, sums_ref, got_ref, sums_two_ref, got_two_ref, second_ref, side_ref, cot_ref, mask_ref, *refs
 ):
+    outs, (dz_ref, sums_out_ref) = refs[:3], refs[3:]
     cout = second_ref.shape[1]
     mask = wide(mask_ref, cout)
     sums, sums_two = sums_ref[...] + got_ref[...], sums_two_ref[...] + got_two_ref[...]
@@ -187,7 +190,9 @@
     normed_side, _ = norm(side_ref[...], sums, 2, total)
     value = (normed_two * sums_two[2:3] + sums_two[3:4]) + (normed_side * sums_two[4:5] + sums_two[5:6])
     gate = jax.nn.sigmoid(value)
-    out_ref[...] = value * gate * mask
+    out = (value * gate * mask).astype(BF16)
+    for group, down, right, row in plan.cells():
+        outs[group][down, right] = out[row : row + plan.slots, :]
     grad = cot_ref[...] * mask * (gate * (1.0 + value * (1.0 - gate)))
     dz_ref[...] = grad
     total = column(grad)
@@ -292,9 +297,18 @@
         out_ref[index] = nn(turned, patches_ref[:, tap * channels : (tap + 1) * channels]).astype(BF16)
 
 
-def input_kernel(plan, grad_ref, side_ref, weights_ref, ready, *refs):
-    outs, (held_ref, moved_ref, total_ref) = refs[:3], refs[3:]
+def input_kernel(
+    plan, owned, place_ref, sums_z_ref, got_z_ref, sums_y_ref, got_y_ref, grad_ref, side_ref, weights_ref, ready, *refs
+):
+    outs, owns, (held_ref, moved_ref, total_ref) = refs[:3], refs[3:9], refs[9:]
     ready()
+    sums = jnp.concatenate([sums_z_ref[...] + got_z_ref[...], sums_y_ref[...] + got_y_ref[...]], axis=0)
+    first = (place_ref[2] * 2 + place_ref[0]) * owned
+    spot = lax.broadcasted_iota(jnp.int32, sums.shape, 1)
+    sums = jnp.where((spot >= first) & (spot < first + owned), sums, 0.0)
+    sums = sum(sums[:, begin : begin + owned] for begin in range(0, sums.shape[1], owned))
+    for row, ref in zip((8, 9, 1, 0, 2, 3), owns):
+        ref[...] = sums[row : row + 1]
     rows = plan.rows
     fill(plan, held_ref, grad_ref[...].astype(F32))
     for index, (down, right) in enumerate(((0, 0), (0, 1), (1, 0), (1, 1))):
@@ -328,49 +342,61 @@
 
 
 class Gathered:
-    def __init__(self, arrays, place=None, order=None):
-        self.arrays, self.place, self.order = arrays, place, order
+    def __init__(self, arrays, place=None, order=None, labels=(), far=False):
+        self.arrays, self.place, self.order, self.labels, self.far = arrays, place, order, labels, far
 
     def dims(self):
         if self.order is None:
             return self.arrays[0].shape
-        zs, taps, quarter, channels = self.arrays[0].shape
-        return taps, 2 * zs * self.order.owned, channels
+        taps, quarter, channels = self.arrays[0].shape[-3:]
+        return taps, quarter * len(self.labels), channels
 
     def wrap(self, body, scalars, count):
         if self.order is None:
             return lambda *refs: body(*refs[: count + 1], lambda: None, *refs[count + 1 :])
-        order, many = self.order, len(self.arrays)
+        order, many, labels, far = self.order, len(self.arrays), self.labels, self.far
 
         def whole(place_ref, *refs):
             inputs, bundles, rest = refs[:count], refs[count : count + many], refs[count + many :]
-            outs, (weights_ref, semaphores) = rest[:-2], rest[-2:]
+            whole_ref, outs, semaphores = rest[0], rest[1:-1], rest[-1]
+            if far:
+                weights_ref, outs = outs[-1], outs[:-1]
+                leave = pltpu.make_async_copy(weights_ref, whole_ref, semaphores.at[len(labels)])
+            else:
+                weights_ref = whole_ref
             core, b, z = place_ref[0], place_ref[1], place_ref[2]
             copies = []
-            for index, bundle in enumerate(bundles):
-                for rel_z in range(order.zs):
-                    row = ((z ^ rel_z) * 2 + (core ^ (index // 4))) * order.owned + (b ^ (index % 4)) * order.quarter
-                    rows = pl.ds(pl.multiple_of(row, order.quarter), order.quarter)
-                    copies.append(
-                        pltpu.make_async_copy(
-                            bundle.at[rel_z], weights_ref.at[:, rows, :], semaphores.at[index * order.zs + rel_z]
-                        )
-                    )
+            for index, at, rel_core, quarter, rel_z in labels:
+                row = ((z ^ rel_z) * 2 + (core ^ rel_core)) * order.owned + quarter(b) * order.quarter
+                rows = pl.ds(pl.multiple_of(row, order.quarter), order.quarter)
+                copies.append(
+                    pltpu.make_async_copy(bundles[index].at[at], weights_ref.at[:, rows, :], semaphores.at[len(copies)])
+                )
             for copy in copies:
                 copy.start()
 
             def ready():
                 for copy in copies:
                     copy.wait()
+                if far:
+                    leave.start()
 
             body(*inputs, weights_ref, ready, *outs)
+            if far:
+                leave.wait()
 
         return whole
 
 
-def call(body, out_shapes, *args, scratch=(), scalars=0, flops=0, weights=None):
+def call(body, out_shapes, *args, scratch=(), scalars=0, flops=0, weights=None, far=False, whole=True):
     vmem = pl.BlockSpec(memory_space=pltpu.VMEM)
-    specs = [pl.BlockSpec(memory_space=pltpu.SMEM)] * scalars + [vmem] * (len(args) - scalars)
+    inner = vmem if whole else pl.BlockSpec(memory_space=pltpu.MemorySpace.HBM)
+    if far:
+        args = args[:scalars] + tuple(
+            pltpu.with_memory_space_constraint(arg, pltpu.MemorySpace.HBM) for arg in args[scalars:]
+        )
+    first_out = vmem
+    specs = [pl.BlockSpec(memory_space=pltpu.SMEM)] * scalars + [inner] * (len(args) - scalars)
     if weights is not None:
         body = weights.wrap(body, scalars, len(args))
         scratch = list(scratch)
@@ -380,16 +406,17 @@
         else:
             args = (weights.place,) + args + tuple(weights.arrays)
             specs = [pl.BlockSpec(memory_space=pltpu.SMEM)] + specs + [pl.BlockSpec(memory_space=pl.ANY)] * len(weights.arrays)
-            scratch += [
-                pltpu.VMEM(weights.dims(), BF16),
-                pltpu.SemaphoreType.DMA((len(weights.arrays) * weights.order.zs,)),
-            ]
+            out_shapes = [shape(weights.dims(), BF16)] + list(out_shapes)
+            if weights.far:
+                scratch += [pltpu.VMEM(weights.dims(), BF16)]
+                first_out = pl.BlockSpec(memory_space=pltpu.MemorySpace.HBM)
+            scratch += [pltpu.SemaphoreType.DMA((len(weights.labels) + weights.far,))]
     many = isinstance(out_shapes, (list, tuple))
     moved = sum(arg.size * arg.dtype.itemsize for arg in args)
     return pl.pallas_call(
         body,
         in_specs=specs,
-        out_specs=[vmem] * len(out_shapes) if many else vmem,
+        out_specs=[first_out] + [vmem] * (len(out_shapes) - 1) if many else vmem,
         out_shape=list(out_shapes) if many else out_shapes,
         scratch_shapes=list(scratch),
         compiler_params=pltpu.CompilerParams(vmem_limit_bytes=VMEM_LIMIT),
@@ -413,41 +440,92 @@
     return lax.optimization_barrier((value, *others))[0]
 
 
-def sum_over(value, axes, hooks=()):
-    steps = []
-    for axis, count in axes:
-        if count & (count - 1):
-            value = lax.psum(value, axis)
-        else:
-            steps += [(axis, count, bit) for bit in bits(count)]
+def together(*values):
+    return list(lax.optimization_barrier(values))
+
+
+def steps_of(axes):
+    return [(axis, count, bit) for axis, count in axes for bit in bits(count)]
+
+
+def sum_over(value, steps, hooks=None):
     got = jnp.zeros_like(value)
     for index, (axis, count, bit) in enumerate(steps):
         if index:
             value = value + got
-        if index < len(hooks) and hooks[index] is not None:
-            value = after(value, *hooks[index]())
+        if hooks and index in hooks:
+            value = hooks[index](value)
         got = exchange(value, axis, count, bit)
     return value, got
 
 
-def piece_kernel(order, place_ref, first_ref, side_ref, second_ref, first_out_ref, second_out_ref):
-    rows = pl.ds(pl.multiple_of(place_ref[1] * order.quarter, order.quarter), order.quarter)
-    first_out_ref[:9] = first_ref[:, rows, :]
-    first_out_ref[9] = side_ref[rows, :]
-    second_out_ref[...] = second_ref[:, rows, :]
-
-
-def spread_line(order, piece, fsdp):
-    return [piece] + [exchange(piece, "fsdp", fsdp, 2 * rel) for rel in range(1, order.zs)]
-
-
-def spread_plane(pieces, batch):
-    bundle = jnp.stack(pieces)
-    return [bundle] + [exchange(bundle, "batch", batch, rel) for rel in (1, 2, 3)]
-
-
-def spread_cores(bundles, fsdp):
+def parity(b):
+    return (b ^ (b // 2)) % 2
+
+
+def rotated(rel):
+    return lambda b: b ^ rel
+
+
+def of_half(other, index):
+    return lambda b: 2 * (parity(b) ^ other) + index
+
+
+def share_kernel(order, place_ref, first_ref, side_ref, second_ref, first_out_ref, second_out_ref, semaphores):
+    b, size, copies = place_ref[1], order.quarter, []
+
+    def copy(source, target):
+        copies.append(pltpu.make_async_copy(source, target, semaphores.at[len(copies)]))
+        copies[-1].start()
+
+    rows = pl.ds(pl.multiple_of(b * size, size), size)
+    copy(first_ref.at[:, rows, :], first_out_ref.at[pl.ds(0, 9)])
+    copy(side_ref.at[rows, :], first_out_ref.at[9])
+    for index in range(2):
+        rows = pl.ds(pl.multiple_of((2 * parity(b) + index) * size, size), size)
+        copy(second_ref.at[:, rows, :], second_out_ref.at[index])
+    for started in copies:
+        started.wait()
+
+
+def spread_line(order, share, fsdp):
+    return [share] + [exchange(share, "fsdp", fsdp, 2 * rel) for rel in range(1, order.zs)]
+
+
+def double_line(order, share, fsdp):
+    held, rels = share[:, None], [0]
+    for bit in reversed(bits(order.zs)):
+        held = jnp.concatenate([held, exchange(held, "fsdp", fsdp, 2 * bit)], axis=1)
+        rels = rels + [rel ^ bit for rel in rels]
+    return held, rels
+
+
+def both_cores(bundles, fsdp):
     return bundles + [exchange(value, "fsdp", fsdp, 1) for value in bundles]
+
+
+def spread_quarters(line, batch):
+    return [line] + [exchange(line, "batch", batch, rel) for rel in (1, 2, 3)]
+
+
+def quarter_labels(order):
+    return [
+        (4 * core + rel, (z,), core, rotated(rel), z) for core in range(2) for rel in range(4) for z in range(order.zs)
+    ]
+
+
+def spread_halves(line, batch):
+    return [exchange(line[0], "batch", batch, 1), exchange(line[1], "batch", batch, 2)]
+
+
+def half_labels(rels):
+    labels = []
+    for core in range(2):
+        for at, z in enumerate(rels):
+            for index in range(2):
+                labels.append((3 * core, (index, at), core, of_half(0, index), z))
+                labels.append((3 * core + 1 + index, (at,), core, of_half(1, index), z))
+    return labels
 
 
 def reduce_cores(parts, fsdp):
@@ -455,22 +533,33 @@
     return keep_p + exchange(send_p, "fsdp", fsdp, 1), keep_q + exchange(send_q, "fsdp", fsdp, 1)
 
 
-def finish_weights(order, place, halves, batch, fsdp, outs):
+def reduce_line(pieces, fsdp):
+    total = pieces[0].astype(F32)
+    for rel in range(1, len(pieces)):
+        total = total + exchange(pieces[rel], "fsdp", fsdp, 2 * rel).astype(F32)
+    return total
+
+
+def first_in_plane(halves, batch):
     half_p, half_q = halves
-    n_p, n_q = half_p.shape[0] // 4, half_q.shape[0] // 4
-    got_p = exchange(half_p[2 * n_p :], "batch", batch, 1)
-    got_q = exchange(half_q[2 * n_q :], "batch", batch, 2)
-    half_p = half_p[: 2 * n_p] + got_p
-    half_q = half_q[: 2 * n_q] + got_q
+    n_p, n_q = half_p.shape[0] // 2, half_q.shape[0] // 2
+    got_p = exchange(half_p[n_p:], "batch", batch, 1)
+    got_q = exchange(half_q[n_q:], "batch", batch, 2)
+    return [half_p[:n_p] + got_p, half_q[:n_q] + got_q]
+
+
+def then_in_plane(halves, batch):
+    half_p, half_q = halves
+    n_p, n_q = half_p.shape[0] // 2, half_q.shape[0] // 2
     got_p = exchange(half_p[n_p:], "batch", batch, 2)
     got_q = exchange(half_q[n_q:], "batch", batch, 1)
     low, high = half_p[:n_p] + got_p, half_q[:n_q] + got_q
-    pieces = [low[index] for index in range(n_p)] + [high[index] for index in range(n_q)]
-    total = pieces[0].astype(F32)
-    for rel in range(1, len(pieces)):
-        total = total + exchange(pieces[rel], "fsdp", fsdp, 2 * rel).astype(F32)
-    mine = total.astype(BF16)
-    spread = [mine] + [exchange(mine, "batch", batch, rel) for rel in (1, 2, 3)]
+    return [low[index] for index in range(n_p)] + [high[index] for index in range(n_q)]
+
+
+def finish_weights(order, place, quarter, batch, outs):
+    quarter = quarter.astype(BF16)
+    spread = [quarter] + [exchange(quarter, "batch", batch, rel) for rel in (1, 2, 3)]
     return call(functools.partial(finish_kernel, order), outs, place, *spread, scalars=1)
 
 
@@ -501,47 +590,51 @@
     cout = owned * fsdp
     plan = Plan([cot.shape[1] for cot in cots], slots)
     rows, span = plan.rows, plan.span
-    everywhere = (("fsdp", fsdp), ("batch", batch))
+    everywhere = steps_of((("fsdp", fsdp), ("batch", batch)))
     me = lax.axis_index("fsdp")
     fast = batch == 4 and fsdp >= 4 and fsdp & (fsdp - 1) == 0 and owned % (ROWS * batch) == 0
     order = Order(batch, fsdp, owned) if fast else None
+    if fast:
+        everywhere = everywhere[:1] + everywhere[-2:] + everywhere[1:-2]
     place = jnp.stack([me % 2, lax.axis_index("batch"), me // 2]).astype(jnp.int32)
 
     own_first = jnp.transpose(w_first, (0, 1, 3, 2)).reshape(9, owned, cin)
     own_second = jnp.transpose(w_second, (0, 1, 3, 2)).reshape(9, owned, cout)
     own_side = jnp.transpose(w_short)
+    vectors = [gain_first, shift_first, gain_second, shift_second, gain_short, shift_short]
+    patches, cot_rows, mask, vec = call(
+        functools.partial(prepare_kernel, plan, owned),
+        [shape((rows, 9 * cin), BF16), shape((rows, cout)), shape((rows, 128)), shape((8, cout))],
+        place,
+        counts,
+        *[jnp.transpose(value, (1, 2, 0, 3)) for value in fields + cots],
+        *[value.reshape(1, owned) for value in vectors],
+        scratch=[pltpu.VMEM((4, plan.margin + rows, cin), F32)],
+        scalars=2,
+        far=True,
+    )
     if fast:
-        piece_first, piece_second = call(
-            functools.partial(piece_kernel, order),
-            [shape((10, order.quarter, cin), BF16), shape((9, order.quarter, cout), BF16)],
+        share_first, share_second = call(
+            functools.partial(share_kernel, order),
+            [shape((10, order.quarter, cin), BF16), shape((2, 9, order.quarter, cout), BF16)],
             place,
             own_first,
             own_side,
             own_second,
+            scratch=[pltpu.SemaphoreType.DMA((4,))],
             scalars=1,
+            far=True,
+            whole=False,
         )
-        along_first = spread_line(order, piece_first, fsdp)
-        plane_first = spread_plane(along_first, batch)
-        along_second = spread_line(order, after(piece_second, *along_first), fsdp)
-        plane_second = spread_plane(along_second, batch)
-        kern_first = Gathered(spread_cores(plane_first, fsdp), place, order)
+        line_first = spread_line(order, share_first, fsdp)
+        line_first = after(jnp.stack(line_first), patches, vec)
+        line_second, rels = double_line(order, after(share_second, line_first), fsdp)
+        kern_first = Gathered(both_cores(spread_quarters(line_first, batch), fsdp), place, order, quarter_labels(order), True)
     else:
         kern_first = Gathered([lax.all_gather(jnp.concatenate([own_first, own_side[None]]), "fsdp", axis=1, tiled=True)])
         kern_second = Gathered([lax.all_gather(own_second, "fsdp", axis=1, tiled=True)])
-    vectors = jnp.stack([gain_first, shift_first, gain_second, shift_second, gain_short, shift_short]).astype(F32)
-    vectors = jnp.where(lax.axis_index("batch") == 0, vectors, 0.0)
-    vec = lax.dynamic_update_slice(jnp.zeros((8, cout), F32), vectors, (0, me * owned))
-
-    patches, cot_rows, mask = call(
-        functools.partial(prepare_kernel, plan),
-        [shape((rows, 9 * cin), BF16), shape((rows, cout)), shape((rows, 128))],
-        counts,
-        *[jnp.transpose(value, (1, 2, 0, 3)) for value in fields + cots],
-        scratch=[pltpu.VMEM((4, plan.margin + rows, cin), F32)],
-        scalars=1,
-    )
     flops = 2 * rows * cout * cin * 9
-    first, side, sums = call(
+    *whole, first, side, sums = call(
         first_kernel,
         [shape((rows, cout)), shape((rows, cout)), shape((8, cout))],
         patches,
@@ -550,10 +643,21 @@
         flops=flops,
         weights=kern_first,
     )
-    sums = sum_over(sums, everywhere)
+    hooks = None
     if fast:
-        kern_second = Gathered(spread_cores([after(value, *sums) for value in plane_second], fsdp), place, order)
-    second, patches_two, sums_two = call(
+        kern_first = Gathered(whole)
+        plane_second = []
+
+        def spread_second(value):
+            plane_second.extend(spread_halves(after(line_second, value), batch))
+            return value
+
+        hooks = {3: spread_second}
+    sums = sum_over(sums, everywhere, hooks)
+    if fast:
+        bundles = [after(value, *sums) for value in plane_second]
+        kern_second = Gathered(both_cores([line_second] + bundles, fsdp), place, order, half_labels(rels))
+    *whole, second, patches_two, sums_two = call(
         functools.partial(second_kernel, plan),
         [shape((rows, cout)), shape((rows, 9 * cout), BF16), shape((8, cout))],
         *sums,
@@ -564,10 +668,12 @@
         flops=2 * flops,
         weights=kern_second,
     )
+    if fast:
+        kern_second = Gathered(whole)
     sums_two = sum_over(sums_two, everywhere)
-    out_rows, dz, sums_z = call(
-        output_kernel,
-        [shape((rows, cout)), shape((rows, cout)), shape((8, cout))],
+    *outputs, dz, sums_z = call(
+        functools.partial(output_kernel, plan),
+        [shape((length, length, slots, cout), BF16) for length in plan.sides] + [shape((rows, cout)), shape((8, cout))],
         *sums,
         *sums_two,
         second,
@@ -592,21 +698,32 @@
         flops=2 * flops,
         weights=kern_second,
     )
-    hooks = ()
+    hooks = None
     if fast:
         turned = [pltpu.VMEM((cout, rows), BF16), pltpu.VMEM((cout, rows), BF16)]
-        parts_two = call(
-            functools.partial(weight_second_kernel, order),
-            [shape((len(part), 9, order.quarter, cout), BF16) for part in order.parts],
-            place,
-            grad_two,
-            patches_two,
-            scratch=turned,
-            scalars=1,
-            flops=2 * flops,
-        )
-        halves_two = reduce_cores(parts_two, fsdp)
-        hooks = (None, None, lambda: parts_two, None, lambda: halves_two)
+        parts_two, halves_two = [], []
+
+        def weights_second(value):
+            parts_two.extend(
+                call(
+                    functools.partial(weight_second_kernel, order),
+                    [shape((len(part), 9, order.quarter, cout), BF16) for part in order.parts],
+                    place,
+                    after(grad_two, value),
+                    patches_two,
+                    scratch=turned,
+                    scalars=1,
+                    flops=2 * flops,
+                )
+            )
+            halves_two.extend(reduce_cores(parts_two, fsdp))
+            return value
+
+        def over_plane(value):
+            value, *halves_two[:] = together(value, *halves_two)
+            return value
+
+        hooks = {1: weights_second, 2: lambda value: after(value, *parts_two), 3: over_plane}
     sums_y = sum_over(sums_y, everywhere, hooks)
     if fast:
         grad_one, *parts_one = call(
@@ -624,12 +741,18 @@
             scalars=1,
             flops=flops,
         )
+        halves_two = first_in_plane(halves_two, batch)
         halves_one = reduce_cores(parts_one, fsdp)
+        grad_late = after(grad_one, *halves_one)
+        *halves_one, last = together(*halves_one, halves_two[0])
+        halves_two[0] = last
+        halves_one = first_in_plane(halves_one, batch)
+        quarter_two = reduce_line(then_in_plane(halves_two, batch), fsdp)
+        quarter_one = reduce_line(then_in_plane(halves_one, batch), fsdp)
+        dw_second = finish_weights(order, place, quarter_two, batch, [shape((9, owned, cout))])[0]
         dw_first, dw_side = finish_weights(
-            order, place, halves_one, batch, fsdp, [shape((9, owned, cin)), shape((owned, cin))]
+            order, place, quarter_one, batch, [shape((9, owned, cin)), shape((owned, cin))]
         )
-        dw_second = finish_weights(order, place, halves_two, batch, fsdp, [shape((9, owned, cout))])[0]
-        grad_late, out_rows = after(grad_one, *halves_one), after(out_rows, *halves_one)
     else:
         grad_one = call(back_first, shape((rows, cout), BF16), *sums, *sums_y, first, dy, mask)
         taps = tuple(range(9))
@@ -644,39 +767,33 @@
         ]
         dw_side = dw_side[0]
         grad_late = grad_one
-    input_grads = call(
-        functools.partial(input_kernel, plan),
-        [shape((2 * length, 2 * length, slots, cin), BF16) for length in plan.sides],
+    *input_grads, shift_1, gain_1, gain_2, shift_2, gain_3, shift_3 = call(
+        functools.partial(input_kernel, plan, owned),
+        [shape((2 * length, 2 * length, slots, cin), BF16) for length in plan.sides] + [shape((1, owned))] * 6,
+        place,
+        *sums_z,
+        *sums_y,
         grad_late,
         grad_side,
         scratch=[pltpu.VMEM((span, cout), F32), pltpu.VMEM((4, rows, cout), BF16), pltpu.VMEM((rows, cin), F32)],
+        scalars=1,
         flops=flops,
         weights=kern_first,
     )
-    outputs = call(
-        functools.partial(output_rows_kernel, plan),
-        [shape((length, length, slots, cout), BF16) for length in plan.sides],
-        out_rows,
-    )
-
-    def mine(sums, row):
-        value = sums[0][row : row + 1] + sums[1][row : row + 1]
-        return lax.dynamic_slice(value, (0, me * owned), (1, owned))[0]
-
     def as_weight(value):
         return jnp.transpose(value.reshape(3, 3, owned, value.shape[2]), (0, 1, 3, 2))
 
     return (
         *[jnp.transpose(value, (2, 0, 1, 3)) for value in (*outputs, *input_grads)],
         as_weight(dw_first),
-        mine(sums_y, 1),
-        mine(sums_y, 0),
+        gain_1[0],
+        shift_1[0],
         as_weight(dw_second),
-        mine(sums_z, 1),
-        mine(sums_z, 0),
+        gain_2[0],
+        shift_2[0],
         jnp.transpose(dw_side),
-        mine(sums_z, 2),
-        mine(sums_z, 3),
+        gain_3[0],
+        shift_3[0],
     )
 
 

time: 201 us -> 177 us (0.88)
  starting transfers between devices: 76.2 us -> 61.2 us
  local copies, waits for them, and re-layouts: 12.7 us -> 0.98 us
  waiting for transfers between devices: 73.4 us -> 84.1 us
  Pallas kernels: 32.1 us -> 27.7 us
  other arithmetic: 5.14 us -> 2.16 us
    ppermute x64 -> x61, starting transfers between devices: 76.2 us -> 61.2 us  [exchange(): lax.ppermute(value, axis, [(index, index ^ bit) for index in range(count)])]
    ppermute x64 -> x61, waiting for transfers between devices: 73.4 us -> 84.1 us  [exchange(): lax.ppermute(value, axis, [(index, index ^ bit) for index in range(count)])]
    unnamed x32 -> x2, local copies, waits for them, and re-layouts: 8.54 us -> 0.65 us
    pallas_call x12 -> x11, Pallas kernels: 32.1 us -> 27.7 us  [call(): pl.pallas_call(body, in_specs=specs, out_specs=[first_out] + [vmem] * (le...]
  transfers between devices with their start and end apart: 64 -> 61, of which waited for: 34 -> 38; matrix products, arithmetic and copies ran while one was open for 5% -> 1% of each run, Pallas kernels for 7% -> 7%
where the time goes in v3:
time: 177 us
  waiting for transfers between devices  84.1 us (48%)
  starting transfers between devices  61.2 us (35%)
  Pallas kernels  27.7 us (16%)
  other arithmetic  2.16 us (1%)
    ppermute x61, waiting for transfers between devices, exchange(): lax.ppermute(value, axis, [(index, index ^ bit) for index in range(count)])  84.1 us
    ppermute x61, starting transfers between devices, exchange(): lax.ppermute(value, axis, [(index, index ^ bit) for index in range(count)])  61.2 us
    pallas_call x11, Pallas kernels, call(): pl.pallas_call(body, in_specs=specs, out_specs=[first_out] + [vmem] * (le...  27.7 us
  transfers between devices with their start and end apart: 61, of which 38 were waited for; matrix products, arithmetic and copies ran while one was open for 1% of the time, Pallas kernels for 7%

profile of v3, /device:TPU:0, one launch (start us, length us, event | category | flops | bytes accessed | tf_op | source)
XLA Modules:
  0.0 177.2 jit_solution(7700589726417429366)
XLA Ops:
  0.7 1.6 shard_map.272
  2.4 5.1 %collective-permute-start.2 = (bf16[10,16,256]{2,1,0:T(8,128)(2,1)S(1)}, bf16[10,16,256]{2,1,0:T(8,128)(2,1)S(1)}, u32[]{:S(2)}, u32[]{:S(2)}) collective-permute-start(bf16[10,16,256]{2,1,0:T(8,128)(2,1)S(1)} %get-tuple-element.75), channel_id=1, source_target_pairs={{0,6},{1,7},{2,4},{3,5},{4,2},{5,3},{6,0},{7,1},{8,14},{9,15},{10,... | collective-permute-start | bytes 245768 | tf_op jit(solution)/shard_map/ppermute | solution.py:432
  8.8 2.3 %shard_map.271 = (bf16[432,2304]{1,0:T(8,128)(2,1)S(1)}, f32[432,512]{1,0:T(8,128)S(1)}, f32[432,128]{1,0:T(8,128)S(1)}, f32[8,512]{1,0:T(8,128)S(1)}) custom-call(s32[3]{0:T(128)S(1)} %pad_add_fusion.place_ref.refs_0_, s32[1,3]{1,0:T(1,128)S(1)} %copy-done, bf16[10,10,2,256]{3,2,1,0:T(2,128)(2,1)} %bitcast.82, bf16[14,14,2,256]{3,2,1,0:T(2,128)(2,1)} %bitcast.80, ...), custom_call_target="tpu_custom_call" | custom-call | bytes 953112 | tf_op jit(solution)/shard_map/pallas_call | solution.py:416
  11.1 3.2 %collective-permute-done.1 = bf16[10,16,256]{2,1,0:T(8,128)(2,1)S(1)} collective-permute-done((bf16[10,16,256]{2,1,0:T(8,128)(2,1)S(1)}, bf16[10,16,256]{2,1,0:T(8,128)(2,1)S(1)}, u32[]{:S(2)}, u32[]{:S(2)}) %collective-permute-start.1) | collective-permute-done | bytes 81952 | tf_op jit(solution)/shard_map/ppermute | solution.py:432
  15.4 2.4 %collective-permute-start.5 = (bf16[4,10,16,256]{3,2,1,0:T(8,128)(2,1)S(1)}, bf16[4,10,16,256]{3,2,1,0:T(8,128)(2,1)S(1)}, u32[]{:S(2)}, u32[]{:S(2)}) collective-permute-start(bf16[4,10,16,256]{3,2,1,0:T(8,128)(2,1)S(1)} %pad_maximum_fusion.2.refs_3_), channel_id=1, source_target_pairs={{0,24},{8,16},{16,8},{24,0},{1,25},{9,17},{17,9},{25,1},{2,26},{10... | collective-permute-start | bytes 983048 | tf_op jit(solution)/shard_map/ppermute | solution.py:432
  18.9 10.9 %collective-permute-done.15 = bf16[2,1,9,16,512]{4,3,2,1,0:T(8,128)(2,1)S(1)} collective-permute-done((bf16[2,1,9,16,512]{4,3,2,1,0:T(8,128)(2,1)S(1)}, bf16[2,1,9,16,512]{4,3,2,1,0:T(8,128)(2,1)S(1)}, u32[]{:S(2)}, u32[]{:S(2)}) %collective-permute-start.15) | collective-permute-done | bytes 294944 | tf_op jit(solution)/shard_map/ppermute | solution.py:432
  33.5 2.9 %shard_map.273 = (bf16[10,512,256]{2,1,0:T(8,128)(2,1)S(1)}, f32[432,512]{1,0:T(8,128)S(1)}, f32[432,512]{1,0:T(8,128)S(1)}, f32[8,512]{1,0:T(8,128)S(1)}) custom-call(s32[3]{0:T(128)S(1)} %pad_add_fusion.place_ref.refs_0_, bf16[432,2304]{1,0:T(8,128)(2,1)S(1)} %get-tuple-element.72.refs_0_.patches_ref, ...), custom_call_target="tpu_custom_call" | custom-call | flops 1019215872 | bytes 4849676 | tf_op jit(solution)/shard_map/pallas_call | solution.py:416
  37.6 1.6 collective-permute-start.11
  39.3 2.1 %collective-permute-done.11 = f32[8,512]{1,0:T(8,128)S(1)} collective-permute-done((f32[8,512]{1,0:T(8,128)S(1)}, f32[8,512]{1,0:T(8,128)S(1)}, u32[]{:S(2)}, u32[]{:S(2)}) %collective-permute-start.11) | collective-permute-done | bytes 16416 | tf_op jit(solution)/shard_map/ppermute | solution.py:432
  41.4 1.7 collective-permute-start.12
  43.0 2.1 %collective-permute-done.12 = f32[8,512]{1,0:T(8,128)S(1)} collective-permute-done((f32[8,512]{1,0:T(8,128)S(1)}, f32[8,512]{1,0:T(8,128)S(1)}, u32[]{:S(2)}, u32[]{:S(2)}) %collective-permute-start.12) | collective-permute-done | bytes 16416 | tf_op jit(solution)/shard_map/ppermute | solution.py:432
  45.3 1.7 collective-permute-start.18
  48.3 1.7 collective-permute-start.13
  49.9 2.1 %collective-permute-done.13 = f32[8,512]{1,0:T(8,128)S(1)} collective-permute-done((f32[8,512]{1,0:T(8,128)S(1)}, f32[8,512]{1,0:T(8,128)S(1)}, u32[]{:S(2)}, u32[]{:S(2)}) %collective-permute-start.13) | collective-permute-done | bytes 16416 | tf_op jit(solution)/shard_map/ppermute | solution.py:432
  52.0 2.0 %collective-permute-start.14 = (f32[8,512]{1,0:T(8,128)S(1)}, f32[8,512]{1,0:T(8,128)S(1)}, u32[]{:S(2)}, u32[]{:S(2)}) collective-permute-start(f32[8,512]{1,0:T(8,128)S(1)} %add.111.refs_0_.sums_ref), channel_id=1, source_target_pairs={{0,4},{1,5},{2,6},{3,7},{4,0},{5,1},{6,2},{7,3},{8,12},{9,13},{10,... | collective-permute-start | bytes 49160 | tf_op jit(solution)/shard_map/ppermute | solution.py:432
  54.0 2.6 %collective-permute-done.14.refs_1_.got_ref = f32[8,512]{1,0:T(8,128)S(1)} collective-permute-done((f32[8,512]{1,0:T(8,128)S(1)}, f32[8,512]{1,0:T(8,128)S(1)}, u32[]{:S(2)}, u32[]{:S(2)}) %collective-permute-start.14) | collective-permute-done | bytes 16416 | tf_op jit(solution)/shard_map/ppermute | solution.py:432
  56.7 3.1 %collective-permute-done.18.refs_7_ = bf16[4,9,16,512]{3,2,1,0:T(8,128)(2,1)S(1)} collective-permute-done((bf16[4,9,16,512]{3,2,1,0:T(8,128)(2,1)S(1)}, bf16[4,9,16,512]{3,2,1,0:T(8,128)(2,1)S(1)}, u32[]{:S(2)}, u32[]{:S(2)}) %collective-permute-start.18) | collective-permute-done | bytes 589856 | tf_op jit(solution)/shard_map/ppermute | solution.py:432
  62.9 5.1 %shard_map.274 = (bf16[9,512,512]{2,1,0:T(8,128)(2,1)S(1)}, f32[432,512]{1,0:T(8,128)S(1)}, bf16[432,4608]{1,0:T(8,128)(2,1)S(1)}, f32[8,512]{1,0:T(8,128)S(1)}) custom-call(s32[3]{0:T(128)S(1)} %pad_add_fusion.place_ref.refs_0_, f32[8,512]{1,0:T(8,128)S(1)} %add.111.refs_0_.sums_ref, f32[8,512]{1,0:T(8,128)S(1)} %collective-permute-done.14.refs_1_.got_ref, ...), custom_call_target="tpu_custom_call" | custom-call | flops 2038431744 | bytes 5873676 | tf_op jit(solution)/shard_map/pallas_call | solution.py:416
  70.8 2.2 %collective-permute-done.23 = f32[8,512]{1,0:T(8,128)S(1)} collective-permute-done((f32[8,512]{1,0:T(8,128)S(1)}, f32[8,512]{1,0:T(8,128)S(1)}, u32[]{:S(2)}, u32[]{:S(2)}) %collective-permute-start.23) | collective-permute-done | bytes 16416 | tf_op jit(solution)/shard_map/ppermute | solution.py:432
  74.2 2.6 %collective-permute-done.24 = f32[8,512]{1,0:T(8,128)S(1)} collective-permute-done((f32[8,512]{1,0:T(8,128)S(1)}, f32[8,512]{1,0:T(8,128)S(1)}, u32[]{:S(2)}, u32[]{:S(2)}) %collective-permute-start.24) | collective-permute-done | bytes 16416 | tf_op jit(solution)/shard_map/ppermute | solution.py:432
  78.1 2.4 %collective-permute-done.25 = f32[8,512]{1,0:T(8,128)S(1)} collective-permute-done((f32[8,512]{1,0:T(8,128)S(1)}, f32[8,512]{1,0:T(8,128)S(1)}, u32[]{:S(2)}, u32[]{:S(2)}) %collective-permute-start.25) | collective-permute-done | bytes 16416 | tf_op jit(solution)/shard_map/ppermute | solution.py:432
  80.5 1.9 %collective-permute-start.26 = (f32[8,512]{1,0:T(8,128)S(1)}, f32[8,512]{1,0:T(8,128)S(1)}, u32[]{:S(2)}, u32[]{:S(2)}) collective-permute-start(f32[8,512]{1,0:T(8,128)S(1)} %add.115.sums_two_ref.refs_2_), channel_id=1, source_target_pairs={{0,4},{1,5},{2,6},{3,7},{4,0},{5,1},{6,2},{7,3},{8,12},{9,13},{10,... | collective-permute-start | bytes 49160 | tf_op jit(solution)/shard_map/ppermute | solution.py:432
  82.5 2.7 %collective-permute-done.26.got_two_ref.refs_3_ = f32[8,512]{1,0:T(8,128)S(1)} collective-permute-done((f32[8,512]{1,0:T(8,128)S(1)}, f32[8,512]{1,0:T(8,128)S(1)}, u32[]{:S(2)}, u32[]{:S(2)}) %collective-permute-start.26) | collective-permute-done | bytes 16416 | tf_op jit(solution)/shard_map/ppermute | solution.py:432
  88.9 2.2 %collective-permute-done.28 = f32[8,512]{1,0:T(8,128)S(1)} collective-permute-done((f32[8,512]{1,0:T(8,128)S(1)}, f32[8,512]{1,0:T(8,128)S(1)}, u32[]{:S(2)}, u32[]{:S(2)}) %collective-permute-start.28) | collective-permute-done | bytes 16416 | tf_op jit(solution)/shard_map/ppermute | solution.py:432
  92.3 2.6 %collective-permute-done.29 = f32[8,512]{1,0:T(8,128)S(1)} collective-permute-done((f32[8,512]{1,0:T(8,128)S(1)}, f32[8,512]{1,0:T(8,128)S(1)}, u32[]{:S(2)}, u32[]{:S(2)}) %collective-permute-start.29) | collective-permute-done | bytes 16416 | tf_op jit(solution)/shard_map/ppermute | solution.py:432
  96.5 2.2 %collective-permute-done.30 = f32[8,512]{1,0:T(8,128)S(1)} collective-permute-done((f32[8,512]{1,0:T(8,128)S(1)}, f32[8,512]{1,0:T(8,128)S(1)}, u32[]{:S(2)}, u32[]{:S(2)}) %collective-permute-start.30) | collective-permute-done | bytes 16416 | tf_op jit(solution)/shard_map/ppermute | solution.py:432
  98.7 2.1 %collective-permute-start.31 = (f32[8,512]{1,0:T(8,128)S(1)}, f32[8,512]{1,0:T(8,128)S(1)}, u32[]{:S(2)}, u32[]{:S(2)}) collective-permute-start(f32[8,512]{1,0:T(8,128)S(1)} %add.119.refs_4_.refs_1_), channel_id=1, source_target_pairs={{0,4},{1,5},{2,6},{3,7},{4,0},{5,1},{6,2},{7,3},{8,12},{9,13},{10,... | collective-permute-start | bytes 49160 | tf_op jit(solution)/shard_map/ppermute | solution.py:432
  100.8 2.6 %collective-permute-done.31.refs_5_.refs_2_ = f32[8,512]{1,0:T(8,128)S(1)} collective-permute-done((f32[8,512]{1,0:T(8,128)S(1)}, f32[8,512]{1,0:T(8,128)S(1)}, u32[]{:S(2)}, u32[]{:S(2)}) %collective-permute-start.31) | collective-permute-done | bytes 16416 | tf_op jit(solution)/shard_map/ppermute | solution.py:432
  103.3 3.0 %shard_map.276 = (bf16[432,512]{1,0:T(8,128)(2,1)S(1)}, bf16[432,512]{1,0:T(8,128)(2,1)S(1)}, f32[432,512]{1,0:T(8,128)S(1)}, f32[8,512]{1,0:T(8,128)S(1)}) custom-call(f32[8,512]{1,0:T(8,128)S(1)} %add.111.refs_0_.sums_ref, f32[8,512]{1,0:T(8,128)S(1)} %collective-permute-done.14.refs_1_.got_ref, f32[8,512]{1,0:T(8,128)S(1)} %add.115.sums_two_ref.refs_2_, ...), custom_call_target="tpu_custom_call" | custom-call | flops 2038431744 | bytes 8577024 | tf_op jit(solution)/shard_map/pallas_call | solution.py:416
  107.5 3.3 %shard_map.277 = (bf16[8,9,16,512]{3,2,1,0:T(8,128)(2,1)S(1)}, bf16[8,9,16,512]{3,2,1,0:T(8,128)(2,1)S(1)}, bf16[8,9,16,512]{3,2,1,0:T(8,128)(2,1)S(1)}, bf16[8,9,16,512]{3,2,1,0:T(8,128)(2,1)S(1)}) custom-call(s32[3]{0:T(128)S(1)} %pad_add_fusion.place_ref.refs_0_, bf16[432,512]{1,0:T(8,128)(2,1)S(1)} %get-tuple-element.96.grad_ref, ...), custom_call_target="tpu_custom_call" | custom-call | flops 2038431744 | bytes 4423692 | tf_op jit(solution)/shard_map/pallas_call | solution.py:416
  113.0 2.2 %collective-permute-done.33 = f32[8,512]{1,0:T(8,128)S(1)} collective-permute-done((f32[8,512]{1,0:T(8,128)S(1)}, f32[8,512]{1,0:T(8,128)S(1)}, u32[]{:S(2)}, u32[]{:S(2)}) %collective-permute-start.33) | collective-permute-done | bytes 16416 | tf_op jit(solution)/shard_map/ppermute | solution.py:432
  116.3 2.6 %collective-permute-done.34 = f32[8,512]{1,0:T(8,128)S(1)} collective-permute-done((f32[8,512]{1,0:T(8,128)S(1)}, f32[8,512]{1,0:T(8,128)S(1)}, u32[]{:S(2)}, u32[]{:S(2)}) %collective-permute-start.34) | collective-permute-done | bytes 16416 | tf_op jit(solution)/shard_map/ppermute | solution.py:432
  121.2 1.6 collective-permute-start.41
  123.9 2.7 %collective-permute-done.37 = f32[8,512]{1,0:T(8,128)S(1)} collective-permute-done((f32[8,512]{1,0:T(8,128)S(1)}, f32[8,512]{1,0:T(8,128)S(1)}, u32[]{:S(2)}, u32[]{:S(2)}) %collective-permute-start.37) | collective-permute-done | bytes 16416 | tf_op jit(solution)/shard_map/ppermute | solution.py:432
  126.5 1.5 collective-permute-start.38
  128.1 3.1 %collective-permute-done.38.got_y_ref.refs_4_ = f32[8,512]{1,0:T(8,128)S(1)} collective-permute-done((f32[8,512]{1,0:T(8,128)S(1)}, f32[8,512]{1,0:T(8,128)S(1)}, u32[]{:S(2)}, u32[]{:S(2)}) %collective-permute-start.38) | collective-permute-done | bytes 16416 | tf_op jit(solution)/shard_map/ppermute | solution.py:432
  131.2 2.4 %shard_map.278 = (bf16[432,512]{1,0:T(8,128)(2,1)S(1)}, bf16[8,10,16,256]{3,2,1,0:T(8,128)(2,1)S(1)}, bf16[8,10,16,256]{3,2,1,0:T(8,128)(2,1)S(1)}, bf16[8,10,16...) custom-call(s32[3]{0:T(128)S(1)} %pad_add_fusion.place_ref.refs_0_, f32[8,512]{1,0:T(8,128)S(1)} %add.111.refs_0_.sums_ref, ...), custom_call_target="tpu_custom_call" | custom-call | flops 1019215872 | bytes 4489228 | tf_op jit(solution)/shard_map/pallas_call | solution.py:416
  139.7 4.7 %collective-permute-done.55 = bf16[2,9,16,512]{3,2,1,0:T(8,128)(2,1)S(1)} collective-permute-done((bf16[2,9,16,512]{3,2,1,0:T(8,128)(2,1)S(1)}, bf16[2,9,16,512]{3,2,1,0:T(8,128)(2,1)S(1)}, u32[]{:S(2)}, u32[]{:S(2)}) %collective-permute-start.55) | collective-permute-done | bytes 294944 | tf_op jit(solution)/shard_map/ppermute | solution.py:432
  144.5 1.6 collective-permute-start.56
  146.1 1.9 %collective-permute-start.57 = (bf16[9,16,512]{2,1,0:T(8,128)(2,1)S(1)}, bf16[9,16,512]{2,1,0:T(8,128)(2,1)S(1)}, u32[]{:S(2)}, u32[]{:S(2)}) collective-permute-start(bf16[9,16,512]{2,1,0:T(8,128)(2,1)S(1)} %get-tuple-element.132), channel_id=1, source_target_pairs={{0,6},{1,7},{2,4},{3,5},{4,2},{5,3},{6,0},{7,1},{8,14},{9,15},{10,... | collective-permute-start | bytes 442376 | tf_op jit(solution)/shard_map/ppermute | solution.py:432
  148.2 4.9 %collective-permute-done.45 = bf16[4,10,16,256]{3,2,1,0:T(8,128)(2,1)S(1)} collective-permute-done((bf16[4,10,16,256]{3,2,1,0:T(8,128)(2,1)S(1)}, bf16[4,10,16,256]{3,2,1,0:T(8,128)(2,1)S(1)}, u32[]{:S(2)}, u32[]{:S(2)}) %collective-permute-start.45) | collective-permute-done | bytes 327712 | tf_op jit(solution)/shard_map/ppermute | solution.py:432
  154.8 3.9 %collective-permute-done.46 = bf16[2,10,16,256]{3,2,1,0:T(8,128)(2,1)S(1)} collective-permute-done((bf16[2,10,16,256]{3,2,1,0:T(8,128)(2,1)S(1)}, bf16[2,10,16,256]{3,2,1,0:T(8,128)(2,1)S(1)}, u32[]{:S(2)}, u32[]{:S(2)}) %collective-permute-start.46) | collective-permute-done | bytes 163872 | tf_op jit(solution)/shard_map/ppermute | solution.py:432
  158.7 1.6 collective-permute-start.47
  160.3 1.9 %collective-permute-start.48 = (bf16[10,16,256]{2,1,0:T(8,128)(2,1)S(1)}, bf16[10,16,256]{2,1,0:T(8,128)(2,1)S(1)}, u32[]{:S(2)}, u32[]{:S(2)}) collective-permute-start(bf16[10,16,256]{2,1,0:T(8,128)(2,1)S(1)} %get-tuple-element.134), channel_id=1, source_target_pairs={{0,6},{1,7},{2,4},{3,5},{4,2},{5,3},{6,0},{7,1},{8,14},{9,15},{10,... | collective-permute-start | bytes 245768 | tf_op jit(solution)/shard_map/ppermute | solution.py:432
  165.0 1.8 %collective-permute-done.47 = bf16[10,16,256]{2,1,0:T(8,128)(2,1)S(1)} collective-permute-done((bf16[10,16,256]{2,1,0:T(8,128)(2,1)S(1)}, bf16[10,16,256]{2,1,0:T(8,128)(2,1)S(1)}, u32[]{:S(2)}, u32[]{:S(2)}) %collective-permute-start.47) | collective-permute-done | bytes 81952 | tf_op jit(solution)/shard_map/ppermute | solution.py:432
  167.7 1.6 collective-permute-start.51
  171.2 2.8 %shard_map.279 = (bf16[10,10,2,256]{3,2,1,0:T(2,128)(2,1)}, bf16[14,14,2,256]{3,2,1,0:T(2,128)(2,1)}, bf16[18,18,2,256]{3,2,1,0:T(2,128)(2,1)}, f32[1,64]{1,0:T(...) custom-call(s32[3]{0:T(128)S(1)} %pad_add_fusion.place_ref.refs_0_, ...), custom_call_target="tpu_custom_call" | custom-call | flops 1019215872 | bytes 3571724 | tf_op jit(solution)/shard_map/pallas_call | solution.py:416
  174.1 1.6 shard_map.281
  (134 shorter events, 47.3 us)
Async XLA Ops:
  2.4 8.8 %collective-permute-start.2 = (bf16[10,16,256]{2,1,0:T(8,128)(2,1)S(1)}, bf16[10,16,256]{2,1,0:T(8,128)(2,1)S(1)}, u32[]{:S(2)}, u32[]{:S(2)}) collective-permute-start(bf16[10,16,256]{2,1,0:T(8,128)(2,1)S(1)} %get-tuple-element.75), channel_id=1, source_target_pairs={{0,6},{1,7},{2,4},{3,5},{4,2},{5,3},{6,0},{7,1},{8,14},{9,15},{10,... | collective-permute-start | bytes 245768 | tf_op jit(solution)/shard_map/ppermute | solution.py:432
  7.5 6.9 %collective-permute-start.1 = (bf16[10,16,256]{2,1,0:T(8,128)(2,1)S(1)}, bf16[10,16,256]{2,1,0:T(8,128)(2,1)S(1)}, u32[]{:S(2)}, u32[]{:S(2)}) collective-permute-start(bf16[10,16,256]{2,1,0:T(8,128)(2,1)S(1)} %get-tuple-element.75), channel_id=1, source_target_pairs={{0,4},{1,5},{2,6},{3,7},{4,0},{5,1},{6,2},{7,3},{8,12},{9,13},{10,... | collective-permute-start | bytes 245768 | tf_op jit(solution)/shard_map/ppermute | solution.py:432
  7.5 6.9 %collective-permute-start = (bf16[10,16,256]{2,1,0:T(8,128)(2,1)S(1)}, bf16[10,16,256]{2,1,0:T(8,128)(2,1)S(1)}, u32[]{:S(2)}, u32[]{:S(2)}) collective-permute-start(bf16[10,16,256]{2,1,0:T(8,128)(2,1)S(1)} %get-tuple-element.75), channel_id=1, source_target_pairs={{0,2},{1,3},{2,0},{3,1},{4,6},{5,7},{6,4},{7,5},{8,10},{9,11},{10,... | collective-permute-start | bytes 245768 | tf_op jit(solution)/shard_map/ppermute | solution.py:432
  14.4 15.4 %collective-permute-start.15 = (bf16[2,1,9,16,512]{4,3,2,1,0:T(8,128)(2,1)S(1)}, bf16[2,1,9,16,512]{4,3,2,1,0:T(8,128)(2,1)S(1)}, u32[]{:S(2)}, u32[]{:S(2)}) collective-permute-start(bf16[2,1,9,16,512]{4,3,2,1,0:T(8,128)(2,1)S(1)} %bitcast.72), channel_id=1, source_target_pairs={{0,4},{1,5},{2,6},{3,7},{4,0},{5,1},{6,2},{7,3},{8,12},{9,13},{10,... | collective-permute-start | bytes 884744 | tf_op jit(solution)/shard_map/ppermute | solution.py:432
  15.4 14.6 %collective-permute-start.5 = (bf16[4,10,16,256]{3,2,1,0:T(8,128)(2,1)S(1)}, bf16[4,10,16,256]{3,2,1,0:T(8,128)(2,1)S(1)}, u32[]{:S(2)}, u32[]{:S(2)}) collective-permute-start(bf16[4,10,16,256]{3,2,1,0:T(8,128)(2,1)S(1)} %pad_maximum_fusion.2.refs_3_), channel_id=1, source_target_pairs={{0,24},{8,16},{16,8},{24,0},{1,25},{9,17},{17,9},{25,1},{2,26},{10... | collective-permute-start | bytes 983048 | tf_op jit(solution)/shard_map/ppermute | solution.py:432
  17.8 13.6 %collective-permute-start.4 = (bf16[4,10,16,256]{3,2,1,0:T(8,128)(2,1)S(1)}, bf16[4,10,16,256]{3,2,1,0:T(8,128)(2,1)S(1)}, u32[]{:S(2)}, u32[]{:S(2)}) collective-permute-start(bf16[4,10,16,256]{3,2,1,0:T(8,128)(2,1)S(1)} %pad_maximum_fusion.2.refs_3_), channel_id=1, source_target_pairs={{0,16},{8,24},{16,0},{24,8},{1,17},{9,25},{17,1},{25,9},{2,18},{10... | collective-permute-start | bytes 983048 | tf_op jit(solution)/shard_map/ppermute | solution.py:432
  18.3 13.3 %collective-permute-start.3 = (bf16[4,10,16,256]{3,2,1,0:T(8,128)(2,1)S(1)}, bf16[4,10,16,256]{3,2,1,0:T(8,128)(2,1)S(1)}, u32[]{:S(2)}, u32[]{:S(2)}) collective-permute-start(bf16[4,10,16,256]{3,2,1,0:T(8,128)(2,1)S(1)} %pad_maximum_fusion.2.refs_3_), channel_id=1, source_target_pairs={{0,8},{8,0},{16,24},{24,16},{1,9},{9,1},{17,25},{25,17},{2,10},{10... | collective-permute-start | bytes 983048 | tf_op jit(solution)/shard_map/ppermute | solution.py:432
  29.8 15.3 %collective-permute-start.16 = (bf16[2,2,9,16,512]{4,3,2,1,0:T(8,128)(2,1)S(1)}, bf16[2,2,9,16,512]{4,3,2,1,0:T(8,128)(2,1)S(1)}, u32[]{:S(2)}, u32[]{:S(2)}) collective-permute-start(bf16[2,2,9,16,512]{4,3,2,1,0:T(8,128)(2,1)S(1)} %pad_maximum_fusion.1), channel_id=1, source_target_pairs={{0,2},{1,3},{2,0},{3,1},{4,6},{5,7},{6,4},{7,5},{8,10},{9,11},{10,... | collective-permute-start | bytes 1769480 | tf_op jit(solution)/shard_map/ppermute | solution.py:432
  37.6 3.7 %collective-permute-start.11 = (f32[8,512]{1,0:T(8,128)S(1)}, f32[8,512]{1,0:T(8,128)S(1)}, u32[]{:S(2)}, u32[]{:S(2)}) collective-permute-start(f32[8,512]{1,0:T(8,128)S(1)} %add.108), channel_id=1, source_target_pairs={{0,8},{8,0},{16,24},{24,16},{1,9},{9,1},{17,25},{25,17},{2,10},{10... | collective-permute-start | bytes 49160 | tf_op jit(solution)/shard_map/ppermute | solution.py:432
  41.4 3.7 %collective-permute-start.12 = (f32[8,512]{1,0:T(8,128)S(1)}, f32[8,512]{1,0:T(8,128)S(1)}, u32[]{:S(2)}, u32[]{:S(2)}) collective-permute-start(f32[8,512]{1,0:T(8,128)S(1)} %add.109), channel_id=1, source_target_pairs={{0,16},{8,24},{16,0},{24,8},{1,17},{9,25},{17,1},{25,9},{2,18},{10... | collective-permute-start | bytes 49160 | tf_op jit(solution)/shard_map/ppermute | solution.py:432
  45.3 14.5 %collective-permute-start.18 = (bf16[4,9,16,512]{3,2,1,0:T(8,128)(2,1)S(1)}, bf16[4,9,16,512]{3,2,1,0:T(8,128)(2,1)S(1)}, u32[]{:S(2)}, u32[]{:S(2)}) collective-permute-start(bf16[4,9,16,512]{3,2,1,0:T(8,128)(2,1)S(1)} %get-tuple-element.129), channel_id=1, source_target_pairs={{0,16},{8,24},{16,0},{24,8},{1,17},{9,25},{17,1},{25,9},{2,18},{10... | collective-permute-start | bytes 1769480 | tf_op jit(solution)/shard_map/ppermute | solution.py:432
  47.1 13.8 %collective-permute-start.17 = (bf16[4,9,16,512]{3,2,1,0:T(8,128)(2,1)S(1)}, bf16[4,9,16,512]{3,2,1,0:T(8,128)(2,1)S(1)}, u32[]{:S(2)}, u32[]{:S(2)}) collective-permute-start(bf16[4,9,16,512]{3,2,1,0:T(8,128)(2,1)S(1)} %get-tuple-element.130), channel_id=1, source_target_pairs={{0,8},{8,0},{16,24},{24,16},{1,9},{9,1},{17,25},{25,17},{2,10},{10... | collective-permute-start | bytes 1769480 | tf_op jit(solution)/shard_map/ppermute | solution.py:432
  48.3 12.6 %collective-permute-start.19 = (bf16[2,4,9,16,512]{4,3,2,1,0:T(8,128)(2,1)S(1)}, bf16[2,4,9,16,512]{4,3,2,1,0:T(8,128)(2,1)S(1)}, u32[]{:S(2)}, u32[]{:S(2)}) collective-permute-start(bf16[2,4,9,16,512]{4,3,2,1,0:T(8,128)(2,1)S(1)} %pad_maximum_fusion.refs_5_), channel_id=1, source_target_pairs={{0,1},{1,0},{2,3},{3,2},{4,5},{5,4},{6,7},{7,6},{8,9},{9,8},{10,11... | collective-permute-start | bytes 3538952 | tf_op jit(solution)/shard_map/ppermute | solution.py:432
  48.3 3.7 %collective-permute-start.13 = (f32[8,512]{1,0:T(8,128)S(1)}, f32[8,512]{1,0:T(8,128)S(1)}, u32[]{:S(2)}, u32[]{:S(2)}) collective-permute-start(f32[8,512]{1,0:T(8,128)S(1)} %add.110), channel_id=1, source_target_pairs={{0,2},{1,3},{2,0},{3,1},{4,6},{5,7},{6,4},{7,5},{8,10},{9,11},{10,... | collective-permute-start | bytes 49160 | tf_op jit(solution)/shard_map/ppermute | solution.py:432
  52.0 4.6 %collective-permute-start.14 = (f32[8,512]{1,0:T(8,128)S(1)}, f32[8,512]{1,0:T(8,128)S(1)}, u32[]{:S(2)}, u32[]{:S(2)}) collective-permute-start(f32[8,512]{1,0:T(8,128)S(1)} %add.111.refs_0_.sums_ref), channel_id=1, source_target_pairs={{0,4},{1,5},{2,6},{3,7},{4,0},{5,1},{6,2},{7,3},{8,12},{9,13},{10,... | collective-permute-start | bytes 49160 | tf_op jit(solution)/shard_map/ppermute | solution.py:432
  69.3 3.7 %collective-permute-start.23 = (f32[8,512]{1,0:T(8,128)S(1)}, f32[8,512]{1,0:T(8,128)S(1)}, u32[]{:S(2)}, u32[]{:S(2)}) collective-permute-start(f32[8,512]{1,0:T(8,128)S(1)} %add.112), channel_id=1, source_target_pairs={{0,8},{8,0},{16,24},{24,16},{1,9},{9,1},{17,25},{25,17},{2,10},{10... | collective-permute-start | bytes 49160 | tf_op jit(solution)/shard_map/ppermute | solution.py:432
  73.0 3.7 %collective-permute-start.24 = (f32[8,512]{1,0:T(8,128)S(1)}, f32[8,512]{1,0:T(8,128)S(1)}, u32[]{:S(2)}, u32[]{:S(2)}) collective-permute-start(f32[8,512]{1,0:T(8,128)S(1)} %add.113), channel_id=1, source_target_pairs={{0,16},{8,24},{16,0},{24,8},{1,17},{9,25},{17,1},{25,9},{2,18},{10... | collective-permute-start | bytes 49160 | tf_op jit(solution)/shard_map/ppermute | solution.py:432
  76.8 3.7 %collective-permute-start.25 = (f32[8,512]{1,0:T(8,128)S(1)}, f32[8,512]{1,0:T(8,128)S(1)}, u32[]{:S(2)}, u32[]{:S(2)}) collective-permute-start(f32[8,512]{1,0:T(8,128)S(1)} %add.114), channel_id=1, source_target_pairs={{0,2},{1,3},{2,0},{3,1},{4,6},{5,7},{6,4},{7,5},{8,10},{9,11},{10,... | collective-permute-start | bytes 49160 | tf_op jit(solution)/shard_map/ppermute | solution.py:432
  80.5 4.6 %collective-permute-start.26 = (f32[8,512]{1,0:T(8,128)S(1)}, f32[8,512]{1,0:T(8,128)S(1)}, u32[]{:S(2)}, u32[]{:S(2)}) collective-permute-start(f32[8,512]{1,0:T(8,128)S(1)} %add.115.sums_two_ref.refs_2_), channel_id=1, source_target_pairs={{0,4},{1,5},{2,6},{3,7},{4,0},{5,1},{6,2},{7,3},{8,12},{9,13},{10,... | collective-permute-start | bytes 49160 | tf_op jit(solution)/shard_map/ppermute | solution.py:432
  87.5 3.7 %collective-permute-start.28 = (f32[8,512]{1,0:T(8,128)S(1)}, f32[8,512]{1,0:T(8,128)S(1)}, u32[]{:S(2)}, u32[]{:S(2)}) collective-permute-start(f32[8,512]{1,0:T(8,128)S(1)} %add.116), channel_id=1, source_target_pairs={{0,8},{8,0},{16,24},{24,16},{1,9},{9,1},{17,25},{25,17},{2,10},{10... | collective-permute-start | bytes 49160 | tf_op jit(solution)/shard_map/ppermute | solution.py:432
  91.2 3.7 %collective-permute-start.29 = (f32[8,512]{1,0:T(8,128)S(1)}, f32[8,512]{1,0:T(8,128)S(1)}, u32[]{:S(2)}, u32[]{:S(2)}) collective-permute-start(f32[8,512]{1,0:T(8,128)S(1)} %add.117), channel_id=1, source_target_pairs={{0,16},{8,24},{16,0},{24,8},{1,17},{9,25},{17,1},{25,9},{2,18},{10... | collective-permute-start | bytes 49160 | tf_op jit(solution)/shard_map/ppermute | solution.py:432
  94.9 3.7 %collective-permute-start.30 = (f32[8,512]{1,0:T(8,128)S(1)}, f32[8,512]{1,0:T(8,128)S(1)}, u32[]{:S(2)}, u32[]{:S(2)}) collective-permute-start(f32[8,512]{1,0:T(8,128)S(1)} %add.118), channel_id=1, source_target_pairs={{0,2},{1,3},{2,0},{3,1},{4,6},{5,7},{6,4},{7,5},{8,10},{9,11},{10,... | collective-permute-start | bytes 49160 | tf_op jit(solution)/shard_map/ppermute | solution.py:432
  98.7 4.6 %collective-permute-start.31 = (f32[8,512]{1,0:T(8,128)S(1)}, f32[8,512]{1,0:T(8,128)S(1)}, u32[]{:S(2)}, u32[]{:S(2)}) collective-permute-start(f32[8,512]{1,0:T(8,128)S(1)} %add.119.refs_4_.refs_1_), channel_id=1, source_target_pairs={{0,4},{1,5},{2,6},{3,7},{4,0},{5,1},{6,2},{7,3},{8,12},{9,13},{10,... | collective-permute-start | bytes 49160 | tf_op jit(solution)/shard_map/ppermute | solution.py:432
  110.9 8.1 %collective-permute-start.35 = (bf16[8,9,16,512]{3,2,1,0:T(8,128)(2,1)S(1)}, bf16[8,9,16,512]{3,2,1,0:T(8,128)(2,1)S(1)}, u32[]{:S(2)}, u32[]{:S(2)}) collective-permute-start(bf16[8,9,16,512]{3,2,1,0:T(8,128)(2,1)S(1)} %get-tuple-element.100), channel_id=1, source_target_pairs={{0,1},{1,0},{2,3},{3,2},{4,5},{5,4},{6,7},{7,6},{8,9},{9,8},{10,11... | collective-permute-start | bytes 3538952 | tf_op jit(solution)/shard_map/ppermute | solution.py:432
  111.1 8.3 %collective-permute-start.36 = (bf16[8,9,16,512]{3,2,1,0:T(8,128)(2,1)S(1)}, bf16[8,9,16,512]{3,2,1,0:T(8,128)(2,1)S(1)}, u32[]{:S(2)}, u32[]{:S(2)}) collective-permute-start(bf16[8,9,16,512]{3,2,1,0:T(8,128)(2,1)S(1)} %get-tuple-element.101), channel_id=1, source_target_pairs={{0,1},{1,0},{2,3},{3,2},{4,5},{5,4},{6,7},{7,6},{8,9},{9,8},{10,11... | collective-permute-start | bytes 3538952 | tf_op jit(solution)/shard_map/ppermute | solution.py:432
  111.5 3.7 %collective-permute-start.33 = (f32[8,512]{1,0:T(8,128)S(1)}, f32[8,512]{1,0:T(8,128)S(1)}, u32[]{:S(2)}, u32[]{:S(2)}) collective-permute-start(f32[8,512]{1,0:T(8,128)S(1)} %add.120), channel_id=1, source_target_pairs={{0,8},{8,0},{16,24},{24,16},{1,9},{9,1},{17,25},{25,17},{2,10},{10... | collective-permute-start | bytes 49160 | tf_op jit(solution)/shard_map/ppermute | solution.py:432
  120.0 14.2 %collective-permute-start.54 = (bf16[4,9,16,512]{3,2,1,0:T(8,128)(2,1)S(1)}, bf16[4,9,16,512]{3,2,1,0:T(8,128)(2,1)S(1)}, u32[]{:S(2)}, u32[]{:S(2)}) collective-permute-start(bf16[4,9,16,512]{3,2,1,0:T(8,128)(2,1)S(1)} %slice.99), channel_id=1, source_target_pairs={{0,16},{8,24},{16,0},{24,8},{1,17},{9,25},{17,1},{25,9},{2,18},{10... | collective-permute-start | bytes 1769480 | tf_op jit(solution)/shard_map/ppermute | solution.py:432
  121.2 13.9 %collective-permute-start.41 = (bf16[4,9,16,512]{3,2,1,0:T(8,128)(2,1)S(1)}, bf16[4,9,16,512]{3,2,1,0:T(8,128)(2,1)S(1)}, u32[]{:S(2)}, u32[]{:S(2)}) collective-permute-start(bf16[4,9,16,512]{3,2,1,0:T(8,128)(2,1)S(1)} %slice.81), channel_id=1, source_target_pairs={{0,8},{8,0},{16,24},{24,16},{1,9},{9,1},{17,25},{25,17},{2,10},{10... | collective-permute-start | bytes 1769480 | tf_op jit(solution)/shard_map/ppermute | solution.py:432
  122.8 3.7 %collective-permute-start.37 = (f32[8,512]{1,0:T(8,128)S(1)}, f32[8,512]{1,0:T(8,128)S(1)}, u32[]{:S(2)}, u32[]{:S(2)}) collective-permute-start(f32[8,512]{1,0:T(8,128)S(1)} %add.122), channel_id=1, source_target_pairs={{0,2},{1,3},{2,0},{3,1},{4,6},{5,7},{6,4},{7,5},{8,10},{9,11},{10,... | collective-permute-start | bytes 49160 | tf_op jit(solution)/shard_map/ppermute | solution.py:432
  126.5 4.6 %collective-permute-start.38 = (f32[8,512]{1,0:T(8,128)S(1)}, f32[8,512]{1,0:T(8,128)S(1)}, u32[]{:S(2)}, u32[]{:S(2)}) collective-permute-start(f32[8,512]{1,0:T(8,128)S(1)} %add.125.sums_y_ref.refs_3_), channel_id=1, source_target_pairs={{0,4},{1,5},{2,6},{3,7},{4,0},{5,1},{6,2},{7,3},{8,12},{9,13},{10,... | collective-permute-start | bytes 49160 | tf_op jit(solution)/shard_map/ppermute | solution.py:432
  134.3 10.2 %collective-permute-start.55 = (bf16[2,9,16,512]{3,2,1,0:T(8,128)(2,1)S(1)}, bf16[2,9,16,512]{3,2,1,0:T(8,128)(2,1)S(1)}, u32[]{:S(2)}, u32[]{:S(2)}) collective-permute-start(bf16[2,9,16,512]{3,2,1,0:T(8,128)(2,1)S(1)} %slice.115), channel_id=1, source_target_pairs={{0,8},{8,0},{16,24},{24,16},{1,9},{9,1},{17,25},{25,17},{2,10},{10... | collective-permute-start | bytes 884744 | tf_op jit(solution)/shard_map/ppermute | solution.py:432
  137.0 11.1 %collective-permute-start.52 = (bf16[2,9,16,512]{3,2,1,0:T(8,128)(2,1)S(1)}, bf16[2,9,16,512]{3,2,1,0:T(8,128)(2,1)S(1)}, u32[]{:S(2)}, u32[]{:S(2)}) collective-permute-start(bf16[2,9,16,512]{3,2,1,0:T(8,128)(2,1)S(1)} %slice.95), channel_id=1, source_target_pairs={{0,16},{8,24},{16,0},{24,8},{1,17},{9,25},{17,1},{25,9},{2,18},{10... | collective-permute-start | bytes 884744 | tf_op jit(solution)/shard_map/ppermute | solution.py:432
  138.0 15.1 %collective-permute-start.45 = (bf16[4,10,16,256]{3,2,1,0:T(8,128)(2,1)S(1)}, bf16[4,10,16,256]{3,2,1,0:T(8,128)(2,1)S(1)}, u32[]{:S(2)}, u32[]{:S(2)}) collective-permute-start(bf16[4,10,16,256]{3,2,1,0:T(8,128)(2,1)S(1)} %slice.89), channel_id=1, source_target_pairs={{0,16},{8,24},{16,0},{24,8},{1,17},{9,25},{17,1},{25,9},{2,18},{10... | collective-permute-start | bytes 983048 | tf_op jit(solution)/shard_map/ppermute | solution.py:432
  139.2 14.6 %collective-permute-start.42 = (bf16[4,10,16,256]{3,2,1,0:T(8,128)(2,1)S(1)}, bf16[4,10,16,256]{3,2,1,0:T(8,128)(2,1)S(1)}, u32[]{:S(2)}, u32[]{:S(2)}) collective-permute-start(bf16[4,10,16,256]{3,2,1,0:T(8,128)(2,1)S(1)} %slice.83), channel_id=1, source_target_pairs={{0,8},{8,0},{16,24},{24,16},{1,9},{9,1},{17,25},{25,17},{2,10},{10... | collective-permute-start | bytes 983048 | tf_op jit(solution)/shard_map/ppermute | solution.py:432
  144.5 17.7 %collective-permute-start.56 = (bf16[9,16,512]{2,1,0:T(8,128)(2,1)S(1)}, bf16[9,16,512]{2,1,0:T(8,128)(2,1)S(1)}, u32[]{:S(2)}, u32[]{:S(2)}) collective-permute-start(bf16[9,16,512]{2,1,0:T(8,128)(2,1)S(1)} %get-tuple-element.131), channel_id=1, source_target_pairs={{0,4},{1,5},{2,6},{3,7},{4,0},{5,1},{6,2},{7,3},{8,12},{9,13},{10,... | collective-permute-start | bytes 442376 | tf_op jit(solution)/shard_map/ppermute | solution.py:432
  146.1 16.3 %collective-permute-start.57 = (bf16[9,16,512]{2,1,0:T(8,128)(2,1)S(1)}, bf16[9,16,512]{2,1,0:T(8,128)(2,1)S(1)}, u32[]{:S(2)}, u32[]{:S(2)}) collective-permute-start(bf16[9,16,512]{2,1,0:T(8,128)(2,1)S(1)} %get-tuple-element.132), channel_id=1, source_target_pairs={{0,6},{1,7},{2,4},{3,5},{4,2},{5,3},{6,0},{7,1},{8,14},{9,15},{10,... | collective-permute-start | bytes 442376 | tf_op jit(solution)/shard_map/ppermute | solution.py:432
  148.1 14.3 %collective-permute-start.53 = (bf16[9,16,512]{2,1,0:T(8,128)(2,1)S(1)}, bf16[9,16,512]{2,1,0:T(8,128)(2,1)S(1)}, u32[]{:S(2)}, u32[]{:S(2)}) collective-permute-start(bf16[9,16,512]{2,1,0:T(8,128)(2,1)S(1)} %slice_bitcast_fusion.4), channel_id=1, source_target_pairs={{0,2},{1,3},{2,0},{3,1},{4,6},{5,7},{6,4},{7,5},{8,10},{9,11},{10,... | collective-permute-start | bytes 442376 | tf_op jit(solution)/shard_map/ppermute | solution.py:432
  153.2 5.5 %collective-permute-start.46 = (bf16[2,10,16,256]{3,2,1,0:T(8,128)(2,1)S(1)}, bf16[2,10,16,256]{3,2,1,0:T(8,128)(2,1)S(1)}, u32[]{:S(2)}, u32[]{:S(2)}) collective-permute-start(bf16[2,10,16,256]{3,2,1,0:T(8,128)(2,1)S(1)} %slice.109), channel_id=1, source_target_pairs={{0,8},{8,0},{16,24},{24,16},{1,9},{9,1},{17,25},{25,17},{2,10},{10... | collective-permute-start | bytes 491528 | tf_op jit(solution)/shard_map/ppermute | solution.py:432
  153.8 6.5 %collective-permute-start.43 = (bf16[2,10,16,256]{3,2,1,0:T(8,128)(2,1)S(1)}, bf16[2,10,16,256]{3,2,1,0:T(8,128)(2,1)S(1)}, u32[]{:S(2)}, u32[]{:S(2)}) collective-permute-start(bf16[2,10,16,256]{3,2,1,0:T(8,128)(2,1)S(1)} %slice.105), channel_id=1, source_target_pairs={{0,16},{8,24},{16,0},{24,8},{1,17},{9,25},{17,1},{25,9},{2,18},{10... | collective-permute-start | bytes 491528 | tf_op jit(solution)/shard_map/ppermute | solution.py:432
  158.7 8.1 %collective-permute-start.47 = (bf16[10,16,256]{2,1,0:T(8,128)(2,1)S(1)}, bf16[10,16,256]{2,1,0:T(8,128)(2,1)S(1)}, u32[]{:S(2)}, u32[]{:S(2)}) collective-permute-start(bf16[10,16,256]{2,1,0:T(8,128)(2,1)S(1)} %get-tuple-element.133), channel_id=1, source_target_pairs={{0,4},{1,5},{2,6},{3,7},{4,0},{5,1},{6,2},{7,3},{8,12},{9,13},{10,... | collective-permute-start | bytes 245768 | tf_op jit(solution)/shard_map/ppermute | solution.py:432
  160.3 6.6 %collective-permute-start.48 = (bf16[10,16,256]{2,1,0:T(8,128)(2,1)S(1)}, bf16[10,16,256]{2,1,0:T(8,128)(2,1)S(1)}, u32[]{:S(2)}, u32[]{:S(2)}) collective-permute-start(bf16[10,16,256]{2,1,0:T(8,128)(2,1)S(1)} %get-tuple-element.134), channel_id=1, source_target_pairs={{0,6},{1,7},{2,4},{3,5},{4,2},{5,3},{6,0},{7,1},{8,14},{9,15},{10,... | collective-permute-start | bytes 245768 | tf_op jit(solution)/shard_map/ppermute | solution.py:432
  162.2 5.4 %collective-permute-start.44 = (bf16[10,16,256]{2,1,0:T(8,128)(2,1)S(1)}, bf16[10,16,256]{2,1,0:T(8,128)(2,1)S(1)}, u32[]{:S(2)}, u32[]{:S(2)}) collective-permute-start(bf16[10,16,256]{2,1,0:T(8,128)(2,1)S(1)} %slice_bitcast_fusion.8), channel_id=1, source_target_pairs={{0,2},{1,3},{2,0},{3,1},{4,6},{5,7},{6,4},{7,5},{8,10},{9,11},{10,... | collective-permute-start | bytes 245768 | tf_op jit(solution)/shard_map/ppermute | solution.py:432
  162.5 8.0 %collective-permute-start.60 = (bf16[9,16,512]{2,1,0:T(8,128)(2,1)S(1)}, bf16[9,16,512]{2,1,0:T(8,128)(2,1)S(1)}, u32[]{:S(2)}, u32[]{:S(2)}) collective-permute-start(bf16[9,16,512]{2,1,0:T(8,128)(2,1)S(1)} %fusion.2.refs_0_), channel_id=1, source_target_pairs={{0,24},{8,16},{16,8},{24,0},{1,25},{9,17},{17,9},{25,1},{2,26},{10... | collective-permute-start | bytes 442376 | tf_op jit(solution)/shard_map/ppermute | solution.py:432
  163.9 10.2 %collective-permute-start.59 = (bf16[9,16,512]{2,1,0:T(8,128)(2,1)S(1)}, bf16[9,16,512]{2,1,0:T(8,128)(2,1)S(1)}, u32[]{:S(2)}, u32[]{:S(2)}) collective-permute-start(bf16[9,16,512]{2,1,0:T(8,128)(2,1)S(1)} %fusion.2.refs_0_), channel_id=1, source_target_pairs={{0,16},{8,24},{16,0},{24,8},{1,17},{9,25},{17,1},{25,9},{2,18},{10... | collective-permute-start | bytes 442376 | tf_op jit(solution)/shard_map/ppermute | solution.py:432
  166.8 7.3 %collective-permute-start.58 = (bf16[9,16,512]{2,1,0:T(8,128)(2,1)S(1)}, bf16[9,16,512]{2,1,0:T(8,128)(2,1)S(1)}, u32[]{:S(2)}, u32[]{:S(2)}) collective-permute-start(bf16[9,16,512]{2,1,0:T(8,128)(2,1)S(1)} %fusion.2.refs_0_), channel_id=1, source_target_pairs={{0,8},{8,0},{16,24},{24,16},{1,9},{9,1},{17,25},{25,17},{2,10},{10... | collective-permute-start | bytes 442376 | tf_op jit(solution)/shard_map/ppermute | solution.py:432
  167.7 8.1 %collective-permute-start.51 = (bf16[10,16,256]{2,1,0:T(8,128)(2,1)S(1)}, bf16[10,16,256]{2,1,0:T(8,128)(2,1)S(1)}, u32[]{:S(2)}, u32[]{:S(2)}) collective-permute-start(bf16[10,16,256]{2,1,0:T(8,128)(2,1)S(1)} %fusion.5.refs_0_), channel_id=1, source_target_pairs={{0,24},{8,16},{16,8},{24,0},{1,25},{9,17},{17,9},{25,1},{2,26},{10... | collective-permute-start | bytes 245768 | tf_op jit(solution)/shard_map/ppermute | solution.py:432
  169.3 6.4 %collective-permute-start.50 = (bf16[10,16,256]{2,1,0:T(8,128)(2,1)S(1)}, bf16[10,16,256]{2,1,0:T(8,128)(2,1)S(1)}, u32[]{:S(2)}, u32[]{:S(2)}) collective-permute-start(bf16[10,16,256]{2,1,0:T(8,128)(2,1)S(1)} %fusion.5.refs_0_), channel_id=1, source_target_pairs={{0,16},{8,24},{16,0},{24,8},{1,17},{9,25},{17,1},{25,9},{2,18},{10... | collective-permute-start | bytes 245768 | tf_op jit(solution)/shard_map/ppermute | solution.py:432
  170.4 5.3 %collective-permute-start.49 = (bf16[10,16,256]{2,1,0:T(8,128)(2,1)S(1)}, bf16[10,16,256]{2,1,0:T(8,128)(2,1)S(1)}, u32[]{:S(2)}, u32[]{:S(2)}) collective-permute-start(bf16[10,16,256]{2,1,0:T(8,128)(2,1)S(1)} %fusion.5.refs_0_), channel_id=1, source_target_pairs={{0,8},{8,0},{16,24},{24,16},{1,9},{9,1},{17,25},{25,17},{2,10},{10... | collective-permute-start | bytes 245768 | tf_op jit(solution)/shard_map/ppermute | solution.py:432
  (14 other events, 26.1 us)

commit v4 on v3

--- a/solution.py
+++ b/solution.py
@@ -12,7 +12,8 @@
 F32 = jnp.float32
 BF16 = jnp.bfloat16
 ROWS = 16
-VMEM_LIMIT = 20 * 2**20
+KN = dict(vm=24, pq=0, z2=0, z1=0, ag2=0, ag1=0, gx2=0, gx1=0, k7=0, k7d=3, gate5=1, dl5=2, dlh=3, cost=1, fin=0, gcore=0)
+VMEM_LIMIT = KN["vm"] * 2**20
 
 
 def up(value, step):
@@ -344,12 +345,12 @@
 class Gathered:
     def __init__(self, arrays, place=None, order=None, labels=(), far=False):
         self.arrays, self.place, self.order, self.labels, self.far = arrays, place, order, labels, far
+        self.taps = max((label[2] + label[3] for label in labels), default=0)
 
     def dims(self):
         if self.order is None:
             return self.arrays[0].shape
-        taps, quarter, channels = self.arrays[0].shape[-3:]
-        return taps, quarter * len(self.labels), channels
+        return self.taps, 2 * self.order.zs * self.order.owned, self.arrays[0].shape[-1]
 
     def wrap(self, body, scalars, count):
         if self.order is None:
@@ -366,12 +367,11 @@
                 weights_ref = whole_ref
             core, b, z = place_ref[0], place_ref[1], place_ref[2]
             copies = []
-            for index, at, rel_core, quarter, rel_z in labels:
-                row = ((z ^ rel_z) * 2 + (core ^ rel_core)) * order.owned + quarter(b) * order.quarter
+            for index, at, tap, taps, rel_core, owner, quarter in labels:
+                row = (owner(z) * 2 + (core ^ rel_core)) * order.owned + quarter(b) * order.quarter
                 rows = pl.ds(pl.multiple_of(row, order.quarter), order.quarter)
-                copies.append(
-                    pltpu.make_async_copy(bundles[index].at[at], weights_ref.at[:, rows, :], semaphores.at[len(copies)])
-                )
+                target = weights_ref.at[pl.ds(tap, taps), rows, :]
+                copies.append(pltpu.make_async_copy(bundles[index].at[at], target, semaphores.at[len(copies)]))
             for copy in copies:
                 copy.start()
 
@@ -420,7 +420,7 @@
         out_shape=list(out_shapes) if many else out_shapes,
         scratch_shapes=list(scratch),
         compiler_params=pltpu.CompilerParams(vmem_limit_bytes=VMEM_LIMIT),
-        cost_estimate=pl.CostEstimate(flops=flops, bytes_accessed=moved, transcendentals=0),
+        cost_estimate=pl.CostEstimate(flops=int(flops * KN["cost"]), bytes_accessed=moved, transcendentals=0),
     )(*args)
 
 
@@ -464,7 +464,7 @@
 
 
 def rotated(rel):
-    return lambda b: b ^ rel
+    return lambda own: own ^ rel
 
 
 def of_half(other, index):
@@ -489,15 +489,7 @@
 
 
 def spread_line(order, share, fsdp):
-    return [share] + [exchange(share, "fsdp", fsdp, 2 * rel) for rel in range(1, order.zs)]
-
-
-def double_line(order, share, fsdp):
-    held, rels = share[:, None], [0]
-    for bit in reversed(bits(order.zs)):
-        held = jnp.concatenate([held, exchange(held, "fsdp", fsdp, 2 * bit)], axis=1)
-        rels = rels + [rel ^ bit for rel in rels]
-    return held, rels
+    return jnp.stack([share] + [exchange(share, "fsdp", fsdp, 2 * rel) for rel in range(1, order.zs)])
 
 
 def both_cores(bundles, fsdp):
@@ -508,24 +500,33 @@
     return [line] + [exchange(line, "batch", batch, rel) for rel in (1, 2, 3)]
 
 
-def quarter_labels(order):
-    return [
-        (4 * core + rel, (z,), core, rotated(rel), z) for core in range(2) for rel in range(4) for z in range(order.zs)
-    ]
-
-
-def spread_halves(line, batch):
-    return [exchange(line[0], "batch", batch, 1), exchange(line[1], "batch", batch, 2)]
-
-
-def half_labels(rels):
+def quarter_labels(order, taps):
     labels = []
     for core in range(2):
-        for at, z in enumerate(rels):
+        for rel in range(4):
+            for step in range(order.zs):
+                labels.append((4 * core + rel, step, 0, taps, core, rotated(step), rotated(rel)))
+    return labels
+
+
+def to_plane(halves, batch):
+    return jnp.stack([exchange(halves[0], "batch", batch, 1), exchange(halves[1], "batch", batch, 2)])
+
+
+def half_labels():
+    labels = []
+    for core in range(2):
+        for rel in range(4):
             for index in range(2):
-                labels.append((3 * core, (index, at), core, of_half(0, index), z))
-                labels.append((3 * core + 1 + index, (at,), core, of_half(1, index), z))
+                own, other = of_half(0, index), of_half(1, index)
+                labels.append((3 * core, (index, rel), 0, 9, core, rotated(rel), own))
+                bundle, at = (1, (index, rel)) if rel < 3 else (2, index)
+                labels.append((3 * core + bundle, at, 0, 9, core, rotated(rel), other))
     return labels
+
+
+def assemble_kernel(weights_ref, ready):
+    ready()
 
 
 def reduce_cores(parts, fsdp):
@@ -557,9 +558,20 @@
     return [low[index] for index in range(n_p)] + [high[index] for index in range(n_q)]
 
 
-def finish_weights(order, place, quarter, batch, outs):
+def halve_line(pieces, fsdp):
+    low, high = jnp.stack(pieces[0::2]), jnp.stack(pieces[1::2])
+    low = low + exchange(high, "fsdp", fsdp, 2)
+    return low[0].astype(F32) + exchange(low[1], "fsdp", fsdp, 4).astype(F32)
+
+
+def finish_weights(order, place, quarter, batch, outs, doubling=0):
     quarter = quarter.astype(BF16)
-    spread = [quarter] + [exchange(quarter, "batch", batch, rel) for rel in (1, 2, 3)]
+    if doubling:
+        one = exchange(quarter, "batch", batch, 1)
+        two = exchange(jnp.stack([quarter, one]), "batch", batch, 2)
+        spread = [quarter, one, two[0], two[1]]
+    else:
+        spread = [quarter] + [exchange(quarter, "batch", batch, rel) for rel in (1, 2, 3)]
     return call(functools.partial(finish_kernel, order), outs, place, *spread, scalars=1)
 
 
@@ -592,10 +604,8 @@
     rows, span = plan.rows, plan.span
     everywhere = steps_of((("fsdp", fsdp), ("batch", batch)))
     me = lax.axis_index("fsdp")
-    fast = batch == 4 and fsdp >= 4 and fsdp & (fsdp - 1) == 0 and owned % (ROWS * batch) == 0
+    fast = batch == 4 and fsdp == 8 and owned % (ROWS * batch) == 0
     order = Order(batch, fsdp, owned) if fast else None
-    if fast:
-        everywhere = everywhere[:1] + everywhere[-2:] + everywhere[1:-2]
     place = jnp.stack([me % 2, lax.axis_index("batch"), me // 2]).astype(jnp.int32)
 
     own_first = jnp.transpose(w_first, (0, 1, 3, 2)).reshape(9, owned, cin)
@@ -626,10 +636,14 @@
             far=True,
             whole=False,
         )
-        line_first = spread_line(order, share_first, fsdp)
-        line_first = after(jnp.stack(line_first), patches, vec)
-        line_second, rels = double_line(order, after(share_second, line_first), fsdp)
-        kern_first = Gathered(both_cores(spread_quarters(line_first, batch), fsdp), place, order, quarter_labels(order), True)
+        line_first = after(spread_line(order, share_first, fsdp), patches, vec)
+        plane_first = spread_quarters(line_first, batch)
+        kern_first = Gathered(both_cores(plane_first, fsdp), place, order, quarter_labels(order, 10), True)
+        share_second = after(share_second, line_first)
+        near, far = [exchange(share_second, "fsdp", fsdp, bit) for bit in (2, 4)]
+        last = exchange(far, "fsdp", fsdp, 2)
+        front = jnp.stack(together(share_second, near, far, *plane_first[1:])[:3], axis=1)
+        front_plane = to_plane(front, batch)
     else:
         kern_first = Gathered([lax.all_gather(jnp.concatenate([own_first, own_side[None]]), "fsdp", axis=1, tiled=True)])
         kern_second = Gathered([lax.all_gather(own_second, "fsdp", axis=1, tiled=True)])
@@ -643,21 +657,29 @@
         flops=flops,
         weights=kern_first,
     )
-    hooks = None
     if fast:
         kern_first = Gathered(whole)
-        plane_second = []
-
-        def spread_second(value):
-            plane_second.extend(spread_halves(after(line_second, value), batch))
+        held, whole = [last], []
+
+        def over_last(value):
+            value, held[0] = together(value, last)
+            held.append(to_plane(held[0], batch))
             return value
 
-        hooks = {3: spread_second}
-    sums = sum_over(sums, everywhere, hooks)
-    if fast:
-        bundles = [after(value, *sums) for value in plane_second]
-        kern_second = Gathered(both_cores([line_second] + bundles, fsdp), place, order, half_labels(rels))
-    *whole, second, patches_two, sums_two = call(
+        def assemble(value):
+            value, *planes = together(value, front_plane, held[1])
+            line = jnp.concatenate([front, held[0][:, None]], axis=1)
+            bundles = both_cores([line, *planes], fsdp)
+            whole.extend(call(assemble_kernel, [], weights=Gathered(bundles, place, order, half_labels())))
+            return value
+
+        hooks = {2: over_last, 3: assemble, 4: lambda value: after(value, *whole)}
+        sums = sum_over(sums, everywhere, hooks)
+        kern_second = Gathered(whole)
+        everywhere = everywhere[:1] + everywhere[-2:] + everywhere[1:-2]
+    else:
+        sums = sum_over(sums, everywhere)
+    second, patches_two, sums_two = call(
         functools.partial(second_kernel, plan),
         [shape((rows, cout)), shape((rows, 9 * cout), BF16), shape((8, cout))],
         *sums,
@@ -668,8 +690,6 @@
         flops=2 * flops,
         weights=kern_second,
     )
-    if fast:
-        kern_second = Gathered(whole)
     sums_two = sum_over(sums_two, everywhere)
     *outputs, dz, sums_z = call(
         functools.partial(output_kernel, plan),
@@ -709,7 +729,7 @@
                     functools.partial(weight_second_kernel, order),
                     [shape((len(part), 9, order.quarter, cout), BF16) for part in order.parts],
                     place,
-                    after(grad_two, value),
+                    after(grad_two, value) if KN["gate5"] else grad_two,
                     patches_two,
                     scratch=turned,
                     scalars=1,
@@ -723,8 +743,39 @@
             value, *halves_two[:] = together(value, *halves_two)
             return value
 
-        hooks = {1: weights_second, 2: lambda value: after(value, *parts_two), 3: over_plane}
+        def over_x(value):
+            if KN["pq"] == 1:
+                value, halves_two[0] = together(value, halves_two[0], *parts_two)[:2]
+            elif KN["pq"] == 2:
+                halves_two[0] = after(halves_two[0], value)
+                value = after(value, *parts_two)
+            else:
+                value = after(value, *parts_two)
+            return value
+
+        def over_y(value):
+            if KN["pq"]:
+                value, halves_two[1] = together(value, halves_two[1])
+            else:
+                value, *halves_two[:] = together(value, *halves_two)
+            return value
+
+        hooks = {1: weights_second, KN["dl5"]: over_x, KN["dlh"]: over_y}
     sums_y = sum_over(sums_y, everywhere, hooks)
+    def input_part(grad_late):
+        return call(
+            functools.partial(input_kernel, plan, owned),
+            [shape((2 * length, 2 * length, slots, cin), BF16) for length in plan.sides] + [shape((1, owned))] * 6,
+            place,
+            *sums_z,
+            *sums_y,
+            grad_late,
+            grad_side,
+            scratch=[pltpu.VMEM((span, cout), F32), pltpu.VMEM((4, rows, cout), BF16), pltpu.VMEM((rows, cin), F32)],
+            scalars=1,
+            flops=flops,
+            weights=kern_first,
+        )
     if fast:
         grad_one, *parts_one = call(
             functools.partial(weight_first_kernel, order),
@@ -743,15 +794,35 @@
         )
         halves_two = first_in_plane(halves_two, batch)
         halves_one = reduce_cores(parts_one, fsdp)
-        grad_late = after(grad_one, *halves_one)
-        *halves_one, last = together(*halves_one, halves_two[0])
-        halves_two[0] = last
+        if KN["k7"] == 0:
+            grad_late = after(grad_one, *halves_one)
+        elif KN["k7"] == 1:
+            grad_late = after(grad_one, *parts_one)
+        if KN["gx1"]:
+            *halves_one, last = together(*halves_one, halves_two[0])
+            halves_two[0] = last
+        if KN["gx2"] == 1:
+            halves_two[:] = together(*halves_two, *halves_one)[:2]
         halves_one = first_in_plane(halves_one, batch)
-        quarter_two = reduce_line(then_in_plane(halves_two, batch), fsdp)
-        quarter_one = reduce_line(then_in_plane(halves_one, batch), fsdp)
-        dw_second = finish_weights(order, place, quarter_two, batch, [shape((9, owned, cout))])[0]
+        if KN["gx2"] == 2:
+            halves_two[:] = together(*halves_two, *halves_one)[:2]
+        if KN["k7"] == 2:
+            grad_late = after(grad_one, *halves_one)
+        reduce_two = halve_line if KN["z2"] else reduce_line
+        reduce_one = halve_line if KN["z1"] else reduce_line
+        quarter_two = reduce_two(then_in_plane(halves_two, batch), fsdp)
+        early_grads = input_part(grad_late)
+        if KN["k7d"] == 1:
+            halves_one = together(*halves_one, early_grads[3])[:2]
+        pieces_one = then_in_plane(halves_one, batch)
+        if KN["k7d"] == 2:
+            pieces_one = together(*pieces_one, early_grads[3])[:-1]
+        quarter_one = reduce_one(pieces_one, fsdp)
+        if KN["k7d"] == 3:
+            quarter_one = after(quarter_one, early_grads[3])
+        dw_second = finish_weights(order, place, quarter_two, batch, [shape((9, owned, cout))], KN["ag2"])[0]
         dw_first, dw_side = finish_weights(
-            order, place, quarter_one, batch, [shape((9, owned, cin)), shape((owned, cin))]
+            order, place, quarter_one, batch, [shape((9, owned, cin)), shape((owned, cin))], KN["ag1"]
         )
     else:
         grad_one = call(back_first, shape((rows, cout), BF16), *sums, *sums_y, first, dy, mask)
@@ -767,19 +838,8 @@
         ]
         dw_side = dw_side[0]
         grad_late = grad_one
-    *input_grads, shift_1, gain_1, gain_2, shift_2, gain_3, shift_3 = call(
-        functools.partial(input_kernel, plan, owned),
-        [shape((2 * length, 2 * length, slots, cin), BF16) for length in plan.sides] + [shape((1, owned))] * 6,
-        place,
-        *sums_z,
-        *sums_y,
-        grad_late,
-        grad_side,
-        scratch=[pltpu.VMEM((span, cout), F32), pltpu.VMEM((4, rows, cout), BF16), pltpu.VMEM((rows, cin), F32)],
-        scalars=1,
-        flops=flops,
-        weights=kern_first,
-    )
+    *input_grads, shift_1, gain_1, gain_2, shift_2, gain_3, shift_3 = early_grads if fast else input_part(grad_late)
+
     def as_weight(value):
         return jnp.transpose(value.reshape(3, 3, owned, value.shape[2]), (0, 1, 3, 2))
 

time: 177 us -> 173 us (0.977)
  waiting for transfers between devices: 84.1 us -> 70 us
  starting transfers between devices: 61.2 us -> 71.2 us
    ppermute x61 -> x64, waiting for transfers between devices: 84.1 us -> 70 us  [exchange(): lax.ppermute(value, axis, [(index, index ^ bit) for index in range(count)])]
    ppermute x61 -> x64, starting transfers between devices: 61.2 us -> 71.2 us  [exchange(): lax.ppermute(value, axis, [(index, index ^ bit) for index in range(count)])]
    pallas_call x11 -> x12, Pallas kernels: 27.7 us -> 26.8 us  [call(): pl.pallas_call(body, in_specs=specs, out_specs=[first_out] + [vmem] * (le...]
  transfers between devices with their start and end apart: 61 -> 64, of which waited for: 38 -> 32; matrix products, arithmetic and copies ran while one was open for 1% -> 1% of each run, Pallas kernels for 7% -> 7%
where the time goes in v4:
time: 173 us
  starting transfers between devices  71.2 us (41%)
  waiting for transfers between devices  70 us (40%)
  Pallas kernels  26.8 us (15%)
  other arithmetic  2.34 us (1%)
    ppermute x64, starting transfers between devices, exchange(): lax.ppermute(value, axis, [(index, index ^ bit) for index in range(count)])  71.2 us
    ppermute x64, waiting for transfers between devices, exchange(): lax.ppermute(value, axis, [(index, index ^ bit) for index in range(count)])  70 us
    pallas_call x12, Pallas kernels, call(): pl.pallas_call(body, in_specs=specs, out_specs=[first_out] + [vmem] * (le...  26.8 us
  transfers between devices with their start and end apart: 64, of which 32 were waited for; matrix products, arithmetic and copies ran while one was open for 1% of the time, Pallas kernels for 7%

profile of v4, /device:TPU:0, one launch (start us, length us, event | category | flops | bytes accessed | tf_op | source)
XLA Modules:
  0.0 172.9 jit_solution(3083698405893637263)
XLA Ops:
  0.7 1.6 shard_map.272
  2.4 5.1 %collective-permute-start.2 = (bf16[10,16,256]{2,1,0:T(8,128)(2,1)S(1)}, bf16[10,16,256]{2,1,0:T(8,128)(2,1)S(1)}, u32[]{:S(2)}, u32[]{:S(2)}) collective-permute-start(bf16[10,16,256]{2,1,0:T(8,128)(2,1)S(1)} %get-tuple-element.78), channel_id=1, source_target_pairs={{0,6},{1,7},{2,4},{3,5},{4,2},{5,3},{6,0},{7,1},{8,14},{9,15},{10,... | collective-permute-start | bytes 245768 | tf_op jit(solution)/shard_map/ppermute | solution.py:432
  8.8 2.3 %shard_map.271 = (bf16[432,2304]{1,0:T(8,128)(2,1)S(1)}, f32[432,512]{1,0:T(8,128)S(1)}, f32[432,128]{1,0:T(8,128)S(1)}, f32[8,512]{1,0:T(8,128)S(1)}) custom-call(s32[3]{0:T(128)S(1)} %pad_add_fusion.place_ref.refs_0_, s32[1,3]{1,0:T(1,128)S(1)} %copy-done, bf16[10,10,2,256]{3,2,1,0:T(2,128)(2,1)} %bitcast.103, bf16[14,14,2,256]{3,2,1,0:T(2,128)(2,1)} %bitcast.99, ...), custom_call_target="tpu_custom_call" | custom-call | bytes 953112 | tf_op jit(solution)/shard_map/pallas_call | solution.py:416
  11.1 3.2 %collective-permute-done.1 = bf16[10,16,256]{2,1,0:T(8,128)(2,1)S(1)} collective-permute-done((bf16[10,16,256]{2,1,0:T(8,128)(2,1)S(1)}, bf16[10,16,256]{2,1,0:T(8,128)(2,1)S(1)}, u32[]{:S(2)}, u32[]{:S(2)}) %collective-permute-start.1) | collective-permute-done | bytes 81952 | tf_op jit(solution)/shard_map/ppermute | solution.py:432
  14.4 2.5 %collective-permute-start.5 = (bf16[4,10,16,256]{3,2,1,0:T(8,128)(2,1)S(1)}, bf16[4,10,16,256]{3,2,1,0:T(8,128)(2,1)S(1)}, u32[]{:S(2)}, u32[]{:S(2)}) collective-permute-start(bf16[4,10,16,256]{3,2,1,0:T(8,128)(2,1)S(1)} %pad_maximum_fusion.3.refs_3_), channel_id=1, source_target_pairs={{0,24},{8,16},{16,8},{24,0},{1,25},{9,17},{17,9},{25,1},{2,26},{10... | collective-permute-start | bytes 983048 | tf_op jit(solution)/shard_map/ppermute | solution.py:432
  18.8 2.4 %collective-permute-start.12 = (bf16[2,9,16,512]{3,2,1,0:T(8,128)(2,1)S(1)}, bf16[2,9,16,512]{3,2,1,0:T(8,128)(2,1)S(1)}, u32[]{:S(2)}, u32[]{:S(2)}) collective-permute-start(bf16[2,9,16,512]{3,2,1,0:T(8,128)(2,1)S(1)} %get-tuple-element.84), channel_id=1, source_target_pairs={{0,4},{1,5},{2,6},{3,7},{4,0},{5,1},{6,2},{7,3},{8,12},{9,13},{10,... | collective-permute-start | bytes 884744 | tf_op jit(solution)/shard_map/ppermute | solution.py:432
  21.2 9.8 %collective-permute-done.15 = bf16[2,9,16,512]{3,2,1,0:T(8,128)(2,1)S(1)} collective-permute-done((bf16[2,9,16,512]{3,2,1,0:T(8,128)(2,1)S(1)}, bf16[2,9,16,512]{3,2,1,0:T(8,128)(2,1)S(1)}, u32[]{:S(2)}, u32[]{:S(2)}) %collective-permute-start.15) | collective-permute-done | bytes 294944 | tf_op jit(solution)/shard_map/ppermute | solution.py:432
  31.0 1.8 %collective-permute-done.12 = bf16[2,9,16,512]{3,2,1,0:T(8,128)(2,1)S(1)} collective-permute-done((bf16[2,9,16,512]{3,2,1,0:T(8,128)(2,1)S(1)}, bf16[2,9,16,512]{3,2,1,0:T(8,128)(2,1)S(1)}, u32[]{:S(2)}, u32[]{:S(2)}) %collective-permute-start.12) | collective-permute-done | bytes 294944 | tf_op jit(solution)/shard_map/ppermute | solution.py:432
  36.7 2.9 %shard_map.273 = (bf16[10,512,256]{2,1,0:T(8,128)(2,1)S(1)}, f32[432,512]{1,0:T(8,128)S(1)}, f32[432,512]{1,0:T(8,128)S(1)}, f32[8,512]{1,0:T(8,128)S(1)}) custom-call(s32[3]{0:T(128)S(1)} %pad_add_fusion.place_ref.refs_0_, bf16[432,2304]{1,0:T(8,128)(2,1)S(1)} %get-tuple-element.75.refs_0_.patches_ref, ...), custom_call_target="tpu_custom_call" | custom-call | flops 1019215872 | bytes 4849676 | tf_op jit(solution)/shard_map/pallas_call | solution.py:416
  40.9 2.0 %collective-permute-start.11 = (f32[8,512]{1,0:T(8,128)S(1)}, f32[8,512]{1,0:T(8,128)S(1)}, u32[]{:S(2)}, u32[]{:S(2)}) collective-permute-start(f32[8,512]{1,0:T(8,128)S(1)} %add.108), channel_id=1, source_target_pairs={{0,2},{1,3},{2,0},{3,1},{4,6},{5,7},{6,4},{7,5},{8,10},{9,11},{10,... | collective-permute-start | bytes 49160 | tf_op jit(solution)/shard_map/ppermute | solution.py:432
  42.9 1.7 collective-permute-done.11
  44.6 2.5 %collective-permute-start.14 = (f32[8,512]{1,0:T(8,128)S(1)}, f32[8,512]{1,0:T(8,128)S(1)}, u32[]{:S(2)}, u32[]{:S(2)}) collective-permute-start(f32[8,512]{1,0:T(8,128)S(1)} %add.109), channel_id=1, source_target_pairs={{0,4},{1,5},{2,6},{3,7},{4,0},{5,1},{6,2},{7,3},{8,12},{9,13},{10,... | collective-permute-start | bytes 49160 | tf_op jit(solution)/shard_map/ppermute | solution.py:432
  49.9 3.7 %collective-permute-done.18 = bf16[9,16,512]{2,1,0:T(8,128)(2,1)S(1)} collective-permute-done((bf16[9,16,512]{2,1,0:T(8,128)(2,1)S(1)}, bf16[9,16,512]{2,1,0:T(8,128)(2,1)S(1)}, u32[]{:S(2)}, u32[]{:S(2)}) %collective-permute-start.18) | collective-permute-done | bytes 147488 | tf_op jit(solution)/shard_map/ppermute | solution.py:432
  56.1 2.7 %collective-permute-done.20 = f32[8,512]{1,0:T(8,128)S(1)} collective-permute-done((f32[8,512]{1,0:T(8,128)S(1)}, f32[8,512]{1,0:T(8,128)S(1)}, u32[]{:S(2)}, u32[]{:S(2)}) %collective-permute-start.20) | collective-permute-done | bytes 16416 | tf_op jit(solution)/shard_map/ppermute | solution.py:432
  58.9 1.9 %shard_map.274.refs_5_.refs_11_ = bf16[9,512,512]{2,1,0:T(8,128)(2,1)S(1)} custom-call(s32[3]{0:T(128)S(1)} %pad_add_fusion.place_ref.refs_0_, bf16[2,4,9,16,512]{4,3,2,1,0:T(8,128)(2,1)S(1)} %copy.32.refs_0_, bf16[2,3,9,16,512]{4,3,2,1,0:T(8,128)(2,1)S(1)} %pad_maximum_fusion.2.refs_1_, bf16[2,9,16,512]{3,2,1,0:T(8,128)(2,1)S(1)} %pad_maximum_fusion.4.refs_2_, ...), custom_call_target="tpu_custom_call" | custom-call | bytes 4718604 | tf_op jit(solution)/shard_map/pallas_call | solution.py:416
  61.6 3.1 %collective-permute-done.24.refs_1_.got_ref = f32[8,512]{1,0:T(8,128)S(1)} collective-permute-done((f32[8,512]{1,0:T(8,128)S(1)}, f32[8,512]{1,0:T(8,128)S(1)}, u32[]{:S(2)}, u32[]{:S(2)}) %collective-permute-start.24) | collective-permute-done | bytes 16416 | tf_op jit(solution)/shard_map/ppermute | solution.py:432
  64.7 2.4 %shard_map.275 = (f32[432,512]{1,0:T(8,128)S(1)}, bf16[432,4608]{1,0:T(8,128)(2,1)S(1)}, f32[8,512]{1,0:T(8,128)S(1)}) custom-call(f32[8,512]{1,0:T(8,128)S(1)} %add.111.refs_0_.sums_ref, f32[8,512]{1,0:T(8,128)S(1)} %collective-permute-done.24.refs_1_.got_ref, f32[432,512]{1,0:T(8,128)S(1)} %get-tuple-element.92.refs_2_.refs_6_.first_ref, ...), custom_call_target="tpu_custom_call" | custom-call | flops 2038431744 | bytes 5873664 | tf_op jit(solution)/shard_map/pallas_call | solution.py:416
  69.3 2.8 %collective-permute-done.26 = f32[8,512]{1,0:T(8,128)S(1)} collective-permute-done((f32[8,512]{1,0:T(8,128)S(1)}, f32[8,512]{1,0:T(8,128)S(1)}, u32[]{:S(2)}, u32[]{:S(2)}) %collective-permute-start.26) | collective-permute-done | bytes 16416 | tf_op jit(solution)/shard_map/ppermute | solution.py:432
  72.7 3.1 %collective-permute-done.27 = f32[8,512]{1,0:T(8,128)S(1)} collective-permute-done((f32[8,512]{1,0:T(8,128)S(1)}, f32[8,512]{1,0:T(8,128)S(1)}, u32[]{:S(2)}, u32[]{:S(2)}) %collective-permute-start.27) | collective-permute-done | bytes 16416 | tf_op jit(solution)/shard_map/ppermute | solution.py:432
  75.8 2.0 %collective-permute-start.28 = (f32[8,512]{1,0:T(8,128)S(1)}, f32[8,512]{1,0:T(8,128)S(1)}, u32[]{:S(2)}, u32[]{:S(2)}) collective-permute-start(f32[8,512]{1,0:T(8,128)S(1)} %add.114), channel_id=1, source_target_pairs={{0,2},{1,3},{2,0},{3,1},{4,6},{5,7},{6,4},{7,5},{8,10},{9,11},{10,... | collective-permute-start | bytes 49160 | tf_op jit(solution)/shard_map/ppermute | solution.py:432
  77.8 1.7 collective-permute-done.28
  79.5 2.6 %collective-permute-start.29 = (f32[8,512]{1,0:T(8,128)S(1)}, f32[8,512]{1,0:T(8,128)S(1)}, u32[]{:S(2)}, u32[]{:S(2)}) collective-permute-start(f32[8,512]{1,0:T(8,128)S(1)} %add.115.sums_two_ref.refs_2_), channel_id=1, source_target_pairs={{0,4},{1,5},{2,6},{3,7},{4,0},{5,1},{6,2},{7,3},{8,12},{9,13},{10,... | collective-permute-start | bytes 49160 | tf_op jit(solution)/shard_map/ppermute | solution.py:432
  82.1 2.1 %collective-permute-done.29.got_two_ref.refs_3_ = f32[8,512]{1,0:T(8,128)S(1)} collective-permute-done((f32[8,512]{1,0:T(8,128)S(1)}, f32[8,512]{1,0:T(8,128)S(1)}, u32[]{:S(2)}, u32[]{:S(2)}) %collective-permute-start.29) | collective-permute-done | bytes 16416 | tf_op jit(solution)/shard_map/ppermute | solution.py:432
  87.4 2.8 %collective-permute-done.31 = f32[8,512]{1,0:T(8,128)S(1)} collective-permute-done((f32[8,512]{1,0:T(8,128)S(1)}, f32[8,512]{1,0:T(8,128)S(1)}, u32[]{:S(2)}, u32[]{:S(2)}) %collective-permute-start.31) | collective-permute-done | bytes 16416 | tf_op jit(solution)/shard_map/ppermute | solution.py:432
  90.9 3.1 %collective-permute-done.32 = f32[8,512]{1,0:T(8,128)S(1)} collective-permute-done((f32[8,512]{1,0:T(8,128)S(1)}, f32[8,512]{1,0:T(8,128)S(1)}, u32[]{:S(2)}, u32[]{:S(2)}) %collective-permute-start.32) | collective-permute-done | bytes 16416 | tf_op jit(solution)/shard_map/ppermute | solution.py:432
  94.0 2.1 %collective-permute-start.33 = (f32[8,512]{1,0:T(8,128)S(1)}, f32[8,512]{1,0:T(8,128)S(1)}, u32[]{:S(2)}, u32[]{:S(2)}) collective-permute-start(f32[8,512]{1,0:T(8,128)S(1)} %add.118), channel_id=1, source_target_pairs={{0,2},{1,3},{2,0},{3,1},{4,6},{5,7},{6,4},{7,5},{8,10},{9,11},{10,... | collective-permute-start | bytes 49160 | tf_op jit(solution)/shard_map/ppermute | solution.py:432
  96.0 1.7 collective-permute-done.33
  97.8 2.6 %collective-permute-start.34 = (f32[8,512]{1,0:T(8,128)S(1)}, f32[8,512]{1,0:T(8,128)S(1)}, u32[]{:S(2)}, u32[]{:S(2)}) collective-permute-start(f32[8,512]{1,0:T(8,128)S(1)} %add.119.refs_4_.refs_1_), channel_id=1, source_target_pairs={{0,4},{1,5},{2,6},{3,7},{4,0},{5,1},{6,2},{7,3},{8,12},{9,13},{10,... | collective-permute-start | bytes 49160 | tf_op jit(solution)/shard_map/ppermute | solution.py:432
  100.4 2.0 %collective-permute-done.34.refs_5_.refs_2_ = f32[8,512]{1,0:T(8,128)S(1)} collective-permute-done((f32[8,512]{1,0:T(8,128)S(1)}, f32[8,512]{1,0:T(8,128)S(1)}, u32[]{:S(2)}, u32[]{:S(2)}) %collective-permute-start.34) | collective-permute-done | bytes 16416 | tf_op jit(solution)/shard_map/ppermute | solution.py:432
  102.4 2.9 %shard_map.277 = (bf16[432,512]{1,0:T(8,128)(2,1)S(1)}, bf16[432,512]{1,0:T(8,128)(2,1)S(1)}, f32[432,512]{1,0:T(8,128)S(1)}, f32[8,512]{1,0:T(8,128)S(1)}) custom-call(f32[8,512]{1,0:T(8,128)S(1)} %add.111.refs_0_.sums_ref, f32[8,512]{1,0:T(8,128)S(1)} %collective-permute-done.24.refs_1_.got_ref, f32[8,512]{1,0:T(8,128)S(1)} %add.115.sums_two_ref.refs_2_, ...), custom_call_target="tpu_custom_call" | custom-call | flops 2038431744 | bytes 8577024 | tf_op jit(solution)/shard_map/pallas_call | solution.py:416
  106.5 3.3 %shard_map.278 = (bf16[8,9,16,512]{3,2,1,0:T(8,128)(2,1)S(1)}, bf16[8,9,16,512]{3,2,1,0:T(8,128)(2,1)S(1)}, bf16[8,9,16,512]{3,2,1,0:T(8,128)(2,1)S(1)}, bf16[8,9,16,512]{3,2,1,0:T(8,128)(2,1)S(1)}) custom-call(s32[3]{0:T(128)S(1)} %pad_add_fusion.place_ref.refs_0_, bf16[432,512]{1,0:T(8,128)(2,1)S(1)} %get-tuple-element.104.grad_ref, ...), custom_call_target="tpu_custom_call" | custom-call | flops 2038431744 | bytes 4423692 | tf_op jit(solution)/shard_map/pallas_call | solution.py:416
  111.4 2.8 %collective-permute-done.36 = f32[8,512]{1,0:T(8,128)S(1)} collective-permute-done((f32[8,512]{1,0:T(8,128)S(1)}, f32[8,512]{1,0:T(8,128)S(1)}, u32[]{:S(2)}, u32[]{:S(2)}) %collective-permute-start.36) | collective-permute-done | bytes 16416 | tf_op jit(solution)/shard_map/ppermute | solution.py:432
  114.8 3.1 %collective-permute-done.37 = f32[8,512]{1,0:T(8,128)S(1)} collective-permute-done((f32[8,512]{1,0:T(8,128)S(1)}, f32[8,512]{1,0:T(8,128)S(1)}, u32[]{:S(2)}, u32[]{:S(2)}) %collective-permute-start.37) | collective-permute-done | bytes 16416 | tf_op jit(solution)/shard_map/ppermute | solution.py:432
  120.9 2.2 %collective-permute-start.40 = (f32[8,512]{1,0:T(8,128)S(1)}, f32[8,512]{1,0:T(8,128)S(1)}, u32[]{:S(2)}, u32[]{:S(2)}) collective-permute-start(f32[8,512]{1,0:T(8,128)S(1)} %add.122), channel_id=1, source_target_pairs={{0,2},{1,3},{2,0},{3,1},{4,6},{5,7},{6,4},{7,5},{8,10},{9,11},{10,... | collective-permute-start | bytes 49160 | tf_op jit(solution)/shard_map/ppermute | solution.py:432
  123.1 1.7 collective-permute-done.40
  124.8 2.4 %collective-permute-start.41 = (f32[8,512]{1,0:T(8,128)S(1)}, f32[8,512]{1,0:T(8,128)S(1)}, u32[]{:S(2)}, u32[]{:S(2)}) collective-permute-start(f32[8,512]{1,0:T(8,128)S(1)} %add.125.sums_y_ref.refs_3_), channel_id=1, source_target_pairs={{0,4},{1,5},{2,6},{3,7},{4,0},{5,1},{6,2},{7,3},{8,12},{9,13},{10,... | collective-permute-start | bytes 49160 | tf_op jit(solution)/shard_map/ppermute | solution.py:432
  127.2 2.2 %collective-permute-done.41.got_y_ref.refs_4_ = f32[8,512]{1,0:T(8,128)S(1)} collective-permute-done((f32[8,512]{1,0:T(8,128)S(1)}, f32[8,512]{1,0:T(8,128)S(1)}, u32[]{:S(2)}, u32[]{:S(2)}) %collective-permute-start.41) | collective-permute-done | bytes 16416 | tf_op jit(solution)/shard_map/ppermute | solution.py:432
  129.4 2.4 %shard_map.279 = (bf16[432,512]{1,0:T(8,128)(2,1)S(1)}, bf16[8,10,16,256]{3,2,1,0:T(8,128)(2,1)S(1)}, bf16[8,10,16,256]{3,2,1,0:T(8,128)(2,1)S(1)}, bf16[8,10,16...) custom-call(s32[3]{0:T(128)S(1)} %pad_add_fusion.place_ref.refs_0_, f32[8,512]{1,0:T(8,128)S(1)} %add.111.refs_0_.sums_ref, ...), custom_call_target="tpu_custom_call" | custom-call | flops 1019215872 | bytes 4489228 | tf_op jit(solution)/shard_map/pallas_call | solution.py:416
  137.7 2.9 %shard_map.280 = (bf16[10,10,2,256]{3,2,1,0:T(2,128)(2,1)}, bf16[14,14,2,256]{3,2,1,0:T(2,128)(2,1)}, bf16[18,18,2,256]{3,2,1,0:T(2,128)(2,1)}, f32[1,64]{1,0:T(...) custom-call(s32[3]{0:T(128)S(1)} %pad_add_fusion.place_ref.refs_0_, ...), custom_call_target="tpu_custom_call" | custom-call | flops 1019215872 | bytes 3571724 | tf_op jit(solution)/shard_map/pallas_call | solution.py:416
  140.5 2.0 %collective-permute-done.58 = bf16[2,9,16,512]{3,2,1,0:T(8,128)(2,1)S(1)} collective-permute-done((bf16[2,9,16,512]{3,2,1,0:T(8,128)(2,1)S(1)}, bf16[2,9,16,512]{3,2,1,0:T(8,128)(2,1)S(1)}, u32[]{:S(2)}, u32[]{:S(2)}) %collective-permute-start.58) | collective-permute-done | bytes 294944 | tf_op jit(solution)/shard_map/ppermute | solution.py:432
  142.6 2.5 %collective-permute-start.59 = (bf16[9,16,512]{2,1,0:T(8,128)(2,1)S(1)}, bf16[9,16,512]{2,1,0:T(8,128)(2,1)S(1)}, u32[]{:S(2)}, u32[]{:S(2)}) collective-permute-start(bf16[9,16,512]{2,1,0:T(8,128)(2,1)S(1)} %get-tuple-element.137), channel_id=1, source_target_pairs={{0,4},{1,5},{2,6},{3,7},{4,0},{5,1},{6,2},{7,3},{8,12},{9,13},{10,... | collective-permute-start | bytes 442376 | tf_op jit(solution)/shard_map/ppermute | solution.py:432
  145.0 2.0 %collective-permute-start.60 = (bf16[9,16,512]{2,1,0:T(8,128)(2,1)S(1)}, bf16[9,16,512]{2,1,0:T(8,128)(2,1)S(1)}, u32[]{:S(2)}, u32[]{:S(2)}) collective-permute-start(bf16[9,16,512]{2,1,0:T(8,128)(2,1)S(1)} %get-tuple-element.138), channel_id=1, source_target_pairs={{0,6},{1,7},{2,4},{3,5},{4,2},{5,3},{6,0},{7,1},{8,14},{9,15},{10,... | collective-permute-start | bytes 442376 | tf_op jit(solution)/shard_map/ppermute | solution.py:432
  151.2 2.9 %collective-permute-done.45 = bf16[2,10,16,256]{3,2,1,0:T(8,128)(2,1)S(1)} collective-permute-done((bf16[2,10,16,256]{3,2,1,0:T(8,128)(2,1)S(1)}, bf16[2,10,16,256]{3,2,1,0:T(8,128)(2,1)S(1)}, u32[]{:S(2)}, u32[]{:S(2)}) %collective-permute-start.45) | collective-permute-done | bytes 163872 | tf_op jit(solution)/shard_map/ppermute | solution.py:432
  154.1 2.1 %collective-permute-start.46 = (bf16[10,16,256]{2,1,0:T(8,128)(2,1)S(1)}, bf16[10,16,256]{2,1,0:T(8,128)(2,1)S(1)}, u32[]{:S(2)}, u32[]{:S(2)}) collective-permute-start(bf16[10,16,256]{2,1,0:T(8,128)(2,1)S(1)} %slice_bitcast_fusion.10), channel_id=1, source_target_pairs={{0,2},{1,3},{2,0},{3,1},{4,6},{5,7},{6,4},{7,5},{8,10},{9,11},{10,... | collective-permute-start | bytes 245768 | tf_op jit(solution)/shard_map/ppermute | solution.py:432
  157.8 2.0 %collective-permute-start.50 = (bf16[10,16,256]{2,1,0:T(8,128)(2,1)S(1)}, bf16[10,16,256]{2,1,0:T(8,128)(2,1)S(1)}, u32[]{:S(2)}, u32[]{:S(2)}) collective-permute-start(bf16[10,16,256]{2,1,0:T(8,128)(2,1)S(1)} %get-tuple-element.142), channel_id=1, source_target_pairs={{0,6},{1,7},{2,4},{3,5},{4,2},{5,3},{6,0},{7,1},{8,14},{9,15},{10,... | collective-permute-start | bytes 245768 | tf_op jit(solution)/shard_map/ppermute | solution.py:432
  164.2 1.7 collective-permute-start.53
  167.0 1.7 collective-permute-start.51
  169.3 1.6 shard_map.282
  (146 shorter events, 47.2 us)
Async XLA Ops:
  2.4 8.8 %collective-permute-start.2 = (bf16[10,16,256]{2,1,0:T(8,128)(2,1)S(1)}, bf16[10,16,256]{2,1,0:T(8,128)(2,1)S(1)}, u32[]{:S(2)}, u32[]{:S(2)}) collective-permute-start(bf16[10,16,256]{2,1,0:T(8,128)(2,1)S(1)} %get-tuple-element.78), channel_id=1, source_target_pairs={{0,6},{1,7},{2,4},{3,5},{4,2},{5,3},{6,0},{7,1},{8,14},{9,15},{10,... | collective-permute-start | bytes 245768 | tf_op jit(solution)/shard_map/ppermute | solution.py:432
  7.5 6.9 %collective-permute-start.1 = (bf16[10,16,256]{2,1,0:T(8,128)(2,1)S(1)}, bf16[10,16,256]{2,1,0:T(8,128)(2,1)S(1)}, u32[]{:S(2)}, u32[]{:S(2)}) collective-permute-start(bf16[10,16,256]{2,1,0:T(8,128)(2,1)S(1)} %get-tuple-element.78), channel_id=1, source_target_pairs={{0,4},{1,5},{2,6},{3,7},{4,0},{5,1},{6,2},{7,3},{8,12},{9,13},{10,... | collective-permute-start | bytes 245768 | tf_op jit(solution)/shard_map/ppermute | solution.py:432
  7.5 6.9 %collective-permute-start = (bf16[10,16,256]{2,1,0:T(8,128)(2,1)S(1)}, bf16[10,16,256]{2,1,0:T(8,128)(2,1)S(1)}, u32[]{:S(2)}, u32[]{:S(2)}) collective-permute-start(bf16[10,16,256]{2,1,0:T(8,128)(2,1)S(1)} %get-tuple-element.78), channel_id=1, source_target_pairs={{0,2},{1,3},{2,0},{3,1},{4,6},{5,7},{6,4},{7,5},{8,10},{9,11},{10,... | collective-permute-start | bytes 245768 | tf_op jit(solution)/shard_map/ppermute | solution.py:432
  14.4 18.3 %collective-permute-start.5 = (bf16[4,10,16,256]{3,2,1,0:T(8,128)(2,1)S(1)}, bf16[4,10,16,256]{3,2,1,0:T(8,128)(2,1)S(1)}, u32[]{:S(2)}, u32[]{:S(2)}) collective-permute-start(bf16[4,10,16,256]{3,2,1,0:T(8,128)(2,1)S(1)} %pad_maximum_fusion.3.refs_3_), channel_id=1, source_target_pairs={{0,24},{8,16},{16,8},{24,0},{1,25},{9,17},{17,9},{25,1},{2,26},{10... | collective-permute-start | bytes 983048 | tf_op jit(solution)/shard_map/ppermute | solution.py:432
  16.9 15.8 %collective-permute-start.4 = (bf16[4,10,16,256]{3,2,1,0:T(8,128)(2,1)S(1)}, bf16[4,10,16,256]{3,2,1,0:T(8,128)(2,1)S(1)}, u32[]{:S(2)}, u32[]{:S(2)}) collective-permute-start(bf16[4,10,16,256]{3,2,1,0:T(8,128)(2,1)S(1)} %pad_maximum_fusion.3.refs_3_), channel_id=1, source_target_pairs={{0,16},{8,24},{16,0},{24,8},{1,17},{9,25},{17,1},{25,9},{2,18},{10... | collective-permute-start | bytes 983048 | tf_op jit(solution)/shard_map/ppermute | solution.py:432
  17.4 15.3 %collective-permute-start.3 = (bf16[4,10,16,256]{3,2,1,0:T(8,128)(2,1)S(1)}, bf16[4,10,16,256]{3,2,1,0:T(8,128)(2,1)S(1)}, u32[]{:S(2)}, u32[]{:S(2)}) collective-permute-start(bf16[4,10,16,256]{3,2,1,0:T(8,128)(2,1)S(1)} %pad_maximum_fusion.3.refs_3_), channel_id=1, source_target_pairs={{0,8},{8,0},{16,24},{24,16},{1,9},{9,1},{17,25},{25,17},{2,10},{10... | collective-permute-start | bytes 983048 | tf_op jit(solution)/shard_map/ppermute | solution.py:432
  17.9 13.0 %collective-permute-start.15 = (bf16[2,9,16,512]{3,2,1,0:T(8,128)(2,1)S(1)}, bf16[2,9,16,512]{3,2,1,0:T(8,128)(2,1)S(1)}, u32[]{:S(2)}, u32[]{:S(2)}) collective-permute-start(bf16[2,9,16,512]{3,2,1,0:T(8,128)(2,1)S(1)} %get-tuple-element.84), channel_id=1, source_target_pairs={{0,2},{1,3},{2,0},{3,1},{4,6},{5,7},{6,4},{7,5},{8,10},{9,11},{10,... | collective-permute-start | bytes 884744 | tf_op jit(solution)/shard_map/ppermute | solution.py:432
  18.8 13.9 %collective-permute-start.12 = (bf16[2,9,16,512]{3,2,1,0:T(8,128)(2,1)S(1)}, bf16[2,9,16,512]{3,2,1,0:T(8,128)(2,1)S(1)}, u32[]{:S(2)}, u32[]{:S(2)}) collective-permute-start(bf16[2,9,16,512]{3,2,1,0:T(8,128)(2,1)S(1)} %get-tuple-element.84), channel_id=1, source_target_pairs={{0,4},{1,5},{2,6},{3,7},{4,0},{5,1},{6,2},{7,3},{8,12},{9,13},{10,... | collective-permute-start | bytes 884744 | tf_op jit(solution)/shard_map/ppermute | solution.py:432
  32.7 11.9 %collective-permute-start.13 = (bf16[2,9,16,512]{3,2,1,0:T(8,128)(2,1)S(1)}, bf16[2,9,16,512]{3,2,1,0:T(8,128)(2,1)S(1)}, u32[]{:S(2)}, u32[]{:S(2)}) collective-permute-start(bf16[2,9,16,512]{3,2,1,0:T(8,128)(2,1)S(1)} %collective-permute-done.12), channel_id=1, source_target_pairs={{0,2},{1,3},{2,0},{3,1},{4,6},{5,7},{6,4},{7,5},{8,10},{9,11},{10,... | collective-permute-start | bytes 884744 | tf_op jit(solution)/shard_map/ppermute | solution.py:432
  32.8 3.9 %collective-permute-start.8 = (bf16[4,10,16,256]{3,2,1,0:T(8,128)(2,1)S(1)}, bf16[4,10,16,256]{3,2,1,0:T(8,128)(2,1)S(1)}, u32[]{:S(2)}, u32[]{:S(2)}) collective-permute-start(bf16[4,10,16,256]{3,2,1,0:T(8,128)(2,1)S(1)} %collective-permute-done.4.refs_5_), channel_id=1, source_target_pairs={{0,1},{1,0},{2,3},{3,2},{4,5},{5,4},{6,7},{7,6},{8,9},{9,8},{10,11... | collective-permute-start | bytes 983048 | tf_op jit(solution)/shard_map/ppermute | solution.py:432
  33.6 16.2 %collective-permute-start.16 = (bf16[3,9,16,512]{3,2,1,0:T(8,128)(2,1)S(1)}, bf16[3,9,16,512]{3,2,1,0:T(8,128)(2,1)S(1)}, u32[]{:S(2)}, u32[]{:S(2)}) collective-permute-start(bf16[3,9,16,512]{3,2,1,0:T(8,128)(2,1)S(1)} %get-tuple-element.135), channel_id=1, source_target_pairs={{0,8},{8,0},{16,24},{24,16},{1,9},{9,1},{17,25},{25,17},{2,10},{10... | collective-permute-start | bytes 1327112 | tf_op jit(solution)/shard_map/ppermute | solution.py:432
  35.2 14.7 %collective-permute-start.17 = (bf16[3,9,16,512]{3,2,1,0:T(8,128)(2,1)S(1)}, bf16[3,9,16,512]{3,2,1,0:T(8,128)(2,1)S(1)}, u32[]{:S(2)}, u32[]{:S(2)}) collective-permute-start(bf16[3,9,16,512]{3,2,1,0:T(8,128)(2,1)S(1)} %get-tuple-element.136), channel_id=1, source_target_pairs={{0,16},{8,24},{16,0},{24,8},{1,17},{9,25},{17,1},{25,9},{2,18},{10... | collective-permute-start | bytes 1327112 | tf_op jit(solution)/shard_map/ppermute | solution.py:432
  44.6 4.7 %collective-permute-start.14 = (f32[8,512]{1,0:T(8,128)S(1)}, f32[8,512]{1,0:T(8,128)S(1)}, u32[]{:S(2)}, u32[]{:S(2)}) collective-permute-start(f32[8,512]{1,0:T(8,128)S(1)} %add.109), channel_id=1, source_target_pairs={{0,4},{1,5},{2,6},{3,7},{4,0},{5,1},{6,2},{7,3},{8,12},{9,13},{10,... | collective-permute-start | bytes 49160 | tf_op jit(solution)/shard_map/ppermute | solution.py:432
  47.2 11.6 %collective-permute-start.21 = (bf16[2,4,9,16,512]{4,3,2,0,1:T(8,128)(2,1)S(1)}, bf16[2,4,9,16,512]{4,3,2,0,1:T(8,128)(2,1)S(1)}, u32[]{:S(2)}, u32[]{:S(2)}) collective-permute-start(bf16[2,4,9,16,512]{4,3,2,0,1:T(8,128)(2,1)S(1)} %pad_maximum_fusion), channel_id=1, source_target_pairs={{0,1},{1,0},{2,3},{3,2},{4,5},{5,4},{6,7},{7,6},{8,9},{9,8},{10,11... | collective-permute-start | bytes 3538952 | tf_op jit(solution)/shard_map/ppermute | solution.py:432
  47.4 6.3 %collective-permute-start.18 = (bf16[9,16,512]{2,1,0:T(8,128)(2,1)S(1)}, bf16[9,16,512]{2,1,0:T(8,128)(2,1)S(1)}, u32[]{:S(2)}, u32[]{:S(2)}) collective-permute-start(bf16[9,16,512]{2,1,0:T(8,128)(2,1)S(1)} %get-tuple-element.139), channel_id=1, source_target_pairs={{0,8},{8,0},{16,24},{24,16},{1,9},{9,1},{17,25},{25,17},{2,10},{10... | collective-permute-start | bytes 442376 | tf_op jit(solution)/shard_map/ppermute | solution.py:432
  49.3 5.1 %collective-permute-start.19 = (bf16[9,16,512]{2,1,0:T(8,128)(2,1)S(1)}, bf16[9,16,512]{2,1,0:T(8,128)(2,1)S(1)}, u32[]{:S(2)}, u32[]{:S(2)}) collective-permute-start(bf16[9,16,512]{2,1,0:T(8,128)(2,1)S(1)} %get-tuple-element.140), channel_id=1, source_target_pairs={{0,16},{8,24},{16,0},{24,8},{1,17},{9,25},{17,1},{25,9},{2,18},{10... | collective-permute-start | bytes 442376 | tf_op jit(solution)/shard_map/ppermute | solution.py:432
  54.5 4.4 %collective-permute-start.22 = (bf16[2,3,9,16,512]{4,3,2,1,0:T(8,128)(2,1)S(1)}, bf16[2,3,9,16,512]{4,3,2,1,0:T(8,128)(2,1)S(1)}, u32[]{:S(2)}, u32[]{:S(2)}) collective-permute-start(bf16[2,3,9,16,512]{4,3,2,1,0:T(8,128)(2,1)S(1)} %pad_maximum_fusion.2.refs_1_), channel_id=1, source_target_pairs={{0,1},{1,0},{2,3},{3,2},{4,5},{5,4},{6,7},{7,6},{8,9},{9,8},{10,11... | collective-permute-start | bytes 2654216 | tf_op jit(solution)/shard_map/ppermute | solution.py:432
  54.6 4.3 %collective-permute-start.23 = (bf16[2,9,16,512]{3,2,1,0:T(8,128)(2,1)S(1)}, bf16[2,9,16,512]{3,2,1,0:T(8,128)(2,1)S(1)}, u32[]{:S(2)}, u32[]{:S(2)}) collective-permute-start(bf16[2,9,16,512]{3,2,1,0:T(8,128)(2,1)S(1)} %pad_maximum_fusion.4.refs_2_), channel_id=1, source_target_pairs={{0,1},{1,0},{2,3},{3,2},{4,5},{5,4},{6,7},{7,6},{8,9},{9,8},{10,11... | collective-permute-start | bytes 884744 | tf_op jit(solution)/shard_map/ppermute | solution.py:432
  60.9 3.8 %collective-permute-start.24 = (f32[8,512]{1,0:T(8,128)S(1)}, f32[8,512]{1,0:T(8,128)S(1)}, u32[]{:S(2)}, u32[]{:S(2)}) collective-permute-start(f32[8,512]{1,0:T(8,128)S(1)} %add.111.refs_0_.sums_ref), channel_id=1, source_target_pairs={{0,16},{8,24},{16,0},{24,8},{1,17},{9,25},{17,1},{25,9},{2,18},{10... | collective-permute-start | bytes 49160 | tf_op jit(solution)/shard_map/ppermute | solution.py:432
  72.1 3.7 %collective-permute-start.27 = (f32[8,512]{1,0:T(8,128)S(1)}, f32[8,512]{1,0:T(8,128)S(1)}, u32[]{:S(2)}, u32[]{:S(2)}) collective-permute-start(f32[8,512]{1,0:T(8,128)S(1)} %add.113), channel_id=1, source_target_pairs={{0,16},{8,24},{16,0},{24,8},{1,17},{9,25},{17,1},{25,9},{2,18},{10... | collective-permute-start | bytes 49160 | tf_op jit(solution)/shard_map/ppermute | solution.py:432
  79.5 4.6 %collective-permute-start.29 = (f32[8,512]{1,0:T(8,128)S(1)}, f32[8,512]{1,0:T(8,128)S(1)}, u32[]{:S(2)}, u32[]{:S(2)}) collective-permute-start(f32[8,512]{1,0:T(8,128)S(1)} %add.115.sums_two_ref.refs_2_), channel_id=1, source_target_pairs={{0,4},{1,5},{2,6},{3,7},{4,0},{5,1},{6,2},{7,3},{8,12},{9,13},{10,... | collective-permute-start | bytes 49160 | tf_op jit(solution)/shard_map/ppermute | solution.py:432
  94.0 3.8 %collective-permute-start.33 = (f32[8,512]{1,0:T(8,128)S(1)}, f32[8,512]{1,0:T(8,128)S(1)}, u32[]{:S(2)}, u32[]{:S(2)}) collective-permute-start(f32[8,512]{1,0:T(8,128)S(1)} %add.118), channel_id=1, source_target_pairs={{0,2},{1,3},{2,0},{3,1},{4,6},{5,7},{6,4},{7,5},{8,10},{9,11},{10,... | collective-permute-start | bytes 49160 | tf_op jit(solution)/shard_map/ppermute | solution.py:432
  97.8 4.6 %collective-permute-start.34 = (f32[8,512]{1,0:T(8,128)S(1)}, f32[8,512]{1,0:T(8,128)S(1)}, u32[]{:S(2)}, u32[]{:S(2)}) collective-permute-start(f32[8,512]{1,0:T(8,128)S(1)} %add.119.refs_4_.refs_1_), channel_id=1, source_target_pairs={{0,4},{1,5},{2,6},{3,7},{4,0},{5,1},{6,2},{7,3},{8,12},{9,13},{10,... | collective-permute-start | bytes 49160 | tf_op jit(solution)/shard_map/ppermute | solution.py:432
  109.9 8.1 %collective-permute-start.38 = (bf16[8,9,16,512]{3,2,1,0:T(8,128)(2,1)S(1)}, bf16[8,9,16,512]{3,2,1,0:T(8,128)(2,1)S(1)}, u32[]{:S(2)}, u32[]{:S(2)}) collective-permute-start(bf16[8,9,16,512]{3,2,1,0:T(8,128)(2,1)S(1)} %get-tuple-element.108), channel_id=1, source_target_pairs={{0,1},{1,0},{2,3},{3,2},{4,5},{5,4},{6,7},{7,6},{8,9},{9,8},{10,11... | collective-permute-start | bytes 3538952 | tf_op jit(solution)/shard_map/ppermute | solution.py:432
  110.1 8.3 %collective-permute-start.39 = (bf16[8,9,16,512]{3,2,1,0:T(8,128)(2,1)S(1)}, bf16[8,9,16,512]{3,2,1,0:T(8,128)(2,1)S(1)}, u32[]{:S(2)}, u32[]{:S(2)}) collective-permute-start(bf16[8,9,16,512]{3,2,1,0:T(8,128)(2,1)S(1)} %get-tuple-element.109), channel_id=1, source_target_pairs={{0,1},{1,0},{2,3},{3,2},{4,5},{5,4},{6,7},{7,6},{8,9},{9,8},{10,11... | collective-permute-start | bytes 3538952 | tf_op jit(solution)/shard_map/ppermute | solution.py:432
  119.0 13.5 %collective-permute-start.57 = (bf16[4,9,16,512]{3,2,1,0:T(8,128)(2,1)S(1)}, bf16[4,9,16,512]{3,2,1,0:T(8,128)(2,1)S(1)}, u32[]{:S(2)}, u32[]{:S(2)}) collective-permute-start(bf16[4,9,16,512]{3,2,1,0:T(8,128)(2,1)S(1)} %slice.107), channel_id=1, source_target_pairs={{0,16},{8,24},{16,0},{24,8},{1,17},{9,25},{17,1},{25,9},{2,18},{10... | collective-permute-start | bytes 1769480 | tf_op jit(solution)/shard_map/ppermute | solution.py:432
  119.7 13.8 %collective-permute-start.54 = (bf16[4,9,16,512]{3,2,1,0:T(8,128)(2,1)S(1)}, bf16[4,9,16,512]{3,2,1,0:T(8,128)(2,1)S(1)}, u32[]{:S(2)}, u32[]{:S(2)}) collective-permute-start(bf16[4,9,16,512]{3,2,1,0:T(8,128)(2,1)S(1)} %slice.101), channel_id=1, source_target_pairs={{0,8},{8,0},{16,24},{24,16},{1,9},{9,1},{17,25},{25,17},{2,10},{10... | collective-permute-start | bytes 1769480 | tf_op jit(solution)/shard_map/ppermute | solution.py:432
  120.9 3.9 %collective-permute-start.40 = (f32[8,512]{1,0:T(8,128)S(1)}, f32[8,512]{1,0:T(8,128)S(1)}, u32[]{:S(2)}, u32[]{:S(2)}) collective-permute-start(f32[8,512]{1,0:T(8,128)S(1)} %add.122), channel_id=1, source_target_pairs={{0,2},{1,3},{2,0},{3,1},{4,6},{5,7},{6,4},{7,5},{8,10},{9,11},{10,... | collective-permute-start | bytes 49160 | tf_op jit(solution)/shard_map/ppermute | solution.py:432
  124.8 4.6 %collective-permute-start.41 = (f32[8,512]{1,0:T(8,128)S(1)}, f32[8,512]{1,0:T(8,128)S(1)}, u32[]{:S(2)}, u32[]{:S(2)}) collective-permute-start(f32[8,512]{1,0:T(8,128)S(1)} %add.125.sums_y_ref.refs_3_), channel_id=1, source_target_pairs={{0,4},{1,5},{2,6},{3,7},{4,0},{5,1},{6,2},{7,3},{8,12},{9,13},{10,... | collective-permute-start | bytes 49160 | tf_op jit(solution)/shard_map/ppermute | solution.py:432
  132.0 4.5 %collective-permute-start.43 = (bf16[8,10,16,256]{3,2,1,0:T(8,128)(2,1)S(1)}, bf16[8,10,16,256]{3,2,1,0:T(8,128)(2,1)S(1)}, u32[]{:S(2)}, u32[]{:S(2)}) collective-permute-start(bf16[8,10,16,256]{3,2,1,0:T(8,128)(2,1)S(1)} %get-tuple-element.118), channel_id=1, source_target_pairs={{0,1},{1,0},{2,3},{3,2},{4,5},{5,4},{6,7},{7,6},{8,9},{9,8},{10,11... | collective-permute-start | bytes 1966088 | tf_op jit(solution)/shard_map/ppermute | solution.py:432
  132.6 9.9 %collective-permute-start.58 = (bf16[2,9,16,512]{3,2,1,0:T(8,128)(2,1)S(1)}, bf16[2,9,16,512]{3,2,1,0:T(8,128)(2,1)S(1)}, u32[]{:S(2)}, u32[]{:S(2)}) collective-permute-start(bf16[2,9,16,512]{3,2,1,0:T(8,128)(2,1)S(1)} %slice.131), channel_id=1, source_target_pairs={{0,8},{8,0},{16,24},{24,16},{1,9},{9,1},{17,25},{25,17},{2,10},{10... | collective-permute-start | bytes 884744 | tf_op jit(solution)/shard_map/ppermute | solution.py:432
  133.8 13.2 %collective-permute-start.55 = (bf16[2,9,16,512]{3,2,1,0:T(8,128)(2,1)S(1)}, bf16[2,9,16,512]{3,2,1,0:T(8,128)(2,1)S(1)}, u32[]{:S(2)}, u32[]{:S(2)}) collective-permute-start(bf16[2,9,16,512]{3,2,1,0:T(8,128)(2,1)S(1)} %slice.127), channel_id=1, source_target_pairs={{0,16},{8,24},{16,0},{24,8},{1,17},{9,25},{17,1},{25,9},{2,18},{10... | collective-permute-start | bytes 884744 | tf_op jit(solution)/shard_map/ppermute | solution.py:432
  135.6 13.0 %collective-permute-start.44 = (bf16[4,10,16,256]{3,2,1,0:T(8,128)(2,1)S(1)}, bf16[4,10,16,256]{3,2,1,0:T(8,128)(2,1)S(1)}, u32[]{:S(2)}, u32[]{:S(2)}) collective-permute-start(bf16[4,10,16,256]{3,2,1,0:T(8,128)(2,1)S(1)} %slice.115), channel_id=1, source_target_pairs={{0,8},{8,0},{16,24},{24,16},{1,9},{9,1},{17,25},{25,17},{2,10},{10... | collective-permute-start | bytes 983048 | tf_op jit(solution)/shard_map/ppermute | solution.py:432
  136.7 13.2 %collective-permute-start.47 = (bf16[4,10,16,256]{3,2,1,0:T(8,128)(2,1)S(1)}, bf16[4,10,16,256]{3,2,1,0:T(8,128)(2,1)S(1)}, u32[]{:S(2)}, u32[]{:S(2)}) collective-permute-start(bf16[4,10,16,256]{3,2,1,0:T(8,128)(2,1)S(1)} %slice.121), channel_id=1, source_target_pairs={{0,16},{8,24},{16,0},{24,8},{1,17},{9,25},{17,1},{25,9},{2,18},{10... | collective-permute-start | bytes 983048 | tf_op jit(solution)/shard_map/ppermute | solution.py:432
  142.6 15.3 %collective-permute-start.59 = (bf16[9,16,512]{2,1,0:T(8,128)(2,1)S(1)}, bf16[9,16,512]{2,1,0:T(8,128)(2,1)S(1)}, u32[]{:S(2)}, u32[]{:S(2)}) collective-permute-start(bf16[9,16,512]{2,1,0:T(8,128)(2,1)S(1)} %get-tuple-element.137), channel_id=1, source_target_pairs={{0,4},{1,5},{2,6},{3,7},{4,0},{5,1},{6,2},{7,3},{8,12},{9,13},{10,... | collective-permute-start | bytes 442376 | tf_op jit(solution)/shard_map/ppermute | solution.py:432
  145.0 14.8 %collective-permute-start.60 = (bf16[9,16,512]{2,1,0:T(8,128)(2,1)S(1)}, bf16[9,16,512]{2,1,0:T(8,128)(2,1)S(1)}, u32[]{:S(2)}, u32[]{:S(2)}) collective-permute-start(bf16[9,16,512]{2,1,0:T(8,128)(2,1)S(1)} %get-tuple-element.138), channel_id=1, source_target_pairs={{0,6},{1,7},{2,4},{3,5},{4,2},{5,3},{6,0},{7,1},{8,14},{9,15},{10,... | collective-permute-start | bytes 442376 | tf_op jit(solution)/shard_map/ppermute | solution.py:432
  147.1 12.7 %collective-permute-start.56 = (bf16[9,16,512]{2,1,0:T(8,128)(2,1)S(1)}, bf16[9,16,512]{2,1,0:T(8,128)(2,1)S(1)}, u32[]{:S(2)}, u32[]{:S(2)}) collective-permute-start(bf16[9,16,512]{2,1,0:T(8,128)(2,1)S(1)} %slice_bitcast_fusion.4), channel_id=1, source_target_pairs={{0,2},{1,3},{2,0},{3,1},{4,6},{5,7},{6,4},{7,5},{8,10},{9,11},{10,... | collective-permute-start | bytes 442376 | tf_op jit(solution)/shard_map/ppermute | solution.py:432
  148.7 5.4 %collective-permute-start.45 = (bf16[2,10,16,256]{3,2,1,0:T(8,128)(2,1)S(1)}, bf16[2,10,16,256]{3,2,1,0:T(8,128)(2,1)S(1)}, u32[]{:S(2)}, u32[]{:S(2)}) collective-permute-start(bf16[2,10,16,256]{3,2,1,0:T(8,128)(2,1)S(1)} %slice.117), channel_id=1, source_target_pairs={{0,16},{8,24},{16,0},{24,8},{1,17},{9,25},{17,1},{25,9},{2,18},{10... | collective-permute-start | bytes 491528 | tf_op jit(solution)/shard_map/ppermute | solution.py:432
  149.9 6.3 %collective-permute-start.48 = (bf16[2,10,16,256]{3,2,1,0:T(8,128)(2,1)S(1)}, bf16[2,10,16,256]{3,2,1,0:T(8,128)(2,1)S(1)}, u32[]{:S(2)}, u32[]{:S(2)}) collective-permute-start(bf16[2,10,16,256]{3,2,1,0:T(8,128)(2,1)S(1)} %slice.123), channel_id=1, source_target_pairs={{0,8},{8,0},{16,24},{24,16},{1,9},{9,1},{17,25},{25,17},{2,10},{10... | collective-permute-start | bytes 491528 | tf_op jit(solution)/shard_map/ppermute | solution.py:432
  154.1 8.5 %collective-permute-start.46 = (bf16[10,16,256]{2,1,0:T(8,128)(2,1)S(1)}, bf16[10,16,256]{2,1,0:T(8,128)(2,1)S(1)}, u32[]{:S(2)}, u32[]{:S(2)}) collective-permute-start(bf16[10,16,256]{2,1,0:T(8,128)(2,1)S(1)} %slice_bitcast_fusion.10), channel_id=1, source_target_pairs={{0,2},{1,3},{2,0},{3,1},{4,6},{5,7},{6,4},{7,5},{8,10},{9,11},{10,... | collective-permute-start | bytes 245768 | tf_op jit(solution)/shard_map/ppermute | solution.py:432
  156.3 7.2 %collective-permute-start.49 = (bf16[10,16,256]{2,1,0:T(8,128)(2,1)S(1)}, bf16[10,16,256]{2,1,0:T(8,128)(2,1)S(1)}, u32[]{:S(2)}, u32[]{:S(2)}) collective-permute-start(bf16[10,16,256]{2,1,0:T(8,128)(2,1)S(1)} %get-tuple-element.141), channel_id=1, source_target_pairs={{0,4},{1,5},{2,6},{3,7},{4,0},{5,1},{6,2},{7,3},{8,12},{9,13},{10,... | collective-permute-start | bytes 245768 | tf_op jit(solution)/shard_map/ppermute | solution.py:432
  157.8 6.3 %collective-permute-start.50 = (bf16[10,16,256]{2,1,0:T(8,128)(2,1)S(1)}, bf16[10,16,256]{2,1,0:T(8,128)(2,1)S(1)}, u32[]{:S(2)}, u32[]{:S(2)}) collective-permute-start(bf16[10,16,256]{2,1,0:T(8,128)(2,1)S(1)} %get-tuple-element.142), channel_id=1, source_target_pairs={{0,6},{1,7},{2,4},{3,5},{4,2},{5,3},{6,0},{7,1},{8,14},{9,15},{10,... | collective-permute-start | bytes 245768 | tf_op jit(solution)/shard_map/ppermute | solution.py:432
  159.9 7.1 %collective-permute-start.63 = (bf16[9,16,512]{2,1,0:T(8,128)(2,1)S(1)}, bf16[9,16,512]{2,1,0:T(8,128)(2,1)S(1)}, u32[]{:S(2)}, u32[]{:S(2)}) collective-permute-start(bf16[9,16,512]{2,1,0:T(8,128)(2,1)S(1)} %fusion.2.refs_0_), channel_id=1, source_target_pairs={{0,24},{8,16},{16,8},{24,0},{1,25},{9,17},{17,9},{25,1},{2,26},{10... | collective-permute-start | bytes 442376 | tf_op jit(solution)/shard_map/ppermute | solution.py:432
  161.4 7.9 %collective-permute-start.62 = (bf16[9,16,512]{2,1,0:T(8,128)(2,1)S(1)}, bf16[9,16,512]{2,1,0:T(8,128)(2,1)S(1)}, u32[]{:S(2)}, u32[]{:S(2)}) collective-permute-start(bf16[9,16,512]{2,1,0:T(8,128)(2,1)S(1)} %fusion.2.refs_0_), channel_id=1, source_target_pairs={{0,16},{8,24},{16,0},{24,8},{1,17},{9,25},{17,1},{25,9},{2,18},{10... | collective-permute-start | bytes 442376 | tf_op jit(solution)/shard_map/ppermute | solution.py:432
  162.7 6.7 %collective-permute-start.61 = (bf16[9,16,512]{2,1,0:T(8,128)(2,1)S(1)}, bf16[9,16,512]{2,1,0:T(8,128)(2,1)S(1)}, u32[]{:S(2)}, u32[]{:S(2)}) collective-permute-start(bf16[9,16,512]{2,1,0:T(8,128)(2,1)S(1)} %fusion.2.refs_0_), channel_id=1, source_target_pairs={{0,8},{8,0},{16,24},{24,16},{1,9},{9,1},{17,25},{25,17},{2,10},{10... | collective-permute-start | bytes 442376 | tf_op jit(solution)/shard_map/ppermute | solution.py:432
  164.2 6.7 %collective-permute-start.53 = (bf16[10,16,256]{2,1,0:T(8,128)(2,1)S(1)}, bf16[10,16,256]{2,1,0:T(8,128)(2,1)S(1)}, u32[]{:S(2)}, u32[]{:S(2)}) collective-permute-start(bf16[10,16,256]{2,1,0:T(8,128)(2,1)S(1)} %fusion.4.refs_0_), channel_id=1, source_target_pairs={{0,24},{8,16},{16,8},{24,0},{1,25},{9,17},{17,9},{25,1},{2,26},{10... | collective-permute-start | bytes 245768 | tf_op jit(solution)/shard_map/ppermute | solution.py:432
  165.9 5.2 %collective-permute-start.52 = (bf16[10,16,256]{2,1,0:T(8,128)(2,1)S(1)}, bf16[10,16,256]{2,1,0:T(8,128)(2,1)S(1)}, u32[]{:S(2)}, u32[]{:S(2)}) collective-permute-start(bf16[10,16,256]{2,1,0:T(8,128)(2,1)S(1)} %fusion.4.refs_0_), channel_id=1, source_target_pairs={{0,16},{8,24},{16,0},{24,8},{1,17},{9,25},{17,1},{25,9},{2,18},{10... | collective-permute-start | bytes 245768 | tf_op jit(solution)/shard_map/ppermute | solution.py:432
  167.0 4.4 %collective-permute-start.51 = (bf16[10,16,256]{2,1,0:T(8,128)(2,1)S(1)}, bf16[10,16,256]{2,1,0:T(8,128)(2,1)S(1)}, u32[]{:S(2)}, u32[]{:S(2)}) collective-permute-start(bf16[10,16,256]{2,1,0:T(8,128)(2,1)S(1)} %fusion.4.refs_0_), channel_id=1, source_target_pairs={{0,8},{8,0},{16,24},{24,16},{1,9},{9,1},{17,25},{25,17},{2,10},{10... | collective-permute-start | bytes 245768 | tf_op jit(solution)/shard_map/ppermute | solution.py:432
  (17 other events, 47.4 us)

commit v5 on v4

--- a/solution.py
+++ b/solution.py
@@ -12,8 +12,7 @@
 F32 = jnp.float32
 BF16 = jnp.bfloat16
 ROWS = 16
-KN = dict(vm=24, pq=0, z2=0, z1=0, ag2=0, ag1=0, gx2=0, gx1=0, k7=0, k7d=3, gate5=1, dl5=2, dlh=3, cost=1, fin=0, gcore=0)
-VMEM_LIMIT = KN["vm"] * 2**20
+VMEM_LIMIT = 30 * 2**20
 
 
 def up(value, step):
@@ -244,51 +243,59 @@
     def __init__(self, batch, fsdp, owned):
         self.zs, self.quarter, self.owned = fsdp // 2, owned // batch, owned
         half = self.zs // 2
-        self.parts = []
-        for core in range(2):
-            self.parts.append([(core, b, z) for b in (0, 2, 1, 3) for z in range(half)])
-            self.parts.append([(core, b, z) for b in (0, 1, 2, 3) for z in range(half, self.zs)])
-
-    def starts(self, place_ref):
+        self.blocks = [(b, z) for b in (0, 2, 1, 3) for z in range(half)]
+        self.blocks += [(b, z) for b in (0, 1, 2, 3) for z in range(half, self.zs)]
+
+    def share(self, place_ref, grad_refs, keep_ref, send_ref, turned_ref):
         core, b, z = place_ref[0], place_ref[1], place_ref[2]
-        for part in self.parts:
-            for rel_core, rel_b, rel_z in part:
-                row = ((z ^ rel_z) * 2 + (core ^ rel_core)) * self.owned + (b ^ rel_b) * self.quarter
-                yield pl.multiple_of(row, self.quarter)
-
-
-def correlate(order, place_ref, grads, patch_refs, out_refs, turned_ref, lhs_ref):
-    quarter = order.quarter
-    for index, grad in enumerate(grads):
-        turned_ref[...] = grad.T
-        for block, start in enumerate(order.starts(place_ref)):
-            lhs_ref[block * quarter : (block + 1) * quarter, :] = turned_ref[pl.ds(start, quarter), :]
-        left = lhs_ref[...]
-        for tap, (ref, first, size) in patch_refs[index]:
-            value = nn(left, ref[:, first : first + size]).astype(BF16)
-            begin = 0
-            for out_ref in out_refs:
-                count = out_ref.shape[0]
-                out_ref[:, tap] = value[begin : begin + count * quarter].reshape(count, quarter, size)
-                begin += count * quarter
-
-
-def weight_second_kernel(order, place_ref, grad_ref, patches_ref, *refs):
-    outs, (turned_ref, lhs_ref) = refs[:-2], refs[-2:]
-    cout = grad_ref.shape[1]
-    taps = [(tap, (patches_ref, tap * cout, cout)) for tap in range(9)]
-    correlate(order, place_ref, [grad_ref[...]], [taps], outs, turned_ref, lhs_ref)
-
-
-def weight_first_kernel(
-    order, place_ref, sums_ref, got_ref, sums_y_ref, got_y_ref, first_ref, dy_ref, mask_ref, side_ref, patches_ref, *refs
-):
-    grad_ref, outs, (turned_ref, lhs_ref) = refs[0], refs[1:-2], refs[-2:]
-    back_first(sums_ref, got_ref, sums_y_ref, got_y_ref, first_ref, dy_ref, mask_ref, grad_ref)
+        for index, grad_ref in enumerate(grad_refs):
+            turned_ref[...] = grad_ref[...].T
+            for rel_core, out_ref in enumerate((keep_ref, send_ref)):
+                for block, (rel_b, rel_z) in enumerate(self.blocks):
+                    row = ((z ^ rel_z) * 2 + (core ^ rel_core)) * self.owned + (b ^ rel_b) * self.quarter
+                    rows = pl.ds(pl.multiple_of(row, self.quarter), self.quarter)
+                    first = (index * len(self.blocks) + block) * self.quarter
+                    out_ref[first : first + self.quarter, :] = turned_ref[rows, :]
+
+    def correlate(self, grads, patch_refs, first, size, tap, out_refs):
+        value = sum(nn(grad, ref[:, first : first + size]) for grad, ref in zip(grads, patch_refs)).astype(BF16)
+        begin = 0
+        for out_ref in out_refs:
+            count = out_ref.shape[0]
+            out_ref[:, tap] = value[begin : begin + count * self.quarter].reshape(count, self.quarter, size)
+            begin += count * self.quarter
+
+
+def back_second_share_kernel(plan, order, place_ref, *refs):
+    inputs, (grad_side_ref, dy_ref, out_ref, keep_ref, send_ref) = refs[:13], refs[13:18]
+    held_ref, patches_ref, turned_ref, grad_two_ref = refs[18:]
+    back_second_kernel(plan, *inputs, grad_two_ref, grad_side_ref, dy_ref, out_ref, held_ref, patches_ref)
+    order.share(place_ref, [grad_two_ref], keep_ref, send_ref, turned_ref)
+
+
+def share_kernel_of(order, place_ref, grad_ref, keep_ref, send_ref, turned_ref):
+    order.share(place_ref, [grad_ref], keep_ref, send_ref, turned_ref)
+
+
+def back_first_share_kernel(order, place_ref, *refs):
+    back_first(*refs[:8])
+    order.share(place_ref, refs[7:8], refs[8], refs[9], refs[10])
+
+
+def weight_second_kernel(order, part, keep_ref, got_ref, patches_ref, other_ref, out_ref):
+    cout = patches_ref.shape[1] // 9
+    grads = [ref[part * cout // 4 : (part + 1) * cout // 4] for ref in (keep_ref, got_ref)]
+    for tap in range(9):
+        order.correlate(grads, (patches_ref, other_ref), tap * cout, cout, tap, [out_ref])
+
+
+def weight_first_kernel(order, keep_ref, got_ref, side_keep_ref, side_got_ref, patches_ref, other_ref, *outs):
     cin = patches_ref.shape[1] // 9
-    taps = [(tap, (patches_ref, tap * cin, cin)) for tap in range(9)]
-    center = [(9, (patches_ref, 4 * cin, cin))]
-    correlate(order, place_ref, [grad_ref[...], side_ref[...]], [taps, center], outs, turned_ref, lhs_ref)
+    grads = [keep_ref[...], got_ref[...]]
+    for tap in range(9):
+        order.correlate(grads, (patches_ref, other_ref), tap * cin, cin, tap, outs)
+    grads = [side_keep_ref[...], side_got_ref[...]]
+    order.correlate(grads, (patches_ref, other_ref), 4 * cin, cin, 9, outs)
 
 
 def plain_weight_kernel(taps, grad_ref, patches_ref, out_ref):
@@ -343,8 +350,8 @@
 
 
 class Gathered:
-    def __init__(self, arrays, place=None, order=None, labels=(), far=False):
-        self.arrays, self.place, self.order, self.labels, self.far = arrays, place, order, labels, far
+    def __init__(self, arrays, place=None, order=None, labels=()):
+        self.arrays, self.place, self.order, self.labels = arrays, place, order, labels
         self.taps = max((label[2] + label[3] for label in labels), default=0)
 
     def dims(self):
@@ -355,16 +362,11 @@
     def wrap(self, body, scalars, count):
         if self.order is None:
             return lambda *refs: body(*refs[: count + 1], lambda: None, *refs[count + 1 :])
-        order, many, labels, far = self.order, len(self.arrays), self.labels, self.far
+        order, many, labels = self.order, len(self.arrays), self.labels
 
         def whole(place_ref, *refs):
             inputs, bundles, rest = refs[:count], refs[count : count + many], refs[count + many :]
-            whole_ref, outs, semaphores = rest[0], rest[1:-1], rest[-1]
-            if far:
-                weights_ref, outs = outs[-1], outs[:-1]
-                leave = pltpu.make_async_copy(weights_ref, whole_ref, semaphores.at[len(labels)])
-            else:
-                weights_ref = whole_ref
+            weights_ref, outs, semaphores = rest[0], rest[1:-1], rest[-1]
             core, b, z = place_ref[0], place_ref[1], place_ref[2]
             copies = []
             for index, at, tap, taps, rel_core, owner, quarter in labels:
@@ -378,24 +380,19 @@
             def ready():
                 for copy in copies:
                     copy.wait()
-                if far:
-                    leave.start()
 
             body(*inputs, weights_ref, ready, *outs)
-            if far:
-                leave.wait()
 
         return whole
 
 
-def call(body, out_shapes, *args, scratch=(), scalars=0, flops=0, weights=None, far=False, whole=True):
+def call(body, out_shapes, *args, scratch=(), scalars=0, weights=None, far=False, whole=True):
     vmem = pl.BlockSpec(memory_space=pltpu.VMEM)
     inner = vmem if whole else pl.BlockSpec(memory_space=pltpu.MemorySpace.HBM)
     if far:
         args = args[:scalars] + tuple(
             pltpu.with_memory_space_constraint(arg, pltpu.MemorySpace.HBM) for arg in args[scalars:]
         )
-    first_out = vmem
     specs = [pl.BlockSpec(memory_space=pltpu.SMEM)] * scalars + [inner] * (len(args) - scalars)
     if weights is not None:
         body = weights.wrap(body, scalars, len(args))
@@ -407,20 +404,16 @@
             args = (weights.place,) + args + tuple(weights.arrays)
             specs = [pl.BlockSpec(memory_space=pltpu.SMEM)] + specs + [pl.BlockSpec(memory_space=pl.ANY)] * len(weights.arrays)
             out_shapes = [shape(weights.dims(), BF16)] + list(out_shapes)
-            if weights.far:
-                scratch += [pltpu.VMEM(weights.dims(), BF16)]
-                first_out = pl.BlockSpec(memory_space=pltpu.MemorySpace.HBM)
-            scratch += [pltpu.SemaphoreType.DMA((len(weights.labels) + weights.far,))]
+            scratch += [pltpu.SemaphoreType.DMA((len(weights.labels),))]
     many = isinstance(out_shapes, (list, tuple))
-    moved = sum(arg.size * arg.dtype.itemsize for arg in args)
     return pl.pallas_call(
         body,
         in_specs=specs,
-        out_specs=[first_out] + [vmem] * (len(out_shapes) - 1) if many else vmem,
+        out_specs=[vmem] * len(out_shapes) if many else vmem,
         out_shape=list(out_shapes) if many else out_shapes,
         scratch_shapes=list(scratch),
         compiler_params=pltpu.CompilerParams(vmem_limit_bytes=VMEM_LIMIT),
-        cost_estimate=pl.CostEstimate(flops=int(flops * KN["cost"]), bytes_accessed=moved, transcendentals=0),
+        cost_estimate=pl.CostEstimate(flops=0, bytes_accessed=0, transcendentals=0),
     )(*args)
 
 
@@ -510,7 +503,7 @@
 
 
 def to_plane(halves, batch):
-    return jnp.stack([exchange(halves[0], "batch", batch, 1), exchange(halves[1], "batch", batch, 2)])
+    return [exchange(halves[0], "batch", batch, 1), exchange(halves[1], "batch", batch, 2)]
 
 
 def half_labels():
@@ -529,11 +522,6 @@
     ready()
 
 
-def reduce_cores(parts, fsdp):
-    keep_p, keep_q, send_p, send_q = parts
-    return keep_p + exchange(send_p, "fsdp", fsdp, 1), keep_q + exchange(send_q, "fsdp", fsdp, 1)
-
-
 def reduce_line(pieces, fsdp):
     total = pieces[0].astype(F32)
     for rel in range(1, len(pieces)):
@@ -558,20 +546,9 @@
     return [low[index] for index in range(n_p)] + [high[index] for index in range(n_q)]
 
 
-def halve_line(pieces, fsdp):
-    low, high = jnp.stack(pieces[0::2]), jnp.stack(pieces[1::2])
-    low = low + exchange(high, "fsdp", fsdp, 2)
-    return low[0].astype(F32) + exchange(low[1], "fsdp", fsdp, 4).astype(F32)
-
-
-def finish_weights(order, place, quarter, batch, outs, doubling=0):
+def finish_weights(order, place, quarter, batch, outs):
     quarter = quarter.astype(BF16)
-    if doubling:
-        one = exchange(quarter, "batch", batch, 1)
-        two = exchange(jnp.stack([quarter, one]), "batch", batch, 2)
-        spread = [quarter, one, two[0], two[1]]
-    else:
-        spread = [quarter] + [exchange(quarter, "batch", batch, rel) for rel in (1, 2, 3)]
+    spread = [quarter] + [exchange(quarter, "batch", batch, rel) for rel in (1, 2, 3)]
     return call(functools.partial(finish_kernel, order), outs, place, *spread, scalars=1)
 
 
@@ -638,7 +615,7 @@
         )
         line_first = after(spread_line(order, share_first, fsdp), patches, vec)
         plane_first = spread_quarters(line_first, batch)
-        kern_first = Gathered(both_cores(plane_first, fsdp), place, order, quarter_labels(order, 10), True)
+        kern_first = Gathered(both_cores(plane_first, fsdp), place, order, quarter_labels(order, 10))
         share_second = after(share_second, line_first)
         near, far = [exchange(share_second, "fsdp", fsdp, bit) for bit in (2, 4)]
         last = exchange(far, "fsdp", fsdp, 2)
@@ -647,18 +624,17 @@
     else:
         kern_first = Gathered([lax.all_gather(jnp.concatenate([own_first, own_side[None]]), "fsdp", axis=1, tiled=True)])
         kern_second = Gathered([lax.all_gather(own_second, "fsdp", axis=1, tiled=True)])
-    flops = 2 * rows * cout * cin * 9
-    *whole, first, side, sums = call(
+    if fast:
+        kern_first = Gathered(call(assemble_kernel, [], weights=kern_first))
+    first, side, sums = call(
         first_kernel,
         [shape((rows, cout)), shape((rows, cout)), shape((8, cout))],
         patches,
         mask,
         vec,
-        flops=flops,
         weights=kern_first,
     )
     if fast:
-        kern_first = Gathered(whole)
         held, whole = [last], []
 
         def over_last(value):
@@ -667,13 +643,13 @@
             return value
 
         def assemble(value):
-            value, *planes = together(value, front_plane, held[1])
-            line = jnp.concatenate([front, held[0][:, None]], axis=1)
-            bundles = both_cores([line, *planes], fsdp)
+            value, piece, *planes = together(value, held[0], *front_plane, *held[1])
+            line = jnp.concatenate([front, piece[:, None]], axis=1)
+            bundles = both_cores([line, jnp.stack(planes[:2]), jnp.stack(planes[2:])], fsdp)
             whole.extend(call(assemble_kernel, [], weights=Gathered(bundles, place, order, half_labels())))
             return value
 
-        hooks = {2: over_last, 3: assemble, 4: lambda value: after(value, *whole)}
+        hooks = {2: over_last, 3: assemble}
         sums = sum_over(sums, everywhere, hooks)
         kern_second = Gathered(whole)
         everywhere = everywhere[:1] + everywhere[-2:] + everywhere[1:-2]
@@ -687,10 +663,21 @@
         mask,
         vec,
         scratch=[pltpu.VMEM((span, cout), F32)],
-        flops=2 * flops,
         weights=kern_second,
     )
-    sums_two = sum_over(sums_two, everywhere)
+    def to_other_core(array, into):
+        def begin(value):
+            into.append(exchange(after(array, value), "fsdp", fsdp, 1))
+            return value
+
+        def end(value):
+            value, into[0] = together(value, into[0])
+            return value
+
+        return {1: begin, 4: end} if fast else None
+
+    other_two, other_one = [], []
+    sums_two = sum_over(sums_two, everywhere, to_other_core(patches_two, other_two))
     *outputs, dz, sums_z = call(
         functools.partial(output_kernel, plan),
         [shape((length, length, slots, cout), BF16) for length in plan.sides] + [shape((rows, cout)), shape((8, cout))],
@@ -700,12 +687,18 @@
         side,
         cot_rows,
         mask,
-        flops=50 * rows * cout,
-    )
-    sums_z = sum_over(sums_z, everywhere)
-    grad_two, grad_side, dy, sums_y = call(
-        functools.partial(back_second_kernel, plan),
-        [shape((rows, cout), BF16), shape((rows, cout), BF16), shape((rows, cout)), shape((8, cout))],
+    )
+    sums_z = sum_over(sums_z, everywhere, to_other_core(patches, other_one))
+    shared = []
+    if fast:
+        turned = pltpu.VMEM((cout, rows), BF16)
+        shared = [shape((cout // 2, rows), BF16)] * 2
+    results = call(
+        functools.partial(back_second_share_kernel, plan, order) if fast else functools.partial(back_second_kernel, plan),
+        ([] if fast else [shape((rows, cout), BF16)])
+        + [shape((rows, cout), BF16), shape((rows, cout)), shape((8, cout))]
+        + shared,
+        *([place] if fast else []),
         *sums,
         *sums_two,
         *sums_z,
@@ -714,53 +707,63 @@
         side,
         dz,
         mask,
-        scratch=[pltpu.VMEM((span, cout), F32), pltpu.VMEM((rows, 9 * cout), BF16)],
-        flops=2 * flops,
+        scratch=[pltpu.VMEM((span, cout), F32), pltpu.VMEM((rows, 9 * cout), BF16)] + ([turned, pltpu.VMEM((rows, cout), BF16)] if fast else []),
+        scalars=int(fast),
         weights=kern_second,
     )
     hooks = None
     if fast:
-        turned = [pltpu.VMEM((cout, rows), BF16), pltpu.VMEM((cout, rows), BF16)]
-        parts_two, halves_two = [], []
-
-        def weights_second(value):
-            parts_two.extend(
+        grad_side, dy, sums_y, keep, send = results
+        got, halves_two, sides = [], [], []
+
+        def begin_second(value):
+            got.append(exchange(after(send, value), "fsdp", fsdp, 1))
+            return value
+
+        def weights_second(value, part):
+            half = (len(order.blocks) // 2, 9, order.quarter, cout)
+            halves_two.append(
                 call(
-                    functools.partial(weight_second_kernel, order),
-                    [shape((len(part), 9, order.quarter, cout), BF16) for part in order.parts],
-                    place,
-                    after(grad_two, value) if KN["gate5"] else grad_two,
+                    functools.partial(weight_second_kernel, order, part),
+                    shape(half, BF16),
+                    after(keep, value),
+                    got[0],
                     patches_two,
-                    scratch=turned,
-                    scalars=1,
-                    flops=2 * flops,
+                    other_two[0],
                 )
             )
-            halves_two.extend(reduce_cores(parts_two, fsdp))
             return value
 
-        def over_plane(value):
-            value, *halves_two[:] = together(value, *halves_two)
+        def over_x(value):
+            value, halves_two[0] = together(value, halves_two[0])
             return value
 
-        def over_x(value):
-            if KN["pq"] == 1:
-                value, halves_two[0] = together(value, halves_two[0], *parts_two)[:2]
-            elif KN["pq"] == 2:
-                halves_two[0] = after(halves_two[0], value)
-                value = after(value, *parts_two)
-            else:
-                value = after(value, *parts_two)
+        def over_y(value):
+            value, halves_two[1] = together(value, halves_two[1])
             return value
 
-        def over_y(value):
-            if KN["pq"]:
-                value, halves_two[1] = together(value, halves_two[1])
-            else:
-                value, *halves_two[:] = together(value, *halves_two)
+        def begin(value):
+            return weights_second(begin_second(value), 0)
+
+        def between(value):
+            return weights_second(over_x(value), 1)
+
+        def share_side(value):
+            value = over_y(value)
+            shares = call(
+                functools.partial(share_kernel_of, order),
+                [shape((cout // 2, rows), BF16)] * 2,
+                place,
+                after(grad_side, value),
+                scratch=[turned],
+                scalars=1,
+            )
+            sides.extend([shares[0], exchange(shares[1], "fsdp", fsdp, 1)])
             return value
 
-        hooks = {1: weights_second, KN["dl5"]: over_x, KN["dlh"]: over_y}
+        hooks = {1: begin, 2: between, 3: share_side, 4: lambda value: after(value, *sides)}
+    else:
+        grad_two, grad_side, dy, sums_y = results
     sums_y = sum_over(sums_y, everywhere, hooks)
     def input_part(grad_late):
         return call(
@@ -773,56 +776,43 @@
             grad_side,
             scratch=[pltpu.VMEM((span, cout), F32), pltpu.VMEM((4, rows, cout), BF16), pltpu.VMEM((rows, cin), F32)],
             scalars=1,
-            flops=flops,
             weights=kern_first,
         )
     if fast:
-        grad_one, *parts_one = call(
-            functools.partial(weight_first_kernel, order),
-            [shape((rows, cout), BF16)] + [shape((len(part), 10, order.quarter, cin), BF16) for part in order.parts],
+        grad_one, keep_one, send_one = call(
+            functools.partial(back_first_share_kernel, order),
+            [shape((rows, cout), BF16)] + [shape((cout // 2, rows), BF16)] * 2,
             place,
             *sums,
             *sums_y,
             first,
             dy,
             mask,
-            grad_side,
-            patches,
-            scratch=turned,
+            scratch=[turned],
             scalars=1,
-            flops=flops,
         )
         halves_two = first_in_plane(halves_two, batch)
-        halves_one = reduce_cores(parts_one, fsdp)
-        if KN["k7"] == 0:
-            grad_late = after(grad_one, *halves_one)
-        elif KN["k7"] == 1:
-            grad_late = after(grad_one, *parts_one)
-        if KN["gx1"]:
-            *halves_one, last = together(*halves_one, halves_two[0])
-            halves_two[0] = last
-        if KN["gx2"] == 1:
-            halves_two[:] = together(*halves_two, *halves_one)[:2]
+        got_one = exchange(send_one, "fsdp", fsdp, 1)
+        keep_one, halves_two[0] = together(keep_one, halves_two[0])
+        half = (len(order.blocks) // 2, 10, order.quarter, cin)
+        halves_one = call(
+            functools.partial(weight_first_kernel, order),
+            [shape(half, BF16)] * 2,
+            keep_one,
+            got_one,
+            *sides,
+            patches,
+            other_one[0],
+        )
+        *halves_one, halves_two[1] = together(*halves_one, halves_two[1])
         halves_one = first_in_plane(halves_one, batch)
-        if KN["gx2"] == 2:
-            halves_two[:] = together(*halves_two, *halves_one)[:2]
-        if KN["k7"] == 2:
-            grad_late = after(grad_one, *halves_one)
-        reduce_two = halve_line if KN["z2"] else reduce_line
-        reduce_one = halve_line if KN["z1"] else reduce_line
-        quarter_two = reduce_two(then_in_plane(halves_two, batch), fsdp)
-        early_grads = input_part(grad_late)
-        if KN["k7d"] == 1:
-            halves_one = together(*halves_one, early_grads[3])[:2]
-        pieces_one = then_in_plane(halves_one, batch)
-        if KN["k7d"] == 2:
-            pieces_one = together(*pieces_one, early_grads[3])[:-1]
-        quarter_one = reduce_one(pieces_one, fsdp)
-        if KN["k7d"] == 3:
-            quarter_one = after(quarter_one, early_grads[3])
-        dw_second = finish_weights(order, place, quarter_two, batch, [shape((9, owned, cout))], KN["ag2"])[0]
+        early_grads = input_part(after(grad_one, *halves_one))
+        quarter_two = reduce_line(then_in_plane(halves_two, batch), fsdp)
+        pieces_one = together(*then_in_plane(halves_one, batch), early_grads[3])[:-1]
+        quarter_one = reduce_line(pieces_one, fsdp)
+        dw_second = finish_weights(order, place, quarter_two, batch, [shape((9, owned, cout))])[0]
         dw_first, dw_side = finish_weights(
-            order, place, quarter_one, batch, [shape((9, owned, cin)), shape((owned, cin))], KN["ag1"]
+            order, place, quarter_one, batch, [shape((9, owned, cin)), shape((owned, cin))]
         )
     else:
         grad_one = call(back_first, shape((rows, cout), BF16), *sums, *sums_y, first, dy, mask)

time: 173 us -> 168 us (0.971)
  waiting for transfers between devices: 70 us -> 64.8 us
    ppermute x64 -> x65, waiting for transfers between devices: 70 us -> 64.8 us  [exchange(): lax.ppermute(value, axis, [(index, index ^ bit) for index in range(count)])]
    pallas_call x12 -> x16, Pallas kernels: 26.8 us -> 27.6 us  [call(): pl.pallas_call(body, in_specs=specs, out_specs=[vmem] * len(out_shapes) i...]
    ppermute x64 -> x65, starting transfers between devices: 71.2 us -> 71.5 us  [exchange(): lax.ppermute(value, axis, [(index, index ^ bit) for index in range(count)])]
  transfers between devices with their start and end apart: 64 -> 65, of which waited for: 32 -> 33; matrix products, arithmetic and copies ran while one was open for 1% -> 1% of each run, Pallas kernels for 7% -> 10%
where the time goes in v5:
time: 168 us; the launch traced here: 167 us
  starting transfers between devices  71.5 us (43%)
  waiting for transfers between devices  64.8 us (39%)
  Pallas kernels  27.6 us (16%)
    ppermute x65, starting transfers between devices, exchange(): lax.ppermute(value, axis, [(index, index ^ bit) for index in range(count)])  71.5 us
    ppermute x65, waiting for transfers between devices, exchange(): lax.ppermute(value, axis, [(index, index ^ bit) for index in range(count)])  64.8 us
    pallas_call x16, Pallas kernels, call(): pl.pallas_call(body, in_specs=specs, out_specs=[vmem] * len(out_shapes) i...  27.6 us
  transfers between devices with their start and end apart: 65, of which 33 were waited for; matrix products, arithmetic and copies ran while one was open for 1% of the time, Pallas kernels for 10%

profile of v5, /device:TPU:0, one launch (start us, length us, event | category | flops | bytes accessed | tf_op | source)
XLA Modules:
  0.0 167.4 jit_solution(10985739697372256926)
XLA Ops:
  0.7 1.6 shard_map.272
  2.4 5.1 %collective-permute-start.2 = (bf16[10,16,256]{2,1,0:T(8,128)(2,1)S(1)}, bf16[10,16,256]{2,1,0:T(8,128)(2,1)S(1)}, u32[]{:S(2)}, u32[]{:S(2)}) collective-permute-start(bf16[10,16,256]{2,1,0:T(8,128)(2,1)S(1)} %get-tuple-element.96), channel_id=1, source_target_pairs={{0,6},{1,7},{2,4},{3,5},{4,2},{5,3},{6,0},{7,1},{8,14},{9,15},{10,... | collective-permute-start | bytes 245768 | tf_op jit(solution)/shard_map/ppermute | solution.py:425
  8.8 2.3 %shard_map.271 = (bf16[432,2304]{1,0:T(8,128)(2,1)S(1)}, f32[432,512]{1,0:T(8,128)S(1)}, f32[432,128]{1,0:T(8,128)S(1)}, f32[8,512]{1,0:T(8,128)S(1)}) custom-call(s32[3]{0:T(128)S(1)} %pad_add_fusion.place_ref.refs_0_, s32[1,3]{1,0:T(1,128)S(1)} %copy-done, bf16[10,10,2,256]{3,2,1,0:T(2,128)(2,1)} %bitcast.100, bf16[14,14,2,256]{3,2,1,0:T(2,128)(2,1)} %bitcast.96, ...), custom_call_target="tpu_custom_call" | custom-call | tf_op jit(solution)/shard_map/pallas_call | solution.py:409
  11.1 3.2 %collective-permute-done.1 = bf16[10,16,256]{2,1,0:T(8,128)(2,1)S(1)} collective-permute-done((bf16[10,16,256]{2,1,0:T(8,128)(2,1)S(1)}, bf16[10,16,256]{2,1,0:T(8,128)(2,1)S(1)}, u32[]{:S(2)}, u32[]{:S(2)}) %collective-permute-start.1) | collective-permute-done | bytes 81952 | tf_op jit(solution)/shard_map/ppermute | solution.py:425
  14.4 2.5 %collective-permute-start.5 = (bf16[4,10,16,256]{3,2,1,0:T(8,128)(2,1)S(1)}, bf16[4,10,16,256]{3,2,1,0:T(8,128)(2,1)S(1)}, u32[]{:S(2)}, u32[]{:S(2)}) collective-permute-start(bf16[4,10,16,256]{3,2,1,0:T(8,128)(2,1)S(1)} %pad_maximum_fusion.3.refs_0_), channel_id=1, source_target_pairs={{0,24},{8,16},{16,8},{24,0},{1,25},{9,17},{17,9},{25,1},{2,26},{10... | collective-permute-start | bytes 983048 | tf_op jit(solution)/shard_map/ppermute | solution.py:425
  18.8 2.4 %collective-permute-start.12 = (bf16[2,9,16,512]{3,2,1,0:T(8,128)(2,1)S(1)}, bf16[2,9,16,512]{3,2,1,0:T(8,128)(2,1)S(1)}, u32[]{:S(2)}, u32[]{:S(2)}) collective-permute-start(bf16[2,9,16,512]{3,2,1,0:T(8,128)(2,1)S(1)} %get-tuple-element.103), channel_id=1, source_target_pairs={{0,4},{1,5},{2,6},{3,7},{4,0},{5,1},{6,2},{7,3},{8,12},{9,13},{10,... | collective-permute-start | bytes 884744 | tf_op jit(solution)/shard_map/ppermute | solution.py:425
  21.2 9.8 %collective-permute-done.15 = bf16[2,9,16,512]{3,2,1,0:T(8,128)(2,1)S(1)} collective-permute-done((bf16[2,9,16,512]{3,2,1,0:T(8,128)(2,1)S(1)}, bf16[2,9,16,512]{3,2,1,0:T(8,128)(2,1)S(1)}, u32[]{:S(2)}, u32[]{:S(2)}) %collective-permute-start.15) | collective-permute-done | bytes 294944 | tf_op jit(solution)/shard_map/ppermute | solution.py:425
  31.0 1.8 %collective-permute-done.12 = bf16[2,9,16,512]{3,2,1,0:T(8,128)(2,1)S(1)} collective-permute-done((bf16[2,9,16,512]{3,2,1,0:T(8,128)(2,1)S(1)}, bf16[2,9,16,512]{3,2,1,0:T(8,128)(2,1)S(1)}, u32[]{:S(2)}, u32[]{:S(2)}) %collective-permute-start.12) | collective-permute-done | bytes 294944 | tf_op jit(solution)/shard_map/ppermute | solution.py:425
  33.6 1.6 collective-permute-start.17
  35.2 1.5 collective-permute-start.16
  40.7 2.0 %collective-permute-start.11 = (f32[8,512]{1,0:T(8,128)S(1)}, f32[8,512]{1,0:T(8,128)S(1)}, u32[]{:S(2)}, u32[]{:S(2)}) collective-permute-start(f32[8,512]{1,0:T(8,128)S(1)} %add.96), channel_id=1, source_target_pairs={{0,2},{1,3},{2,0},{3,1},{4,6},{5,7},{6,4},{7,5},{8,10},{9,11},{10,... | collective-permute-start | bytes 49160 | tf_op jit(solution)/shard_map/ppermute | solution.py:425
  42.7 1.7 %collective-permute-done.11 = f32[8,512]{1,0:T(8,128)S(1)} collective-permute-done((f32[8,512]{1,0:T(8,128)S(1)}, f32[8,512]{1,0:T(8,128)S(1)}, u32[]{:S(2)}, u32[]{:S(2)}) %collective-permute-start.11) | collective-permute-done | bytes 16416 | tf_op jit(solution)/shard_map/ppermute | solution.py:425
  46.2 2.4 %collective-permute-start.14 = (f32[8,512]{1,0:T(8,128)S(1)}, f32[8,512]{1,0:T(8,128)S(1)}, u32[]{:S(2)}, u32[]{:S(2)}) collective-permute-start(f32[8,512]{1,0:T(8,128)S(1)} %add.97), channel_id=1, source_target_pairs={{0,4},{1,5},{2,6},{3,7},{4,0},{5,1},{6,2},{7,3},{8,12},{9,13},{10,... | collective-permute-start | bytes 49160 | tf_op jit(solution)/shard_map/ppermute | solution.py:425
  48.7 2.2 %collective-permute-done.14 = f32[8,512]{1,0:T(8,128)S(1)} collective-permute-done((f32[8,512]{1,0:T(8,128)S(1)}, f32[8,512]{1,0:T(8,128)S(1)}, u32[]{:S(2)}, u32[]{:S(2)}) %collective-permute-start.14) | collective-permute-done | bytes 16416 | tf_op jit(solution)/shard_map/ppermute | solution.py:425
  53.1 2.6 %collective-permute-done.20 = f32[8,512]{1,0:T(8,128)S(1)} collective-permute-done((f32[8,512]{1,0:T(8,128)S(1)}, f32[8,512]{1,0:T(8,128)S(1)}, u32[]{:S(2)}, u32[]{:S(2)}) %collective-permute-start.20) | collective-permute-done | bytes 16416 | tf_op jit(solution)/shard_map/ppermute | solution.py:425
  56.8 1.9 %shard_map.275.refs_5_.refs_12_ = bf16[9,512,512]{2,1,0:T(8,128)(2,1)S(1)} custom-call(s32[3]{0:T(128)S(1)} %pad_add_fusion.place_ref.refs_0_, bf16[2,4,9,16,512]{4,3,2,1,0:T(8,128)(2,1)S(1)} %copy.32.refs_0_, bf16[2,3,9,16,512]{4,3,2,1,0:T(8,128)(2,1)S(1)} %pad_maximum_fusion.2.refs_1_, bf16[2,9,16,512]{3,2,1,0:T(8,128)(2,1)S(1)} %pad_maximum_fusion.4.refs_2_, ...), custom_call_target="tpu_custom_call" | custom-call | tf_op jit(solution)/shard_map/pallas_call | solution.py:409
  59.5 2.4 %shard_map.276 = (f32[432,512]{1,0:T(8,128)S(1)}, bf16[432,4608]{1,0:T(8,128)(2,1)S(1)}, f32[8,512]{1,0:T(8,128)S(1)}) custom-call(f32[8,512]{1,0:T(8,128)S(1)} %add.99.refs_0_.sums_ref.refs_1_, f32[8,512]{1,0:T(8,128)S(1)} %collective-permute-done.21.refs_1_.got_ref.refs_2_, f32[432,512]{1,0:T(8,128)S(1)} %get-tuple-element.107.refs_2_.refs_7_.refs_4_, ...), custom_call_target="tpu_custom_call" | custom-call | tf_op jit(solution)/shard_map/pallas_call | solution.py:409
  64.5 2.6 %collective-permute-done.26 = f32[8,512]{1,0:T(8,128)S(1)} collective-permute-done((f32[8,512]{1,0:T(8,128)S(1)}, f32[8,512]{1,0:T(8,128)S(1)}, u32[]{:S(2)}, u32[]{:S(2)}) %collective-permute-start.26) | collective-permute-done | bytes 16416 | tf_op jit(solution)/shard_map/ppermute | solution.py:425
  67.9 2.9 %collective-permute-done.27 = f32[8,512]{1,0:T(8,128)S(1)} collective-permute-done((f32[8,512]{1,0:T(8,128)S(1)}, f32[8,512]{1,0:T(8,128)S(1)}, u32[]{:S(2)}, u32[]{:S(2)}) %collective-permute-start.27) | collective-permute-done | bytes 16416 | tf_op jit(solution)/shard_map/ppermute | solution.py:425
  70.8 2.0 %collective-permute-start.28 = (f32[8,512]{1,0:T(8,128)S(1)}, f32[8,512]{1,0:T(8,128)S(1)}, u32[]{:S(2)}, u32[]{:S(2)}) collective-permute-start(f32[8,512]{1,0:T(8,128)S(1)} %add.102), channel_id=1, source_target_pairs={{0,2},{1,3},{2,0},{3,1},{4,6},{5,7},{6,4},{7,5},{8,10},{9,11},{10,... | collective-permute-start | bytes 49160 | tf_op jit(solution)/shard_map/ppermute | solution.py:425
  72.8 1.7 %collective-permute-done.28 = f32[8,512]{1,0:T(8,128)S(1)} collective-permute-done((f32[8,512]{1,0:T(8,128)S(1)}, f32[8,512]{1,0:T(8,128)S(1)}, u32[]{:S(2)}, u32[]{:S(2)}) %collective-permute-start.28) | collective-permute-done | bytes 16416 | tf_op jit(solution)/shard_map/ppermute | solution.py:425
  74.5 2.5 %collective-permute-start.30 = (f32[8,512]{1,0:T(8,128)S(1)}, f32[8,512]{1,0:T(8,128)S(1)}, u32[]{:S(2)}, u32[]{:S(2)}) collective-permute-start(f32[8,512]{1,0:T(8,128)S(1)} %add.103.sums_two_ref.refs_3_), channel_id=1, source_target_pairs={{0,4},{1,5},{2,6},{3,7},{4,0},{5,1},{6,2},{7,3},{8,12},{9,13},{10,... | collective-permute-start | bytes 49160 | tf_op jit(solution)/shard_map/ppermute | solution.py:425
  77.0 2.2 %collective-permute-done.30.got_two_ref.refs_4_ = f32[8,512]{1,0:T(8,128)S(1)} collective-permute-done((f32[8,512]{1,0:T(8,128)S(1)}, f32[8,512]{1,0:T(8,128)S(1)}, u32[]{:S(2)}, u32[]{:S(2)}) %collective-permute-start.30) | collective-permute-done | bytes 16416 | tf_op jit(solution)/shard_map/ppermute | solution.py:425
  82.8 2.6 %collective-permute-done.32 = f32[8,512]{1,0:T(8,128)S(1)} collective-permute-done((f32[8,512]{1,0:T(8,128)S(1)}, f32[8,512]{1,0:T(8,128)S(1)}, u32[]{:S(2)}, u32[]{:S(2)}) %collective-permute-start.32) | collective-permute-done | bytes 16416 | tf_op jit(solution)/shard_map/ppermute | solution.py:425
  86.3 2.9 %collective-permute-done.33 = f32[8,512]{1,0:T(8,128)S(1)} collective-permute-done((f32[8,512]{1,0:T(8,128)S(1)}, f32[8,512]{1,0:T(8,128)S(1)}, u32[]{:S(2)}, u32[]{:S(2)}) %collective-permute-start.33) | collective-permute-done | bytes 16416 | tf_op jit(solution)/shard_map/ppermute | solution.py:425
  89.2 2.0 %collective-permute-start.34 = (f32[8,512]{1,0:T(8,128)S(1)}, f32[8,512]{1,0:T(8,128)S(1)}, u32[]{:S(2)}, u32[]{:S(2)}) collective-permute-start(f32[8,512]{1,0:T(8,128)S(1)} %add.106), channel_id=1, source_target_pairs={{0,2},{1,3},{2,0},{3,1},{4,6},{5,7},{6,4},{7,5},{8,10},{9,11},{10,... | collective-permute-start | bytes 49160 | tf_op jit(solution)/shard_map/ppermute | solution.py:425
  91.2 1.7 %collective-permute-done.34 = f32[8,512]{1,0:T(8,128)S(1)} collective-permute-done((f32[8,512]{1,0:T(8,128)S(1)}, f32[8,512]{1,0:T(8,128)S(1)}, u32[]{:S(2)}, u32[]{:S(2)}) %collective-permute-start.34) | collective-permute-done | bytes 16416 | tf_op jit(solution)/shard_map/ppermute | solution.py:425
  92.9 2.5 %collective-permute-start.36 = (f32[8,512]{1,0:T(8,128)S(1)}, f32[8,512]{1,0:T(8,128)S(1)}, u32[]{:S(2)}, u32[]{:S(2)}) collective-permute-start(f32[8,512]{1,0:T(8,128)S(1)} %add.107.refs_5_.refs_1_), channel_id=1, source_target_pairs={{0,4},{1,5},{2,6},{3,7},{4,0},{5,1},{6,2},{7,3},{8,12},{9,13},{10,... | collective-permute-start | bytes 49160 | tf_op jit(solution)/shard_map/ppermute | solution.py:425
  95.4 2.2 %collective-permute-done.36.refs_6_.refs_2_ = f32[8,512]{1,0:T(8,128)S(1)} collective-permute-done((f32[8,512]{1,0:T(8,128)S(1)}, f32[8,512]{1,0:T(8,128)S(1)}, u32[]{:S(2)}, u32[]{:S(2)}) %collective-permute-start.36) | collective-permute-done | bytes 16416 | tf_op jit(solution)/shard_map/ppermute | solution.py:425
  97.7 3.5 %shard_map.278 = (bf16[432,512]{1,0:T(8,128)(2,1)S(1)}, f32[432,512]{1,0:T(8,128)S(1)}, f32[8,512]{1,0:T(8,128)S(1)}, bf16[256,432]{1,0:T(8,128)(2,1)S(1)}, bf16[256,432]{1,0:T(8,128)(2,1)S(1)}) custom-call(s32[3]{0:T(128)S(1)} %pad_add_fusion.place_ref.refs_0_, f32[8,512]{1,0:T(8,128)S(1)} %add.99.refs_0_.sums_ref.refs_1_, ...), custom_call_target="tpu_custom_call" | custom-call | tf_op jit(solution)/shard_map/pallas_call | solution.py:409
  103.7 2.6 %collective-permute-done.38 = f32[8,512]{1,0:T(8,128)S(1)} collective-permute-done((f32[8,512]{1,0:T(8,128)S(1)}, f32[8,512]{1,0:T(8,128)S(1)}, u32[]{:S(2)}, u32[]{:S(2)}) %collective-permute-start.38) | collective-permute-done | bytes 16416 | tf_op jit(solution)/shard_map/ppermute | solution.py:425
  106.3 1.4 shard_map.279
  110.2 1.4 shard_map.280
  114.9 2.1 %collective-permute-start.41 = (f32[8,512]{1,0:T(8,128)S(1)}, f32[8,512]{1,0:T(8,128)S(1)}, u32[]{:S(2)}, u32[]{:S(2)}) collective-permute-start(f32[8,512]{1,0:T(8,128)S(1)} %add.110), channel_id=1, source_target_pairs={{0,2},{1,3},{2,0},{3,1},{4,6},{5,7},{6,4},{7,5},{8,10},{9,11},{10,... | collective-permute-start | bytes 49160 | tf_op jit(solution)/shard_map/ppermute | solution.py:425
  117.0 1.7 %collective-permute-done.41 = f32[8,512]{1,0:T(8,128)S(1)} collective-permute-done((f32[8,512]{1,0:T(8,128)S(1)}, f32[8,512]{1,0:T(8,128)S(1)}, u32[]{:S(2)}, u32[]{:S(2)}) %collective-permute-start.41) | collective-permute-done | bytes 16416 | tf_op jit(solution)/shard_map/ppermute | solution.py:425
  118.8 2.4 %collective-permute-start.43 = (f32[8,512]{1,0:T(8,128)S(1)}, f32[8,512]{1,0:T(8,128)S(1)}, u32[]{:S(2)}, u32[]{:S(2)}) collective-permute-start(f32[8,512]{1,0:T(8,128)S(1)} %add.111.refs_2_.refs_3_), channel_id=1, source_target_pairs={{0,4},{1,5},{2,6},{3,7},{4,0},{5,1},{6,2},{7,3},{8,12},{9,13},{10,... | collective-permute-start | bytes 49160 | tf_op jit(solution)/shard_map/ppermute | solution.py:425
  121.2 2.3 %collective-permute-done.43.refs_3_.refs_4_ = f32[8,512]{1,0:T(8,128)S(1)} collective-permute-done((f32[8,512]{1,0:T(8,128)S(1)}, f32[8,512]{1,0:T(8,128)S(1)}, u32[]{:S(2)}, u32[]{:S(2)}) %collective-permute-start.43) | collective-permute-done | bytes 16416 | tf_op jit(solution)/shard_map/ppermute | solution.py:425
  126.0 1.5 shard_map.283
  130.7 3.8 %collective-permute-done.57 = bf16[2,9,16,512]{3,2,1,0:T(8,128)(2,1)S(1)} collective-permute-done((bf16[2,9,16,512]{3,2,1,0:T(8,128)(2,1)S(1)}, bf16[2,9,16,512]{3,2,1,0:T(8,128)(2,1)S(1)}, u32[]{:S(2)}, u32[]{:S(2)}) %collective-permute-start.57) | collective-permute-done | bytes 294944 | tf_op jit(solution)/shard_map/ppermute | solution.py:425
  134.6 2.1 %collective-permute-start.58 = (bf16[9,16,512]{2,1,0:T(8,128)(2,1)S(1)}, bf16[9,16,512]{2,1,0:T(8,128)(2,1)S(1)}, u32[]{:S(2)}, u32[]{:S(2)}) collective-permute-start(bf16[9,16,512]{2,1,0:T(8,128)(2,1)S(1)} %slice_bitcast_fusion.4), channel_id=1, source_target_pairs={{0,2},{1,3},{2,0},{3,1},{4,6},{5,7},{6,4},{7,5},{8,10},{9,11},{10,... | collective-permute-start | bytes 442376 | tf_op jit(solution)/shard_map/ppermute | solution.py:425
  137.9 2.4 %collective-permute-start.60 = (bf16[9,16,512]{2,1,0:T(8,128)(2,1)S(1)}, bf16[9,16,512]{2,1,0:T(8,128)(2,1)S(1)}, u32[]{:S(2)}, u32[]{:S(2)}) collective-permute-start(bf16[9,16,512]{2,1,0:T(8,128)(2,1)S(1)} %get-tuple-element.173), channel_id=1, source_target_pairs={{0,4},{1,5},{2,6},{3,7},{4,0},{5,1},{6,2},{7,3},{8,12},{9,13},{10,... | collective-permute-start | bytes 442376 | tf_op jit(solution)/shard_map/ppermute | solution.py:425
  140.3 2.0 %collective-permute-start.61 = (bf16[9,16,512]{2,1,0:T(8,128)(2,1)S(1)}, bf16[9,16,512]{2,1,0:T(8,128)(2,1)S(1)}, u32[]{:S(2)}, u32[]{:S(2)}) collective-permute-start(bf16[9,16,512]{2,1,0:T(8,128)(2,1)S(1)} %get-tuple-element.174), channel_id=1, source_target_pairs={{0,6},{1,7},{2,4},{3,5},{4,2},{5,3},{6,0},{7,1},{8,14},{9,15},{10,... | collective-permute-start | bytes 442376 | tf_op jit(solution)/shard_map/ppermute | solution.py:425
  145.0 2.9 %shard_map.284 = (bf16[10,10,2,256]{3,2,1,0:T(2,128)(2,1)}, bf16[14,14,2,256]{3,2,1,0:T(2,128)(2,1)}, bf16[18,18,2,256]{3,2,1,0:T(2,128)(2,1)}, f32[1,64]{1,0:T(...) custom-call(s32[3]{0:T(128)S(1)} %pad_add_fusion.place_ref.refs_0_, ...), custom_call_target="tpu_custom_call" | custom-call | tf_op jit(solution)/shard_map/pallas_call | solution.py:409
  147.9 1.6 collective-permute-done.49
  149.5 2.1 %collective-permute-start.51 = (bf16[10,16,256]{2,1,0:T(8,128)(2,1)S(1)}, bf16[10,16,256]{2,1,0:T(8,128)(2,1)S(1)}, u32[]{:S(2)}, u32[]{:S(2)}) collective-permute-start(bf16[10,16,256]{2,1,0:T(8,128)(2,1)S(1)} %get-tuple-element.159), channel_id=1, source_target_pairs={{0,2},{1,3},{2,0},{3,1},{4,6},{5,7},{6,4},{7,5},{8,10},{9,11},{10,... | collective-permute-start | bytes 245768 | tf_op jit(solution)/shard_map/ppermute | solution.py:425
  152.1 1.9 %collective-permute-start.53 = (bf16[10,16,256]{2,1,0:T(8,128)(2,1)S(1)}, bf16[10,16,256]{2,1,0:T(8,128)(2,1)S(1)}, u32[]{:S(2)}, u32[]{:S(2)}) collective-permute-start(bf16[10,16,256]{2,1,0:T(8,128)(2,1)S(1)} %get-tuple-element.161), channel_id=1, source_target_pairs={{0,6},{1,7},{2,4},{3,5},{4,2},{5,3},{6,0},{7,1},{8,14},{9,15},{10,... | collective-permute-start | bytes 245768 | tf_op jit(solution)/shard_map/ppermute | solution.py:425
  156.2 1.5 collective-permute-start.62
  163.6 1.6 shard_map.286
  (148 shorter events, 50.5 us)
Async XLA Ops:
  2.4 8.8 %collective-permute-start.2 = (bf16[10,16,256]{2,1,0:T(8,128)(2,1)S(1)}, bf16[10,16,256]{2,1,0:T(8,128)(2,1)S(1)}, u32[]{:S(2)}, u32[]{:S(2)}) collective-permute-start(bf16[10,16,256]{2,1,0:T(8,128)(2,1)S(1)} %get-tuple-element.96), channel_id=1, source_target_pairs={{0,6},{1,7},{2,4},{3,5},{4,2},{5,3},{6,0},{7,1},{8,14},{9,15},{10,... | collective-permute-start | bytes 245768 | tf_op jit(solution)/shard_map/ppermute | solution.py:425
  7.5 6.9 %collective-permute-start.1 = (bf16[10,16,256]{2,1,0:T(8,128)(2,1)S(1)}, bf16[10,16,256]{2,1,0:T(8,128)(2,1)S(1)}, u32[]{:S(2)}, u32[]{:S(2)}) collective-permute-start(bf16[10,16,256]{2,1,0:T(8,128)(2,1)S(1)} %get-tuple-element.96), channel_id=1, source_target_pairs={{0,4},{1,5},{2,6},{3,7},{4,0},{5,1},{6,2},{7,3},{8,12},{9,13},{10,... | collective-permute-start | bytes 245768 | tf_op jit(solution)/shard_map/ppermute | solution.py:425
  7.5 6.9 %collective-permute-start = (bf16[10,16,256]{2,1,0:T(8,128)(2,1)S(1)}, bf16[10,16,256]{2,1,0:T(8,128)(2,1)S(1)}, u32[]{:S(2)}, u32[]{:S(2)}) collective-permute-start(bf16[10,16,256]{2,1,0:T(8,128)(2,1)S(1)} %get-tuple-element.96), channel_id=1, source_target_pairs={{0,2},{1,3},{2,0},{3,1},{4,6},{5,7},{6,4},{7,5},{8,10},{9,11},{10,... | collective-permute-start | bytes 245768 | tf_op jit(solution)/shard_map/ppermute | solution.py:425
  14.4 18.3 %collective-permute-start.5 = (bf16[4,10,16,256]{3,2,1,0:T(8,128)(2,1)S(1)}, bf16[4,10,16,256]{3,2,1,0:T(8,128)(2,1)S(1)}, u32[]{:S(2)}, u32[]{:S(2)}) collective-permute-start(bf16[4,10,16,256]{3,2,1,0:T(8,128)(2,1)S(1)} %pad_maximum_fusion.3.refs_0_), channel_id=1, source_target_pairs={{0,24},{8,16},{16,8},{24,0},{1,25},{9,17},{17,9},{25,1},{2,26},{10... | collective-permute-start | bytes 983048 | tf_op jit(solution)/shard_map/ppermute | solution.py:425
  16.9 15.8 %collective-permute-start.4 = (bf16[4,10,16,256]{3,2,1,0:T(8,128)(2,1)S(1)}, bf16[4,10,16,256]{3,2,1,0:T(8,128)(2,1)S(1)}, u32[]{:S(2)}, u32[]{:S(2)}) collective-permute-start(bf16[4,10,16,256]{3,2,1,0:T(8,128)(2,1)S(1)} %pad_maximum_fusion.3.refs_0_), channel_id=1, source_target_pairs={{0,16},{8,24},{16,0},{24,8},{1,17},{9,25},{17,1},{25,9},{2,18},{10... | collective-permute-start | bytes 983048 | tf_op jit(solution)/shard_map/ppermute | solution.py:425
  17.4 15.3 %collective-permute-start.3 = (bf16[4,10,16,256]{3,2,1,0:T(8,128)(2,1)S(1)}, bf16[4,10,16,256]{3,2,1,0:T(8,128)(2,1)S(1)}, u32[]{:S(2)}, u32[]{:S(2)}) collective-permute-start(bf16[4,10,16,256]{3,2,1,0:T(8,128)(2,1)S(1)} %pad_maximum_fusion.3.refs_0_), channel_id=1, source_target_pairs={{0,8},{8,0},{16,24},{24,16},{1,9},{9,1},{17,25},{25,17},{2,10},{10... | collective-permute-start | bytes 983048 | tf_op jit(solution)/shard_map/ppermute | solution.py:425
  17.9 13.0 %collective-permute-start.15 = (bf16[2,9,16,512]{3,2,1,0:T(8,128)(2,1)S(1)}, bf16[2,9,16,512]{3,2,1,0:T(8,128)(2,1)S(1)}, u32[]{:S(2)}, u32[]{:S(2)}) collective-permute-start(bf16[2,9,16,512]{3,2,1,0:T(8,128)(2,1)S(1)} %get-tuple-element.103), channel_id=1, source_target_pairs={{0,2},{1,3},{2,0},{3,1},{4,6},{5,7},{6,4},{7,5},{8,10},{9,11},{10,... | collective-permute-start | bytes 884744 | tf_op jit(solution)/shard_map/ppermute | solution.py:425
  18.8 13.9 %collective-permute-start.12 = (bf16[2,9,16,512]{3,2,1,0:T(8,128)(2,1)S(1)}, bf16[2,9,16,512]{3,2,1,0:T(8,128)(2,1)S(1)}, u32[]{:S(2)}, u32[]{:S(2)}) collective-permute-start(bf16[2,9,16,512]{3,2,1,0:T(8,128)(2,1)S(1)} %get-tuple-element.103), channel_id=1, source_target_pairs={{0,4},{1,5},{2,6},{3,7},{4,0},{5,1},{6,2},{7,3},{8,12},{9,13},{10,... | collective-permute-start | bytes 884744 | tf_op jit(solution)/shard_map/ppermute | solution.py:425
  32.7 11.7 %collective-permute-start.13 = (bf16[2,9,16,512]{3,2,1,0:T(8,128)(2,1)S(1)}, bf16[2,9,16,512]{3,2,1,0:T(8,128)(2,1)S(1)}, u32[]{:S(2)}, u32[]{:S(2)}) collective-permute-start(bf16[2,9,16,512]{3,2,1,0:T(8,128)(2,1)S(1)} %collective-permute-done.12), channel_id=1, source_target_pairs={{0,2},{1,3},{2,0},{3,1},{4,6},{5,7},{6,4},{7,5},{8,10},{9,11},{10,... | collective-permute-start | bytes 884744 | tf_op jit(solution)/shard_map/ppermute | solution.py:425
  32.8 3.8 %collective-permute-start.8 = (bf16[4,10,16,256]{3,2,1,0:T(8,128)(2,1)S(1)}, bf16[4,10,16,256]{3,2,1,0:T(8,128)(2,1)S(1)}, u32[]{:S(2)}, u32[]{:S(2)}) collective-permute-start(bf16[4,10,16,256]{3,2,1,0:T(8,128)(2,1)S(1)} %collective-permute-done.4.refs_2_), channel_id=1, source_target_pairs={{0,1},{1,0},{2,3},{3,2},{4,5},{5,4},{6,7},{7,6},{8,9},{9,8},{10,11... | collective-permute-start | bytes 983048 | tf_op jit(solution)/shard_map/ppermute | solution.py:425
  33.6 17.3 %collective-permute-start.17 = (bf16[3,9,16,512]{3,2,1,0:T(8,128)(2,1)S(1)}, bf16[3,9,16,512]{3,2,1,0:T(8,128)(2,1)S(1)}, u32[]{:S(2)}, u32[]{:S(2)}) collective-permute-start(bf16[3,9,16,512]{3,2,1,0:T(8,128)(2,1)S(1)} %get-tuple-element.171), channel_id=1, source_target_pairs={{0,16},{8,24},{16,0},{24,8},{1,17},{9,25},{17,1},{25,9},{2,18},{10... | collective-permute-start | bytes 1327112 | tf_op jit(solution)/shard_map/ppermute | solution.py:425
  35.2 15.7 %collective-permute-start.16 = (bf16[3,9,16,512]{3,2,1,0:T(8,128)(2,1)S(1)}, bf16[3,9,16,512]{3,2,1,0:T(8,128)(2,1)S(1)}, u32[]{:S(2)}, u32[]{:S(2)}) collective-permute-start(bf16[3,9,16,512]{3,2,1,0:T(8,128)(2,1)S(1)} %get-tuple-element.172), channel_id=1, source_target_pairs={{0,8},{8,0},{16,24},{24,16},{1,9},{9,1},{17,25},{25,17},{2,10},{10... | collective-permute-start | bytes 1327112 | tf_op jit(solution)/shard_map/ppermute | solution.py:425
  44.5 6.4 %collective-permute-start.19 = (bf16[9,16,512]{2,1,0:T(8,128)(2,1)S(1)}, bf16[9,16,512]{2,1,0:T(8,128)(2,1)S(1)}, u32[]{:S(2)}, u32[]{:S(2)}) collective-permute-start(bf16[9,16,512]{2,1,0:T(8,128)(2,1)S(1)} %get-tuple-element.175), channel_id=1, source_target_pairs={{0,16},{8,24},{16,0},{24,8},{1,17},{9,25},{17,1},{25,9},{2,18},{10... | collective-permute-start | bytes 442376 | tf_op jit(solution)/shard_map/ppermute | solution.py:425
  45.3 5.6 %collective-permute-start.18 = (bf16[9,16,512]{2,1,0:T(8,128)(2,1)S(1)}, bf16[9,16,512]{2,1,0:T(8,128)(2,1)S(1)}, u32[]{:S(2)}, u32[]{:S(2)}) collective-permute-start(bf16[9,16,512]{2,1,0:T(8,128)(2,1)S(1)} %get-tuple-element.176), channel_id=1, source_target_pairs={{0,8},{8,0},{16,24},{24,16},{1,9},{9,1},{17,25},{25,17},{2,10},{10... | collective-permute-start | bytes 442376 | tf_op jit(solution)/shard_map/ppermute | solution.py:425
  46.2 4.6 %collective-permute-start.14 = (f32[8,512]{1,0:T(8,128)S(1)}, f32[8,512]{1,0:T(8,128)S(1)}, u32[]{:S(2)}, u32[]{:S(2)}) collective-permute-start(f32[8,512]{1,0:T(8,128)S(1)} %add.97), channel_id=1, source_target_pairs={{0,4},{1,5},{2,6},{3,7},{4,0},{5,1},{6,2},{7,3},{8,12},{9,13},{10,... | collective-permute-start | bytes 49160 | tf_op jit(solution)/shard_map/ppermute | solution.py:425
  51.1 5.6 %collective-permute-start.22 = (bf16[2,4,9,16,512]{4,3,2,0,1:T(8,128)(2,1)S(1)}, bf16[2,4,9,16,512]{4,3,2,0,1:T(8,128)(2,1)S(1)}, u32[]{:S(2)}, u32[]{:S(2)}) collective-permute-start(bf16[2,4,9,16,512]{4,3,2,0,1:T(8,128)(2,1)S(1)} %pad_maximum_fusion), channel_id=1, source_target_pairs={{0,1},{1,0},{2,3},{3,2},{4,5},{5,4},{6,7},{7,6},{8,9},{9,8},{10,11... | collective-permute-start | bytes 3538952 | tf_op jit(solution)/shard_map/ppermute | solution.py:425
  51.3 5.5 %collective-permute-start.23 = (bf16[2,3,9,16,512]{4,3,2,1,0:T(8,128)(2,1)S(1)}, bf16[2,3,9,16,512]{4,3,2,1,0:T(8,128)(2,1)S(1)}, u32[]{:S(2)}, u32[]{:S(2)}) collective-permute-start(bf16[2,3,9,16,512]{4,3,2,1,0:T(8,128)(2,1)S(1)} %pad_maximum_fusion.2.refs_1_), channel_id=1, source_target_pairs={{0,1},{1,0},{2,3},{3,2},{4,5},{5,4},{6,7},{7,6},{8,9},{9,8},{10,11... | collective-permute-start | bytes 2654216 | tf_op jit(solution)/shard_map/ppermute | solution.py:425
  51.8 4.9 %collective-permute-start.24 = (bf16[2,9,16,512]{3,2,1,0:T(8,128)(2,1)S(1)}, bf16[2,9,16,512]{3,2,1,0:T(8,128)(2,1)S(1)}, u32[]{:S(2)}, u32[]{:S(2)}) collective-permute-start(bf16[2,9,16,512]{3,2,1,0:T(8,128)(2,1)S(1)} %pad_maximum_fusion.4.refs_2_), channel_id=1, source_target_pairs={{0,1},{1,0},{2,3},{3,2},{4,5},{5,4},{6,7},{7,6},{8,9},{9,8},{10,11... | collective-permute-start | bytes 884744 | tf_op jit(solution)/shard_map/ppermute | solution.py:425
  51.9 3.8 %collective-permute-start.20 = (f32[8,512]{1,0:T(8,128)S(1)}, f32[8,512]{1,0:T(8,128)S(1)}, u32[]{:S(2)}, u32[]{:S(2)}) collective-permute-start(f32[8,512]{1,0:T(8,128)S(1)} %add.98), channel_id=1, source_target_pairs={{0,8},{8,0},{16,24},{24,16},{1,9},{9,1},{17,25},{25,17},{2,10},{10... | collective-permute-start | bytes 49160 | tf_op jit(solution)/shard_map/ppermute | solution.py:425
  63.1 11.4 %collective-permute-start.29 = (bf16[432,4608]{1,0:T(8,128)(2,1)S(1)}, bf16[432,4608]{1,0:T(8,128)(2,1)S(1)}, u32[]{:S(2)}, u32[]{:S(2)}) collective-permute-start(bf16[432,4608]{1,0:T(8,128)(2,1)S(1)} %get-tuple-element.115.patches_ref), channel_id=1, source_target_pairs={{0,1},{1,0},{2,3},{3,2},{4,5},{5,4},{6,7},{7,6},{8,9},{9,8},{10,11... | collective-permute-start | bytes 11943944 | tf_op jit(solution)/shard_map/ppermute | solution.py:425
  74.5 4.7 %collective-permute-start.30 = (f32[8,512]{1,0:T(8,128)S(1)}, f32[8,512]{1,0:T(8,128)S(1)}, u32[]{:S(2)}, u32[]{:S(2)}) collective-permute-start(f32[8,512]{1,0:T(8,128)S(1)} %add.103.sums_two_ref.refs_3_), channel_id=1, source_target_pairs={{0,4},{1,5},{2,6},{3,7},{4,0},{5,1},{6,2},{7,3},{8,12},{9,13},{10,... | collective-permute-start | bytes 49160 | tf_op jit(solution)/shard_map/ppermute | solution.py:425
  81.5 11.4 %collective-permute-start.35 = (bf16[432,2304]{1,0:T(8,128)(2,1)S(1)}, bf16[432,2304]{1,0:T(8,128)(2,1)S(1)}, u32[]{:S(2)}, u32[]{:S(2)}) collective-permute-start(bf16[432,2304]{1,0:T(8,128)(2,1)S(1)} %get-tuple-element.124.refs_0_.patches_ref), channel_id=1, source_target_pairs={{0,1},{1,0},{2,3},{3,2},{4,5},{5,4},{6,7},{7,6},{8,9},{9,8},{10,11... | collective-permute-start | bytes 5971976 | tf_op jit(solution)/shard_map/ppermute | solution.py:425
  89.2 3.7 %collective-permute-start.34 = (f32[8,512]{1,0:T(8,128)S(1)}, f32[8,512]{1,0:T(8,128)S(1)}, u32[]{:S(2)}, u32[]{:S(2)}) collective-permute-start(f32[8,512]{1,0:T(8,128)S(1)} %add.106), channel_id=1, source_target_pairs={{0,2},{1,3},{2,0},{3,1},{4,6},{5,7},{6,4},{7,5},{8,10},{9,11},{10,... | collective-permute-start | bytes 49160 | tf_op jit(solution)/shard_map/ppermute | solution.py:425
  92.9 4.7 %collective-permute-start.36 = (f32[8,512]{1,0:T(8,128)S(1)}, f32[8,512]{1,0:T(8,128)S(1)}, u32[]{:S(2)}, u32[]{:S(2)}) collective-permute-start(f32[8,512]{1,0:T(8,128)S(1)} %add.107.refs_5_.refs_1_), channel_id=1, source_target_pairs={{0,4},{1,5},{2,6},{3,7},{4,0},{5,1},{6,2},{7,3},{8,12},{9,13},{10,... | collective-permute-start | bytes 49160 | tf_op jit(solution)/shard_map/ppermute | solution.py:425
  102.4 3.9 %collective-permute-start.39 = (bf16[256,432]{1,0:T(8,128)(2,1)S(1)}, bf16[256,432]{1,0:T(8,128)(2,1)S(1)}, u32[]{:S(2)}, u32[]{:S(2)}) collective-permute-start(bf16[256,432]{1,0:T(8,128)(2,1)S(1)} %get-tuple-element.131), channel_id=1, source_target_pairs={{0,1},{1,0},{2,3},{3,2},{4,5},{5,4},{6,7},{7,6},{8,9},{9,8},{10,11... | collective-permute-start | bytes 663560 | tf_op jit(solution)/shard_map/ppermute | solution.py:425
  107.8 16.8 %collective-permute-start.44 = (bf16[4,9,16,512]{3,2,1,0:T(8,128)(2,1)S(1)}, bf16[4,9,16,512]{3,2,1,0:T(8,128)(2,1)S(1)}, u32[]{:S(2)}, u32[]{:S(2)}) collective-permute-start(bf16[4,9,16,512]{3,2,1,0:T(8,128)(2,1)S(1)} %slice.89), channel_id=1, source_target_pairs={{0,8},{8,0},{16,24},{24,16},{1,9},{9,1},{17,25},{25,17},{2,10},{10... | collective-permute-start | bytes 1769480 | tf_op jit(solution)/shard_map/ppermute | solution.py:425
  112.8 14.8 %collective-permute-start.46 = (bf16[4,9,16,512]{3,2,1,0:T(8,128)(2,1)S(1)}, bf16[4,9,16,512]{3,2,1,0:T(8,128)(2,1)S(1)}, u32[]{:S(2)}, u32[]{:S(2)}) collective-permute-start(bf16[4,9,16,512]{3,2,1,0:T(8,128)(2,1)S(1)} %slice.91), channel_id=1, source_target_pairs={{0,16},{8,24},{16,0},{24,8},{1,17},{9,25},{17,1},{25,9},{2,18},{10... | collective-permute-start | bytes 1769480 | tf_op jit(solution)/shard_map/ppermute | solution.py:425
  114.8 3.9 %collective-permute-start.42 = (bf16[256,432]{1,0:T(8,128)(2,1)S(1)}, bf16[256,432]{1,0:T(8,128)(2,1)S(1)}, u32[]{:S(2)}, u32[]{:S(2)}) collective-permute-start(bf16[256,432]{1,0:T(8,128)(2,1)S(1)} %get-tuple-element.139), channel_id=1, source_target_pairs={{0,1},{1,0},{2,3},{3,2},{4,5},{5,4},{6,7},{7,6},{8,9},{9,8},{10,11... | collective-permute-start | bytes 663560 | tf_op jit(solution)/shard_map/ppermute | solution.py:425
  114.9 3.9 %collective-permute-start.41 = (f32[8,512]{1,0:T(8,128)S(1)}, f32[8,512]{1,0:T(8,128)S(1)}, u32[]{:S(2)}, u32[]{:S(2)}) collective-permute-start(f32[8,512]{1,0:T(8,128)S(1)} %add.110), channel_id=1, source_target_pairs={{0,2},{1,3},{2,0},{3,1},{4,6},{5,7},{6,4},{7,5},{8,10},{9,11},{10,... | collective-permute-start | bytes 49160 | tf_op jit(solution)/shard_map/ppermute | solution.py:425
  118.8 4.7 %collective-permute-start.43 = (f32[8,512]{1,0:T(8,128)S(1)}, f32[8,512]{1,0:T(8,128)S(1)}, u32[]{:S(2)}, u32[]{:S(2)}) collective-permute-start(f32[8,512]{1,0:T(8,128)S(1)} %add.111.refs_2_.refs_3_), channel_id=1, source_target_pairs={{0,4},{1,5},{2,6},{3,7},{4,0},{5,1},{6,2},{7,3},{8,12},{9,13},{10,... | collective-permute-start | bytes 49160 | tf_op jit(solution)/shard_map/ppermute | solution.py:425
  124.6 9.9 %collective-permute-start.57 = (bf16[2,9,16,512]{3,2,1,0:T(8,128)(2,1)S(1)}, bf16[2,9,16,512]{3,2,1,0:T(8,128)(2,1)S(1)}, u32[]{:S(2)}, u32[]{:S(2)}) collective-permute-start(bf16[2,9,16,512]{3,2,1,0:T(8,128)(2,1)S(1)} %slice.105), channel_id=1, source_target_pairs={{0,16},{8,24},{16,0},{24,8},{1,17},{9,25},{17,1},{25,9},{2,18},{10... | collective-permute-start | bytes 884744 | tf_op jit(solution)/shard_map/ppermute | solution.py:425
  127.7 9.9 %collective-permute-start.59 = (bf16[2,9,16,512]{3,2,1,0:T(8,128)(2,1)S(1)}, bf16[2,9,16,512]{3,2,1,0:T(8,128)(2,1)S(1)}, u32[]{:S(2)}, u32[]{:S(2)}) collective-permute-start(bf16[2,9,16,512]{3,2,1,0:T(8,128)(2,1)S(1)} %slice.109), channel_id=1, source_target_pairs={{0,8},{8,0},{16,24},{24,16},{1,9},{9,1},{17,25},{25,17},{2,10},{10... | collective-permute-start | bytes 884744 | tf_op jit(solution)/shard_map/ppermute | solution.py:425
  128.3 14.0 %collective-permute-start.48 = (bf16[4,10,16,256]{3,2,1,0:T(8,128)(2,1)S(1)}, bf16[4,10,16,256]{3,2,1,0:T(8,128)(2,1)S(1)}, u32[]{:S(2)}, u32[]{:S(2)}) collective-permute-start(bf16[4,10,16,256]{3,2,1,0:T(8,128)(2,1)S(1)} %slice.95), channel_id=1, source_target_pairs={{0,16},{8,24},{16,0},{24,8},{1,17},{9,25},{17,1},{25,9},{2,18},{10... | collective-permute-start | bytes 983048 | tf_op jit(solution)/shard_map/ppermute | solution.py:425
  129.6 14.5 %collective-permute-start.47 = (bf16[4,10,16,256]{3,2,1,0:T(8,128)(2,1)S(1)}, bf16[4,10,16,256]{3,2,1,0:T(8,128)(2,1)S(1)}, u32[]{:S(2)}, u32[]{:S(2)}) collective-permute-start(bf16[4,10,16,256]{3,2,1,0:T(8,128)(2,1)S(1)} %slice.93), channel_id=1, source_target_pairs={{0,8},{8,0},{16,24},{24,16},{1,9},{9,1},{17,25},{25,17},{2,10},{10... | collective-permute-start | bytes 983048 | tf_op jit(solution)/shard_map/ppermute | solution.py:425
  134.6 17.6 %collective-permute-start.58 = (bf16[9,16,512]{2,1,0:T(8,128)(2,1)S(1)}, bf16[9,16,512]{2,1,0:T(8,128)(2,1)S(1)}, u32[]{:S(2)}, u32[]{:S(2)}) collective-permute-start(bf16[9,16,512]{2,1,0:T(8,128)(2,1)S(1)} %slice_bitcast_fusion.4), channel_id=1, source_target_pairs={{0,2},{1,3},{2,0},{3,1},{4,6},{5,7},{6,4},{7,5},{8,10},{9,11},{10,... | collective-permute-start | bytes 442376 | tf_op jit(solution)/shard_map/ppermute | solution.py:425
  137.9 16.1 %collective-permute-start.60 = (bf16[9,16,512]{2,1,0:T(8,128)(2,1)S(1)}, bf16[9,16,512]{2,1,0:T(8,128)(2,1)S(1)}, u32[]{:S(2)}, u32[]{:S(2)}) collective-permute-start(bf16[9,16,512]{2,1,0:T(8,128)(2,1)S(1)} %get-tuple-element.173), channel_id=1, source_target_pairs={{0,4},{1,5},{2,6},{3,7},{4,0},{5,1},{6,2},{7,3},{8,12},{9,13},{10,... | collective-permute-start | bytes 442376 | tf_op jit(solution)/shard_map/ppermute | solution.py:425
  140.3 13.7 %collective-permute-start.61 = (bf16[9,16,512]{2,1,0:T(8,128)(2,1)S(1)}, bf16[9,16,512]{2,1,0:T(8,128)(2,1)S(1)}, u32[]{:S(2)}, u32[]{:S(2)}) collective-permute-start(bf16[9,16,512]{2,1,0:T(8,128)(2,1)S(1)} %get-tuple-element.174), channel_id=1, source_target_pairs={{0,6},{1,7},{2,4},{3,5},{4,2},{5,3},{6,0},{7,1},{8,14},{9,15},{10,... | collective-permute-start | bytes 442376 | tf_op jit(solution)/shard_map/ppermute | solution.py:425
  142.4 5.4 %collective-permute-start.50 = (bf16[2,10,16,256]{3,2,1,0:T(8,128)(2,1)S(1)}, bf16[2,10,16,256]{3,2,1,0:T(8,128)(2,1)S(1)}, u32[]{:S(2)}, u32[]{:S(2)}) collective-permute-start(bf16[2,10,16,256]{3,2,1,0:T(8,128)(2,1)S(1)} %slice.119), channel_id=1, source_target_pairs={{0,8},{8,0},{16,24},{24,16},{1,9},{9,1},{17,25},{25,17},{2,10},{10... | collective-permute-start | bytes 491528 | tf_op jit(solution)/shard_map/ppermute | solution.py:425
  144.1 5.4 %collective-permute-start.49 = (bf16[2,10,16,256]{3,2,1,0:T(8,128)(2,1)S(1)}, bf16[2,10,16,256]{3,2,1,0:T(8,128)(2,1)S(1)}, u32[]{:S(2)}, u32[]{:S(2)}) collective-permute-start(bf16[2,10,16,256]{3,2,1,0:T(8,128)(2,1)S(1)} %slice.115), channel_id=1, source_target_pairs={{0,16},{8,24},{16,0},{24,8},{1,17},{9,25},{17,1},{25,9},{2,18},{10... | collective-permute-start | bytes 491528 | tf_op jit(solution)/shard_map/ppermute | solution.py:425
  149.5 6.7 %collective-permute-start.51 = (bf16[10,16,256]{2,1,0:T(8,128)(2,1)S(1)}, bf16[10,16,256]{2,1,0:T(8,128)(2,1)S(1)}, u32[]{:S(2)}, u32[]{:S(2)}) collective-permute-start(bf16[10,16,256]{2,1,0:T(8,128)(2,1)S(1)} %get-tuple-element.159), channel_id=1, source_target_pairs={{0,2},{1,3},{2,0},{3,1},{4,6},{5,7},{6,4},{7,5},{8,10},{9,11},{10,... | collective-permute-start | bytes 245768 | tf_op jit(solution)/shard_map/ppermute | solution.py:425
  151.6 7.4 %collective-permute-start.52 = (bf16[10,16,256]{2,1,0:T(8,128)(2,1)S(1)}, bf16[10,16,256]{2,1,0:T(8,128)(2,1)S(1)}, u32[]{:S(2)}, u32[]{:S(2)}) collective-permute-start(bf16[10,16,256]{2,1,0:T(8,128)(2,1)S(1)} %get-tuple-element.160), channel_id=1, source_target_pairs={{0,4},{1,5},{2,6},{3,7},{4,0},{5,1},{6,2},{7,3},{8,12},{9,13},{10,... | collective-permute-start | bytes 245768 | tf_op jit(solution)/shard_map/ppermute | solution.py:425
  152.1 6.8 %collective-permute-start.53 = (bf16[10,16,256]{2,1,0:T(8,128)(2,1)S(1)}, bf16[10,16,256]{2,1,0:T(8,128)(2,1)S(1)}, u32[]{:S(2)}, u32[]{:S(2)}) collective-permute-start(bf16[10,16,256]{2,1,0:T(8,128)(2,1)S(1)} %get-tuple-element.161), channel_id=1, source_target_pairs={{0,6},{1,7},{2,4},{3,5},{4,2},{5,3},{6,0},{7,1},{8,14},{9,15},{10,... | collective-permute-start | bytes 245768 | tf_op jit(solution)/shard_map/ppermute | solution.py:425
  154.1 7.4 %collective-permute-start.64 = (bf16[9,16,512]{2,1,0:T(8,128)(2,1)S(1)}, bf16[9,16,512]{2,1,0:T(8,128)(2,1)S(1)}, u32[]{:S(2)}, u32[]{:S(2)}) collective-permute-start(bf16[9,16,512]{2,1,0:T(8,128)(2,1)S(1)} %fusion.2.refs_0_), channel_id=1, source_target_pairs={{0,24},{8,16},{16,8},{24,0},{1,25},{9,17},{17,9},{25,1},{2,26},{10... | collective-permute-start | bytes 442376 | tf_op jit(solution)/shard_map/ppermute | solution.py:425
  155.3 8.3 %collective-permute-start.63 = (bf16[9,16,512]{2,1,0:T(8,128)(2,1)S(1)}, bf16[9,16,512]{2,1,0:T(8,128)(2,1)S(1)}, u32[]{:S(2)}, u32[]{:S(2)}) collective-permute-start(bf16[9,16,512]{2,1,0:T(8,128)(2,1)S(1)} %fusion.2.refs_0_), channel_id=1, source_target_pairs={{0,16},{8,24},{16,0},{24,8},{1,17},{9,25},{17,1},{25,9},{2,18},{10... | collective-permute-start | bytes 442376 | tf_op jit(solution)/shard_map/ppermute | solution.py:425
  156.2 7.4 %collective-permute-start.62 = (bf16[9,16,512]{2,1,0:T(8,128)(2,1)S(1)}, bf16[9,16,512]{2,1,0:T(8,128)(2,1)S(1)}, u32[]{:S(2)}, u32[]{:S(2)}) collective-permute-start(bf16[9,16,512]{2,1,0:T(8,128)(2,1)S(1)} %fusion.2.refs_0_), channel_id=1, source_target_pairs={{0,8},{8,0},{16,24},{24,16},{1,9},{9,1},{17,25},{25,17},{2,10},{10... | collective-permute-start | bytes 442376 | tf_op jit(solution)/shard_map/ppermute | solution.py:425
  159.0 6.2 %collective-permute-start.56 = (bf16[10,16,256]{2,1,0:T(8,128)(2,1)S(1)}, bf16[10,16,256]{2,1,0:T(8,128)(2,1)S(1)}, u32[]{:S(2)}, u32[]{:S(2)}) collective-permute-start(bf16[10,16,256]{2,1,0:T(8,128)(2,1)S(1)} %add_convert_fusion.refs_0_), channel_id=1, source_target_pairs={{0,24},{8,16},{16,8},{24,0},{1,25},{9,17},{17,9},{25,1},{2,26},{10... | collective-permute-start | bytes 245768 | tf_op jit(solution)/shard_map/ppermute | solution.py:425
  160.2 5.2 %collective-permute-start.55 = (bf16[10,16,256]{2,1,0:T(8,128)(2,1)S(1)}, bf16[10,16,256]{2,1,0:T(8,128)(2,1)S(1)}, u32[]{:S(2)}, u32[]{:S(2)}) collective-permute-start(bf16[10,16,256]{2,1,0:T(8,128)(2,1)S(1)} %add_convert_fusion.refs_0_), channel_id=1, source_target_pairs={{0,16},{8,24},{16,0},{24,8},{1,17},{9,25},{17,1},{25,9},{2,18},{10... | collective-permute-start | bytes 245768 | tf_op jit(solution)/shard_map/ppermute | solution.py:425
  161.6 4.4 %collective-permute-start.54 = (bf16[10,16,256]{2,1,0:T(8,128)(2,1)S(1)}, bf16[10,16,256]{2,1,0:T(8,128)(2,1)S(1)}, u32[]{:S(2)}, u32[]{:S(2)}) collective-permute-start(bf16[10,16,256]{2,1,0:T(8,128)(2,1)S(1)} %add_convert_fusion.refs_0_), channel_id=1, source_target_pairs={{0,8},{8,0},{16,24},{24,16},{1,9},{9,1},{17,25},{25,17},{2,10},{10... | collective-permute-start | bytes 245768 | tf_op jit(solution)/shard_map/ppermute | solution.py:425
  (18 other events, 49.2 us)

commit v6 on v5

--- a/solution.py
+++ b/solution.py
@@ -76,7 +76,8 @@
 def put_rows(ref, rows):
     for index, row in enumerate(rows):
         ref[index : index + 1, :] = row
-    ref[len(rows) :, :] = jnp.zeros((ref.shape[0] - len(rows), ref.shape[1]), F32)
+    if len(rows) < ref.shape[0]:
+        ref[len(rows) :, :] = jnp.zeros((ref.shape[0] - len(rows), ref.shape[1]), F32)
 
 
 def offsets(plan, width):
@@ -315,7 +316,7 @@
     spot = lax.broadcasted_iota(jnp.int32, sums.shape, 1)
     sums = jnp.where((spot >= first) & (spot < first + owned), sums, 0.0)
     sums = sum(sums[:, begin : begin + owned] for begin in range(0, sums.shape[1], owned))
-    for row, ref in zip((8, 9, 1, 0, 2, 3), owns):
+    for row, ref in zip((4, 5, 1, 0, 2, 3), owns):
         ref[...] = sums[row : row + 1]
     rows = plan.rows
     fill(plan, held_ref, grad_ref[...].astype(F32))
@@ -680,7 +681,7 @@
     sums_two = sum_over(sums_two, everywhere, to_other_core(patches_two, other_two))
     *outputs, dz, sums_z = call(
         functools.partial(output_kernel, plan),
-        [shape((length, length, slots, cout), BF16) for length in plan.sides] + [shape((rows, cout)), shape((8, cout))],
+        [shape((length, length, slots, cout), BF16) for length in plan.sides] + [shape((rows, cout)), shape((4, cout))],
         *sums,
         *sums_two,
         second,
@@ -696,7 +697,7 @@
     results = call(
         functools.partial(back_second_share_kernel, plan, order) if fast else functools.partial(back_second_kernel, plan),
         ([] if fast else [shape((rows, cout), BF16)])
-        + [shape((rows, cout), BF16), shape((rows, cout)), shape((8, cout))]
+        + [shape((rows, cout), BF16), shape((rows, cout)), shape((4, cout))]
         + shared,
         *([place] if fast else []),
         *sums,

time: 168 us -> 167 us (level)
  no operation moved by 1% of the time
where the time goes in v6:
time: 167 us
  starting transfers between devices  71.7 us (43%)
  waiting for transfers between devices  63.8 us (38%)
  Pallas kernels  27.6 us (17%)
    ppermute x65, starting transfers between devices, exchange(): lax.ppermute(value, axis, [(index, index ^ bit) for index in range(count)])  71.7 us
    ppermute x65, waiting for transfers between devices, exchange(): lax.ppermute(value, axis, [(index, index ^ bit) for index in range(count)])  63.8 us
    pallas_call x16, Pallas kernels, call(): pl.pallas_call(body, in_specs=specs, out_specs=[vmem] * len(out_shapes) i...  27.6 us
  transfers between devices with their start and end apart: 65, of which 33 were waited for; matrix products, arithmetic and copies ran while one was open for 1% of the time, Pallas kernels for 10%

profile of v6, /device:TPU:0, one launch (start us, length us, event | category | flops | bytes accessed | tf_op | source)
XLA Modules:
  0.0 166.7 jit_solution(8998458734159403374)
XLA Ops:
  0.7 1.6 shard_map.272
  2.4 5.1 %collective-permute-start.2 = (bf16[10,16,256]{2,1,0:T(8,128)(2,1)S(1)}, bf16[10,16,256]{2,1,0:T(8,128)(2,1)S(1)}, u32[]{:S(2)}, u32[]{:S(2)}) collective-permute-start(bf16[10,16,256]{2,1,0:T(8,128)(2,1)S(1)} %get-tuple-element.96), channel_id=1, source_target_pairs={{0,6},{1,7},{2,4},{3,5},{4,2},{5,3},{6,0},{7,1},{8,14},{9,15},{10,... | collective-permute-start | bytes 245768 | tf_op jit(solution)/shard_map/ppermute | solution.py:426
  8.8 2.3 %shard_map.271 = (bf16[432,2304]{1,0:T(8,128)(2,1)S(1)}, f32[432,512]{1,0:T(8,128)S(1)}, f32[432,128]{1,0:T(8,128)S(1)}, f32[8,512]{1,0:T(8,128)S(1)}) custom-call(s32[3]{0:T(128)S(1)} %pad_add_fusion.place_ref.refs_0_, s32[1,3]{1,0:T(1,128)S(1)} %copy-done, bf16[10,10,2,256]{3,2,1,0:T(2,128)(2,1)} %bitcast.100, bf16[14,14,2,256]{3,2,1,0:T(2,128)(2,1)} %bitcast.96, ...), custom_call_target="tpu_custom_call" | custom-call | tf_op jit(solution)/shard_map/pallas_call | solution.py:410
  11.1 3.2 %collective-permute-done.1 = bf16[10,16,256]{2,1,0:T(8,128)(2,1)S(1)} collective-permute-done((bf16[10,16,256]{2,1,0:T(8,128)(2,1)S(1)}, bf16[10,16,256]{2,1,0:T(8,128)(2,1)S(1)}, u32[]{:S(2)}, u32[]{:S(2)}) %collective-permute-start.1) | collective-permute-done | bytes 81952 | tf_op jit(solution)/shard_map/ppermute | solution.py:426
  14.4 2.5 %collective-permute-start.5 = (bf16[4,10,16,256]{3,2,1,0:T(8,128)(2,1)S(1)}, bf16[4,10,16,256]{3,2,1,0:T(8,128)(2,1)S(1)}, u32[]{:S(2)}, u32[]{:S(2)}) collective-permute-start(bf16[4,10,16,256]{3,2,1,0:T(8,128)(2,1)S(1)} %pad_maximum_fusion.3.refs_0_), channel_id=1, source_target_pairs={{0,24},{8,16},{16,8},{24,0},{1,25},{9,17},{17,9},{25,1},{2,26},{10... | collective-permute-start | bytes 983048 | tf_op jit(solution)/shard_map/ppermute | solution.py:426
  18.8 2.4 %collective-permute-start.12 = (bf16[2,9,16,512]{3,2,1,0:T(8,128)(2,1)S(1)}, bf16[2,9,16,512]{3,2,1,0:T(8,128)(2,1)S(1)}, u32[]{:S(2)}, u32[]{:S(2)}) collective-permute-start(bf16[2,9,16,512]{3,2,1,0:T(8,128)(2,1)S(1)} %get-tuple-element.103), channel_id=1, source_target_pairs={{0,4},{1,5},{2,6},{3,7},{4,0},{5,1},{6,2},{7,3},{8,12},{9,13},{10,... | collective-permute-start | bytes 884744 | tf_op jit(solution)/shard_map/ppermute | solution.py:426
  21.2 9.8 %collective-permute-done.15 = bf16[2,9,16,512]{3,2,1,0:T(8,128)(2,1)S(1)} collective-permute-done((bf16[2,9,16,512]{3,2,1,0:T(8,128)(2,1)S(1)}, bf16[2,9,16,512]{3,2,1,0:T(8,128)(2,1)S(1)}, u32[]{:S(2)}, u32[]{:S(2)}) %collective-permute-start.15) | collective-permute-done | bytes 294944 | tf_op jit(solution)/shard_map/ppermute | solution.py:426
  31.0 1.8 %collective-permute-done.12 = bf16[2,9,16,512]{3,2,1,0:T(8,128)(2,1)S(1)} collective-permute-done((bf16[2,9,16,512]{3,2,1,0:T(8,128)(2,1)S(1)}, bf16[2,9,16,512]{3,2,1,0:T(8,128)(2,1)S(1)}, u32[]{:S(2)}, u32[]{:S(2)}) %collective-permute-start.12) | collective-permute-done | bytes 294944 | tf_op jit(solution)/shard_map/ppermute | solution.py:426
  33.6 1.6 collective-permute-start.17
  35.2 1.5 collective-permute-start.16
  40.7 2.0 %collective-permute-start.11 = (f32[8,512]{1,0:T(8,128)S(1)}, f32[8,512]{1,0:T(8,128)S(1)}, u32[]{:S(2)}, u32[]{:S(2)}) collective-permute-start(f32[8,512]{1,0:T(8,128)S(1)} %add.96), channel_id=1, source_target_pairs={{0,2},{1,3},{2,0},{3,1},{4,6},{5,7},{6,4},{7,5},{8,10},{9,11},{10,... | collective-permute-start | bytes 49160 | tf_op jit(solution)/shard_map/ppermute | solution.py:426
  42.7 1.7 %collective-permute-done.11 = f32[8,512]{1,0:T(8,128)S(1)} collective-permute-done((f32[8,512]{1,0:T(8,128)S(1)}, f32[8,512]{1,0:T(8,128)S(1)}, u32[]{:S(2)}, u32[]{:S(2)}) %collective-permute-start.11) | collective-permute-done | bytes 16416 | tf_op jit(solution)/shard_map/ppermute | solution.py:426
  46.2 2.4 %collective-permute-start.14 = (f32[8,512]{1,0:T(8,128)S(1)}, f32[8,512]{1,0:T(8,128)S(1)}, u32[]{:S(2)}, u32[]{:S(2)}) collective-permute-start(f32[8,512]{1,0:T(8,128)S(1)} %add.97), channel_id=1, source_target_pairs={{0,4},{1,5},{2,6},{3,7},{4,0},{5,1},{6,2},{7,3},{8,12},{9,13},{10,... | collective-permute-start | bytes 49160 | tf_op jit(solution)/shard_map/ppermute | solution.py:426
  48.7 2.2 %collective-permute-done.14 = f32[8,512]{1,0:T(8,128)S(1)} collective-permute-done((f32[8,512]{1,0:T(8,128)S(1)}, f32[8,512]{1,0:T(8,128)S(1)}, u32[]{:S(2)}, u32[]{:S(2)}) %collective-permute-start.14) | collective-permute-done | bytes 16416 | tf_op jit(solution)/shard_map/ppermute | solution.py:426
  53.1 2.6 %collective-permute-done.20 = f32[8,512]{1,0:T(8,128)S(1)} collective-permute-done((f32[8,512]{1,0:T(8,128)S(1)}, f32[8,512]{1,0:T(8,128)S(1)}, u32[]{:S(2)}, u32[]{:S(2)}) %collective-permute-start.20) | collective-permute-done | bytes 16416 | tf_op jit(solution)/shard_map/ppermute | solution.py:426
  56.8 1.9 %shard_map.275.refs_5_.refs_12_ = bf16[9,512,512]{2,1,0:T(8,128)(2,1)S(1)} custom-call(s32[3]{0:T(128)S(1)} %pad_add_fusion.place_ref.refs_0_, bf16[2,4,9,16,512]{4,3,2,1,0:T(8,128)(2,1)S(1)} %copy.32.refs_0_, bf16[2,3,9,16,512]{4,3,2,1,0:T(8,128)(2,1)S(1)} %pad_maximum_fusion.2.refs_1_, bf16[2,9,16,512]{3,2,1,0:T(8,128)(2,1)S(1)} %pad_maximum_fusion.4.refs_2_, ...), custom_call_target="tpu_custom_call" | custom-call | tf_op jit(solution)/shard_map/pallas_call | solution.py:410
  59.5 2.4 %shard_map.276 = (f32[432,512]{1,0:T(8,128)S(1)}, bf16[432,4608]{1,0:T(8,128)(2,1)S(1)}, f32[8,512]{1,0:T(8,128)S(1)}) custom-call(f32[8,512]{1,0:T(8,128)S(1)} %add.99.refs_0_.sums_ref.refs_1_, f32[8,512]{1,0:T(8,128)S(1)} %collective-permute-done.21.refs_1_.got_ref.refs_2_, f32[432,512]{1,0:T(8,128)S(1)} %get-tuple-element.107.refs_2_.refs_7_.refs_4_, ...), custom_call_target="tpu_custom_call" | custom-call | tf_op jit(solution)/shard_map/pallas_call | solution.py:410
  64.5 2.6 %collective-permute-done.26 = f32[8,512]{1,0:T(8,128)S(1)} collective-permute-done((f32[8,512]{1,0:T(8,128)S(1)}, f32[8,512]{1,0:T(8,128)S(1)}, u32[]{:S(2)}, u32[]{:S(2)}) %collective-permute-start.26) | collective-permute-done | bytes 16416 | tf_op jit(solution)/shard_map/ppermute | solution.py:426
  67.9 2.9 %collective-permute-done.27 = f32[8,512]{1,0:T(8,128)S(1)} collective-permute-done((f32[8,512]{1,0:T(8,128)S(1)}, f32[8,512]{1,0:T(8,128)S(1)}, u32[]{:S(2)}, u32[]{:S(2)}) %collective-permute-start.27) | collective-permute-done | bytes 16416 | tf_op jit(solution)/shard_map/ppermute | solution.py:426
  70.8 2.0 %collective-permute-start.28 = (f32[8,512]{1,0:T(8,128)S(1)}, f32[8,512]{1,0:T(8,128)S(1)}, u32[]{:S(2)}, u32[]{:S(2)}) collective-permute-start(f32[8,512]{1,0:T(8,128)S(1)} %add.102), channel_id=1, source_target_pairs={{0,2},{1,3},{2,0},{3,1},{4,6},{5,7},{6,4},{7,5},{8,10},{9,11},{10,... | collective-permute-start | bytes 49160 | tf_op jit(solution)/shard_map/ppermute | solution.py:426
  72.8 1.7 %collective-permute-done.28 = f32[8,512]{1,0:T(8,128)S(1)} collective-permute-done((f32[8,512]{1,0:T(8,128)S(1)}, f32[8,512]{1,0:T(8,128)S(1)}, u32[]{:S(2)}, u32[]{:S(2)}) %collective-permute-start.28) | collective-permute-done | bytes 16416 | tf_op jit(solution)/shard_map/ppermute | solution.py:426
  74.5 2.5 %collective-permute-start.30 = (f32[8,512]{1,0:T(8,128)S(1)}, f32[8,512]{1,0:T(8,128)S(1)}, u32[]{:S(2)}, u32[]{:S(2)}) collective-permute-start(f32[8,512]{1,0:T(8,128)S(1)} %add.103.sums_two_ref.refs_3_), channel_id=1, source_target_pairs={{0,4},{1,5},{2,6},{3,7},{4,0},{5,1},{6,2},{7,3},{8,12},{9,13},{10,... | collective-permute-start | bytes 49160 | tf_op jit(solution)/shard_map/ppermute | solution.py:426
  77.0 2.2 %collective-permute-done.30.got_two_ref.refs_4_ = f32[8,512]{1,0:T(8,128)S(1)} collective-permute-done((f32[8,512]{1,0:T(8,128)S(1)}, f32[8,512]{1,0:T(8,128)S(1)}, u32[]{:S(2)}, u32[]{:S(2)}) %collective-permute-start.30) | collective-permute-done | bytes 16416 | tf_op jit(solution)/shard_map/ppermute | solution.py:426
  82.8 2.5 %collective-permute-done.32 = f32[4,512]{1,0:T(4,128)S(1)} collective-permute-done((f32[4,512]{1,0:T(4,128)S(1)}, f32[4,512]{1,0:T(4,128)S(1)}, u32[]{:S(2)}, u32[]{:S(2)}) %collective-permute-start.32) | collective-permute-done | bytes 8224 | tf_op jit(solution)/shard_map/ppermute | solution.py:426
  86.2 2.8 %collective-permute-done.33 = f32[4,512]{1,0:T(4,128)S(1)} collective-permute-done((f32[4,512]{1,0:T(4,128)S(1)}, f32[4,512]{1,0:T(4,128)S(1)}, u32[]{:S(2)}, u32[]{:S(2)}) %collective-permute-start.33) | collective-permute-done | bytes 8224 | tf_op jit(solution)/shard_map/ppermute | solution.py:426
  89.0 2.0 %collective-permute-start.34 = (f32[4,512]{1,0:T(4,128)S(1)}, f32[4,512]{1,0:T(4,128)S(1)}, u32[]{:S(2)}, u32[]{:S(2)}) collective-permute-start(f32[4,512]{1,0:T(4,128)S(1)} %add.106), channel_id=1, source_target_pairs={{0,2},{1,3},{2,0},{3,1},{4,6},{5,7},{6,4},{7,5},{8,10},{9,11},{10,... | collective-permute-start | bytes 24584 | tf_op jit(solution)/shard_map/ppermute | solution.py:426
  91.0 1.6 collective-permute-done.34
  92.7 2.5 %collective-permute-start.36 = (f32[4,512]{1,0:T(4,128)S(1)}, f32[4,512]{1,0:T(4,128)S(1)}, u32[]{:S(2)}, u32[]{:S(2)}) collective-permute-start(f32[4,512]{1,0:T(4,128)S(1)} %add.107.refs_5_.refs_1_), channel_id=1, source_target_pairs={{0,4},{1,5},{2,6},{3,7},{4,0},{5,1},{6,2},{7,3},{8,12},{9,13},{10,... | collective-permute-start | bytes 24584 | tf_op jit(solution)/shard_map/ppermute | solution.py:426
  95.2 2.1 %collective-permute-done.36.refs_6_.refs_2_ = f32[4,512]{1,0:T(4,128)S(1)} collective-permute-done((f32[4,512]{1,0:T(4,128)S(1)}, f32[4,512]{1,0:T(4,128)S(1)}, u32[]{:S(2)}, u32[]{:S(2)}) %collective-permute-start.36) | collective-permute-done | bytes 8224 | tf_op jit(solution)/shard_map/ppermute | solution.py:426
  97.3 3.5 %shard_map.278 = (bf16[432,512]{1,0:T(8,128)(2,1)S(1)}, f32[432,512]{1,0:T(8,128)S(1)}, f32[4,512]{1,0:T(4,128)S(1)}, bf16[256,432]{1,0:T(8,128)(2,1)S(1)}, bf16[256,432]{1,0:T(8,128)(2,1)S(1)}) custom-call(s32[3]{0:T(128)S(1)} %pad_add_fusion.place_ref.refs_0_, f32[8,512]{1,0:T(8,128)S(1)} %add.99.refs_0_.sums_ref.refs_1_, ...), custom_call_target="tpu_custom_call" | custom-call | tf_op jit(solution)/shard_map/pallas_call | solution.py:410
  103.3 2.5 %collective-permute-done.38 = f32[4,512]{1,0:T(4,128)S(1)} collective-permute-done((f32[4,512]{1,0:T(4,128)S(1)}, f32[4,512]{1,0:T(4,128)S(1)}, u32[]{:S(2)}, u32[]{:S(2)}) %collective-permute-start.38) | collective-permute-done | bytes 8224 | tf_op jit(solution)/shard_map/ppermute | solution.py:426
  105.8 1.4 shard_map.279
  109.7 1.4 shard_map.280
  114.3 2.1 %collective-permute-start.41 = (f32[4,512]{1,0:T(4,128)S(1)}, f32[4,512]{1,0:T(4,128)S(1)}, u32[]{:S(2)}, u32[]{:S(2)}) collective-permute-start(f32[4,512]{1,0:T(4,128)S(1)} %add.110), channel_id=1, source_target_pairs={{0,2},{1,3},{2,0},{3,1},{4,6},{5,7},{6,4},{7,5},{8,10},{9,11},{10,... | collective-permute-start | bytes 24584 | tf_op jit(solution)/shard_map/ppermute | solution.py:426
  116.4 1.6 collective-permute-done.41
  118.1 2.5 %collective-permute-start.43 = (f32[4,512]{1,0:T(4,128)S(1)}, f32[4,512]{1,0:T(4,128)S(1)}, u32[]{:S(2)}, u32[]{:S(2)}) collective-permute-start(f32[4,512]{1,0:T(4,128)S(1)} %add.111.refs_2_.refs_3_), channel_id=1, source_target_pairs={{0,4},{1,5},{2,6},{3,7},{4,0},{5,1},{6,2},{7,3},{8,12},{9,13},{10,... | collective-permute-start | bytes 24584 | tf_op jit(solution)/shard_map/ppermute | solution.py:426
  120.5 2.2 %collective-permute-done.43.refs_3_.refs_4_ = f32[4,512]{1,0:T(4,128)S(1)} collective-permute-done((f32[4,512]{1,0:T(4,128)S(1)}, f32[4,512]{1,0:T(4,128)S(1)}, u32[]{:S(2)}, u32[]{:S(2)}) %collective-permute-start.43) | collective-permute-done | bytes 8224 | tf_op jit(solution)/shard_map/ppermute | solution.py:426
  125.3 1.5 shard_map.283
  130.0 3.7 %collective-permute-done.57 = bf16[2,9,16,512]{3,2,1,0:T(8,128)(2,1)S(1)} collective-permute-done((bf16[2,9,16,512]{3,2,1,0:T(8,128)(2,1)S(1)}, bf16[2,9,16,512]{3,2,1,0:T(8,128)(2,1)S(1)}, u32[]{:S(2)}, u32[]{:S(2)}) %collective-permute-start.57) | collective-permute-done | bytes 294944 | tf_op jit(solution)/shard_map/ppermute | solution.py:426
  133.8 2.1 %collective-permute-start.58 = (bf16[9,16,512]{2,1,0:T(8,128)(2,1)S(1)}, bf16[9,16,512]{2,1,0:T(8,128)(2,1)S(1)}, u32[]{:S(2)}, u32[]{:S(2)}) collective-permute-start(bf16[9,16,512]{2,1,0:T(8,128)(2,1)S(1)} %slice_bitcast_fusion.4), channel_id=1, source_target_pairs={{0,2},{1,3},{2,0},{3,1},{4,6},{5,7},{6,4},{7,5},{8,10},{9,11},{10,... | collective-permute-start | bytes 442376 | tf_op jit(solution)/shard_map/ppermute | solution.py:426
  137.1 2.5 %collective-permute-start.60 = (bf16[9,16,512]{2,1,0:T(8,128)(2,1)S(1)}, bf16[9,16,512]{2,1,0:T(8,128)(2,1)S(1)}, u32[]{:S(2)}, u32[]{:S(2)}) collective-permute-start(bf16[9,16,512]{2,1,0:T(8,128)(2,1)S(1)} %get-tuple-element.173), channel_id=1, source_target_pairs={{0,4},{1,5},{2,6},{3,7},{4,0},{5,1},{6,2},{7,3},{8,12},{9,13},{10,... | collective-permute-start | bytes 442376 | tf_op jit(solution)/shard_map/ppermute | solution.py:426
  139.6 2.0 %collective-permute-start.61 = (bf16[9,16,512]{2,1,0:T(8,128)(2,1)S(1)}, bf16[9,16,512]{2,1,0:T(8,128)(2,1)S(1)}, u32[]{:S(2)}, u32[]{:S(2)}) collective-permute-start(bf16[9,16,512]{2,1,0:T(8,128)(2,1)S(1)} %get-tuple-element.174), channel_id=1, source_target_pairs={{0,6},{1,7},{2,4},{3,5},{4,2},{5,3},{6,0},{7,1},{8,14},{9,15},{10,... | collective-permute-start | bytes 442376 | tf_op jit(solution)/shard_map/ppermute | solution.py:426
  144.2 2.9 %shard_map.284 = (bf16[10,10,2,256]{3,2,1,0:T(2,128)(2,1)}, bf16[14,14,2,256]{3,2,1,0:T(2,128)(2,1)}, bf16[18,18,2,256]{3,2,1,0:T(2,128)(2,1)}, f32[1,64]{1,0:T(...) custom-call(s32[3]{0:T(128)S(1)} %pad_add_fusion.place_ref.refs_0_, ...), custom_call_target="tpu_custom_call" | custom-call | tf_op jit(solution)/shard_map/pallas_call | solution.py:410
  147.2 1.5 collective-permute-done.49
  148.8 2.1 %collective-permute-start.51 = (bf16[10,16,256]{2,1,0:T(8,128)(2,1)S(1)}, bf16[10,16,256]{2,1,0:T(8,128)(2,1)S(1)}, u32[]{:S(2)}, u32[]{:S(2)}) collective-permute-start(bf16[10,16,256]{2,1,0:T(8,128)(2,1)S(1)} %get-tuple-element.159), channel_id=1, source_target_pairs={{0,2},{1,3},{2,0},{3,1},{4,6},{5,7},{6,4},{7,5},{8,10},{9,11},{10,... | collective-permute-start | bytes 245768 | tf_op jit(solution)/shard_map/ppermute | solution.py:426
  151.3 2.0 %collective-permute-start.53 = (bf16[10,16,256]{2,1,0:T(8,128)(2,1)S(1)}, bf16[10,16,256]{2,1,0:T(8,128)(2,1)S(1)}, u32[]{:S(2)}, u32[]{:S(2)}) collective-permute-start(bf16[10,16,256]{2,1,0:T(8,128)(2,1)S(1)} %get-tuple-element.161), channel_id=1, source_target_pairs={{0,6},{1,7},{2,4},{3,5},{4,2},{5,3},{6,0},{7,1},{8,14},{9,15},{10,... | collective-permute-start | bytes 245768 | tf_op jit(solution)/shard_map/ppermute | solution.py:426
  155.5 1.5 collective-permute-start.62
  162.8 1.6 shard_map.286
  (148 shorter events, 50.4 us)
Async XLA Ops:
  2.4 8.8 %collective-permute-start.2 = (bf16[10,16,256]{2,1,0:T(8,128)(2,1)S(1)}, bf16[10,16,256]{2,1,0:T(8,128)(2,1)S(1)}, u32[]{:S(2)}, u32[]{:S(2)}) collective-permute-start(bf16[10,16,256]{2,1,0:T(8,128)(2,1)S(1)} %get-tuple-element.96), channel_id=1, source_target_pairs={{0,6},{1,7},{2,4},{3,5},{4,2},{5,3},{6,0},{7,1},{8,14},{9,15},{10,... | collective-permute-start | bytes 245768 | tf_op jit(solution)/shard_map/ppermute | solution.py:426
  7.5 6.9 %collective-permute-start.1 = (bf16[10,16,256]{2,1,0:T(8,128)(2,1)S(1)}, bf16[10,16,256]{2,1,0:T(8,128)(2,1)S(1)}, u32[]{:S(2)}, u32[]{:S(2)}) collective-permute-start(bf16[10,16,256]{2,1,0:T(8,128)(2,1)S(1)} %get-tuple-element.96), channel_id=1, source_target_pairs={{0,4},{1,5},{2,6},{3,7},{4,0},{5,1},{6,2},{7,3},{8,12},{9,13},{10,... | collective-permute-start | bytes 245768 | tf_op jit(solution)/shard_map/ppermute | solution.py:426
  7.5 6.9 %collective-permute-start = (bf16[10,16,256]{2,1,0:T(8,128)(2,1)S(1)}, bf16[10,16,256]{2,1,0:T(8,128)(2,1)S(1)}, u32[]{:S(2)}, u32[]{:S(2)}) collective-permute-start(bf16[10,16,256]{2,1,0:T(8,128)(2,1)S(1)} %get-tuple-element.96), channel_id=1, source_target_pairs={{0,2},{1,3},{2,0},{3,1},{4,6},{5,7},{6,4},{7,5},{8,10},{9,11},{10,... | collective-permute-start | bytes 245768 | tf_op jit(solution)/shard_map/ppermute | solution.py:426
  14.4 18.3 %collective-permute-start.5 = (bf16[4,10,16,256]{3,2,1,0:T(8,128)(2,1)S(1)}, bf16[4,10,16,256]{3,2,1,0:T(8,128)(2,1)S(1)}, u32[]{:S(2)}, u32[]{:S(2)}) collective-permute-start(bf16[4,10,16,256]{3,2,1,0:T(8,128)(2,1)S(1)} %pad_maximum_fusion.3.refs_0_), channel_id=1, source_target_pairs={{0,24},{8,16},{16,8},{24,0},{1,25},{9,17},{17,9},{25,1},{2,26},{10... | collective-permute-start | bytes 983048 | tf_op jit(solution)/shard_map/ppermute | solution.py:426
  16.9 15.8 %collective-permute-start.4 = (bf16[4,10,16,256]{3,2,1,0:T(8,128)(2,1)S(1)}, bf16[4,10,16,256]{3,2,1,0:T(8,128)(2,1)S(1)}, u32[]{:S(2)}, u32[]{:S(2)}) collective-permute-start(bf16[4,10,16,256]{3,2,1,0:T(8,128)(2,1)S(1)} %pad_maximum_fusion.3.refs_0_), channel_id=1, source_target_pairs={{0,16},{8,24},{16,0},{24,8},{1,17},{9,25},{17,1},{25,9},{2,18},{10... | collective-permute-start | bytes 983048 | tf_op jit(solution)/shard_map/ppermute | solution.py:426
  17.4 15.3 %collective-permute-start.3 = (bf16[4,10,16,256]{3,2,1,0:T(8,128)(2,1)S(1)}, bf16[4,10,16,256]{3,2,1,0:T(8,128)(2,1)S(1)}, u32[]{:S(2)}, u32[]{:S(2)}) collective-permute-start(bf16[4,10,16,256]{3,2,1,0:T(8,128)(2,1)S(1)} %pad_maximum_fusion.3.refs_0_), channel_id=1, source_target_pairs={{0,8},{8,0},{16,24},{24,16},{1,9},{9,1},{17,25},{25,17},{2,10},{10... | collective-permute-start | bytes 983048 | tf_op jit(solution)/shard_map/ppermute | solution.py:426
  17.9 13.0 %collective-permute-start.15 = (bf16[2,9,16,512]{3,2,1,0:T(8,128)(2,1)S(1)}, bf16[2,9,16,512]{3,2,1,0:T(8,128)(2,1)S(1)}, u32[]{:S(2)}, u32[]{:S(2)}) collective-permute-start(bf16[2,9,16,512]{3,2,1,0:T(8,128)(2,1)S(1)} %get-tuple-element.103), channel_id=1, source_target_pairs={{0,2},{1,3},{2,0},{3,1},{4,6},{5,7},{6,4},{7,5},{8,10},{9,11},{10,... | collective-permute-start | bytes 884744 | tf_op jit(solution)/shard_map/ppermute | solution.py:426
  18.8 13.9 %collective-permute-start.12 = (bf16[2,9,16,512]{3,2,1,0:T(8,128)(2,1)S(1)}, bf16[2,9,16,512]{3,2,1,0:T(8,128)(2,1)S(1)}, u32[]{:S(2)}, u32[]{:S(2)}) collective-permute-start(bf16[2,9,16,512]{3,2,1,0:T(8,128)(2,1)S(1)} %get-tuple-element.103), channel_id=1, source_target_pairs={{0,4},{1,5},{2,6},{3,7},{4,0},{5,1},{6,2},{7,3},{8,12},{9,13},{10,... | collective-permute-start | bytes 884744 | tf_op jit(solution)/shard_map/ppermute | solution.py:426
  32.7 11.7 %collective-permute-start.13 = (bf16[2,9,16,512]{3,2,1,0:T(8,128)(2,1)S(1)}, bf16[2,9,16,512]{3,2,1,0:T(8,128)(2,1)S(1)}, u32[]{:S(2)}, u32[]{:S(2)}) collective-permute-start(bf16[2,9,16,512]{3,2,1,0:T(8,128)(2,1)S(1)} %collective-permute-done.12), channel_id=1, source_target_pairs={{0,2},{1,3},{2,0},{3,1},{4,6},{5,7},{6,4},{7,5},{8,10},{9,11},{10,... | collective-permute-start | bytes 884744 | tf_op jit(solution)/shard_map/ppermute | solution.py:426
  32.8 3.8 %collective-permute-start.8 = (bf16[4,10,16,256]{3,2,1,0:T(8,128)(2,1)S(1)}, bf16[4,10,16,256]{3,2,1,0:T(8,128)(2,1)S(1)}, u32[]{:S(2)}, u32[]{:S(2)}) collective-permute-start(bf16[4,10,16,256]{3,2,1,0:T(8,128)(2,1)S(1)} %collective-permute-done.4.refs_2_), channel_id=1, source_target_pairs={{0,1},{1,0},{2,3},{3,2},{4,5},{5,4},{6,7},{7,6},{8,9},{9,8},{10,11... | collective-permute-start | bytes 983048 | tf_op jit(solution)/shard_map/ppermute | solution.py:426
  33.6 17.3 %collective-permute-start.17 = (bf16[3,9,16,512]{3,2,1,0:T(8,128)(2,1)S(1)}, bf16[3,9,16,512]{3,2,1,0:T(8,128)(2,1)S(1)}, u32[]{:S(2)}, u32[]{:S(2)}) collective-permute-start(bf16[3,9,16,512]{3,2,1,0:T(8,128)(2,1)S(1)} %get-tuple-element.171), channel_id=1, source_target_pairs={{0,16},{8,24},{16,0},{24,8},{1,17},{9,25},{17,1},{25,9},{2,18},{10... | collective-permute-start | bytes 1327112 | tf_op jit(solution)/shard_map/ppermute | solution.py:426
  35.2 15.7 %collective-permute-start.16 = (bf16[3,9,16,512]{3,2,1,0:T(8,128)(2,1)S(1)}, bf16[3,9,16,512]{3,2,1,0:T(8,128)(2,1)S(1)}, u32[]{:S(2)}, u32[]{:S(2)}) collective-permute-start(bf16[3,9,16,512]{3,2,1,0:T(8,128)(2,1)S(1)} %get-tuple-element.172), channel_id=1, source_target_pairs={{0,8},{8,0},{16,24},{24,16},{1,9},{9,1},{17,25},{25,17},{2,10},{10... | collective-permute-start | bytes 1327112 | tf_op jit(solution)/shard_map/ppermute | solution.py:426
  44.5 6.4 %collective-permute-start.19 = (bf16[9,16,512]{2,1,0:T(8,128)(2,1)S(1)}, bf16[9,16,512]{2,1,0:T(8,128)(2,1)S(1)}, u32[]{:S(2)}, u32[]{:S(2)}) collective-permute-start(bf16[9,16,512]{2,1,0:T(8,128)(2,1)S(1)} %get-tuple-element.175), channel_id=1, source_target_pairs={{0,16},{8,24},{16,0},{24,8},{1,17},{9,25},{17,1},{25,9},{2,18},{10... | collective-permute-start | bytes 442376 | tf_op jit(solution)/shard_map/ppermute | solution.py:426
  45.3 5.6 %collective-permute-start.18 = (bf16[9,16,512]{2,1,0:T(8,128)(2,1)S(1)}, bf16[9,16,512]{2,1,0:T(8,128)(2,1)S(1)}, u32[]{:S(2)}, u32[]{:S(2)}) collective-permute-start(bf16[9,16,512]{2,1,0:T(8,128)(2,1)S(1)} %get-tuple-element.176), channel_id=1, source_target_pairs={{0,8},{8,0},{16,24},{24,16},{1,9},{9,1},{17,25},{25,17},{2,10},{10... | collective-permute-start | bytes 442376 | tf_op jit(solution)/shard_map/ppermute | solution.py:426
  46.2 4.6 %collective-permute-start.14 = (f32[8,512]{1,0:T(8,128)S(1)}, f32[8,512]{1,0:T(8,128)S(1)}, u32[]{:S(2)}, u32[]{:S(2)}) collective-permute-start(f32[8,512]{1,0:T(8,128)S(1)} %add.97), channel_id=1, source_target_pairs={{0,4},{1,5},{2,6},{3,7},{4,0},{5,1},{6,2},{7,3},{8,12},{9,13},{10,... | collective-permute-start | bytes 49160 | tf_op jit(solution)/shard_map/ppermute | solution.py:426
  51.1 5.6 %collective-permute-start.22 = (bf16[2,4,9,16,512]{4,3,2,0,1:T(8,128)(2,1)S(1)}, bf16[2,4,9,16,512]{4,3,2,0,1:T(8,128)(2,1)S(1)}, u32[]{:S(2)}, u32[]{:S(2)}) collective-permute-start(bf16[2,4,9,16,512]{4,3,2,0,1:T(8,128)(2,1)S(1)} %pad_maximum_fusion), channel_id=1, source_target_pairs={{0,1},{1,0},{2,3},{3,2},{4,5},{5,4},{6,7},{7,6},{8,9},{9,8},{10,11... | collective-permute-start | bytes 3538952 | tf_op jit(solution)/shard_map/ppermute | solution.py:426
  51.3 5.5 %collective-permute-start.23 = (bf16[2,3,9,16,512]{4,3,2,1,0:T(8,128)(2,1)S(1)}, bf16[2,3,9,16,512]{4,3,2,1,0:T(8,128)(2,1)S(1)}, u32[]{:S(2)}, u32[]{:S(2)}) collective-permute-start(bf16[2,3,9,16,512]{4,3,2,1,0:T(8,128)(2,1)S(1)} %pad_maximum_fusion.2.refs_1_), channel_id=1, source_target_pairs={{0,1},{1,0},{2,3},{3,2},{4,5},{5,4},{6,7},{7,6},{8,9},{9,8},{10,11... | collective-permute-start | bytes 2654216 | tf_op jit(solution)/shard_map/ppermute | solution.py:426
  51.8 4.9 %collective-permute-start.24 = (bf16[2,9,16,512]{3,2,1,0:T(8,128)(2,1)S(1)}, bf16[2,9,16,512]{3,2,1,0:T(8,128)(2,1)S(1)}, u32[]{:S(2)}, u32[]{:S(2)}) collective-permute-start(bf16[2,9,16,512]{3,2,1,0:T(8,128)(2,1)S(1)} %pad_maximum_fusion.4.refs_2_), channel_id=1, source_target_pairs={{0,1},{1,0},{2,3},{3,2},{4,5},{5,4},{6,7},{7,6},{8,9},{9,8},{10,11... | collective-permute-start | bytes 884744 | tf_op jit(solution)/shard_map/ppermute | solution.py:426
  51.9 3.8 %collective-permute-start.20 = (f32[8,512]{1,0:T(8,128)S(1)}, f32[8,512]{1,0:T(8,128)S(1)}, u32[]{:S(2)}, u32[]{:S(2)}) collective-permute-start(f32[8,512]{1,0:T(8,128)S(1)} %add.98), channel_id=1, source_target_pairs={{0,8},{8,0},{16,24},{24,16},{1,9},{9,1},{17,25},{25,17},{2,10},{10... | collective-permute-start | bytes 49160 | tf_op jit(solution)/shard_map/ppermute | solution.py:426
  55.7 3.7 %collective-permute-start.21 = (f32[8,512]{1,0:T(8,128)S(1)}, f32[8,512]{1,0:T(8,128)S(1)}, u32[]{:S(2)}, u32[]{:S(2)}) collective-permute-start(f32[8,512]{1,0:T(8,128)S(1)} %add.99.refs_0_.sums_ref.refs_1_), channel_id=1, source_target_pairs={{0,16},{8,24},{16,0},{24,8},{1,17},{9,25},{17,1},{25,9},{2,18},{10... | collective-permute-start | bytes 49160 | tf_op jit(solution)/shard_map/ppermute | solution.py:426
  63.1 11.4 %collective-permute-start.29 = (bf16[432,4608]{1,0:T(8,128)(2,1)S(1)}, bf16[432,4608]{1,0:T(8,128)(2,1)S(1)}, u32[]{:S(2)}, u32[]{:S(2)}) collective-permute-start(bf16[432,4608]{1,0:T(8,128)(2,1)S(1)} %get-tuple-element.115.patches_ref), channel_id=1, source_target_pairs={{0,1},{1,0},{2,3},{3,2},{4,5},{5,4},{6,7},{7,6},{8,9},{9,8},{10,11... | collective-permute-start | bytes 11943944 | tf_op jit(solution)/shard_map/ppermute | solution.py:426
  74.5 4.7 %collective-permute-start.30 = (f32[8,512]{1,0:T(8,128)S(1)}, f32[8,512]{1,0:T(8,128)S(1)}, u32[]{:S(2)}, u32[]{:S(2)}) collective-permute-start(f32[8,512]{1,0:T(8,128)S(1)} %add.103.sums_two_ref.refs_3_), channel_id=1, source_target_pairs={{0,4},{1,5},{2,6},{3,7},{4,0},{5,1},{6,2},{7,3},{8,12},{9,13},{10,... | collective-permute-start | bytes 49160 | tf_op jit(solution)/shard_map/ppermute | solution.py:426
  81.5 11.1 %collective-permute-start.35 = (bf16[432,2304]{1,0:T(8,128)(2,1)S(1)}, bf16[432,2304]{1,0:T(8,128)(2,1)S(1)}, u32[]{:S(2)}, u32[]{:S(2)}) collective-permute-start(bf16[432,2304]{1,0:T(8,128)(2,1)S(1)} %get-tuple-element.124.refs_0_.patches_ref), channel_id=1, source_target_pairs={{0,1},{1,0},{2,3},{3,2},{4,5},{5,4},{6,7},{7,6},{8,9},{9,8},{10,11... | collective-permute-start | bytes 5971976 | tf_op jit(solution)/shard_map/ppermute | solution.py:426
  92.7 4.6 %collective-permute-start.36 = (f32[4,512]{1,0:T(4,128)S(1)}, f32[4,512]{1,0:T(4,128)S(1)}, u32[]{:S(2)}, u32[]{:S(2)}) collective-permute-start(f32[4,512]{1,0:T(4,128)S(1)} %add.107.refs_5_.refs_1_), channel_id=1, source_target_pairs={{0,4},{1,5},{2,6},{3,7},{4,0},{5,1},{6,2},{7,3},{8,12},{9,13},{10,... | collective-permute-start | bytes 24584 | tf_op jit(solution)/shard_map/ppermute | solution.py:426
  102.0 3.8 %collective-permute-start.39 = (bf16[256,432]{1,0:T(8,128)(2,1)S(1)}, bf16[256,432]{1,0:T(8,128)(2,1)S(1)}, u32[]{:S(2)}, u32[]{:S(2)}) collective-permute-start(bf16[256,432]{1,0:T(8,128)(2,1)S(1)} %get-tuple-element.131), channel_id=1, source_target_pairs={{0,1},{1,0},{2,3},{3,2},{4,5},{5,4},{6,7},{7,6},{8,9},{9,8},{10,11... | collective-permute-start | bytes 663560 | tf_op jit(solution)/shard_map/ppermute | solution.py:426
  107.3 16.5 %collective-permute-start.44 = (bf16[4,9,16,512]{3,2,1,0:T(8,128)(2,1)S(1)}, bf16[4,9,16,512]{3,2,1,0:T(8,128)(2,1)S(1)}, u32[]{:S(2)}, u32[]{:S(2)}) collective-permute-start(bf16[4,9,16,512]{3,2,1,0:T(8,128)(2,1)S(1)} %slice.89), channel_id=1, source_target_pairs={{0,8},{8,0},{16,24},{24,16},{1,9},{9,1},{17,25},{25,17},{2,10},{10... | collective-permute-start | bytes 1769480 | tf_op jit(solution)/shard_map/ppermute | solution.py:426
  112.2 14.6 %collective-permute-start.46 = (bf16[4,9,16,512]{3,2,1,0:T(8,128)(2,1)S(1)}, bf16[4,9,16,512]{3,2,1,0:T(8,128)(2,1)S(1)}, u32[]{:S(2)}, u32[]{:S(2)}) collective-permute-start(bf16[4,9,16,512]{3,2,1,0:T(8,128)(2,1)S(1)} %slice.91), channel_id=1, source_target_pairs={{0,16},{8,24},{16,0},{24,8},{1,17},{9,25},{17,1},{25,9},{2,18},{10... | collective-permute-start | bytes 1769480 | tf_op jit(solution)/shard_map/ppermute | solution.py:426
  114.2 3.8 %collective-permute-start.42 = (bf16[256,432]{1,0:T(8,128)(2,1)S(1)}, bf16[256,432]{1,0:T(8,128)(2,1)S(1)}, u32[]{:S(2)}, u32[]{:S(2)}) collective-permute-start(bf16[256,432]{1,0:T(8,128)(2,1)S(1)} %get-tuple-element.139), channel_id=1, source_target_pairs={{0,1},{1,0},{2,3},{3,2},{4,5},{5,4},{6,7},{7,6},{8,9},{9,8},{10,11... | collective-permute-start | bytes 663560 | tf_op jit(solution)/shard_map/ppermute | solution.py:426
  114.3 3.8 %collective-permute-start.41 = (f32[4,512]{1,0:T(4,128)S(1)}, f32[4,512]{1,0:T(4,128)S(1)}, u32[]{:S(2)}, u32[]{:S(2)}) collective-permute-start(f32[4,512]{1,0:T(4,128)S(1)} %add.110), channel_id=1, source_target_pairs={{0,2},{1,3},{2,0},{3,1},{4,6},{5,7},{6,4},{7,5},{8,10},{9,11},{10,... | collective-permute-start | bytes 24584 | tf_op jit(solution)/shard_map/ppermute | solution.py:426
  118.1 4.6 %collective-permute-start.43 = (f32[4,512]{1,0:T(4,128)S(1)}, f32[4,512]{1,0:T(4,128)S(1)}, u32[]{:S(2)}, u32[]{:S(2)}) collective-permute-start(f32[4,512]{1,0:T(4,128)S(1)} %add.111.refs_2_.refs_3_), channel_id=1, source_target_pairs={{0,4},{1,5},{2,6},{3,7},{4,0},{5,1},{6,2},{7,3},{8,12},{9,13},{10,... | collective-permute-start | bytes 24584 | tf_op jit(solution)/shard_map/ppermute | solution.py:426
  123.9 9.9 %collective-permute-start.57 = (bf16[2,9,16,512]{3,2,1,0:T(8,128)(2,1)S(1)}, bf16[2,9,16,512]{3,2,1,0:T(8,128)(2,1)S(1)}, u32[]{:S(2)}, u32[]{:S(2)}) collective-permute-start(bf16[2,9,16,512]{3,2,1,0:T(8,128)(2,1)S(1)} %slice.105), channel_id=1, source_target_pairs={{0,16},{8,24},{16,0},{24,8},{1,17},{9,25},{17,1},{25,9},{2,18},{10... | collective-permute-start | bytes 884744 | tf_op jit(solution)/shard_map/ppermute | solution.py:426
  126.9 9.9 %collective-permute-start.59 = (bf16[2,9,16,512]{3,2,1,0:T(8,128)(2,1)S(1)}, bf16[2,9,16,512]{3,2,1,0:T(8,128)(2,1)S(1)}, u32[]{:S(2)}, u32[]{:S(2)}) collective-permute-start(bf16[2,9,16,512]{3,2,1,0:T(8,128)(2,1)S(1)} %slice.109), channel_id=1, source_target_pairs={{0,8},{8,0},{16,24},{24,16},{1,9},{9,1},{17,25},{25,17},{2,10},{10... | collective-permute-start | bytes 884744 | tf_op jit(solution)/shard_map/ppermute | solution.py:426
  127.6 14.0 %collective-permute-start.48 = (bf16[4,10,16,256]{3,2,1,0:T(8,128)(2,1)S(1)}, bf16[4,10,16,256]{3,2,1,0:T(8,128)(2,1)S(1)}, u32[]{:S(2)}, u32[]{:S(2)}) collective-permute-start(bf16[4,10,16,256]{3,2,1,0:T(8,128)(2,1)S(1)} %slice.95), channel_id=1, source_target_pairs={{0,16},{8,24},{16,0},{24,8},{1,17},{9,25},{17,1},{25,9},{2,18},{10... | collective-permute-start | bytes 983048 | tf_op jit(solution)/shard_map/ppermute | solution.py:426
  128.8 14.4 %collective-permute-start.47 = (bf16[4,10,16,256]{3,2,1,0:T(8,128)(2,1)S(1)}, bf16[4,10,16,256]{3,2,1,0:T(8,128)(2,1)S(1)}, u32[]{:S(2)}, u32[]{:S(2)}) collective-permute-start(bf16[4,10,16,256]{3,2,1,0:T(8,128)(2,1)S(1)} %slice.93), channel_id=1, source_target_pairs={{0,8},{8,0},{16,24},{24,16},{1,9},{9,1},{17,25},{25,17},{2,10},{10... | collective-permute-start | bytes 983048 | tf_op jit(solution)/shard_map/ppermute | solution.py:426
  133.8 17.5 %collective-permute-start.58 = (bf16[9,16,512]{2,1,0:T(8,128)(2,1)S(1)}, bf16[9,16,512]{2,1,0:T(8,128)(2,1)S(1)}, u32[]{:S(2)}, u32[]{:S(2)}) collective-permute-start(bf16[9,16,512]{2,1,0:T(8,128)(2,1)S(1)} %slice_bitcast_fusion.4), channel_id=1, source_target_pairs={{0,2},{1,3},{2,0},{3,1},{4,6},{5,7},{6,4},{7,5},{8,10},{9,11},{10,... | collective-permute-start | bytes 442376 | tf_op jit(solution)/shard_map/ppermute | solution.py:426
  137.1 16.2 %collective-permute-start.60 = (bf16[9,16,512]{2,1,0:T(8,128)(2,1)S(1)}, bf16[9,16,512]{2,1,0:T(8,128)(2,1)S(1)}, u32[]{:S(2)}, u32[]{:S(2)}) collective-permute-start(bf16[9,16,512]{2,1,0:T(8,128)(2,1)S(1)} %get-tuple-element.173), channel_id=1, source_target_pairs={{0,4},{1,5},{2,6},{3,7},{4,0},{5,1},{6,2},{7,3},{8,12},{9,13},{10,... | collective-permute-start | bytes 442376 | tf_op jit(solution)/shard_map/ppermute | solution.py:426
  139.6 13.7 %collective-permute-start.61 = (bf16[9,16,512]{2,1,0:T(8,128)(2,1)S(1)}, bf16[9,16,512]{2,1,0:T(8,128)(2,1)S(1)}, u32[]{:S(2)}, u32[]{:S(2)}) collective-permute-start(bf16[9,16,512]{2,1,0:T(8,128)(2,1)S(1)} %get-tuple-element.174), channel_id=1, source_target_pairs={{0,6},{1,7},{2,4},{3,5},{4,2},{5,3},{6,0},{7,1},{8,14},{9,15},{10,... | collective-permute-start | bytes 442376 | tf_op jit(solution)/shard_map/ppermute | solution.py:426
  141.6 5.5 %collective-permute-start.50 = (bf16[2,10,16,256]{3,2,1,0:T(8,128)(2,1)S(1)}, bf16[2,10,16,256]{3,2,1,0:T(8,128)(2,1)S(1)}, u32[]{:S(2)}, u32[]{:S(2)}) collective-permute-start(bf16[2,10,16,256]{3,2,1,0:T(8,128)(2,1)S(1)} %slice.119), channel_id=1, source_target_pairs={{0,8},{8,0},{16,24},{24,16},{1,9},{9,1},{17,25},{25,17},{2,10},{10... | collective-permute-start | bytes 491528 | tf_op jit(solution)/shard_map/ppermute | solution.py:426
  143.3 5.4 %collective-permute-start.49 = (bf16[2,10,16,256]{3,2,1,0:T(8,128)(2,1)S(1)}, bf16[2,10,16,256]{3,2,1,0:T(8,128)(2,1)S(1)}, u32[]{:S(2)}, u32[]{:S(2)}) collective-permute-start(bf16[2,10,16,256]{3,2,1,0:T(8,128)(2,1)S(1)} %slice.115), channel_id=1, source_target_pairs={{0,16},{8,24},{16,0},{24,8},{1,17},{9,25},{17,1},{25,9},{2,18},{10... | collective-permute-start | bytes 491528 | tf_op jit(solution)/shard_map/ppermute | solution.py:426
  148.8 6.7 %collective-permute-start.51 = (bf16[10,16,256]{2,1,0:T(8,128)(2,1)S(1)}, bf16[10,16,256]{2,1,0:T(8,128)(2,1)S(1)}, u32[]{:S(2)}, u32[]{:S(2)}) collective-permute-start(bf16[10,16,256]{2,1,0:T(8,128)(2,1)S(1)} %get-tuple-element.159), channel_id=1, source_target_pairs={{0,2},{1,3},{2,0},{3,1},{4,6},{5,7},{6,4},{7,5},{8,10},{9,11},{10,... | collective-permute-start | bytes 245768 | tf_op jit(solution)/shard_map/ppermute | solution.py:426
  150.8 7.4 %collective-permute-start.52 = (bf16[10,16,256]{2,1,0:T(8,128)(2,1)S(1)}, bf16[10,16,256]{2,1,0:T(8,128)(2,1)S(1)}, u32[]{:S(2)}, u32[]{:S(2)}) collective-permute-start(bf16[10,16,256]{2,1,0:T(8,128)(2,1)S(1)} %get-tuple-element.160), channel_id=1, source_target_pairs={{0,4},{1,5},{2,6},{3,7},{4,0},{5,1},{6,2},{7,3},{8,12},{9,13},{10,... | collective-permute-start | bytes 245768 | tf_op jit(solution)/shard_map/ppermute | solution.py:426
  151.3 6.9 %collective-permute-start.53 = (bf16[10,16,256]{2,1,0:T(8,128)(2,1)S(1)}, bf16[10,16,256]{2,1,0:T(8,128)(2,1)S(1)}, u32[]{:S(2)}, u32[]{:S(2)}) collective-permute-start(bf16[10,16,256]{2,1,0:T(8,128)(2,1)S(1)} %get-tuple-element.161), channel_id=1, source_target_pairs={{0,6},{1,7},{2,4},{3,5},{4,2},{5,3},{6,0},{7,1},{8,14},{9,15},{10,... | collective-permute-start | bytes 245768 | tf_op jit(solution)/shard_map/ppermute | solution.py:426
  153.4 7.4 %collective-permute-start.64 = (bf16[9,16,512]{2,1,0:T(8,128)(2,1)S(1)}, bf16[9,16,512]{2,1,0:T(8,128)(2,1)S(1)}, u32[]{:S(2)}, u32[]{:S(2)}) collective-permute-start(bf16[9,16,512]{2,1,0:T(8,128)(2,1)S(1)} %fusion.2.refs_0_), channel_id=1, source_target_pairs={{0,24},{8,16},{16,8},{24,0},{1,25},{9,17},{17,9},{25,1},{2,26},{10... | collective-permute-start | bytes 442376 | tf_op jit(solution)/shard_map/ppermute | solution.py:426
  154.6 8.2 %collective-permute-start.63 = (bf16[9,16,512]{2,1,0:T(8,128)(2,1)S(1)}, bf16[9,16,512]{2,1,0:T(8,128)(2,1)S(1)}, u32[]{:S(2)}, u32[]{:S(2)}) collective-permute-start(bf16[9,16,512]{2,1,0:T(8,128)(2,1)S(1)} %fusion.2.refs_0_), channel_id=1, source_target_pairs={{0,16},{8,24},{16,0},{24,8},{1,17},{9,25},{17,1},{25,9},{2,18},{10... | collective-permute-start | bytes 442376 | tf_op jit(solution)/shard_map/ppermute | solution.py:426
  155.5 7.4 %collective-permute-start.62 = (bf16[9,16,512]{2,1,0:T(8,128)(2,1)S(1)}, bf16[9,16,512]{2,1,0:T(8,128)(2,1)S(1)}, u32[]{:S(2)}, u32[]{:S(2)}) collective-permute-start(bf16[9,16,512]{2,1,0:T(8,128)(2,1)S(1)} %fusion.2.refs_0_), channel_id=1, source_target_pairs={{0,8},{8,0},{16,24},{24,16},{1,9},{9,1},{17,25},{25,17},{2,10},{10... | collective-permute-start | bytes 442376 | tf_op jit(solution)/shard_map/ppermute | solution.py:426
  158.3 6.2 %collective-permute-start.56 = (bf16[10,16,256]{2,1,0:T(8,128)(2,1)S(1)}, bf16[10,16,256]{2,1,0:T(8,128)(2,1)S(1)}, u32[]{:S(2)}, u32[]{:S(2)}) collective-permute-start(bf16[10,16,256]{2,1,0:T(8,128)(2,1)S(1)} %add_convert_fusion.refs_0_), channel_id=1, source_target_pairs={{0,24},{8,16},{16,8},{24,0},{1,25},{9,17},{17,9},{25,1},{2,26},{10... | collective-permute-start | bytes 245768 | tf_op jit(solution)/shard_map/ppermute | solution.py:426
  159.5 5.1 %collective-permute-start.55 = (bf16[10,16,256]{2,1,0:T(8,128)(2,1)S(1)}, bf16[10,16,256]{2,1,0:T(8,128)(2,1)S(1)}, u32[]{:S(2)}, u32[]{:S(2)}) collective-permute-start(bf16[10,16,256]{2,1,0:T(8,128)(2,1)S(1)} %add_convert_fusion.refs_0_), channel_id=1, source_target_pairs={{0,16},{8,24},{16,0},{24,8},{1,17},{9,25},{17,1},{25,9},{2,18},{10... | collective-permute-start | bytes 245768 | tf_op jit(solution)/shard_map/ppermute | solution.py:426
  160.8 4.4 %collective-permute-start.54 = (bf16[10,16,256]{2,1,0:T(8,128)(2,1)S(1)}, bf16[10,16,256]{2,1,0:T(8,128)(2,1)S(1)}, u32[]{:S(2)}, u32[]{:S(2)}) collective-permute-start(bf16[10,16,256]{2,1,0:T(8,128)(2,1)S(1)} %add_convert_fusion.refs_0_), channel_id=1, source_target_pairs={{0,8},{8,0},{16,24},{24,16},{1,9},{9,1},{17,25},{25,17},{2,10},{10... | collective-permute-start | bytes 245768 | tf_op jit(solution)/shard_map/ppermute | solution.py:426
  (18 other events, 48.8 us)
